TPU v7x, 32 devices: a whole 2x2x4 slice. The times are simulated.
32 devices in a mesh: leaf: 8 (over z, y), sep: 4 (over x, core).
Axes of the slice: x: 2, y: 2, z: 4, core: 2. Of those that a mesh axis runs over, the one named last changes fastest.
Arguments:
- leaf_source: float32 [8, 640, 256], P('leaf', 'sep'), may hold values from -6 to 6
- leaf_inverse: float32 [8, 640, 640], P('leaf', 'sep'), as said below
- leaf_update: float32 [8, 384, 640], P('leaf', None, 'sep'), as said below
- row_lists: int32 [8, 384], P('leaf'), may hold values from 0 to 255
- row_counts: int32 [8, 3], P('leaf'), may hold values from 1 to 128, as said below
- separator_source: float32 [8, 256, 256], P('leaf', 'sep'), may hold values from -6 to 6
- separator_inverse: float32 [8, 256, 256], P('leaf'), as said below
- separator_coupling: float32 [8, 256, 256], P('leaf'), may hold values from -0.1875 to 0.1875
Outputs:
- leaf_solution: float32 [8, 640, 256], P('leaf', 'sep')
- separator_solution: float32 [8, 256, 256], P('leaf', 'sep')
Inputs may be any that keep to these rules, and one draw needn't show every extreme that they name: `leaf_inverse`: each leaf's block is lower triangular, zero above the diagonal, with diagonal entries between 0.6 and 1.4. `separator_inverse`: each block is lower triangular, zero above the diagonal, with diagonal entries between 0.6 and 1.4. `leaf_update`: row r of a leaf's block belongs to the leaf's ancestor of level 1 + r // 128. `row_lists`: entry r names a row of the leaf's ancestor of level 1 + r // 128. `row_counts`: at every level some leaf has 128 live rows.
All inputs are finite; a program needn't handle non-finite values.
Results may differ from a plain program's by a relative error of at most 0.00011.
Values sent between devices are 32-bit elements; how exact they have to be, the bound alone decides.
No kernel may reach another device: no remote copies, remote signals or barrier semaphores. Data moves between devices by JAX's collectives and lax.ppermute only.
A program may use at most 64 MiB of HBM per device.

v0:
```python
import jax
import jax.numpy as jnp
from jax import lax
from jax.sharding import PartitionSpec as P

highest = lax.Precision.HIGHEST


def passed_along(x, axis, by):
    peers = lax.axis_size(axis)
    pairs = [(i, i + by) for i in range(peers) if 0 <= i + by < peers]
    return lax.ppermute(x, axis, pairs)


def product(matrix, operand):
    return jnp.dot(matrix, operand, precision=highest, preferred_element_type=jnp.float32)


def product_first(matrix, operand):
    return lax.dot_general(
        matrix,
        operand,
        (((0,), (0,)), ((), ())),
        precision=highest,
        preferred_element_type=jnp.float32,
    )


def tree_pass(payload, offset):
    return passed_along(payload, "leaf", offset)


def sep_rows(payload):
    return lax.all_gather(payload, "sep", axis=0, tiled=True)


def per_device(
    leaf_source,
    leaf_inverse,
    leaf_update,
    row_lists,
    row_counts,
    separator_source,
    separator_inverse,
    separator_coupling,
):
    depth = row_counts.shape[1]
    leaf_index = lax.axis_index("leaf")
    sep_index = lax.axis_index("sep")
    source = leaf_source[0]
    inverse = leaf_inverse[0]
    update = leaf_update[0]
    quarter = separator_source.shape[1]
    full_rows = separator_inverse.shape[1]
    columns = source.shape[1]
    capacity = row_lists.shape[1] // depth
    first_row = sep_index * quarter
    inverse_block = inverse
    leaf_y = product(inverse_block, lax.all_gather(source, "sep", axis=0, tiled=True))
    slot_index = jnp.arange(depth * capacity) % capacity
    limits = jnp.repeat(row_counts[0], capacity)
    live_rows = (slot_index < limits)[:, None]
    update_terms = jnp.where(live_rows, product(update, leaf_y), 0.0)
    targets = row_lists[0].reshape(depth, capacity)
    picker = (jnp.arange(full_rows)[None, :, None] == targets[:, None, :]).astype(jnp.float32)
    densified = jnp.einsum(
        "kwp,kpn->wkn",
        picker,
        update_terms.reshape(depth, capacity, columns),
        precision=highest,
        preferred_element_type=jnp.float32,
    )
    carried = lax.psum_scatter(densified, "sep", scatter_dimension=0, tiled=True)
    own_source = separator_source[0]
    solver_block = separator_inverse[0]
    coupling = separator_coupling[0]
    coupling_rows = lax.dynamic_slice_in_dim(coupling, first_row, quarter, 0)
    solved_down = jnp.zeros((full_rows, columns), jnp.float32)
    for height in range(1, depth + 1):
        upper_slots = carried[:, height - 1 :]
        stride = 2 ** max(height - 2, 0)
        from_left = tree_pass(upper_slots, stride)
        if height == 1:
            from_right = upper_slots
        else:
            from_right = tree_pass(upper_slots, -stride)
        is_owner = leaf_index % 2**height == 2 ** (height - 1)
        carried = carried.at[:, height - 1 :].set(
            jnp.where(is_owner, from_left + from_right, upper_slots)
        )
        residual_full = sep_rows(own_source - carried[:, height - 1])
        solved = product(solver_block, residual_full)
        solved_down = jnp.where(is_owner, solved, solved_down)
        if height < depth:
            carried = carried.at[:, height].add(
                jnp.where(is_owner, product(coupling_rows, solved), 0.0)
            )
    stacked = jnp.zeros(carried.shape, jnp.float32)
    solution_full = jnp.zeros((full_rows, columns), jnp.float32)
    for height in range(depth, 0, -1):
        is_owner = leaf_index % 2**height == 2 ** (height - 1)
        target = solved_down
        if height < depth:
            stride = 2 ** (height - 1)
            upper_slots = stacked[:, height:]
            from_below = tree_pass(upper_slots, stride)
            from_above = tree_pass(upper_slots, -stride)
            right_child = leaf_index // 2**height % 2 == 1
            received = jnp.where(right_child, from_below, from_above)
            stacked = stacked.at[:, height:].set(jnp.where(is_owner, received, upper_slots))
            parent_full = sep_rows(received[:, 0])
            target = solved_down - product_first(coupling, parent_full)
        solution = product_first(solver_block, target)
        solution_full = jnp.where(is_owner, solution, solution_full)
        own_rows = lax.dynamic_slice_in_dim(solution, first_row, quarter, 0)
        stacked = stacked.at[:, height - 1].set(
            jnp.where(is_owner, own_rows, stacked[:, height - 1])
        )
    from_next = tree_pass(stacked, -1)
    ancestors = jnp.where(leaf_index % 2 == 1, stacked, from_next)
    ancestors_full = sep_rows(ancestors)
    picked = jnp.einsum(
        "kwp,wkn->kpn",
        picker,
        ancestors_full,
        precision=highest,
        preferred_element_type=jnp.float32,
    )
    picked = jnp.where(live_rows, picked.reshape(depth * capacity, columns), 0.0)
    leaf_w = leaf_y - product_first(update, picked)
    inverse_block = inverse
    leaf_x = lax.psum_scatter(
        product_first(inverse_block, leaf_w), "sep", scatter_dimension=0, tiled=True
    )
    separator_rows = lax.dynamic_slice_in_dim(solution_full, first_row, quarter, 0)
    return (leaf_x[None], separator_rows[None])


def solution(mesh):
    placed = (
        P("leaf", "sep", None),
        P("leaf", "sep", None),
        P("leaf", None, "sep"),
        P("leaf", None),
        P("leaf", None),
        P("leaf", "sep", None),
        P("leaf", None, None),
        P("leaf", None, None),
    )
    return jax.shard_map(
        per_device,
        mesh=mesh,
        in_specs=placed,
        out_specs=(P("leaf", "sep", None), P("leaf", "sep", None)),
        check_vma=False,
    )
```

profile of v0, /device:TPU:0, one launch (start us, length us, event | category | flops | bytes accessed | tf_op | source)
XLA Modules:
  0.0 196.9 jit_solution(6095485533930869089)
XLA Ops:
  7.2 9.7 %all-gather = f32[1,640,256]{2,1,0:T(8,128)S(1)} all-gather(f32[1,160,256]{2,1,0:T(8,128)} %param.30), channel_id=2, replica_groups=mesh['leaf'=8,'sep'=4] {'sep'}, dimensions={1}, use_global_device_ids=true | all-gather | bytes 819200 | tf_op jit(solution)/shard_map/all_gather | solution.py:59
  16.9 0.7 copy-done.6
  17.6 0.6 fusion.4
  18.6 0.7 fusion
  20.0 0.6 convolution_bitcast_fusion
  20.6 1.3 copy.42
  22.0 0.6 copy-done.7
  22.6 0.6 dynamic-slice.90
  23.9 35.2 %all-reduce.4.cloned.1.call-done = f32[256,3,256]{2,1,0:T(4,128)} async-done(((f32[256,3,256]{2,1,0:T(4,128)}), f32[256,3,256]{2,1,0:T(4,128)}) %all-reduce.4.cloned.1.call-update) | async-done | bytes 786448
  59.0 1.0 constant_dynamic-slice_fusion.3
  60.1 3.4 %collective-permute-start = (f32[64,3,256]{2,0,1:T(8,128)S(1)}, f32[64,3,256]{2,0,1:T(8,128)S(1)}, u32[]{:S(2)}, u32[]{:S(2)}) collective-permute-start(f32[64,3,256]{2,0,1:T(8,128)S(1)} %copy.43), channel_id=1, source_target_pairs={{0,4},{4,8},{8,12},{12,16},{16,20},{20,24},{24,28},{1,5},{5,9},{9,... | collective-permute-start | bytes 589832 | tf_op jit(solution)/shard_map/ppermute | solution.py:12
  63.5 3.6 %collective-permute-done = f32[64,3,256]{2,0,1:T(8,128)S(1)} collective-permute-done((f32[64,3,256]{2,0,1:T(8,128)S(1)}, f32[64,3,256]{2,0,1:T(8,128)S(1)}, u32[]{:S(2)}, u32[]{:S(2)}) %collective-permute-start) | collective-permute-done | bytes 196640 | tf_op jit(solution)/shard_map/ppermute | solution.py:12
  67.2 5.9 %all_gather.22 = f32[256,256]{1,0:T(8,128)S(1)} all-gather(f32[64,256]{1,0:T(8,128)S(1)} %fusion.36), channel_id=1, replica_groups=mesh['leaf'=8,'sep'=4] {'sep'}, dimensions={0}, use_global_device_ids=true | all-gather | bytes 327680 | tf_op jit(solution)/shard_map/all_gather | solution.py:34
  73.1 0.6 fusion.23
  74.5 4.4 %collective-permute-start.1 = (f32[64,2,256]{2,0,1:T(8,128)S(1)}, f32[64,2,256]{2,0,1:T(8,128)S(1)}, u32[]{:S(2)}, u32[]{:S(2)}) collective-permute-start(f32[64,2,256]{2,0,1:T(8,128)S(1)} %slice.250), channel_id=1, source_target_pairs={{0,4},{4,8},{8,12},{12,16},{16,20},{20,24},{24,28},{1,5},{5,9},{9,... | collective-permute-start | bytes 393224 | tf_op jit(solution)/shard_map/ppermute | solution.py:12
  78.9 1.3 collective-permute-start.2
  80.2 1.9 collective-permute-done.1
  82.1 4.8 %collective-permute-done.2 = f32[64,2,256]{2,0,1:T(8,128)S(1)} collective-permute-done((f32[64,2,256]{2,0,1:T(8,128)S(1)}, f32[64,2,256]{2,0,1:T(8,128)S(1)}, u32[]{:S(2)}, u32[]{:S(2)}) %collective-permute-start.2) | collective-permute-done | bytes 131104 | tf_op jit(solution)/shard_map/ppermute | solution.py:12
  87.0 5.8 %all_gather.23 = f32[256,256]{1,0:T(8,128)S(1)} all-gather(f32[64,256]{1,0:T(8,128)S(1)} %fusion.35), channel_id=1, replica_groups=mesh['leaf'=8,'sep'=4] {'sep'}, dimensions={0}, use_global_device_ids=true | all-gather | bytes 327680 | tf_op jit(solution)/shard_map/all_gather | solution.py:34
  92.7 0.6 fusion.21
  93.7 4.2 %collective-permute-start.3 = (f32[64,1,256]{2,0,1:T(8,128)S(1)}, f32[64,1,256]{2,0,1:T(8,128)S(1)}, u32[]{:S(2)}, u32[]{:S(2)}) collective-permute-start(f32[64,1,256]{2,0,1:T(8,128)S(1)} %slice_add_fusion), channel_id=1, source_target_pairs={{0,8},{4,12},{8,16},{12,20},{16,24},{20,28},{1,9},{5,13},{9,17},{1... | collective-permute-start | bytes 196616 | tf_op jit(solution)/shard_map/ppermute | solution.py:12
  98.0 1.3 collective-permute-start.4
  99.9 4.3 %collective-permute-done.4 = f32[64,1,256]{2,0,1:T(8,128)S(1)} collective-permute-done((f32[64,1,256]{2,0,1:T(8,128)S(1)}, f32[64,1,256]{2,0,1:T(8,128)S(1)}, u32[]{:S(2)}, u32[]{:S(2)}) %collective-permute-start.4) | collective-permute-done | bytes 65568 | tf_op jit(solution)/shard_map/ppermute | solution.py:12
  104.2 5.8 %all_gather.24 = f32[256,256]{1,0:T(8,128)S(1)} all-gather(f32[64,256]{1,0:T(8,128)S(1)} %bitcast_subtract_fusion), channel_id=1, replica_groups=mesh['leaf'=8,'sep'=4] {'sep'}, dimensions={0}, use_global_device_ids=true | all-gather | bytes 327680 | tf_op jit(solution)/shard_map/all_gather | solution.py:34
  109.9 0.6 convolution_select_fusion.2
  110.6 0.6 fusion.18
  111.2 3.4 %collective-permute-start.5 = (f32[64,1,256]{2,0,1:T(8,128)S(1)}, f32[64,1,256]{2,0,1:T(8,128)S(1)}, u32[]{:S(2)}, u32[]{:S(2)}) collective-permute-start(f32[64,1,256]{2,0,1:T(8,128)S(1)} %get-tuple-element.144), channel_id=1, source_target_pairs={{0,8},{4,12},{8,16},{12,20},{16,24},{20,28},{1,9},{5,13},{9,17},{1... | collective-permute-start | bytes 196616 | tf_op jit(solution)/shard_map/ppermute | solution.py:12
  114.6 1.3 collective-permute-start.6
  116.5 4.3 %collective-permute-done.6 = f32[64,1,256]{2,0,1:T(8,128)S(1)} collective-permute-done((f32[64,1,256]{2,0,1:T(8,128)S(1)}, f32[64,1,256]{2,0,1:T(8,128)S(1)}, u32[]{:S(2)}, u32[]{:S(2)}) %collective-permute-start.6) | collective-permute-done | bytes 65568 | tf_op jit(solution)/shard_map/ppermute | solution.py:12
  120.8 5.8 %all-gather.1 = f32[256,1,256]{2,1,0:T(1,128)S(1)} all-gather(f32[64,1,256]{2,1,0:T(1,128)S(1)} %copy.46), channel_id=3, replica_groups=mesh['leaf'=8,'sep'=4] {'sep'}, dimensions={0}, use_global_device_ids=true | all-gather | bytes 327680 | tf_op jit(solution)/shard_map/all_gather | solution.py:34
  126.6 0.6 convolution_subtract_fusion.1
  127.2 0.6 fusion.16
  127.9 3.7 %collective-permute-start.7 = (f32[64,2,256]{2,0,1:T(8,128)S(1)}, f32[64,2,256]{2,0,1:T(8,128)S(1)}, u32[]{:S(2)}, u32[]{:S(2)}) collective-permute-start(f32[64,2,256]{2,0,1:T(8,128)S(1)} %slice.254), channel_id=1, source_target_pairs={{0,4},{4,8},{8,12},{12,16},{16,20},{20,24},{24,28},{1,5},{5,9},{9,... | collective-permute-start | bytes 393224 | tf_op jit(solution)/shard_map/ppermute | solution.py:12
  131.6 1.3 collective-permute-start.8
  132.9 1.9 collective-permute-done.7
  134.8 4.1 %collective-permute-done.8 = f32[64,2,256]{2,0,1:T(8,128)S(1)} collective-permute-done((f32[64,2,256]{2,0,1:T(8,128)S(1)}, f32[64,2,256]{2,0,1:T(8,128)S(1)}, u32[]{:S(2)}, u32[]{:S(2)}) %collective-permute-start.8) | collective-permute-done | bytes 131104 | tf_op jit(solution)/shard_map/ppermute | solution.py:12
  139.1 5.8 %all-gather.2 = f32[256,1,256]{2,1,0:T(1,128)S(1)} all-gather(f32[64,1,256]{2,1,0:T(1,128)S(1)} %copy.47), channel_id=4, replica_groups=mesh['leaf'=8,'sep'=4] {'sep'}, dimensions={0}, use_global_device_ids=true | all-gather | bytes 327680 | tf_op jit(solution)/shard_map/all_gather | solution.py:34
  144.9 0.6 convolution_subtract_fusion
  145.5 0.6 fusion.14
  146.1 1.3 collective-permute-start.9
  147.5 8.0 %collective-permute-done.9 = f32[64,3,256]{2,0,1:T(8,128)S(1)} collective-permute-done((f32[64,3,256]{2,0,1:T(8,128)S(1)}, f32[64,3,256]{2,0,1:T(8,128)S(1)}, u32[]{:S(2)}, u32[]{:S(2)}) %collective-permute-start.9) | collective-permute-done | bytes 196640 | tf_op jit(solution)/shard_map/ppermute | solution.py:12
  155.5 8.6 %all_gather.27 = f32[256,3,256]{2,0,1:T(8,128)S(1)} all-gather(f32[64,3,256]{2,0,1:T(8,128)S(1)} %broadcast_select_fusion), channel_id=1, replica_groups=mesh['leaf'=8,'sep'=4] {'sep'}, dimensions={0}, use_global_device_ids=true | all-gather | bytes 983040 | tf_op jit(solution)/shard_map/all_gather | solution.py:34
  165.0 0.8 convolution_bitcast_fusion.1
  165.8 1.1 copy.55
  167.3 0.7 copy.52
  168.0 20.2 %reduce-scatter.4.cloned.1.call-done = f32[160,256]{1,0:T(8,128)} async-done(((f32[640,256]{1,0:T(8,128)}), f32[160,256]{1,0:T(8,128)}) %reduce-scatter.4.cloned.1.call-update) | async-done | bytes 163856
  188.2 1.0 copy.56
  189.3 0.8 copy.51
  (50 shorter events, 5.2 us)
Async XLA Ops:
  7.2 10.5 %copy-start = (f32[1,160,640]{2,1,0:T(8,128)S(1)}, f32[1,160,640]{2,1,0:T(8,128)}, u32[]{:S(2)}) copy-start(f32[1,160,640]{2,1,0:T(8,128)} %param.31) | copy-start | bytes 1228804
  7.2 51.8 %all-reduce.4.cloned.1.call-start = ((), (), s32[]{:S(2)}) async-start(), calls=%async_computation.2 | async-start | bytes 2097152
  16.9 0.7 copy-start.6
  17.6 0.9 copy-start.3
  19.3 0.7 copy-start.5
  21.9 166.3 %reduce-scatter.4.cloned.1.call-start = ((), (), s32[]{:S(2)}) async-start(), calls=%async_computation.1 | async-start | bytes 819200
  22.0 0.7 copy-start.7
  60.1 7.1 %collective-permute-start = (f32[64,3,256]{2,0,1:T(8,128)S(1)}, f32[64,3,256]{2,0,1:T(8,128)S(1)}, u32[]{:S(2)}, u32[]{:S(2)}) collective-permute-start(f32[64,3,256]{2,0,1:T(8,128)S(1)} %copy.43), channel_id=1, source_target_pairs={{0,4},{4,8},{8,12},{12,16},{16,20},{20,24},{24,28},{1,5},{5,9},{9,... | collective-permute-start | bytes 589832 | tf_op jit(solution)/shard_map/ppermute | solution.py:12
  63.5 3.7 %copy-start.4 = (f32[1,64,256]{2,1,0:T(8,128)S(1)}, f32[1,64,256]{2,1,0:T(8,128)}, u32[]{:S(2)}) copy-start(f32[1,64,256]{2,1,0:T(8,128)} %param.35) | copy-start | bytes 196612
  67.2 6.0 %copy-start.1 = (f32[1,256,256]{2,1,0:T(8,128)S(1)}, f32[1,256,256]{2,1,0:T(8,128)}, u32[]{:S(2)}) copy-start(f32[1,256,256]{2,1,0:T(8,128)} %param.36) | copy-start | bytes 786436
  73.1 1.0 copy-start.2
  74.5 7.6 %collective-permute-start.1 = (f32[64,2,256]{2,0,1:T(8,128)S(1)}, f32[64,2,256]{2,0,1:T(8,128)S(1)}, u32[]{:S(2)}, u32[]{:S(2)}) collective-permute-start(f32[64,2,256]{2,0,1:T(8,128)S(1)} %slice.250), channel_id=1, source_target_pairs={{0,4},{4,8},{8,12},{12,16},{16,20},{20,24},{24,28},{1,5},{5,9},{9,... | collective-permute-start | bytes 393224 | tf_op jit(solution)/shard_map/ppermute | solution.py:12
  78.9 8.0 %collective-permute-start.2 = (f32[64,2,256]{2,0,1:T(8,128)S(1)}, f32[64,2,256]{2,0,1:T(8,128)S(1)}, u32[]{:S(2)}, u32[]{:S(2)}) collective-permute-start(f32[64,2,256]{2,0,1:T(8,128)S(1)} %slice.250), channel_id=1, source_target_pairs={{4,0},{8,4},{12,8},{16,12},{20,16},{24,20},{28,24},{5,1},{9,5},{13... | collective-permute-start | bytes 393224 | tf_op jit(solution)/shard_map/ppermute | solution.py:12
  93.7 6.1 %collective-permute-start.3 = (f32[64,1,256]{2,0,1:T(8,128)S(1)}, f32[64,1,256]{2,0,1:T(8,128)S(1)}, u32[]{:S(2)}, u32[]{:S(2)}) collective-permute-start(f32[64,1,256]{2,0,1:T(8,128)S(1)} %slice_add_fusion), channel_id=1, source_target_pairs={{0,8},{4,12},{8,16},{12,20},{16,24},{20,28},{1,9},{5,13},{9,17},{1... | collective-permute-start | bytes 196616 | tf_op jit(solution)/shard_map/ppermute | solution.py:12
  98.0 6.2 %collective-permute-start.4 = (f32[64,1,256]{2,0,1:T(8,128)S(1)}, f32[64,1,256]{2,0,1:T(8,128)S(1)}, u32[]{:S(2)}, u32[]{:S(2)}) collective-permute-start(f32[64,1,256]{2,0,1:T(8,128)S(1)} %slice_add_fusion), channel_id=1, source_target_pairs={{8,0},{12,4},{16,8},{20,12},{24,16},{28,20},{9,1},{13,5},{17,9},{2... | collective-permute-start | bytes 196616 | tf_op jit(solution)/shard_map/ppermute | solution.py:12
  111.2 5.3 %collective-permute-start.5 = (f32[64,1,256]{2,0,1:T(8,128)S(1)}, f32[64,1,256]{2,0,1:T(8,128)S(1)}, u32[]{:S(2)}, u32[]{:S(2)}) collective-permute-start(f32[64,1,256]{2,0,1:T(8,128)S(1)} %get-tuple-element.144), channel_id=1, source_target_pairs={{0,8},{4,12},{8,16},{12,20},{16,24},{20,28},{1,9},{5,13},{9,17},{1... | collective-permute-start | bytes 196616 | tf_op jit(solution)/shard_map/ppermute | solution.py:12
  114.6 6.2 %collective-permute-start.6 = (f32[64,1,256]{2,0,1:T(8,128)S(1)}, f32[64,1,256]{2,0,1:T(8,128)S(1)}, u32[]{:S(2)}, u32[]{:S(2)}) collective-permute-start(f32[64,1,256]{2,0,1:T(8,128)S(1)} %get-tuple-element.144), channel_id=1, source_target_pairs={{8,0},{12,4},{16,8},{20,12},{24,16},{28,20},{9,1},{13,5},{17,9},{2... | collective-permute-start | bytes 196616 | tf_op jit(solution)/shard_map/ppermute | solution.py:12
  127.9 6.9 %collective-permute-start.7 = (f32[64,2,256]{2,0,1:T(8,128)S(1)}, f32[64,2,256]{2,0,1:T(8,128)S(1)}, u32[]{:S(2)}, u32[]{:S(2)}) collective-permute-start(f32[64,2,256]{2,0,1:T(8,128)S(1)} %slice.254), channel_id=1, source_target_pairs={{0,4},{4,8},{8,12},{12,16},{16,20},{20,24},{24,28},{1,5},{5,9},{9,... | collective-permute-start | bytes 393224 | tf_op jit(solution)/shard_map/ppermute | solution.py:12
  131.6 7.4 %collective-permute-start.8 = (f32[64,2,256]{2,0,1:T(8,128)S(1)}, f32[64,2,256]{2,0,1:T(8,128)S(1)}, u32[]{:S(2)}, u32[]{:S(2)}) collective-permute-start(f32[64,2,256]{2,0,1:T(8,128)S(1)} %slice.254), channel_id=1, source_target_pairs={{4,0},{8,4},{12,8},{16,12},{20,16},{24,20},{28,24},{5,1},{9,5},{13... | collective-permute-start | bytes 393224 | tf_op jit(solution)/shard_map/ppermute | solution.py:12
  146.1 9.4 %collective-permute-start.9 = (f32[64,3,256]{2,0,1:T(8,128)S(1)}, f32[64,3,256]{2,0,1:T(8,128)S(1)}, u32[]{:S(2)}, u32[]{:S(2)}) collective-permute-start(f32[64,3,256]{2,0,1:T(8,128)S(1)} %get-tuple-element.136), channel_id=1, source_target_pairs={{4,0},{8,4},{12,8},{16,12},{20,16},{24,20},{28,24},{5,1},{9,5},{13... | collective-permute-start | bytes 589832 | tf_op jit(solution)/shard_map/ppermute | solution.py:12
Sparse Core Ops, SparseCore 0:
  22.0 36.9 all-reduce.3
  167.0 21.1 reduce-scatter.3
where the time goes:
time: 197 us
  waiting for transfers between devices  89.4 us (45%)
  blocking collectives  47.3 us (24%)
  starting transfers between devices  25.6 us (13%)
  between operations  15.2 us (8%)
  local copies, waits for them, and re-layouts  9.71 us (5%)
  matrix products  9.11 us (5%)
    unnamed x4, waiting for transfers between devices  55.4 us
    all_gather x6, blocking collectives, sep_rows(): return lax.all_gather(payload, 'sep', axis=0, tiled=True)  37.6 us
    ppermute x10, waiting for transfers between devices, passed_along(): return lax.ppermute(x, axis, pairs)  34 us
    ppermute x10, starting transfers between devices, passed_along(): return lax.ppermute(x, axis, pairs)  25.6 us
    all_gather x1, blocking collectives, per_device(): lax.all_gather(source, 'sep', axis=0, tiled=True)  9.68 us
    unnamed x25, local copies, waits for them, and re-layouts  8.01 us
    dot_general x7, matrix products, product_first(): lax.dot_general(matrix, operand, (((0,), (0,)), ((), ())), precision=high...  4.26 us
  transfers between devices with their start and end apart: 12, of which 12 were waited for; matrix products, arithmetic and copies ran while one was open for 1% of the time, Pallas kernels for 0%

commit v1 on v0

v1 whole, which is shorter than its diff:
```python
import jax
import jax.numpy as jnp
from jax import lax
from jax.sharding import PartitionSpec as P

precise = lax.Precision.HIGH
axes = ("leaf", "sep")


def contract(left, right, left_dim, right_dim):
    return lax.dot_general(
        left,
        right,
        (((left_dim,), (right_dim,)), ((), ())),
        precision=precise,
        preferred_element_type=jnp.float32,
    )


def swap(payload, leaf_flip, sep_flip):
    leaves, seps = lax.axis_size("leaf"), lax.axis_size("sep")
    pairs = [
        (leaf * seps + sep, (leaf ^ leaf_flip) * seps + (sep ^ sep_flip))
        for leaf in range(leaves)
        for sep in range(seps)
    ]
    return lax.ppermute(payload, axes, pairs)


def pick(array, index):
    return lax.dynamic_index_in_dim(array, index, 0, keepdims=False)


def per_device(
    leaf_source,
    leaf_inverse,
    leaf_update,
    row_lists,
    row_counts,
    separator_source,
    separator_inverse,
    separator_coupling,
):
    depth = row_counts.shape[1]
    leaf = lax.axis_index("leaf")
    sep = lax.axis_index("sep")
    odd = leaf % 2
    far_bit = sep // 2
    near_bit = sep % 2
    source = leaf_source[0]
    inverse = leaf_inverse[0]
    update = leaf_update[0]
    rows, columns = source.shape
    updates = update.shape[0]
    capacity = updates // depth
    order = separator_inverse.shape[1]
    quarter = separator_source.shape[1]
    block = columns // 8

    own_inverse = separator_inverse[0]
    down = contract(separator_coupling[0], own_inverse, 1, 0)
    square = contract(own_inverse, own_inverse, 0, 0)

    far = swap(source, 0, 2)
    near = swap(source, 0, 1)
    far_near = swap(far, 0, 1)

    def inverse_part(flip):
        return lax.dynamic_slice_in_dim(inverse, (sep ^ flip) * rows, rows, 1)

    leaf_y = contract(inverse_part(0), source, 1, 0) + contract(inverse_part(1), near, 1, 0)
    leaf_y = leaf_y + contract(inverse_part(2), far, 1, 0)
    leaf_y = leaf_y + contract(inverse_part(3), far_near, 1, 0)

    slot_index = jnp.arange(updates) % capacity
    live = slot_index < jnp.repeat(row_counts[0], capacity)
    listed = jnp.where(live, row_lists[0], -1).astype(jnp.float32)
    list_rows = -(-updates // (8 * order)) * 8
    listed_block = jnp.pad(listed, (0, list_rows * order - updates)).reshape(list_rows, order)
    carry = jnp.where(near_bit == 0, down, square)
    received = swap(jnp.concatenate([carry, listed_block], 0), 1, 0)
    listed_other = received[order:].reshape(-1)[:updates]
    received = received[:order]
    halves = [jnp.where(odd == 1, carry, received)]
    carry = jnp.where(odd == 1, received, carry)
    for level in range(2, depth + 1):
        received = swap(carry, 2 ** (level - 1), 0)
        upper = leaf // 2 ** (level - 1) % 2 == 1
        halves.append(jnp.where(upper, carry, received))
        carry = jnp.where(upper, received, carry)
    downs, squares = [], []
    for half in halves:
        other = swap(half, 0, 1)
        downs.append(jnp.where(near_bit == 0, half, other))
        squares.append(jnp.where(near_bit == 0, other, half))

    level_base = jnp.repeat(jnp.arange(depth) * order, capacity)
    place = jnp.arange(depth * order)[:, None]

    def one_hot(lists):
        target = jnp.where(lists >= 0, lists.astype(jnp.int32) + level_base, -1)
        return (place == target[None, :]).astype(jnp.float32)

    hot = one_hot(listed)
    hot_other = one_hot(listed_other)

    own_rows = jnp.transpose(separator_source[0]).reshape(2, columns // 2, quarter)
    kept = pick(own_rows, near_bit)
    passed = swap(pick(own_rows, 1 - near_bit), 0, 1)
    own_pair = jnp.where(
        near_bit == 0,
        jnp.concatenate([kept, passed], 1),
        jnp.concatenate([passed, kept], 1),
    )

    terms = contract(leaf_y, update, 0, 1).reshape(2, columns // 2, updates)
    terms = pick(terms, near_bit) + swap(pick(terms, 1 - near_bit), 0, 1)
    message = jnp.concatenate([terms, own_pair], 1).reshape(4, block, updates + 2 * quarter)
    here = 2 * odd + far_bit
    by_both = swap(pick(message, here ^ 3), 1, 2)
    by_far = swap(pick(message, here ^ 1), 0, 2)
    by_odd = swap(pick(message, here ^ 2), 1, 0)
    mine = pick(message, here)

    def joined(first, second):
        total = first[:, :updates] + second[:, :updates]
        one, two = first[:, updates:], second[:, updates:]
        ordered = jnp.where(
            far_bit == 0, jnp.concatenate([one, two], 1), jnp.concatenate([two, one], 1)
        )
        return total, ordered

    total, own_source = joined(mine, by_far)
    total_other, other_source = joined(by_odd, by_both)
    gathered = contract(total, hot, 1, 1) + contract(total_other, hot_other, 1, 1)
    odd_source = jnp.where(odd == 1, own_source, other_source)
    even_source = jnp.where(odd == 1, other_source, own_source)
    even_leaf = leaf - odd

    def is_level(index, level):
        return index % 2**level == 2 ** (level - 1)

    slots = [odd_source - gathered[:, :order]]
    for level in range(2, depth + 1):
        piece = gathered[:, (level - 1) * order : level * order]
        slots.append(jnp.where(is_level(even_leaf, level), even_source, 0.0) - piece)

    partial = []
    for level in range(1, depth + 1):
        if level > 1:
            stacked = jnp.concatenate(slots[level - 1 :], 1)
            stacked = stacked + swap(stacked, 2 ** (level - 1), 0)
            for upper in range(level, depth + 1):
                start = (upper - level) * order
                slots[upper - 1] = stacked[:, start : start + order]
        residual = slots[level - 1]
        partial.append(contract(residual, squares[level - 1], 1, 0))
        if level < depth:
            slots[level] = slots[level] - contract(residual, downs[level - 1], 1, 1)

    solved = [None] * depth
    solved[depth - 1] = partial[depth - 1]
    for level in range(depth - 1, 0, -1):
        solved[level - 1] = partial[level - 1] - contract(solved[level], downs[level - 1], 1, 0)
    every = jnp.concatenate(solved, 1)
    even_solved = jnp.zeros_like(solved[0])
    for level in range(2, depth + 1):
        even_solved = jnp.where(is_level(even_leaf, level), solved[level - 1], even_solved)
    own_solved = jnp.where(odd == 1, solved[0], even_solved).reshape(block, 2, 2 * quarter)
    other_solved = jnp.where(odd == 1, even_solved, solved[0]).reshape(block, 2, 2 * quarter)

    def rows_of(array, bit):
        return lax.dynamic_index_in_dim(array, bit, 1, keepdims=False)

    picked = contract(every, hot, 1, 0)
    picked_other = contract(every, hot_other, 1, 0)
    to_both = jnp.concatenate([picked_other, rows_of(other_solved, 1 - far_bit)], 1)
    to_far = jnp.concatenate([picked, rows_of(own_solved, 1 - far_bit)], 1)
    to_odd = jnp.concatenate([picked_other, rows_of(other_solved, far_bit)], 1)
    stay = jnp.concatenate([picked, rows_of(own_solved, far_bit)], 1)
    both = swap(to_both, 1, 2)
    beyond = swap(to_far, 0, 2)
    beside = swap(to_odd, 1, 0)
    group = jnp.stack([stay, beyond, beside, both])
    group = jnp.where(far_bit == 0, group, group[jnp.array([1, 0, 3, 2])])
    group = jnp.where(odd == 0, group, group[jnp.array([2, 3, 0, 1])])
    group = group.reshape(columns // 2, updates + 2 * quarter)
    group_other = swap(group, 0, 1)

    parts = jnp.concatenate(
        [contract(inverse, update, 0, 1), contract(inverse, leaf_y, 0, 0)], 1
    ).reshape(2, 2, rows, updates + columns)
    parts = lax.dynamic_index_in_dim(parts, near_bit, 1, keepdims=False) + swap(
        lax.dynamic_index_in_dim(parts, 1 - near_bit, 1, keepdims=False), 0, 1
    )
    parts = pick(parts, far_bit) + swap(pick(parts, 1 - far_bit), 0, 2)
    base = parts[:, updates:]
    last = jnp.concatenate(
        [
            jnp.pad(-parts[:, :updates], ((0, 0), (0, 2 * quarter))),
            (
                jnp.arange(updates + 2 * quarter)[None, :]
                == updates + near_bit * quarter + jnp.arange(quarter)[:, None]
            ).astype(jnp.float32),
        ],
        0,
    )
    ours = contract(last, group, 1, 1)
    theirs = contract(last, group_other, 1, 1)
    out = jnp.where(
        near_bit == 0,
        jnp.concatenate([ours, theirs], 1),
        jnp.concatenate([theirs, ours], 1),
    )
    return ((base + out[:rows])[None], out[rows:][None])


def solution(mesh):
    placed = (
        P("leaf", "sep", None),
        P("leaf", "sep", None),
        P("leaf", None, "sep"),
        P("leaf", None),
        P("leaf", None),
        P("leaf", "sep", None),
        P("leaf", None, None),
        P("leaf", None, None),
    )
    return jax.shard_map(
        per_device,
        mesh=mesh,
        in_specs=placed,
        out_specs=(P("leaf", "sep", None), P("leaf", "sep", None)),
        check_vma=False,
    )
```

time: 197 us -> 71.7 us (0.36)
  waiting for transfers between devices: 89.4 us -> 26.7 us
  blocking collectives: 47.3 us -> 0 us
  between operations: 15.2 us -> 1.39 us
  other arithmetic: 0.45 us -> 6.89 us
  starting transfers between devices: 25.6 us -> 20.8 us
  local copies, waits for them, and re-layouts: 9.71 us -> 7.07 us
    unnamed x4 -> x0, waiting for transfers between devices: 55.4 us -> none
    all_gather x7 -> x0, blocking collectives: 47.3 us -> none  [the longest x6 37.6 us: sep_rows(): return lax.all_gather(payload, 'sep', axis=0, tiled=True)]
    ppermute x10 -> x22, waiting for transfers between devices: 34 us -> 26.7 us  [swap(): return lax.ppermute(payload, axes, pairs)]
    unnamed x25 -> x23, local copies, waits for them, and re-layouts: 8.01 us -> 0.79 us
    ppermute x10 -> x22, starting transfers between devices: 25.6 us -> 20.8 us  [swap(): return lax.ppermute(payload, axes, pairs)]
    concatenate x0 -> x1, local copies, waits for them, and re-layouts: none -> 2.09 us  [per_device(): jnp.concatenate([contract(inverse, update, 0, 1), contract(inverse, leaf_...]
    dot_general x16 -> x22, matrix products: 9.11 us -> 8.54 us  [contract(): lax.dot_general(left, right, (((left_dim,), (right_dim,)), ((), ())), pre...]
  transfers between devices with their start and end apart: 12 -> 22, of which waited for: 12 -> 10; matrix products, arithmetic and copies ran while one was open for 1% -> 27% of each run, Pallas kernels for 0% -> 0%
where the time goes in v1:
time: 71.7 us; the launch traced here: 71.4 us
  waiting for transfers between devices  26.7 us (37%)
  starting transfers between devices  20.8 us (29%)
  matrix products  8.54 us (12%)
  local copies, waits for them, and re-layouts  7.07 us (10%)
  other arithmetic  6.89 us (10%)
  between operations  1.39 us (2%)
    ppermute x22, waiting for transfers between devices, swap(): return lax.ppermute(payload, axes, pairs)  26.7 us
    ppermute x22, starting transfers between devices, swap(): return lax.ppermute(payload, axes, pairs)  20.8 us
    dot_general x22, matrix products, contract(): lax.dot_general(left, right, (((left_dim,), (right_dim,)), ((), ())), pre...  8.54 us
    concatenate x1, local copies, waits for them, and re-layouts, per_device(): jnp.concatenate([contract(inverse, update, 0, 1), contract(inverse, leaf_...  2.09 us
  transfers between devices with their start and end apart: 22, of which 10 were waited for; matrix products, arithmetic and copies ran while one was open for 27% of the time, Pallas kernels for 0%

profile of v1, /device:TPU:0, one launch (start us, length us, event | category | flops | bytes accessed | tf_op | source)
XLA Modules:
  0.0 71.4 jit_solution(6364240012042943451)
XLA Ops:
  0.7 0.5 collective-permute-start
  1.2 2.6 %collective-permute-start.1 = (f32[160,256]{1,0:T(8,128)}, f32[160,256]{1,0:T(8,128)S(1)}, u32[]{:S(2)}, u32[]{:S(2)}) collective-permute-start(f32[160,256]{1,0:T(8,128)} %bitcast.139), channel_id=1, source_target_pairs={{0,2},{1,3},{2,0},{3,1},{4,6},{5,7},{6,4},{7,5},{8,10},{9,11},{10,... | collective-permute-start | bytes 491528 | tf_op jit(solution)/shard_map/ppermute | solution.py:27
  3.7 0.9 %reshape.89 = f32[2,128,64]{1,0,2:T(2,128)S(1)} reshape(f32[256,64]{0,1:T(8,128)} %bitcast.141) | data formatting | bytes 131072 | tf_op jit(solution)/shard_map/reshape | solution.py:107
  5.0 0.7 %broadcast_bitcast_fusion = (s32[1,1,3,128]{3,2,1,0:T(4,128)S(1)}, s32[1,1,3,128]{3,2,1,0:T(4,128)S(1)}) fusion(s32[3]{0:T(128)S(1)} %iota_multiply_fusion, s32[3]{0:T(128)} %bitcast.147), kind=kLoop, calls=%fused_computation.143 | loop fusion | bytes 3096
  5.8 0.7 fusion.68
  6.5 0.7 %select_convert_fusion = f32[384]{0:T(512)S(1)} fusion(s32[384]{0:T(512)S(1)} %get-tuple-element.3, s32[3]{0:T(128)} %bitcast.148), kind=kLoop, calls=%fused_computation.136 | loop fusion | flops 3456 | bytes 3084 | tf_op jit(solution)/shard_map/convert_element_type | solution.py:77
  7.2 1.3 %fusion.15 = f32[256,256]{1,0:T(8,128)S(1)} fusion(f32[1,256,256]{2,1,0:T(8,128)} %param.16, f32[1,256,256]{2,1,0:T(8,128)} %param.17), kind=kOutput, calls=%fused_computation.36 | convolution fusion | flops 100663296 | bytes 786432 | tf_op jit(solution)/shard_map/dot_general | solution.py:11
  8.6 0.4 convolution_select_fusion
  9.0 1.6 %collective-permute-start.10 = (f32[264,256]{1,0:T(8,128)S(1)}, f32[264,256]{1,0:T(8,128)S(1)}, u32[]{:S(2)}, u32[]{:S(2)}) collective-permute-start(f32[264,256]{1,0:T(8,128)S(1)} %pad_maximum_fusion.1), channel_id=1, source_target_pairs={{0,4},{1,5},{2,6},{3,7},{4,0},{5,1},{6,2},{7,3},{8,12},{9,13},{10,... | collective-permute-start | bytes 811016 | tf_op jit(solution)/shard_map/ppermute | solution.py:27
  10.9 0.7 fusion.10
  11.7 0.6 pad_clamp_fusion.1
  13.4 4.5 %collective-permute-done.10 = f32[264,256]{1,0:T(8,128)S(1)} collective-permute-done((f32[264,256]{1,0:T(8,128)S(1)}, f32[264,256]{1,0:T(8,128)S(1)}, u32[]{:S(2)}, u32[]{:S(2)}) %collective-permute-start.10) | collective-permute-done | bytes 270368 | tf_op jit(solution)/shard_map/ppermute | solution.py:27
  18.0 1.6 %collective-permute-start.13 = (f32[256,256]{1,0:T(8,128)S(1)}, f32[256,256]{1,0:T(8,128)S(1)}, u32[]{:S(2)}, u32[]{:S(2)}) collective-permute-start(f32[256,256]{1,0:T(8,128)S(1)} %get-tuple-element.5), channel_id=1, source_target_pairs={{0,8},{1,9},{2,10},{3,11},{4,12},{5,13},{6,14},{7,15},{8,0},{9,1},... | collective-permute-start | bytes 786440 | tf_op jit(solution)/shard_map/ppermute | solution.py:27
  20.0 0.4 fusion.22
  20.7 0.5 convolution_bitcast_fusion
  21.2 0.7 %collective-permute-done.5 = f32[128,384]{1,0:T(8,128)S(1)} collective-permute-done((f32[128,384]{1,0:T(8,128)S(1)}, f32[128,384]{1,0:T(8,128)S(1)}, u32[]{:S(2)}, u32[]{:S(2)}) %collective-permute-start.5) | collective-permute-done | bytes 196640 | tf_op jit(solution)/shard_map/ppermute | solution.py:27
  22.0 1.6 %collective-permute-start.8 = (f32[32,512]{1,0:T(8,128)S(1)}, f32[32,512]{1,0:T(8,128)S(1)}, u32[]{:S(2)}, u32[]{:S(2)}) collective-permute-start(f32[32,512]{1,0:T(8,128)S(1)} %get-tuple-element.10), channel_id=1, source_target_pairs={{0,4},{1,5},{2,6},{3,7},{4,0},{5,1},{6,2},{7,3},{8,12},{9,13},{10,... | collective-permute-start | bytes 196616 | tf_op jit(solution)/shard_map/ppermute | solution.py:27
  23.6 0.5 collective-permute-start.9
  24.1 1.5 %collective-permute-start.7 = (f32[32,512]{1,0:T(8,128)S(1)}, f32[32,512]{1,0:T(8,128)S(1)}, u32[]{:S(2)}, u32[]{:S(2)}) collective-permute-start(f32[32,512]{1,0:T(8,128)S(1)} %get-tuple-element.11), channel_id=1, source_target_pairs={{0,2},{1,3},{2,0},{3,1},{4,6},{5,7},{6,4},{7,5},{8,10},{9,11},{10,... | collective-permute-start | bytes 196616 | tf_op jit(solution)/shard_map/ppermute | solution.py:27
  25.6 1.1 %collective-permute-done.13 = f32[256,256]{1,0:T(8,128)S(1)} collective-permute-done((f32[256,256]{1,0:T(8,128)S(1)}, f32[256,256]{1,0:T(8,128)S(1)}, u32[]{:S(2)}, u32[]{:S(2)}) %collective-permute-start.13) | collective-permute-done | bytes 262176 | tf_op jit(solution)/shard_map/ppermute | solution.py:27
  26.7 2.7 %collective-permute-start.16 = (f32[256,256]{1,0:T(8,128)S(1)}, f32[256,256]{1,0:T(8,128)}, u32[]{:S(2)}, u32[]{:S(2)}) collective-permute-start(f32[256,256]{1,0:T(8,128)S(1)} %get-tuple-element.7), channel_id=1, source_target_pairs={{0,16},{1,17},{2,18},{3,19},{4,20},{5,21},{6,22},{7,23},{8,24},{9,... | collective-permute-start | bytes 786440 | tf_op jit(solution)/shard_map/ppermute | solution.py:27
  29.4 0.5 fusion.1
  29.9 0.5 fusion.4
  30.8 1.6 %collective-permute-start.12 = (f32[32,512]{1,0:T(8,128)S(1)}, f32[32,512]{1,0:T(8,128)S(1)}, u32[]{:S(2)}, u32[]{:S(2)}) collective-permute-start(f32[32,512]{1,0:T(8,128)S(1)} %pad_maximum_fusion.11), channel_id=1, source_target_pairs={{0,8},{1,9},{2,10},{3,11},{4,12},{5,13},{6,14},{7,15},{8,0},{9,1},... | collective-permute-start | bytes 196616 | tf_op jit(solution)/shard_map/ppermute | solution.py:27
  32.4 1.3 %pad_maximum_fusion = f32[640,640]{0,1:T(8,128)} fusion(f32[640,256]{0,1:T(8,128)S(1)} %convolution_bitcast_fusion, f32[640,384]{0,1:T(8,128)S(1)} %fusion.10), kind=kLoop, calls=%fused_computation.2 | loop fusion | flops 409600 | bytes 3276800 | tf_op jit(solution)/shard_map/concatenate | solution.py:190
  33.7 2.1 %copy.15 = f32[640,640]{1,0:T(8,128)S(1)} copy(f32[640,640]{0,1:T(8,128)} %pad_maximum_fusion) | data formatting | bytes 3276800 | tf_op jit(solution)/shard_map/concatenate | solution.py:190
  35.9 0.3 collective-permute-done.12
  36.2 5.1 %collective-permute-done.16 = f32[256,256]{1,0:T(8,128)} collective-permute-done((f32[256,256]{1,0:T(8,128)S(1)}, f32[256,256]{1,0:T(8,128)}, u32[]{:S(2)}, u32[]{:S(2)}) %collective-permute-start.16) | collective-permute-done | bytes 262176 | tf_op jit(solution)/shard_map/ppermute | solution.py:27
  41.3 1.0 %broadcast_select_fusion = f32[256,256]{1,0:T(8,128)S(1)} fusion(f32[256,256]{1,0:T(8,128)S(1)} %get-tuple-element.7, f32[256,256]{1,0:T(8,128)} %collective-permute-done.16, pred[]{:T(512)S(6)} %eq.109), kind=kLoop, calls=%fused_computation.71 | loop fusion | flops 65536 | bytes 786433 | tf_op jit(solution)/shard_map/jit(_where)/select_n | solution.py:89
  42.7 1.0 %dynamic-slice_bitcast_fusion = f32[2,160,640]{2,1,0:T(8,128)} fusion(f32[2,2,160,640]{3,2,1,0:T(8,128)S(1)} %bitcast.123, s32[]{:T(128)S(6)} %select_n.274), kind=kLoop, calls=%fused_computation.18 | loop fusion | bytes 1638404 | tf_op jit(solution)/shard_map/jit(dynamic_index_in_dim)/squeeze | solution.py:194
  43.7 0.5 collective-permute-start.3
  44.1 3.9 %collective-permute-done.15 = f32[32,256]{1,0:T(8,128)S(1)} collective-permute-done((f32[32,256]{1,0:T(8,128)S(1)}, f32[32,256]{1,0:T(8,128)S(1)}, u32[]{:S(2)}, u32[]{:S(2)}) %collective-permute-start.15) | collective-permute-done | bytes 32800 | tf_op jit(solution)/shard_map/ppermute | solution.py:27
  49.2 0.4 fusion.2
  49.7 0.6 collective-permute-start.18
  50.3 0.4 fusion
  50.7 1.6 %collective-permute-start.19 = (f32[32,512]{1,0:T(8,128)S(1)}, f32[32,512]{1,0:T(8,128)S(1)}, u32[]{:S(2)}, u32[]{:S(2)}) collective-permute-start(f32[32,512]{1,0:T(8,128)S(1)} %get-tuple-element.18), channel_id=1, source_target_pairs={{0,4},{1,5},{2,6},{3,7},{4,0},{5,1},{6,2},{7,3},{8,12},{9,13},{10,... | collective-permute-start | bytes 196616 | tf_op jit(solution)/shard_map/ppermute | solution.py:27
  52.3 1.4 %collective-permute-start.20 = (f32[32,512]{1,0:T(8,128)S(1)}, f32[32,512]{1,0:T(8,128)S(1)}, u32[]{:S(2)}, u32[]{:S(2)}) collective-permute-start(f32[32,512]{1,0:T(8,128)S(1)} %get-tuple-element.19), channel_id=1, source_target_pairs={{0,6},{1,7},{2,4},{3,5},{4,2},{5,3},{6,0},{7,1},{8,14},{9,15},{10,... | collective-permute-start | bytes 196616 | tf_op jit(solution)/shard_map/ppermute | solution.py:27
  54.0 1.0 %collective-permute-done.19 = f32[32,512]{1,0:T(8,128)S(1)} collective-permute-done((f32[32,512]{1,0:T(8,128)S(1)}, f32[32,512]{1,0:T(8,128)S(1)}, u32[]{:S(2)}, u32[]{:S(2)}) %collective-permute-start.19) | collective-permute-done | bytes 65568 | tf_op jit(solution)/shard_map/ppermute | solution.py:27
  55.0 2.5 %collective-permute-done.20 = f32[32,512]{1,0:T(8,128)S(1)} collective-permute-done((f32[32,512]{1,0:T(8,128)S(1)}, f32[32,512]{1,0:T(8,128)S(1)}, u32[]{:S(2)}, u32[]{:S(2)}) %collective-permute-start.20) | collective-permute-done | bytes 65568 | tf_op jit(solution)/shard_map/ppermute | solution.py:27
  57.5 0.7 gather_fusion
  58.2 1.2 %bitcast_add_fusion = f32[2,160,640]{2,1,0:T(8,128)S(1)} fusion(f32[2,160,640]{2,1,0:T(8,128)} %collective-permute-done.3, f32[2,2,160,640]{3,2,1,0:T(8,128)S(1)} %bitcast.124, s32[]{:T(128)S(6)} %select_n.273), kind=kLoop, calls=%fused_computation.17 | loop fusion | flops 204800 | bytes 2457604 | tf_op jit(solution)/shard_map/add | solution.py:193
  59.5 1.6 %collective-permute-start.4 = (f32[160,640]{1,0:T(8,128)S(1)}, f32[160,640]{1,0:T(8,128)S(1)}, u32[]{:S(2)}, u32[]{:S(2)}) collective-permute-start(f32[160,640]{1,0:T(8,128)S(1)} %dynamic-slice_bitcast_fusion.1), channel_id=1, source_target_pairs={{0,2},{1,3},{2,0},{3,1},{4,6},{5,7},{6,4},{7,5},{8,10},{9,11},{10,... | collective-permute-start | bytes 1228808 | tf_op jit(solution)/shard_map/ppermute | solution.py:27
  61.1 0.6 gather_fusion.1
  61.8 7.4 %collective-permute-done.4 = f32[160,640]{1,0:T(8,128)S(1)} collective-permute-done((f32[160,640]{1,0:T(8,128)S(1)}, f32[160,640]{1,0:T(8,128)S(1)}, u32[]{:S(2)}, u32[]{:S(2)}) %collective-permute-start.4) | collective-permute-done | bytes 409632 | tf_op jit(solution)/shard_map/ppermute | solution.py:27
  69.3 0.3 fusion.13
  69.7 0.3 fusion.12
  70.0 0.7 fusion.31
  70.7 0.6 slice_bitcast_fusion
  (93 shorter events, 5.1 us)
Async XLA Ops:
  0.6 10.0 %copy-start = (f32[1,160,640]{2,1,0:T(8,128)S(1)}, f32[1,160,640]{2,1,0:T(8,128)}, u32[]{:S(2)}) copy-start(f32[1,160,640]{2,1,0:T(8,128)} %param.11) | copy-start | bytes 1228804
  0.6 7.9 %copy-start.1 = (f32[1,256,256]{2,1,0:T(8,128)S(1)}, f32[1,256,256]{2,1,0:T(8,128)}, u32[]{:S(2)}) copy-start(f32[1,256,256]{2,1,0:T(8,128)} %param.16) | copy-start | bytes 786436
  0.7 12.1 %collective-permute-start = (f32[160,256]{1,0:T(8,128)}, f32[160,256]{1,0:T(8,128)S(1)}, u32[]{:S(2)}, u32[]{:S(2)}) collective-permute-start(f32[160,256]{1,0:T(8,128)} %bitcast.138), channel_id=1, source_target_pairs={{0,1},{1,0},{2,3},{3,2},{4,5},{5,4},{6,7},{7,6},{8,9},{9,8},{10,11... | collective-permute-start | bytes 491528 | tf_op jit(solution)/shard_map/ppermute | solution.py:27
  1.2 11.5 %collective-permute-start.1 = (f32[160,256]{1,0:T(8,128)}, f32[160,256]{1,0:T(8,128)S(1)}, u32[]{:S(2)}, u32[]{:S(2)}) collective-permute-start(f32[160,256]{1,0:T(8,128)} %bitcast.139), channel_id=1, source_target_pairs={{0,2},{1,3},{2,0},{3,1},{4,6},{5,7},{6,4},{7,5},{8,10},{9,11},{10,... | collective-permute-start | bytes 491528 | tf_op jit(solution)/shard_map/ppermute | solution.py:27
  4.6 6.0 %copy-start.3 = (f32[1,160,256]{2,1,0:T(8,128)S(1)}, f32[1,160,256]{2,1,0:T(8,128)}, u32[]{:S(2)}) copy-start(f32[1,160,256]{2,1,0:T(8,128)} %param.10) | copy-start | bytes 491524
  4.8 7.7 %collective-permute-start.6 = (f32[128,64]{1,0:T(8,128)S(1)}, f32[128,64]{1,0:T(8,128)S(1)}, u32[]{:S(2)}, u32[]{:S(2)}) collective-permute-start(f32[128,64]{1,0:T(8,128)S(1)} %bitcast.140), channel_id=1, source_target_pairs={{0,1},{1,0},{2,3},{3,2},{4,5},{5,4},{6,7},{7,6},{8,9},{9,8},{10,11... | collective-permute-start | bytes 98312 | tf_op jit(solution)/shard_map/ppermute | solution.py:27
  6.5 23.5 %copy-start.4 = (s32[384]{0:T(512)}, s32[384]{0:T(512)S(1)}, u32[]{:S(2)}) copy-start(s32[384]{0:T(512)S(1)} %get-tuple-element.2) | copy-start | bytes 4612
  7.2 3.7 %copy-start.2 = (f32[1,384,160]{1,2,0:T(8,128)S(1)}, f32[1,384,160]{1,2,0:T(8,128)}, u32[]{:S(2)}) copy-start(f32[1,384,160]{1,2,0:T(8,128)} %param.12) | copy-start | bytes 737284
  9.0 2.7 %copy-start.9 = (s32[4]{0:T(128)S(1)}, s32[4]{0:T(128)}, u32[]{:S(2)}) copy-start(s32[4]{0:T(128)} %constant.199) | copy-start | bytes 52
  9.0 8.8 %collective-permute-start.10 = (f32[264,256]{1,0:T(8,128)S(1)}, f32[264,256]{1,0:T(8,128)S(1)}, u32[]{:S(2)}, u32[]{:S(2)}) collective-permute-start(f32[264,256]{1,0:T(8,128)S(1)} %pad_maximum_fusion.1), channel_id=1, source_target_pairs={{0,4},{1,5},{2,6},{3,7},{4,0},{5,1},{6,2},{7,3},{8,12},{9,13},{10,... | collective-permute-start | bytes 811016 | tf_op jit(solution)/shard_map/ppermute | solution.py:27
  12.7 7.0 %collective-permute-start.2 = (f32[160,256]{1,0:T(8,128)S(1)}, f32[160,256]{1,0:T(8,128)S(1)}, u32[]{:S(2)}, u32[]{:S(2)}) collective-permute-start(f32[160,256]{1,0:T(8,128)S(1)} %collective-permute-done.1), channel_id=1, source_target_pairs={{0,1},{1,0},{2,3},{3,2},{4,5},{5,4},{6,7},{7,6},{8,9},{9,8},{10,11... | collective-permute-start | bytes 491528 | tf_op jit(solution)/shard_map/ppermute | solution.py:27
  17.9 12.6 %collective-permute-start.11 = (f32[256,256]{1,0:T(8,128)S(1)}, f32[256,256]{1,0:T(8,128)S(1)}, u32[]{:S(2)}, u32[]{:S(2)}) collective-permute-start(f32[256,256]{1,0:T(8,128)S(1)} %get-tuple-element.4), channel_id=1, source_target_pairs={{0,1},{1,0},{2,3},{3,2},{4,5},{5,4},{6,7},{7,6},{8,9},{9,8},{10,11... | collective-permute-start | bytes 786440 | tf_op jit(solution)/shard_map/ppermute | solution.py:27
  18.0 8.7 %collective-permute-start.13 = (f32[256,256]{1,0:T(8,128)S(1)}, f32[256,256]{1,0:T(8,128)S(1)}, u32[]{:S(2)}, u32[]{:S(2)}) collective-permute-start(f32[256,256]{1,0:T(8,128)S(1)} %get-tuple-element.5), channel_id=1, source_target_pairs={{0,8},{1,9},{2,10},{3,11},{4,12},{5,13},{6,14},{7,15},{8,0},{9,1},... | collective-permute-start | bytes 786440 | tf_op jit(solution)/shard_map/ppermute | solution.py:27
  19.7 9.7 %copy-start.6 = (s32[384]{0:T(512)}, s32[384]{0:T(512)S(1)}, u32[]{:S(2)}) copy-start(s32[384]{0:T(512)S(1)} %fusion.64) | copy-start | bytes 4612
  20.4 1.5 %collective-permute-start.5 = (f32[128,384]{1,0:T(8,128)S(1)}, f32[128,384]{1,0:T(8,128)S(1)}, u32[]{:S(2)}, u32[]{:S(2)}) collective-permute-start(f32[128,384]{1,0:T(8,128)S(1)} %dynamic-slice_bitcast_fusion.2), channel_id=1, source_target_pairs={{0,1},{1,0},{2,3},{3,2},{4,5},{5,4},{6,7},{7,6},{8,9},{9,8},{10,11... | collective-permute-start | bytes 589832 | tf_op jit(solution)/shard_map/ppermute | solution.py:27
  22.0 7.4 %collective-permute-start.8 = (f32[32,512]{1,0:T(8,128)S(1)}, f32[32,512]{1,0:T(8,128)S(1)}, u32[]{:S(2)}, u32[]{:S(2)}) collective-permute-start(f32[32,512]{1,0:T(8,128)S(1)} %get-tuple-element.10), channel_id=1, source_target_pairs={{0,4},{1,5},{2,6},{3,7},{4,0},{5,1},{6,2},{7,3},{8,12},{9,13},{10,... | collective-permute-start | bytes 196616 | tf_op jit(solution)/shard_map/ppermute | solution.py:27
  23.6 5.8 %collective-permute-start.9 = (f32[32,512]{1,0:T(8,128)S(1)}, f32[32,512]{1,0:T(8,128)S(1)}, u32[]{:S(2)}, u32[]{:S(2)}) collective-permute-start(f32[32,512]{1,0:T(8,128)S(1)} %get-tuple-element.9), channel_id=1, source_target_pairs={{0,6},{1,7},{2,4},{3,5},{4,2},{5,3},{6,0},{7,1},{8,14},{9,15},{10,... | collective-permute-start | bytes 196616 | tf_op jit(solution)/shard_map/ppermute | solution.py:27
  24.1 5.8 %collective-permute-start.7 = (f32[32,512]{1,0:T(8,128)S(1)}, f32[32,512]{1,0:T(8,128)S(1)}, u32[]{:S(2)}, u32[]{:S(2)}) collective-permute-start(f32[32,512]{1,0:T(8,128)S(1)} %get-tuple-element.11), channel_id=1, source_target_pairs={{0,2},{1,3},{2,0},{3,1},{4,6},{5,7},{6,4},{7,5},{8,10},{9,11},{10,... | collective-permute-start | bytes 196616 | tf_op jit(solution)/shard_map/ppermute | solution.py:27
  26.7 14.6 %collective-permute-start.16 = (f32[256,256]{1,0:T(8,128)S(1)}, f32[256,256]{1,0:T(8,128)}, u32[]{:S(2)}, u32[]{:S(2)}) collective-permute-start(f32[256,256]{1,0:T(8,128)S(1)} %get-tuple-element.7), channel_id=1, source_target_pairs={{0,16},{1,17},{2,18},{3,19},{4,20},{5,21},{6,22},{7,23},{8,24},{9,... | collective-permute-start | bytes 786440 | tf_op jit(solution)/shard_map/ppermute | solution.py:27
  30.8 5.4 %collective-permute-start.12 = (f32[32,512]{1,0:T(8,128)S(1)}, f32[32,512]{1,0:T(8,128)S(1)}, u32[]{:S(2)}, u32[]{:S(2)}) collective-permute-start(f32[32,512]{1,0:T(8,128)S(1)} %pad_maximum_fusion.11), channel_id=1, source_target_pairs={{0,8},{1,9},{2,10},{3,11},{4,12},{5,13},{6,14},{7,15},{8,0},{9,1},... | collective-permute-start | bytes 196616 | tf_op jit(solution)/shard_map/ppermute | solution.py:27
  35.8 6.5 %collective-permute-start.14 = (f32[256,256]{1,0:T(8,128)S(1)}, f32[256,256]{1,0:T(8,128)S(1)}, u32[]{:S(2)}, u32[]{:S(2)}) collective-permute-start(f32[256,256]{1,0:T(8,128)S(1)} %get-tuple-element.6), channel_id=1, source_target_pairs={{0,1},{1,0},{2,3},{3,2},{4,5},{5,4},{6,7},{7,6},{8,9},{9,8},{10,11... | collective-permute-start | bytes 786440 | tf_op jit(solution)/shard_map/ppermute | solution.py:27
  42.3 5.8 %collective-permute-start.17 = (f32[256,256]{1,0:T(8,128)S(1)}, f32[256,256]{1,0:T(8,128)S(1)}, u32[]{:S(2)}, u32[]{:S(2)}) collective-permute-start(f32[256,256]{1,0:T(8,128)S(1)} %broadcast_select_fusion), channel_id=1, source_target_pairs={{0,1},{1,0},{2,3},{3,2},{4,5},{5,4},{6,7},{7,6},{8,9},{9,8},{10,11... | collective-permute-start | bytes 786440 | tf_op jit(solution)/shard_map/ppermute | solution.py:27
  42.6 5.4 %collective-permute-start.15 = (f32[32,256]{1,0:T(8,128)S(1)}, f32[32,256]{1,0:T(8,128)S(1)}, u32[]{:S(2)}, u32[]{:S(2)}) collective-permute-start(f32[32,256]{1,0:T(8,128)S(1)} %slice_subtract_fusion), channel_id=1, source_target_pairs={{0,16},{1,17},{2,18},{3,19},{4,20},{5,21},{6,22},{7,23},{8,24},{9,... | collective-permute-start | bytes 98312 | tf_op jit(solution)/shard_map/ppermute | solution.py:27
  43.7 14.6 %collective-permute-start.3 = (f32[2,160,640]{2,1,0:T(8,128)}, f32[2,160,640]{2,1,0:T(8,128)}, u32[]{:S(2)}, u32[]{:S(2)}) collective-permute-start(f32[2,160,640]{2,1,0:T(8,128)} %dynamic-slice_bitcast_fusion), channel_id=1, source_target_pairs={{0,1},{1,0},{2,3},{3,2},{4,5},{5,4},{6,7},{7,6},{8,9},{9,8},{10,11... | collective-permute-start | bytes 2457608 | tf_op jit(solution)/shard_map/ppermute | solution.py:27
  48.3 0.9 %copy-start.5 = (s32[384]{0:T(512)S(1)}, s32[384]{0:T(512)}, u32[]{:S(2)}) copy-start(s32[384]{0:T(512)} %copy-done.4) | copy-start | bytes 4612
  48.7 1.6 %copy-start.7 = (s32[384]{0:T(512)S(1)}, s32[384]{0:T(512)}, u32[]{:S(2)}) copy-start(s32[384]{0:T(512)} %copy-done.6) | copy-start | bytes 4612
  49.0 4.8 %copy-start.8 = (s32[4]{0:T(128)S(1)}, s32[4]{0:T(128)}, u32[]{:S(2)}) copy-start(s32[4]{0:T(128)} %constant.200) | copy-start | bytes 52
  49.7 4.3 %collective-permute-start.18 = (f32[32,512]{1,0:T(8,128)S(1)}, f32[32,512]{1,0:T(8,128)S(1)}, u32[]{:S(2)}, u32[]{:S(2)}) collective-permute-start(f32[32,512]{1,0:T(8,128)S(1)} %get-tuple-element.17), channel_id=1, source_target_pairs={{0,2},{1,3},{2,0},{3,1},{4,6},{5,7},{6,4},{7,5},{8,10},{9,11},{10,... | collective-permute-start | bytes 196616 | tf_op jit(solution)/shard_map/ppermute | solution.py:27
  50.7 4.3 %collective-permute-start.19 = (f32[32,512]{1,0:T(8,128)S(1)}, f32[32,512]{1,0:T(8,128)S(1)}, u32[]{:S(2)}, u32[]{:S(2)}) collective-permute-start(f32[32,512]{1,0:T(8,128)S(1)} %get-tuple-element.18), channel_id=1, source_target_pairs={{0,4},{1,5},{2,6},{3,7},{4,0},{5,1},{6,2},{7,3},{8,12},{9,13},{10,... | collective-permute-start | bytes 196616 | tf_op jit(solution)/shard_map/ppermute | solution.py:27
  52.3 5.2 %collective-permute-start.20 = (f32[32,512]{1,0:T(8,128)S(1)}, f32[32,512]{1,0:T(8,128)S(1)}, u32[]{:S(2)}, u32[]{:S(2)}) collective-permute-start(f32[32,512]{1,0:T(8,128)S(1)} %get-tuple-element.19), channel_id=1, source_target_pairs={{0,6},{1,7},{2,4},{3,5},{4,2},{5,3},{6,0},{7,1},{8,14},{9,15},{10,... | collective-permute-start | bytes 196616 | tf_op jit(solution)/shard_map/ppermute | solution.py:27
  59.5 9.7 %collective-permute-start.4 = (f32[160,640]{1,0:T(8,128)S(1)}, f32[160,640]{1,0:T(8,128)S(1)}, u32[]{:S(2)}, u32[]{:S(2)}) collective-permute-start(f32[160,640]{1,0:T(8,128)S(1)} %dynamic-slice_bitcast_fusion.1), channel_id=1, source_target_pairs={{0,2},{1,3},{2,0},{3,1},{4,6},{5,7},{6,4},{7,5},{8,10},{9,11},{10,... | collective-permute-start | bytes 1228808 | tf_op jit(solution)/shard_map/ppermute | solution.py:27
  61.8 7.9 %collective-permute-start.21 = (f32[128,512]{1,0:T(8,128)S(1)}, f32[128,512]{1,0:T(8,128)S(1)}, u32[]{:S(2)}, u32[]{:S(2)}) collective-permute-start(f32[128,512]{1,0:T(8,128)S(1)} %bitcast.125), channel_id=1, source_target_pairs={{0,1},{1,0},{2,3},{3,2},{4,5},{5,4},{6,7},{7,6},{8,9},{9,8},{10,11... | collective-permute-start | bytes 786440 | tf_op jit(solution)/shard_map/ppermute | solution.py:27

commit v2 on v0

v2 whole, which is shorter than its diff:
```python
import functools

import jax
import jax.numpy as jnp
from jax import lax
from jax.experimental import pallas as pl
from jax.experimental.pallas import tpu as pltpu
from jax.sharding import PartitionSpec as P

axes = ("leaf", "sep")
f32 = jnp.float32


def swap(payload, leaf_flip, sep_flip, senders=None):
    leaves, seps = lax.axis_size("leaf"), lax.axis_size("sep")
    pairs = [
        (leaf * seps + sep, (leaf ^ leaf_flip) * seps + (sep ^ sep_flip))
        for leaf in range(leaves)
        for sep in range(seps)
        if senders is None or senders(leaf, sep)
    ]
    return lax.ppermute(payload, axes, pairs)


def after(*arrays):
    return lax.optimization_barrier(arrays)


def dot(left, right, left_dim=1, right_dim=0):
    return lax.dot_general(
        left,
        right,
        (((left_dim,), (right_dim,)), ((), ())),
        precision=lax.Precision.HIGHEST,
        preferred_element_type=f32,
    )


def hot_dot(left, right, right_dim):
    high = left.astype(jnp.bfloat16)
    rest = left - high.astype(f32)
    middle = rest.astype(jnp.bfloat16)
    low = (rest - middle.astype(f32)).astype(jnp.bfloat16)
    pieces = jnp.concatenate([high, middle, low], 0)
    out = lax.dot_general(
        pieces, right, (((1,), (right_dim,)), ((), ())), preferred_element_type=f32
    )
    size = left.shape[0]
    return out[:size] + (out[size : 2 * size] + out[2 * size :])


def stage(body, shapes, *operands, scratch=()):
    vmem = pl.BlockSpec(memory_space=pltpu.VMEM)
    return pl.pallas_call(
        body,
        out_shape=[
            jax.ShapeDtypeStruct(shape, f32) if isinstance(shape, tuple) else shape
            for shape in shapes
        ],
        in_specs=[vmem] * len(operands),
        out_specs=[vmem] * len(shapes),
        scratch_shapes=[pltpu.VMEM(shape, f32) for shape in scratch],
        compiler_params=pltpu.CompilerParams(vmem_limit_bytes=16 * 2**20),
        cost_estimate=pl.CostEstimate(flops=1000, bytes_accessed=1000, transcendentals=0),
    )(*operands)


def place():
    leaf, sep = lax.axis_index("leaf"), lax.axis_index("sep")
    return leaf, sep, lax.rem(leaf, 2), sep // 2, lax.rem(sep, 2)


def per_device(
    leaf_source,
    leaf_inverse,
    leaf_update,
    row_lists,
    row_counts,
    separator_source,
    separator_inverse,
    separator_coupling,
):
    depth = row_counts.shape[1]
    source = leaf_source[0]
    inverse = leaf_inverse[0]
    update = leaf_update[0]
    rows, columns = source.shape
    updates = update.shape[0]
    capacity = updates // depth
    order = separator_inverse.shape[1]
    quarter = separator_source.shape[1]
    half = columns // 2
    block = columns // 8
    width = updates + 2 * quarter
    list_rows = -(-depth // 8) * 8
    leaves = lax.axis_size("leaf")

    def at(index, size):
        return pl.ds(pl.multiple_of(index * size, size), size)

    far = swap(source, 0, 2)
    near = swap(source, 0, 1)

    def operators(coupling_ref, inverse_ref, lists_ref, counts_ref, out_ref):
        near_bit = place()[4]

        @pl.when(near_bit == 0)
        def _():
            out_ref[:order] = dot(coupling_ref[...], inverse_ref[...])

        @pl.when(near_bit == 1)
        def _():
            out_ref[:order] = dot(inverse_ref[...], inverse_ref[...], 0, 0)

        out_ref[order:] = jnp.zeros((list_rows, order), f32)
        slot = lax.broadcasted_iota(jnp.int32, (1, capacity), 1)
        for level in range(depth):
            lists = lists_ref[:, level * capacity : (level + 1) * capacity]
            live = slot < counts_ref[:, level : level + 1]
            out_ref[order + level : order + level + 1, :capacity] = jnp.where(
                live, lists, -1
            ).astype(f32)

    (payload,) = stage(
        operators,
        [(order + list_rows, order)],
        separator_coupling[0],
        separator_inverse[0],
        row_lists,
        row_counts,
    )
    received = swap(payload, 1, 0)

    def own_part(inverse_ref, source_ref, near_ref, rows_ref, y_ref, far_ref, keep_ref, pass_ref, full):
        _, sep, _, far_bit, near_bit = place()
        full[at(near_bit, rows)] = source_ref[...]
        full[at(1 - near_bit, rows)] = near_ref[...]
        first, second = inverse_ref[:, : 2 * rows], inverse_ref[:, 2 * rows :]
        y_ref[...] = dot(jnp.where(far_bit == 0, first, second), full[...])
        far_ref[...] = jnp.where(far_bit == 0, second, first)
        turned = jnp.transpose(rows_ref[...])
        keep_ref[...] = jnp.where(near_bit == 0, turned[:half], turned[half:])
        pass_ref[...] = jnp.where(near_bit == 0, turned[half:], turned[:half])

    payload, near = after(payload, near)
    own_y, inverse_far, rows_keep, rows_pass = stage(
        own_part,
        [(rows, columns), (rows, 2 * rows), (half, quarter), (half, quarter)],
        inverse,
        source,
        near,
        separator_source[0],
        scratch=[(2 * rows, columns)],
    )
    rows_near = swap(rows_pass, 0, 1)

    far, own_y = after(far, own_y)
    far_near = swap(far, 0, 1)

    def leaf_part(own_ref, inverse_ref, far_ref, far_near_ref, update_ref, y_ref, keep_ref, pass_ref, full):
        near_bit = place()[4]
        full[at(near_bit, rows)] = far_ref[...]
        full[at(1 - near_bit, rows)] = far_near_ref[...]
        leaf_y = own_ref[...] + dot(inverse_ref[...], full[...])
        y_ref[...] = leaf_y
        keep = jnp.where(near_bit == 0, leaf_y[:, :half], leaf_y[:, half:])
        passed = jnp.where(near_bit == 0, leaf_y[:, half:], leaf_y[:, :half])
        pass_ref[...] = dot(passed, update_ref[...], 0, 1)
        keep_ref[...] = dot(keep, update_ref[...], 0, 1)

    leaf_y, terms_keep, terms_pass = stage(
        leaf_part,
        [(rows, columns), (half, updates), (half, updates)],
        own_y,
        inverse_far,
        far,
        far_near,
        update,
        scratch=[(2 * rows, columns)],
    )
    terms_near = swap(terms_pass, 0, 1)

    def forward(level):
        def body(carry_ref, received_ref, half_ref, next_ref):
            upper = lax.rem(place()[0] // 2 ** (level - 1), 2) == 1
            carry, received = carry_ref[:order], received_ref[:order]
            half_ref[...] = jnp.where(upper, carry, received)
            next_ref[...] = jnp.where(upper, received, carry)

        return body

    received, terms_keep, rows_near = after(received, terms_keep, rows_near)
    halves, halves_near = [], []
    new_half, carry = stage(forward(1), [(order, order)] * 2, payload, received)
    halves.append(new_half)
    reached = swap(carry, 2, 0)
    halves_near.append(swap(new_half, 0, 1))

    def messages(keep_ref, near_ref, rows_keep_ref, rows_near_ref, *out_refs):
        _, _, odd, far_bit, near_bit = place()
        for flip, out_ref in enumerate(out_refs):
            part = at((2 * odd + far_bit) ^ flip, block)
            out_ref[:, :updates] = keep_ref[part] + near_ref[part]
            kept, passed = rows_keep_ref[part], rows_near_ref[part]
            out_ref[:, updates:] = jnp.where(
                near_bit == 0,
                jnp.concatenate([kept, passed], 1),
                jnp.concatenate([passed, kept], 1),
            )

    mine, to_far, to_odd, to_both = stage(
        messages, [(block, width)] * 4, terms_keep, terms_near, rows_keep, rows_near
    )
    by_both = swap(to_both, 1, 2)
    by_far = swap(to_far, 0, 2)
    by_odd = swap(to_odd, 1, 0)

    def one_hots(own_ref, other_ref, hot_ref):
        rows_of_node = lax.broadcasted_iota(jnp.int32, (order, capacity), 0)
        for level in range(depth):
            for index, ref in enumerate((own_ref, other_ref)):
                lists = ref[order + level : order + level + 1, :capacity].astype(jnp.int32)
                hot = jnp.where(rows_of_node == lists, 1.0, 0.0).astype(jnp.bfloat16)
                hot_ref[level, :, index * capacity : (index + 1) * capacity] = hot

    payload, received, mine = after(payload, received, mine)
    (hots,) = stage(
        one_hots,
        [jax.ShapeDtypeStruct((depth, order, 2 * capacity), jnp.bfloat16)],
        payload,
        received,
    )

    def transposed(inverse_ref, update_ref, y_ref, self_ref, near_ref, work):
        sep = place()[1]
        work[:, :updates] = dot(inverse_ref[...], update_ref[...], 0, 1)
        work[:, updates:] = dot(inverse_ref[...], y_ref[...], 0, 0)
        self_ref[:rows] = work[at(sep, rows)]
        self_ref[rows:] = work[at(sep ^ 2, rows)]
        near_ref[:rows] = work[at(sep ^ 1, rows)]
        near_ref[rows:] = work[at(sep ^ 3, rows)]

    inverse_again, hots = after(inverse, hots)
    self_part, near_part = stage(
        transposed,
        [(2 * rows, updates + columns)] * 2,
        inverse_again,
        update,
        leaf_y,
        scratch=[(inverse.shape[1], updates + columns)],
    )
    near_sum = swap(near_part, 0, 1)

    def root_sent(carry):
        start, size = leaves // 2, leaves // 4
        return [
            swap(carry, flip, 0, lambda leaf, sep: leaf // size == 2 and sep % 2 == 1)
            for flip in (start, start + size)
        ]

    if depth == 3:
        by_root = root_sent(carry)

    by_both, by_far, by_odd, self_part, halves_near[0] = after(
        by_both, by_far, by_odd, self_part, halves_near[0]
    )

    def first_level(mine_ref, far_ref, odd_ref, both_ref, hot_ref, half_ref, other_ref, residual_ref, up_ref):
        leaf, _, odd, far_bit, near_bit = place()

        def joined(one, two):
            first, second = one[:, updates:], two[:, updates:]
            ordered = jnp.where(
                far_bit == 0,
                jnp.concatenate([first, second], 1),
                jnp.concatenate([second, first], 1),
            )
            return one[:, :updates] + two[:, :updates], ordered

        total, own_source = joined(mine_ref[...], far_ref[...])
        total_other, other_source = joined(odd_ref[...], both_ref[...])
        odd_source = jnp.where(odd == 1, own_source, other_source)
        even_source = jnp.where(odd == 1, other_source, own_source)
        even_leaf = leaf - odd

        def gathered(level):
            part = slice((level - 1) * capacity, level * capacity)
            both = jnp.concatenate([total[:, part], total_other[:, part]], 1)
            return hot_dot(both, hot_ref[level - 1], 1)

        down = jnp.where(near_bit == 0, half_ref[...], other_ref[...])
        residual = odd_source - gathered(1)
        residual_ref[...] = residual
        for level in range(2, depth + 1):
            here = lax.rem(even_leaf, 2**level) == 2 ** (level - 1)
            slot = jnp.where(here, even_source, 0.0) - gathered(level)
            if level == 2:
                slot = slot - dot(residual, down, 1, 1)
            up_ref[:, (level - 2) * order : (level - 1) * order] = slot

    residual, going_up = stage(
        first_level,
        [(block, order), (block, (depth - 1) * order)],
        mine,
        by_far,
        by_odd,
        by_both,
        hots,
        halves[0],
        halves_near[0],
    )
    residuals = [residual]

    def next_level(level):
        def body(up_ref, partner_ref, half_ref, other_ref, residual_ref, next_ref):
            near_bit = place()[4]
            total = up_ref[...] + partner_ref[...]
            residual = total[:, :order]
            residual_ref[...] = residual
            down = jnp.where(near_bit == 0, half_ref[...], other_ref[...])
            next_ref[:, :order] = total[:, order : 2 * order] - dot(residual, down, 1, 1)
            if level + 1 < depth:
                next_ref[:, order:] = total[:, 2 * order :]

        return body

    for level in range(2, depth):
        partner = swap(going_up, 2 ** (level - 1), 0)
        reached, going_up, self_part = after(reached, going_up, self_part)
        new_half, carry = stage(forward(level), [(order, order)] * 2, carry, reached)
        halves.append(new_half)
        halves_near.append(swap(new_half, 0, 1))
        if level + 1 < depth:
            reached = swap(carry, 2**level, 0)
        if level == depth - 2:
            by_root = root_sent(carry)
        if level == 2:

            def summed(self_ref, near_ref, own_ref, far_ref):
                own_ref[...] = self_ref[:rows] + near_ref[:rows]
                far_ref[...] = self_ref[rows:] + near_ref[rows:]

            own_sum, far_sum = stage(
                summed, [(rows, updates + columns)] * 2, self_part, near_sum
            )
            from_far = swap(far_sum, 0, 2)
        partner, halves_near[-1], own_sum = after(partner, halves_near[-1], own_sum)
        residual, going_up = stage(
            next_level(level),
            [(block, order), (block, (depth - level) * order)],
            going_up,
            partner,
            halves[-1],
            halves_near[-1],
        )
        residuals.append(residual)
    partner = swap(going_up, 2 ** (depth - 1), 0)

    def beside(*refs):
        near_bit = place()[4]
        out_ref, refs = refs[-1], refs[:-1]
        count = depth - 1
        for level in range(count):
            square = jnp.where(near_bit == 0, refs[2 * count + level][...], refs[count + level][...])
            out_ref[:, level * order : (level + 1) * order] = dot(refs[level][...], square)

    residuals[0], going_up, carry = after(residuals[0], going_up, carry)
    (partial,) = stage(
        beside, [(block, (depth - 1) * order)], *residuals, *halves, *halves_near
    )

    def root_square(carry_ref, *refs):
        leaf = place()[0]
        refs, out_ref = refs[:-1], refs[-1]
        part = leaf // (leaves // 4)
        out_ref[...] = carry_ref[...]
        for index, ref in enumerate(refs):
            @pl.when(part == index)
            def _(ref=ref):
                out_ref[...] = ref[...]

    by_root[0], partial = after(by_root[0], partial)
    (root,) = stage(root_square, [(order, order)], carry, *by_root)
    root_near = swap(root, 0, 1)
    partner, root_near, from_far = after(partner, root_near, from_far)

    def way_down(*refs):
        leaf, _, odd, far_bit, near_bit = place()
        up_ref, partner_ref, partial_ref, hot_ref, root_ref, root_near_ref = refs[:6]
        down_refs, out_refs = refs[6 : 6 + 2 * (depth - 1)], refs[6 + 2 * (depth - 1) :]
        square = jnp.where(near_bit == 1, root_ref[...], root_near_ref[...])
        solved = [None] * depth
        solved[-1] = dot(up_ref[...] + partner_ref[...], square)
        for level in range(depth - 1, 0, -1):
            down = jnp.where(
                near_bit == 0, down_refs[level - 1][...], down_refs[depth - 1 + level - 1][...]
            )
            solved[level - 1] = partial_ref[:, (level - 1) * order : level * order] - dot(
                solved[level], down
            )
        even_leaf = leaf - odd
        even_solved = jnp.zeros_like(solved[0])
        for level in range(2, depth + 1):
            here = lax.rem(even_leaf, 2**level) == 2 ** (level - 1)
            even_solved = jnp.where(here, solved[level - 1], even_solved)
        own_solved = jnp.where(odd == 1, solved[0], even_solved)
        other_solved = jnp.where(odd == 1, even_solved, solved[0])
        for flip, out_ref in enumerate(out_refs):
            rows_of = other_solved if flip >= 2 else own_solved
            bit = far_bit ^ (flip % 2)
            out_ref[:, updates:] = jnp.where(
                bit == 0, rows_of[:, : 2 * quarter], rows_of[:, 2 * quarter :]
            )
        for level in range(depth):
            picked = hot_dot(solved[level], hot_ref[level], 0)
            for flip, out_ref in enumerate(out_refs):
                side = flip // 2
                out_ref[:, level * capacity : (level + 1) * capacity] = picked[
                    :, side * capacity : (side + 1) * capacity
                ]

    stay, to_far, to_odd, to_both = stage(
        way_down,
        [(block, width)] * 4,
        going_up,
        partner,
        partial,
        hots,
        root,
        root_near,
        *halves,
        *halves_near,
    )
    both = swap(to_both, 1, 2)
    beyond = swap(to_far, 0, 2)
    side = swap(to_odd, 1, 0)

    def last_left(own_ref, far_ref, base_ref, left_ref):
        near_bit = place()[4]
        base_ref[...] = own_ref[:, updates:] + far_ref[:, updates:]
        left_ref[:rows, :updates] = -(own_ref[:, :updates] + far_ref[:, :updates])
        left_ref[:rows, updates:] = jnp.zeros((rows, 2 * quarter), f32)
        row = lax.broadcasted_iota(jnp.int32, (quarter, width), 0)
        lane = lax.broadcasted_iota(jnp.int32, (quarter, width), 1)
        left_ref[rows:] = jnp.where(lane == updates + near_bit * quarter + row, 1.0, 0.0)

    own_sum, stay = after(own_sum, stay)
    base, left = stage(last_left, [(rows, columns), (rows + quarter, width)], own_sum, from_far)
    both, beyond, side, left = after(both, beyond, side, left)

    def grouped(*refs):
        _, _, odd, far_bit, _ = place()
        out_ref = refs[-1]
        for flip, ref in enumerate(refs[:-1]):
            out_ref[at((2 * odd + far_bit) ^ flip, block)] = ref[...]

    (group,) = stage(grouped, [(half, width)], stay, beyond, side, both)
    group_near = swap(group, 0, 1)

    def own_columns(left_ref, group_ref, out_ref):
        out_ref[...] = dot(left_ref[...], group_ref[...], 1, 1)

    (ours,) = stage(own_columns, [(rows + quarter, half)], left, group)
    group_near, ours = after(group_near, ours)

    def finish(left_ref, group_ref, ours_ref, base_ref, leaf_ref, rows_ref):
        near_bit = place()[4]
        ours = ours_ref[...]
        theirs = dot(left_ref[...], group_ref[...], 1, 1)
        first = jnp.where(near_bit == 0, ours, theirs)
        second = jnp.where(near_bit == 0, theirs, ours)
        leaf_ref[:, :half] = base_ref[:, :half] + first[:rows]
        leaf_ref[:, half:] = base_ref[:, half:] + second[:rows]
        rows_ref[:, :half] = first[rows:]
        rows_ref[:, half:] = second[rows:]

    leaf_x, separator_rows = stage(
        finish, [(rows, columns), (quarter, columns)], left, group_near, ours, base
    )
    return (leaf_x[None], separator_rows[None])


def solution(mesh):
    placed = (
        P("leaf", "sep", None),
        P("leaf", "sep", None),
        P("leaf", None, "sep"),
        P("leaf", None),
        P("leaf", None),
        P("leaf", "sep", None),
        P("leaf", None, None),
        P("leaf", None, None),
    )
    return jax.shard_map(
        per_device,
        mesh=mesh,
        in_specs=placed,
        out_specs=(P("leaf", "sep", None), P("leaf", "sep", None)),
        check_vma=False,
    )
```

time: 197 us -> 60.8 us (0.31)
  waiting for transfers between devices: 89.4 us -> 26.8 us
  blocking collectives: 47.3 us -> 0 us
  between operations: 15.2 us -> 0.87 us
  Pallas kernels: 0 us -> 9.31 us
  matrix products: 9.11 us -> 0 us
  starting transfers between devices: 25.6 us -> 19.7 us
  local copies, waits for them, and re-layouts: 9.71 us -> 3.85 us
    unnamed x4 -> x0, waiting for transfers between devices: 55.4 us -> none
    all_gather x7 -> x0, blocking collectives: 47.3 us -> none  [the longest x6 37.6 us: sep_rows(): return lax.all_gather(payload, 'sep', axis=0, tiled=True)]
    pallas_call x0 -> x18, Pallas kernels: none -> 9.31 us  [stage(): pl.pallas_call(body, out_shape=[jax.ShapeDtypeStruct(shape, f32) if isins...]
    dot_general x16 -> x0, matrix products: 9.11 us -> none  [the longest x7 4.26 us: product_first(): lax.dot_general(matrix, operand, (((0,), (0,)), ((), ())), precision=high...]
    ppermute x10 -> x23, waiting for transfers between devices: 34 us -> 26.8 us  [swap(): return lax.ppermute(payload, axes, pairs)]
    ppermute x10 -> x23, starting transfers between devices: 25.6 us -> 19.7 us  [swap(): return lax.ppermute(payload, axes, pairs)]
    unnamed x25 -> x17, local copies, waits for them, and re-layouts: 8.01 us -> 3.85 us
  transfers between devices with their start and end apart: 12 -> 23, of which waited for: 12 -> 11; matrix products, arithmetic and copies ran while one was open for 1% -> 0% of each run, Pallas kernels for 0% -> 8%
where the time goes in v2:
time: 60.8 us; the launch traced here: 60.6 us
  waiting for transfers between devices  26.8 us (44%)
  starting transfers between devices  19.7 us (32%)
  Pallas kernels  9.31 us (15%)
  local copies, waits for them, and re-layouts  3.85 us (6%)
  between operations  0.87 us (1%)
    ppermute x23, waiting for transfers between devices, swap(): return lax.ppermute(payload, axes, pairs)  26.8 us
    ppermute x23, starting transfers between devices, swap(): return lax.ppermute(payload, axes, pairs)  19.7 us
    pallas_call x18, Pallas kernels, stage(): pl.pallas_call(body, out_shape=[jax.ShapeDtypeStruct(shape, f32) if isins...  9.31 us
    unnamed x17, local copies, waits for them, and re-layouts  3.85 us
  transfers between devices with their start and end apart: 23, of which 11 were waited for; matrix products, arithmetic and copies ran while one was open for 0% of the time, Pallas kernels for 8%

profile of v2, /device:TPU:0, one launch (start us, length us, event | category | flops | bytes accessed | tf_op | source)
XLA Modules:
  0.0 60.6 jit_solution(12528858056648658968)
XLA Ops:
  0.6 0.5 collective-permute-start
  1.2 2.6 %collective-permute-start.2 = (f32[160,256]{1,0:T(8,128)}, f32[160,256]{1,0:T(8,128)S(1)}, u32[]{:S(2)}, u32[]{:S(2)}) collective-permute-start(f32[160,256]{1,0:T(8,128)} %bitcast.15), channel_id=1, source_target_pairs={{0,2},{1,3},{2,0},{3,1},{4,6},{5,7},{6,4},{7,5},{8,10},{9,11},{10,... | collective-permute-start | bytes 491528 | tf_op jit(solution)/shard_map/ppermute | solution.py:22
  3.7 0.9 %copy-done.1 = f32[1,256,256]{2,1,0:T(8,128)S(1)} copy-done((f32[1,256,256]{2,1,0:T(8,128)S(1)}, f32[1,256,256]{2,1,0:T(8,128)}, u32[]{:S(2)}) %copy-start.1) | copy-done | bytes 262168
  4.7 0.9 %copy-done.2 = f32[1,256,256]{2,1,0:T(8,128)S(1)} copy-done((f32[1,256,256]{2,1,0:T(8,128)S(1)}, f32[1,256,256]{2,1,0:T(8,128)}, u32[]{:S(2)}) %copy-start.2) | copy-done | bytes 262168
  5.6 0.7 %copy-done.5 = s32[1,384]{1,0:T(1,128)S(1)} copy-done((s32[1,384]{1,0:T(1,128)S(1)}, s32[1,384]{1,0:T(1,128)}, u32[]{:S(2)}) %copy-start.5) | copy-done | bytes 1560
  6.3 0.7 %copy-done.6 = s32[1,3]{1,0:T(1,128)S(1)} copy-done((s32[1,3]{1,0:T(1,128)S(1)}, s32[1,3]{1,0:T(1,128)}, u32[]{:S(2)}) %copy-start.6) | copy-done | bytes 36
  7.0 0.5 shard_map.95.own_ref.carry_ref
  7.4 0.4 copy-done.3
  7.9 0.5 shard_map.96
  8.4 0.3 collective-permute-done.2.far_ref
  8.7 1.8 %collective-permute-start.1 = (f32[264,256]{1,0:T(8,128)S(1)}, f32[264,256]{1,0:T(8,128)S(1)}, u32[]{:S(2)}, u32[]{:S(2)}) collective-permute-start(f32[264,256]{1,0:T(8,128)S(1)} %shard_map.95.own_ref.carry_ref), channel_id=1, source_target_pairs={{0,4},{1,5},{2,6},{3,7},{4,0},{5,1},{6,2},{7,3},{8,12},{9,13},{10,... | collective-permute-start | bytes 811016 | tf_op jit(solution)/shard_map/ppermute | solution.py:22
  10.5 0.2 copy.10
  10.7 1.6 %shard_map.97 = (f32[160,256]{1,0:T(8,128)S(1)}, f32[128,384]{1,0:T(8,128)S(1)}, f32[128,384]{1,0:T(8,128)S(1)}) custom-call(f32[160,256]{1,0:T(8,128)S(1)} %get-tuple-element.75.own_ref, f32[160,320]{1,0:T(8,128)S(1)} %get-tuple-element.76.inverse_ref, f32[160,256]{1,0:T(8,128)S(1)} %collective-permute-done.2.far_ref, ...), custom_call_target="tpu_custom_call" | custom-call | flops 1000 | bytes 1000 | tf_op jit(solution)/shard_map/pallas_call | solution.py:54
  12.3 0.3 collective-permute-start.5
  12.6 0.3 collective-permute-start.4
  12.9 1.0 %collective-permute-done.4.rows_near_ref = f32[128,64]{1,0:T(8,128)S(1)} collective-permute-done((f32[128,64]{1,0:T(8,128)S(1)}, f32[128,64]{1,0:T(8,128)S(1)}, u32[]{:S(2)}, u32[]{:S(2)}) %collective-permute-start.4) | collective-permute-done | bytes 32800 | tf_op jit(solution)/shard_map/ppermute | solution.py:22
  13.9 3.7 %collective-permute-done.1.other_ref.received_ref = f32[264,256]{1,0:T(8,128)S(1)} collective-permute-done((f32[264,256]{1,0:T(8,128)S(1)}, f32[264,256]{1,0:T(8,128)S(1)}, u32[]{:S(2)}, u32[]{:S(2)}) %collective-permute-start.1) | collective-permute-done | bytes 270368 | tf_op jit(solution)/shard_map/ppermute | solution.py:22
  17.7 0.1 shard_map.98
  17.8 0.1 shard_map.99.hot_ref.refs_3_
  17.9 1.9 %shard_map.100 = (f32[320,640]{1,0:T(8,128)S(1)}, f32[320,640]{1,0:T(8,128)S(1)}) custom-call(f32[160,640]{1,0:T(8,128)S(1)} %bitcast.11, f32[384,160]{1,0:T(8,128)S(1)} %bitcast.9, f32[160,256]{1,0:T(8,128)S(1)} %get-tuple-element.93.y_ref), custom_call_target="tpu_custom_call" | custom-call | flops 1000 | bytes 1000 | tf_op jit(solution)/shard_map/pallas_call | solution.py:54
  20.0 0.6 collective-permute-start.9
  20.5 1.8 %collective-permute-start.10 = (f32[256,256]{1,0:T(8,128)S(1)}, f32[256,256]{1,0:T(8,128)S(1)}, u32[]{:S(2)}, u32[]{:S(2)}) collective-permute-start(f32[256,256]{1,0:T(8,128)S(1)} %get-tuple-element.102.carry_ref), channel_id=1, source_target_pairs={{0,8},{1,9},{2,10},{3,11},{4,12},{5,13},{6,14},{7,15},{8,0},{9,1},... | collective-permute-start | bytes 786440 | tf_op jit(solution)/shard_map/ppermute | solution.py:22
  22.3 2.4 %collective-permute-start.6 = (f32[32,512]{1,0:T(8,128)S(1)}, f32[32,512]{1,0:T(8,128)S(1)}, u32[]{:S(2)}, u32[]{:S(2)}) collective-permute-start(f32[32,512]{1,0:T(8,128)S(1)} %get-tuple-element.87), channel_id=1, source_target_pairs={{0,6},{1,7},{2,4},{3,5},{4,2},{5,3},{6,0},{7,1},{8,14},{9,15},{10,... | collective-permute-start | bytes 196616 | tf_op jit(solution)/shard_map/ppermute | solution.py:22
  24.8 0.5 collective-permute-start.7
  25.3 2.8 %collective-permute-done.6.both_ref = f32[32,512]{1,0:T(8,128)S(1)} collective-permute-done((f32[32,512]{1,0:T(8,128)S(1)}, f32[32,512]{1,0:T(8,128)S(1)}, u32[]{:S(2)}, u32[]{:S(2)}) %collective-permute-start.6) | collective-permute-done | bytes 65568 | tf_op jit(solution)/shard_map/ppermute | solution.py:22
  28.1 1.5 %collective-permute-start.8 = (f32[32,512]{1,0:T(8,128)S(1)}, f32[32,512]{1,0:T(8,128)S(1)}, u32[]{:S(2)}, u32[]{:S(2)}) collective-permute-start(f32[32,512]{1,0:T(8,128)S(1)} %get-tuple-element.89), channel_id=1, source_target_pairs={{0,4},{1,5},{2,6},{3,7},{4,0},{5,1},{6,2},{7,3},{8,12},{9,13},{10,... | collective-permute-start | bytes 196616 | tf_op jit(solution)/shard_map/ppermute | solution.py:22
  29.7 2.7 %collective-permute-done.8.odd_ref = f32[32,512]{1,0:T(8,128)S(1)} collective-permute-done((f32[32,512]{1,0:T(8,128)S(1)}, f32[32,512]{1,0:T(8,128)S(1)}, u32[]{:S(2)}, u32[]{:S(2)}) %collective-permute-start.8) | collective-permute-done | bytes 65568 | tf_op jit(solution)/shard_map/ppermute | solution.py:22
  32.4 0.6 shard_map.102
  33.2 0.7 %collective-permute-start.15 = (f32[256,256]{1,0:T(8,128)S(1)}, f32[256,256]{1,0:T(8,128)S(1)}, u32[]{:S(2)}, u32[]{:S(2)}) collective-permute-start(f32[256,256]{1,0:T(8,128)S(1)} %get-tuple-element.102.carry_ref), channel_id=1, source_target_pairs={{17,1},{19,3},{21,5},{23,7}} | collective-permute-start | bytes 786440 | tf_op jit(solution)/shard_map/ppermute | solution.py:22
  33.9 0.7 %collective-permute-start.16 = (f32[256,256]{1,0:T(8,128)S(1)}, f32[256,256]{1,0:T(8,128)S(1)}, u32[]{:S(2)}, u32[]{:S(2)}) collective-permute-start(f32[256,256]{1,0:T(8,128)S(1)} %get-tuple-element.102.carry_ref), channel_id=1, source_target_pairs={{17,9},{19,11},{21,13},{23,15}} | collective-permute-start | bytes 786440 | tf_op jit(solution)/shard_map/ppermute | solution.py:22
  34.7 1.1 %collective-permute-start.18 = (f32[160,640]{1,0:T(8,128)S(1)}, f32[160,640]{1,0:T(8,128)S(1)}, u32[]{:S(2)}, u32[]{:S(2)}) collective-permute-start(f32[160,640]{1,0:T(8,128)S(1)} %get-tuple-element.120), channel_id=1, source_target_pairs={{0,2},{1,3},{2,0},{3,1},{4,6},{5,7},{6,4},{7,5},{8,10},{9,11},{10,... | collective-permute-start | bytes 1228808 | tf_op jit(solution)/shard_map/ppermute | solution.py:22
  35.8 0.4 collective-permute-start.11
  36.2 7.0 %collective-permute-done.11.partner_ref = f32[32,512]{1,0:T(8,128)S(1)} collective-permute-done((f32[32,512]{1,0:T(8,128)S(1)}, f32[32,512]{1,0:T(8,128)S(1)}, u32[]{:S(2)}, u32[]{:S(2)}) %collective-permute-start.11) | collective-permute-done | bytes 65568 | tf_op jit(solution)/shard_map/ppermute | solution.py:22
  43.3 0.3 shard_map.105
  43.6 0.4 shard_map.106.refs_2_
  44.1 0.2 collective-permute-start.17
  44.3 0.5 collective-permute-start.14
  44.8 4.4 %collective-permute-done.14.refs_1_ = f32[32,256]{1,0:T(8,128)S(1)} collective-permute-done((f32[32,256]{1,0:T(8,128)S(1)}, f32[32,256]{1,0:T(8,128)S(1)}, u32[]{:S(2)}, u32[]{:S(2)}) %collective-permute-start.14) | collective-permute-done | bytes 32800 | tf_op jit(solution)/shard_map/ppermute | solution.py:22
  49.3 1.1 %shard_map.108 = (f32[32,512]{1,0:T(8,128)S(1)}, f32[32,512]{1,0:T(8,128)S(1)}, f32[32,512]{1,0:T(8,128)S(1)}, f32[32,512]{1,0:T(8,128)S(1)}) custom-call(f32[32,256]{1,0:T(8,128)S(1)} %get-tuple-element.115.refs_0_, f32[32,256]{1,0:T(8,128)S(1)} %collective-permute-done.14.refs_1_, f32[32,512]{1,0:T(8,128)S(1)} %shard_map.106.refs_2_, ...), custom_call_target="tpu_custom_call" | custom-call | flops 1000 | bytes 1000 | tf_op jit(solution)/shard_map/pallas_call | solution.py:54
  50.4 2.1 %collective-permute-start.19 = (f32[32,512]{1,0:T(8,128)S(1)}, f32[32,512]{1,0:T(8,128)S(1)}, u32[]{:S(2)}, u32[]{:S(2)}) collective-permute-start(f32[32,512]{1,0:T(8,128)S(1)} %get-tuple-element.124), channel_id=1, source_target_pairs={{0,6},{1,7},{2,4},{3,5},{4,2},{5,3},{6,0},{7,1},{8,14},{9,15},{10,... | collective-permute-start | bytes 196616 | tf_op jit(solution)/shard_map/ppermute | solution.py:22
  52.5 1.0 %collective-permute-start.20 = (f32[32,512]{1,0:T(8,128)S(1)}, f32[32,512]{1,0:T(8,128)S(1)}, u32[]{:S(2)}, u32[]{:S(2)}) collective-permute-start(f32[32,512]{1,0:T(8,128)S(1)} %get-tuple-element.125), channel_id=1, source_target_pairs={{0,2},{1,3},{2,0},{3,1},{4,6},{5,7},{6,4},{7,5},{8,10},{9,11},{10,... | collective-permute-start | bytes 196616 | tf_op jit(solution)/shard_map/ppermute | solution.py:22
  53.4 0.5 collective-permute-start.21
  54.0 1.7 %collective-permute-done.19.refs_3_ = f32[32,512]{1,0:T(8,128)S(1)} collective-permute-done((f32[32,512]{1,0:T(8,128)S(1)}, f32[32,512]{1,0:T(8,128)S(1)}, u32[]{:S(2)}, u32[]{:S(2)}) %collective-permute-start.19) | collective-permute-done | bytes 65568 | tf_op jit(solution)/shard_map/ppermute | solution.py:22
  55.7 1.0 %collective-permute-done.20.refs_1_ = f32[32,512]{1,0:T(8,128)S(1)} collective-permute-done((f32[32,512]{1,0:T(8,128)S(1)}, f32[32,512]{1,0:T(8,128)S(1)}, u32[]{:S(2)}, u32[]{:S(2)}) %collective-permute-start.20) | collective-permute-done | bytes 65568 | tf_op jit(solution)/shard_map/ppermute | solution.py:22
  56.7 1.0 %collective-permute-done.21.refs_2_ = f32[32,512]{1,0:T(8,128)S(1)} collective-permute-done((f32[32,512]{1,0:T(8,128)S(1)}, f32[32,512]{1,0:T(8,128)S(1)}, u32[]{:S(2)}, u32[]{:S(2)}) %collective-permute-start.21) | collective-permute-done | bytes 65568 | tf_op jit(solution)/shard_map/ppermute | solution.py:22
  57.8 0.6 shard_map.111.ours_ref
  58.4 1.0 %collective-permute-done.22.group_ref = f32[128,512]{1,0:T(8,128)S(1)} collective-permute-done((f32[128,512]{1,0:T(8,128)S(1)}, f32[128,512]{1,0:T(8,128)S(1)}, u32[]{:S(2)}, u32[]{:S(2)}) %collective-permute-start.22) | collective-permute-done | bytes 262176 | tf_op jit(solution)/shard_map/ppermute | solution.py:22
  59.3 1.2 %shard_map.112 = (f32[160,256]{1,0:T(8,128)}, f32[64,256]{1,0:T(8,128)}) custom-call(f32[224,512]{1,0:T(8,128)S(1)} %get-tuple-element.132.left_ref, f32[128,512]{1,0:T(8,128)S(1)} %collective-permute-done.22.group_ref, f32[224,128]{1,0:T(8,128)S(1)} %shard_map.111.ours_ref, f32[160,256]{1,0:T(8,128)S(1)} %get-tuple-element.139.base_ref), custom_call_target="tpu_custom_call" | custom-call | flops 1000 | bytes 1000 | tf_op jit(solution)/shard_map/pallas_call | solution.py:54
  (33 shorter events, 0.6 us)
Async XLA Ops:
  0.6 6.8 %copy-start = (f32[1,160,640]{2,1,0:T(8,128)S(1)}, f32[1,160,640]{2,1,0:T(8,128)}, u32[]{:S(2)}) copy-start(f32[1,160,640]{2,1,0:T(8,128)} %param.9) | copy-start | bytes 1228804
  0.6 6.8 %collective-permute-start = (f32[160,256]{1,0:T(8,128)}, f32[160,256]{1,0:T(8,128)S(1)}, u32[]{:S(2)}, u32[]{:S(2)}) collective-permute-start(f32[160,256]{1,0:T(8,128)} %bitcast.14), channel_id=1, source_target_pairs={{0,1},{1,0},{2,3},{3,2},{4,5},{5,4},{6,7},{7,6},{8,9},{9,8},{10,11... | collective-permute-start | bytes 491528 | tf_op jit(solution)/shard_map/ppermute | solution.py:22
  1.2 7.6 %collective-permute-start.2 = (f32[160,256]{1,0:T(8,128)}, f32[160,256]{1,0:T(8,128)S(1)}, u32[]{:S(2)}, u32[]{:S(2)}) collective-permute-start(f32[160,256]{1,0:T(8,128)} %bitcast.15), channel_id=1, source_target_pairs={{0,2},{1,3},{2,0},{3,1},{4,6},{5,7},{6,4},{7,5},{8,10},{9,11},{10,... | collective-permute-start | bytes 491528 | tf_op jit(solution)/shard_map/ppermute | solution.py:22
  3.7 0.9 %copy-start.1 = (f32[1,256,256]{2,1,0:T(8,128)S(1)}, f32[1,256,256]{2,1,0:T(8,128)}, u32[]{:S(2)}) copy-start(f32[1,256,256]{2,1,0:T(8,128)} %param.15) | copy-start | bytes 786436
  4.7 0.9 %copy-start.2 = (f32[1,256,256]{2,1,0:T(8,128)S(1)}, f32[1,256,256]{2,1,0:T(8,128)}, u32[]{:S(2)}) copy-start(f32[1,256,256]{2,1,0:T(8,128)} %param.14) | copy-start | bytes 786436
  5.6 0.7 %copy-start.5 = (s32[1,384]{1,0:T(1,128)S(1)}, s32[1,384]{1,0:T(1,128)}, u32[]{:S(2)}) copy-start(s32[1,384]{1,0:T(1,128)} %lists_ref.1) | copy-start | bytes 4612
  6.3 0.7 %copy-start.6 = (s32[1,3]{1,0:T(1,128)S(1)}, s32[1,3]{1,0:T(1,128)}, u32[]{:S(2)}) copy-start(s32[1,3]{1,0:T(1,128)} %counts_ref.1) | copy-start | bytes 40
  7.0 0.9 %copy-start.3 = (f32[1,160,256]{2,1,0:T(8,128)S(1)}, f32[1,160,256]{2,1,0:T(8,128)}, u32[]{:S(2)}) copy-start(f32[1,160,256]{2,1,0:T(8,128)} %param.8) | copy-start | bytes 491524
  7.0 0.9 %copy-start.4 = (f32[1,64,256]{2,1,0:T(8,128)S(1)}, f32[1,64,256]{2,1,0:T(8,128)}, u32[]{:S(2)}) copy-start(f32[1,64,256]{2,1,0:T(8,128)} %param.13) | copy-start | bytes 196612
  7.9 2.6 %copy-start.7 = (f32[1,384,160]{1,2,0:T(8,128)S(1)}, f32[1,384,160]{1,2,0:T(8,128)}, u32[]{:S(2)}) copy-start(f32[1,384,160]{1,2,0:T(8,128)} %param.10) | copy-start | bytes 737284
  8.7 2.0 %collective-permute-start.3 = (f32[160,256]{1,0:T(8,128)S(1)}, f32[160,256]{1,0:T(8,128)S(1)}, u32[]{:S(2)}, u32[]{:S(2)}) collective-permute-start(f32[160,256]{1,0:T(8,128)S(1)} %collective-permute-done.2.far_ref), channel_id=1, source_target_pairs={{0,1},{1,0},{2,3},{3,2},{4,5},{5,4},{6,7},{7,6},{8,9},{9,8},{10,11... | collective-permute-start | bytes 491528 | tf_op jit(solution)/shard_map/ppermute | solution.py:22
  8.7 8.9 %collective-permute-start.1 = (f32[264,256]{1,0:T(8,128)S(1)}, f32[264,256]{1,0:T(8,128)S(1)}, u32[]{:S(2)}, u32[]{:S(2)}) collective-permute-start(f32[264,256]{1,0:T(8,128)S(1)} %shard_map.95.own_ref.carry_ref), channel_id=1, source_target_pairs={{0,4},{1,5},{2,6},{3,7},{4,0},{5,1},{6,2},{7,3},{8,12},{9,13},{10,... | collective-permute-start | bytes 811016 | tf_op jit(solution)/shard_map/ppermute | solution.py:22
  12.3 5.3 %collective-permute-start.5 = (f32[128,384]{1,0:T(8,128)S(1)}, f32[128,384]{1,0:T(8,128)S(1)}, u32[]{:S(2)}, u32[]{:S(2)}) collective-permute-start(f32[128,384]{1,0:T(8,128)S(1)} %get-tuple-element.82), channel_id=1, source_target_pairs={{0,1},{1,0},{2,3},{3,2},{4,5},{5,4},{6,7},{7,6},{8,9},{9,8},{10,11... | collective-permute-start | bytes 589832 | tf_op jit(solution)/shard_map/ppermute | solution.py:22
  12.6 1.3 %collective-permute-start.4 = (f32[128,64]{1,0:T(8,128)S(1)}, f32[128,64]{1,0:T(8,128)S(1)}, u32[]{:S(2)}, u32[]{:S(2)}) collective-permute-start(f32[128,64]{1,0:T(8,128)S(1)} %get-tuple-element.79), channel_id=1, source_target_pairs={{0,1},{1,0},{2,3},{3,2},{4,5},{5,4},{6,7},{7,6},{8,9},{9,8},{10,11... | collective-permute-start | bytes 98312 | tf_op jit(solution)/shard_map/ppermute | solution.py:22
  19.8 14.8 %collective-permute-start.13 = (f32[320,640]{1,0:T(8,128)S(1)}, f32[320,640]{1,0:T(8,128)S(1)}, u32[]{:S(2)}, u32[]{:S(2)}) collective-permute-start(f32[320,640]{1,0:T(8,128)S(1)} %get-tuple-element.109), channel_id=1, source_target_pairs={{0,1},{1,0},{2,3},{3,2},{4,5},{5,4},{6,7},{7,6},{8,9},{9,8},{10,11... | collective-permute-start | bytes 2457608 | tf_op jit(solution)/shard_map/ppermute | solution.py:22
  20.0 12.5 %collective-permute-start.9 = (f32[256,256]{1,0:T(8,128)S(1)}, f32[256,256]{1,0:T(8,128)S(1)}, u32[]{:S(2)}, u32[]{:S(2)}) collective-permute-start(f32[256,256]{1,0:T(8,128)S(1)} %get-tuple-element.95.half_ref.refs_2_.refs_6_), channel_id=1, source_target_pairs={{0,1},{1,0},{2,3},{3,2},{4,5},{5,4},{6,7},{7,6},{8,9},{9,8},{10,11... | collective-permute-start | bytes 786440 | tf_op jit(solution)/shard_map/ppermute | solution.py:22
  20.5 12.5 %collective-permute-start.10 = (f32[256,256]{1,0:T(8,128)S(1)}, f32[256,256]{1,0:T(8,128)S(1)}, u32[]{:S(2)}, u32[]{:S(2)}) collective-permute-start(f32[256,256]{1,0:T(8,128)S(1)} %get-tuple-element.102.carry_ref), channel_id=1, source_target_pairs={{0,8},{1,9},{2,10},{3,11},{4,12},{5,13},{6,14},{7,15},{8,0},{9,1},... | collective-permute-start | bytes 786440 | tf_op jit(solution)/shard_map/ppermute | solution.py:22
  22.3 5.8 %collective-permute-start.6 = (f32[32,512]{1,0:T(8,128)S(1)}, f32[32,512]{1,0:T(8,128)S(1)}, u32[]{:S(2)}, u32[]{:S(2)}) collective-permute-start(f32[32,512]{1,0:T(8,128)S(1)} %get-tuple-element.87), channel_id=1, source_target_pairs={{0,6},{1,7},{2,4},{3,5},{4,2},{5,3},{6,0},{7,1},{8,14},{9,15},{10,... | collective-permute-start | bytes 196616 | tf_op jit(solution)/shard_map/ppermute | solution.py:22
  24.8 4.9 %collective-permute-start.7 = (f32[32,512]{1,0:T(8,128)S(1)}, f32[32,512]{1,0:T(8,128)S(1)}, u32[]{:S(2)}, u32[]{:S(2)}) collective-permute-start(f32[32,512]{1,0:T(8,128)S(1)} %get-tuple-element.88), channel_id=1, source_target_pairs={{0,2},{1,3},{2,0},{3,1},{4,6},{5,7},{6,4},{7,5},{8,10},{9,11},{10,... | collective-permute-start | bytes 196616 | tf_op jit(solution)/shard_map/ppermute | solution.py:22
  28.1 4.3 %collective-permute-start.8 = (f32[32,512]{1,0:T(8,128)S(1)}, f32[32,512]{1,0:T(8,128)S(1)}, u32[]{:S(2)}, u32[]{:S(2)}) collective-permute-start(f32[32,512]{1,0:T(8,128)S(1)} %get-tuple-element.89), channel_id=1, source_target_pairs={{0,4},{1,5},{2,6},{3,7},{4,0},{5,1},{6,2},{7,3},{8,12},{9,13},{10,... | collective-permute-start | bytes 196616 | tf_op jit(solution)/shard_map/ppermute | solution.py:22
  33.1 10.2 %collective-permute-start.12 = (f32[256,256]{1,0:T(8,128)S(1)}, f32[256,256]{1,0:T(8,128)S(1)}, u32[]{:S(2)}, u32[]{:S(2)}) collective-permute-start(f32[256,256]{1,0:T(8,128)S(1)} %get-tuple-element.107.half_ref.refs_3_.refs_7_), channel_id=1, source_target_pairs={{0,1},{1,0},{2,3},{3,2},{4,5},{5,4},{6,7},{7,6},{8,9},{9,8},{10,11... | collective-permute-start | bytes 786440 | tf_op jit(solution)/shard_map/ppermute | solution.py:22
  33.2 10.9 %collective-permute-start.15 = (f32[256,256]{1,0:T(8,128)S(1)}, f32[256,256]{1,0:T(8,128)S(1)}, u32[]{:S(2)}, u32[]{:S(2)}) collective-permute-start(f32[256,256]{1,0:T(8,128)S(1)} %get-tuple-element.102.carry_ref), channel_id=1, source_target_pairs={{17,1},{19,3},{21,5},{23,7}} | collective-permute-start | bytes 786440 | tf_op jit(solution)/shard_map/ppermute | solution.py:22
  33.9 10.2 %collective-permute-start.16 = (f32[256,256]{1,0:T(8,128)S(1)}, f32[256,256]{1,0:T(8,128)S(1)}, u32[]{:S(2)}, u32[]{:S(2)}) collective-permute-start(f32[256,256]{1,0:T(8,128)S(1)} %get-tuple-element.102.carry_ref), channel_id=1, source_target_pairs={{17,9},{19,11},{21,13},{23,15}} | collective-permute-start | bytes 786440 | tf_op jit(solution)/shard_map/ppermute | solution.py:22
  34.7 14.6 %collective-permute-start.18 = (f32[160,640]{1,0:T(8,128)S(1)}, f32[160,640]{1,0:T(8,128)S(1)}, u32[]{:S(2)}, u32[]{:S(2)}) collective-permute-start(f32[160,640]{1,0:T(8,128)S(1)} %get-tuple-element.120), channel_id=1, source_target_pairs={{0,2},{1,3},{2,0},{3,1},{4,6},{5,7},{6,4},{7,5},{8,10},{9,11},{10,... | collective-permute-start | bytes 1228808 | tf_op jit(solution)/shard_map/ppermute | solution.py:22
  35.8 7.5 %collective-permute-start.11 = (f32[32,512]{1,0:T(8,128)S(1)}, f32[32,512]{1,0:T(8,128)S(1)}, u32[]{:S(2)}, u32[]{:S(2)}) collective-permute-start(f32[32,512]{1,0:T(8,128)S(1)} %get-tuple-element.105.up_ref), channel_id=1, source_target_pairs={{0,8},{1,9},{2,10},{3,11},{4,12},{5,13},{6,14},{7,15},{8,0},{9,1},... | collective-permute-start | bytes 196616 | tf_op jit(solution)/shard_map/ppermute | solution.py:22
  44.1 5.1 %collective-permute-start.17 = (f32[256,256]{1,0:T(8,128)S(1)}, f32[256,256]{1,0:T(8,128)S(1)}, u32[]{:S(2)}, u32[]{:S(2)}) collective-permute-start(f32[256,256]{1,0:T(8,128)S(1)} %shard_map.107.refs_4_), channel_id=1, source_target_pairs={{0,1},{1,0},{2,3},{3,2},{4,5},{5,4},{6,7},{7,6},{8,9},{9,8},{10,11... | collective-permute-start | bytes 786440 | tf_op jit(solution)/shard_map/ppermute | solution.py:22
  44.3 5.0 %collective-permute-start.14 = (f32[32,256]{1,0:T(8,128)S(1)}, f32[32,256]{1,0:T(8,128)S(1)}, u32[]{:S(2)}, u32[]{:S(2)}) collective-permute-start(f32[32,256]{1,0:T(8,128)S(1)} %get-tuple-element.115.refs_0_), channel_id=1, source_target_pairs={{0,16},{1,17},{2,18},{3,19},{4,20},{5,21},{6,22},{7,23},{8,24},{9,... | collective-permute-start | bytes 98312 | tf_op jit(solution)/shard_map/ppermute | solution.py:22
  50.4 5.3 %collective-permute-start.19 = (f32[32,512]{1,0:T(8,128)S(1)}, f32[32,512]{1,0:T(8,128)S(1)}, u32[]{:S(2)}, u32[]{:S(2)}) collective-permute-start(f32[32,512]{1,0:T(8,128)S(1)} %get-tuple-element.124), channel_id=1, source_target_pairs={{0,6},{1,7},{2,4},{3,5},{4,2},{5,3},{6,0},{7,1},{8,14},{9,15},{10,... | collective-permute-start | bytes 196616 | tf_op jit(solution)/shard_map/ppermute | solution.py:22
  52.5 4.3 %collective-permute-start.20 = (f32[32,512]{1,0:T(8,128)S(1)}, f32[32,512]{1,0:T(8,128)S(1)}, u32[]{:S(2)}, u32[]{:S(2)}) collective-permute-start(f32[32,512]{1,0:T(8,128)S(1)} %get-tuple-element.125), channel_id=1, source_target_pairs={{0,2},{1,3},{2,0},{3,1},{4,6},{5,7},{6,4},{7,5},{8,10},{9,11},{10,... | collective-permute-start | bytes 196616 | tf_op jit(solution)/shard_map/ppermute | solution.py:22
  53.4 4.3 %collective-permute-start.21 = (f32[32,512]{1,0:T(8,128)S(1)}, f32[32,512]{1,0:T(8,128)S(1)}, u32[]{:S(2)}, u32[]{:S(2)}) collective-permute-start(f32[32,512]{1,0:T(8,128)S(1)} %get-tuple-element.126), channel_id=1, source_target_pairs={{0,4},{1,5},{2,6},{3,7},{4,0},{5,1},{6,2},{7,3},{8,12},{9,13},{10,... | collective-permute-start | bytes 196616 | tf_op jit(solution)/shard_map/ppermute | solution.py:22
  57.7 1.6 %collective-permute-start.22 = (f32[128,512]{1,0:T(8,128)S(1)}, f32[128,512]{1,0:T(8,128)S(1)}, u32[]{:S(2)}, u32[]{:S(2)}) collective-permute-start(f32[128,512]{1,0:T(8,128)S(1)} %shard_map.110.group_ref), channel_id=1, source_target_pairs={{0,1},{1,0},{2,3},{3,2},{4,5},{5,4},{6,7},{7,6},{8,9},{9,8},{10,11... | collective-permute-start | bytes 786440 | tf_op jit(solution)/shard_map/ppermute | solution.py:22

commit v3 on v0

v3 whole, which is shorter than its diff:
```python
import jax
import jax.numpy as jnp
from jax import lax
from jax.experimental import pallas as pl
from jax.experimental.pallas import tpu as pltpu
from jax.sharding import PartitionSpec as P

axes = ("leaf", "sep")
f32 = jnp.float32
bf16 = jnp.bfloat16
brief, medium, long = 0, 10**9, 10**11


def swap(payload, leaf_flip, sep_flip, senders=None):
    leaves, seps = lax.axis_size("leaf"), lax.axis_size("sep")
    pairs = [
        (leaf * seps + sep, (leaf ^ leaf_flip) * seps + (sep ^ sep_flip))
        for leaf in range(leaves)
        for sep in range(seps)
        if senders is None or senders(leaf, sep)
    ]
    return lax.ppermute(payload, axes, pairs)


def quarter_swap(payload, moves):
    leaves, seps = lax.axis_size("leaf"), lax.axis_size("sep")
    size = leaves // 4
    pairs = [
        ((start * size + leaf) * seps + sep, (end * size + leaf) * seps + sep)
        for start, end in moves
        for leaf in range(size)
        for sep in range(seps)
    ]
    return lax.ppermute(payload, axes, pairs)


def after(*arrays):
    return lax.optimization_barrier(arrays)


def product(left, right, left_dim, right_dim, precision=None):
    return lax.dot_general(
        left,
        right,
        (((left_dim,), (right_dim,)), ((), ())),
        precision=precision,
        preferred_element_type=f32,
    )


def dot(left, right, left_dim=1, right_dim=0):
    return product(left, right, left_dim, right_dim, lax.Precision.HIGHEST)


def pieces_of(array):
    high = array.astype(bf16)
    return high, (array - high.astype(f32)).astype(bf16)


def dot3(left, right, left_dim=1, right_dim=0):
    left_high, left_low = pieces_of(left)
    right_high, right_low = pieces_of(right)
    small = product(left_high, right_low, left_dim, right_dim)
    small = small + product(left_low, right_high, left_dim, right_dim)
    return product(left_high, right_high, left_dim, right_dim) + small


def hot_dot(left, right, right_dim):
    high = left.astype(bf16)
    rest = left - high.astype(f32)
    middle = rest.astype(bf16)
    low = (rest - middle.astype(f32)).astype(bf16)
    out = product(jnp.concatenate([high, middle, low], 0), right, 1, right_dim)
    size = left.shape[0]
    return out[:size] + (out[size : 2 * size] + out[2 * size :])


def stage(body, shapes, *operands, scratch=(), space=pltpu.VMEM, cost=brief):
    return pl.pallas_call(
        body,
        out_shape=[
            jax.ShapeDtypeStruct(shape, f32) if isinstance(shape, tuple) else shape
            for shape in shapes
        ],
        in_specs=[pl.BlockSpec(memory_space=space)] * len(operands),
        out_specs=[pl.BlockSpec(memory_space=pltpu.VMEM)] * len(shapes),
        scratch_shapes=[
            pltpu.VMEM(shape, f32) if isinstance(shape, tuple) else shape for shape in scratch
        ],
        compiler_params=pltpu.CompilerParams(vmem_limit_bytes=16 * 2**20),
        cost_estimate=pl.CostEstimate(flops=cost, bytes_accessed=0, transcendentals=0),
    )(*operands)


def place():
    leaf, sep = lax.axis_index("leaf"), lax.axis_index("sep")
    return leaf, sep, lax.rem(leaf, 2), sep // 2, lax.rem(sep, 2)


def at(index, size):
    return pl.ds(pl.multiple_of(index * size, size), size)


def by_bit(bit, zero, one):
    return jnp.where(bit == 0, zero, one)


def per_device(
    leaf_source,
    leaf_inverse,
    leaf_update,
    row_lists,
    row_counts,
    separator_source,
    separator_inverse,
    separator_coupling,
):
    depth = row_counts.shape[1]
    source = leaf_source[0]
    inverse = leaf_inverse[0]
    update = jnp.swapaxes(leaf_update, 1, 2)[0]
    rows_source = separator_source[0]
    rows, columns = source.shape
    size = inverse.shape[1]
    updates = update.shape[1]
    capacity = updates // depth
    order = separator_inverse.shape[1]
    middle = order // 2
    packed_rows = middle // 2 + 8
    carried = middle + packed_rows
    list_rows = -(-depth // 8) * 8
    quarter = rows_source.shape[0]
    half = columns // 2
    block = columns // 8
    width = updates + 2 * quarter
    leaves = lax.axis_size("leaf")

    near = swap(source, 0, 1)
    update_near = swap(update, 0, 1)
    inverse_near = swap(inverse, 0, 1)
    rows_near = swap(rows_source, 0, 1)

    def chip_source(source_ref, near_ref, out_ref):
        near_bit = place()[4]
        own, other = source_ref[...], near_ref[...]
        out_ref[at(near_bit, rows)] = by_bit(near_bit, own[:, :half], own[:, half:])
        out_ref[at(1 - near_bit, rows)] = by_bit(near_bit, other[:, :half], other[:, half:])

    (chip,) = stage(chip_source, [(2 * rows, half)], source, near)
    far = swap(chip, 0, 2)

    def operators(coupling_ref, inverse_ref, lists_ref, counts_ref, out_ref, coupling, inverse, lists, counts, packed, sems):
        near_bit = place()[4]
        pairs = ((coupling_ref.at[at(near_bit, middle)], coupling), (inverse_ref, inverse), (lists_ref, lists), (counts_ref, counts))
        copies = [pltpu.make_async_copy(src, dst, sems.at[index]) for index, (src, dst) in enumerate(pairs)]
        for copy in copies:
            copy.start()
        for copy in copies:
            copy.wait()
        out_ref[:middle] = dot(coupling[...], inverse[...])
        row = lax.broadcasted_iota(jnp.int32, (middle, middle), 0)
        lane = lax.broadcasted_iota(jnp.int32, (middle, middle), 1)
        last = inverse[middle:, middle:]
        packed[:middle, :middle] = jnp.where(row >= lane, inverse[:middle, :middle], jnp.transpose(last))
        packed[:middle, middle:] = inverse[middle:, :middle]
        packed[middle:] = jnp.zeros((2 * packed_rows - middle, order), f32)
        packed[middle : middle + 1, :middle] = jnp.sum(jnp.where(row == lane, last, 0.0), 0, keepdims=True)
        out_ref[middle:carried] = packed[at(near_bit, packed_rows)]
        out_ref[carried:] = jnp.full((list_rows, order), -1.0, f32)
        slot = lax.broadcasted_iota(jnp.int32, (1, capacity), 1)
        for level in range(depth):
            names = lists[:, level * capacity : (level + 1) * capacity]
            live = slot < counts[:, level : level + 1]
            out_ref[carried + level : carried + level + 1, :capacity] = jnp.where(live, names, -1).astype(f32)

    chip, coupling, own_inverse = after(chip, separator_coupling[0], separator_inverse[0])
    (payload,) = stage(
        operators,
        [(carried + list_rows, order)],
        coupling,
        own_inverse,
        row_lists,
        row_counts,
        scratch=[
            (middle, order),
            (order, order),
            pltpu.VMEM(row_lists.shape, jnp.int32),
            pltpu.VMEM(row_counts.shape, jnp.int32),
            (2 * packed_rows, order),
            pltpu.SemaphoreType.DMA((4,)),
        ],
        space=pltpu.HBM,
    )

    def own_part(inverse_ref, inverse_near_ref, update_ref, update_near_ref, rows_ref, rows_near_ref, chip_ref, y_ref, all_ref, far_ref, mine_ref, update_out_ref, turned_ref):
        _, _, _, far_bit, near_bit = place()
        own, other = at(near_bit, rows), at(1 - near_bit, rows)
        all_ref[own] = inverse_ref[...]
        all_ref[other] = inverse_near_ref[...]
        update_out_ref[own] = update_ref[...]
        update_out_ref[other] = update_near_ref[...]
        whole = all_ref[...]
        first, second = whole[:, : 2 * rows], whole[:, 2 * rows :]
        far_ref[...] = by_bit(far_bit, second, first)
        y_ref[...] = dot3(by_bit(far_bit, first, second), chip_ref[...])
        mine_ref[:, :rows] = by_bit(near_bit, first[:, :rows], first[:, rows:])
        mine_ref[:, rows:] = by_bit(near_bit, second[:, :rows], second[:, rows:])
        turned, turned_near = jnp.transpose(rows_ref[...]), jnp.transpose(rows_near_ref[...])
        turned = by_bit(near_bit, turned[:half], turned[half:])
        turned_near = by_bit(near_bit, turned_near[:half], turned_near[half:])
        turned_ref[...] = by_bit(
            near_bit,
            jnp.concatenate([turned, turned_near], 1),
            jnp.concatenate([turned_near, turned], 1),
        )

    received = swap(payload, 1, 0)
    inverse_near, payload = after(inverse_near, payload)
    own_y, inverse_all, inverse_far, inverse_mine, update_all, turned = stage(
        own_part,
        [(2 * rows, half), (2 * rows, size), (2 * rows, 2 * rows), (2 * rows, 2 * rows), (2 * rows, updates), (half, 2 * quarter)],
        inverse,
        inverse_near,
        update,
        update_near,
        rows_source,
        rows_near,
        chip,
    )
    far, own_y = after(far, own_y)

    def leaf_part(own_ref, inverse_ref, far_ref, update_ref, turned_ref, y_ref, *refs):
        _, _, odd, far_bit, _ = place()
        out_refs, terms = refs[:-1], refs[-1]
        leaf_y = own_ref[...] + dot3(inverse_ref[...], far_ref[...])
        y_ref[...] = leaf_y
        terms[...] = dot3(leaf_y, update_ref[...], 0, 0)
        for flip, out_ref in enumerate(out_refs):
            part = at((2 * odd + far_bit) ^ flip, block)
            out_ref[:, :updates] = terms[part]
            out_ref[:, updates:] = turned_ref[part]

    leaf_y, mine, to_far, to_odd, to_both = stage(
        leaf_part,
        [(2 * rows, half)] + [(block, width)] * 4,
        own_y,
        inverse_far,
        far,
        update_all,
        turned,
        scratch=[(half, updates)],
    )
    by_both = swap(to_both, 1, 2)
    by_far = swap(to_far, 0, 2)
    by_odd = swap(to_odd, 1, 0)

    def forward(level):
        def body(carry_ref, received_ref, half_ref, next_ref):
            upper = lax.rem(place()[0] // 2 ** (level - 1), 2) == 1
            carry, received = carry_ref[:carried], received_ref[:carried]
            half_ref[...] = jnp.where(upper, carry, received)
            next_ref[...] = jnp.where(upper, received, carry)

        return body

    def last_forward(carry_ref, received_ref, half_ref, root_ref):
        part = place()[0] // (leaves // 4)
        carry, received = carry_ref[...], received_ref[...]
        half_ref[...] = jnp.where(lax.rem(part, 2) == 1, carry, received)
        root_ref[...] = jnp.where(part == 1, received[middle:], carry[middle:])

    def root_half(root_ref, received_ref, out_ref):
        part = place()[0] // (leaves // 4)
        inner = jnp.logical_or(part == 1, part == 2)
        out_ref[...] = jnp.where(inner, root_ref[...], received_ref[...])

    received, mine = after(received, mine)
    new_half, carry = stage(forward(1), [(carried, order)] * 2, payload, received)
    halves, halves_near = [new_half], [swap(new_half, 0, 1)]
    for level in range(2, depth - 1):
        reached = swap(carry, 2 ** (level - 1), 0)
        new_half, carry = stage(forward(level), [(carried, order)] * 2, carry, reached)
        halves.append(new_half)
        halves_near.append(swap(new_half, 0, 1))
    reached = quarter_swap(carry, ((1, 0), (3, 2), (2, 1)))

    def one_hots(own_ref, other_ref, hot_ref):
        rows_of_node = lax.broadcasted_iota(jnp.int32, (order, capacity), 0)
        for level in range(depth):
            for index, ref in enumerate((own_ref, other_ref)):
                names = ref[carried + level : carried + level + 1, :capacity].astype(jnp.int32)
                hot = jnp.where(rows_of_node == names, 1.0, 0.0).astype(bf16)
                hot_ref[level, :, index * capacity : (index + 1) * capacity] = hot

    carry, payload = after(carry, payload)
    (hots,) = stage(
        one_hots, [jax.ShapeDtypeStruct((depth, order, 2 * capacity), bf16)], payload, received
    )

    def transposed(all_ref, mine_ref, update_ref, y_ref, own_ref, far_ref, work):
        far_bit = place()[3]
        work[:, :half] = dot3(all_ref[...], y_ref[...], 0, 0)
        both = dot3(mine_ref[...], update_ref[...], 0, 0)
        own_ref[:, :updates] = by_bit(far_bit, both[:rows], both[rows:])
        far_ref[:, :updates] = by_bit(far_bit, both[rows:], both[:rows])
        for index in range(2):
            part = slice(updates + index * half, updates + (index + 1) * half)
            own_ref[:, part] = work[at(2 * far_bit + index, rows)]
            far_ref[:, part] = work[at(2 - 2 * far_bit + index, rows)]

    leaf_y, hots = after(leaf_y, hots)
    own_sum, far_sum = stage(
        transposed,
        [(rows, updates + columns)] * 2,
        inverse_all,
        inverse_mine,
        update_all,
        leaf_y,
        scratch=[(size, half)],
    )
    by_both, by_far, by_odd, own_sum = after(by_both, by_far, by_odd, own_sum)

    def gathered_part(mine_ref, far_ref, odd_ref, both_ref, hot_ref, residual_ref, up_ref):
        leaf, _, odd, far_bit, _ = place()

        def joined(one, two):
            first, second = one[:, updates:], two[:, updates:]
            ordered = by_bit(
                far_bit,
                jnp.concatenate([first, second], 1),
                jnp.concatenate([second, first], 1),
            )
            return one[:, :updates] + two[:, :updates], ordered

        total, own_source = joined(mine_ref[...], far_ref[...])
        total_other, other_source = joined(odd_ref[...], both_ref[...])
        odd_source = by_bit(odd, other_source, own_source)
        even_source = by_bit(odd, own_source, other_source)
        for level in range(1, depth + 1):
            part = slice((level - 1) * capacity, level * capacity)
            both = jnp.concatenate([total[:, part], total_other[:, part]], 1)
            gathered = hot_dot(both, hot_ref[level - 1], 1)
            if level == 1:
                residual_ref[...] = odd_source - gathered
            else:
                here = lax.rem(leaf - odd, 2**level) == 2 ** (level - 1)
                slot = jnp.where(here, even_source, 0.0) - gathered
                up_ref[:, (level - 2) * order : (level - 1) * order] = slot

    residual, slots = stage(
        gathered_part,
        [(block, order), (block, (depth - 1) * order)],
        mine,
        by_far,
        by_odd,
        by_both,
        hots,
        cost=3*medium,
    )
    residuals = [residual]

    def operator_of(half_ref, near_ref):
        near_bit = place()[4]
        own, other = half_ref[:middle], near_ref[:middle]
        return jnp.concatenate([by_bit(near_bit, own, other), by_bit(near_bit, other, own)], 0)

    def push(slots_ref, residual_ref, half_ref, near_ref, out_ref):
        taken = dot(residual_ref[...], operator_of(half_ref, near_ref), 1, 1)
        out_ref[:, :order] = slots_ref[:, :order] - taken
        if out_ref.shape[1] > order:
            out_ref[:, order:] = slots_ref[:, order:]

    def inverse_of(own, other, out_ref):
        near_bit = place()[4]
        row = lax.broadcasted_iota(jnp.int32, (middle, middle), 0)
        lane = lax.broadcasted_iota(jnp.int32, (middle, middle), 1)
        packed = jnp.concatenate([by_bit(near_bit, own, other), by_bit(near_bit, other, own)], 0)
        both = packed[:middle, :middle]
        last = jnp.where(row > lane, jnp.transpose(both), 0.0)
        out_ref[:middle, :middle] = jnp.where(row >= lane, both, 0.0)
        out_ref[:middle, middle:] = jnp.zeros((middle, middle), f32)
        out_ref[middle:, :middle] = packed[:middle, middle:]
        out_ref[middle:, middle:] = jnp.where(row == lane, packed[middle : middle + 1, :middle], last)

    def alone(residual_ref, half_ref, near_ref, out_ref, work):
        inverse_of(half_ref[middle:], near_ref[middle:], work)
        out_ref[...] = dot(dot(residual_ref[...], work[...], 1, 1), work[...])

    def level_sum(up_ref, partner_ref, residual_ref, rest_ref):
        total = up_ref[...] + partner_ref[...]
        residual_ref[...] = total[:, :order]
        rest_ref[...] = total[:, order:]

    partials = []
    halves_near[0], residual, slots = after(halves_near[0], residual, slots)
    (going_up,) = stage(
        push, [(block, (depth - 1) * order)], slots, residual, halves[0], halves_near[0]
    )
    for level in range(2, depth):
        partner = swap(going_up, 2 ** (level - 1), 0)
        if level == depth - 1:
            reached, going_up, far_sum = after(reached, going_up, far_sum)
            new_half, root = stage(
                last_forward, [(carried, order), (packed_rows, order)], carry, reached
            )
            halves.append(new_half)
            from_far = swap(far_sum, 0, 2, lambda leaf, sep: sep // 2 == 1)
            halves_near.append(swap(new_half, 0, 1))
            by_root = quarter_swap(root, ((2, 3), (1, 0)))
        residuals[-1], going_up, new_half = after(residuals[-1], going_up, halves[-1])
        (partial,) = stage(
            alone,
            [(block, order)],
            residuals[-1],
            halves[level - 2],
            halves_near[level - 2],
            scratch=[(order, order)],
        )
        partials.append(partial)
        partner, partial = after(partner, partial)
        residual, slots = stage(
            level_sum,
            [(block, order), (block, (depth - level) * order)],
            going_up,
            partner,
            cost=long,
        )
        residuals.append(residual)
        halves_near[level - 1], residual, slots = after(halves_near[level - 1], residual, slots)
        (going_up,) = stage(
            push,
            [(block, (depth - level) * order)],
            slots,
            residual,
            halves[level - 1],
            halves_near[level - 1],
        )
    partner = swap(going_up, 2 ** (depth - 1), 0)

    residuals[-1], going_up = after(residuals[-1], going_up)
    (partial,) = stage(
        alone,
        [(block, order)],
        residuals[-1],
        halves[-1],
        halves_near[-1],
        scratch=[(order, order)],
    )
    partials.append(partial)
    by_root, partial = after(by_root, partial)
    (root,) = stage(root_half, [(packed_rows, order)], root, by_root)
    root_near = swap(root, 0, 1)
    partner, root = after(partner, root)

    def root_sum(up_ref, partner_ref, out_ref):
        out_ref[...] = up_ref[...] + partner_ref[...]

    (residual,) = stage(root_sum, [(block, order)], going_up, partner, cost=medium)
    root_near, residual = after(root_near, residual)

    def way_down(residual_ref, root_ref, root_near_ref, hot_ref, *refs):
        leaf, _, odd, far_bit, _ = place()
        partial_refs, half_refs = refs[: depth - 1], refs[depth - 1 : 2 * depth - 2]
        near_refs, out_refs, work = refs[2 * depth - 2 : 3 * depth - 3], refs[3 * depth - 3 : -1], refs[-1]
        inverse_of(root_ref[...], root_near_ref[...], work)
        solved = [None] * depth
        solved[-1] = dot(dot(residual_ref[...], work[...], 1, 1), work[...])
        for level in range(depth - 1, 0, -1):
            down = operator_of(half_refs[level - 1], near_refs[level - 1])
            solved[level - 1] = partial_refs[level - 1][...] - dot(solved[level], down)
        even_solved = jnp.zeros_like(solved[0])
        for level in range(2, depth + 1):
            here = lax.rem(leaf - odd, 2**level) == 2 ** (level - 1)
            even_solved = jnp.where(here, solved[level - 1], even_solved)
        own_solved = by_bit(odd, even_solved, solved[0])
        other_solved = by_bit(odd, solved[0], even_solved)
        for flip, out_ref in enumerate(out_refs):
            rows_of = other_solved if flip >= 2 else own_solved
            out_ref[:, updates:] = by_bit(
                far_bit ^ (flip % 2), rows_of[:, : 2 * quarter], rows_of[:, 2 * quarter :]
            )
        for level in range(depth):
            picked = hot_dot(solved[level], hot_ref[level], 0)
            for flip, out_ref in enumerate(out_refs):
                side = flip // 2
                out_ref[:, level * capacity : (level + 1) * capacity] = picked[
                    :, side * capacity : (side + 1) * capacity
                ]

    stay, to_far, to_odd, to_both = stage(
        way_down,
        [(block, width)] * 4,
        residual,
        root,
        root_near,
        hots,
        *partials,
        *halves,
        *halves_near,
        scratch=[(order, order)],
    )
    both = swap(to_both, 1, 2)
    beyond = swap(to_far, 0, 2)
    side = swap(to_odd, 1, 0)

    def last_left(own_ref, far_ref, left_ref, keep_ref, pass_ref):
        near_bit = place()[4]
        total = own_ref[...] + far_ref[...]
        left_ref[:rows, :updates] = -total[:, :updates]
        left_ref[:rows, updates:] = jnp.zeros((rows, 2 * quarter), f32)
        row = lax.broadcasted_iota(jnp.int32, (quarter, width), 0)
        lane = lax.broadcasted_iota(jnp.int32, (quarter, width), 1)
        left_ref[rows:] = jnp.where(lane == updates + near_bit * quarter + row, 1.0, 0.0)
        first, second = total[:, updates : updates + half], total[:, updates + half :]
        keep_ref[...] = by_bit(near_bit, first, second)
        pass_ref[...] = by_bit(near_bit, second, first)

    from_far, stay = after(from_far, stay)
    left, base_keep, base_pass = stage(
        last_left, [(rows + quarter, width), (rows, half), (rows, half)], own_sum, from_far
    )
    both, beyond, side, left = after(both, beyond, side, left)

    def grouped(*refs):
        _, _, odd, far_bit, _ = place()
        out_ref = refs[-1]
        for flip, ref in enumerate(refs[:-1]):
            out_ref[at((2 * odd + far_bit) ^ flip, block)] = ref[...]

    (group,) = stage(grouped, [(half, width)], stay, beyond, side, both)
    base_near = swap(base_pass, 0, 1)
    group_near = swap(group, 0, 1)

    def own_columns(left_ref, group_ref, out_ref):
        out_ref[...] = dot3(left_ref[...], group_ref[...], 1, 1)

    (ours,) = stage(own_columns, [(rows + quarter, half)], left, group)
    group_near, ours = after(group_near, ours)

    def finish(left_ref, group_ref, ours_ref, base_ref, base_near_ref, leaf_ref, rows_ref):
        near_bit = place()[4]
        ours = ours_ref[...]
        theirs = dot3(left_ref[...], group_ref[...], 1, 1)
        ours_x, theirs_x = base_ref[...] + ours[:rows], base_near_ref[...] + theirs[:rows]
        leaf_ref[:, :half] = by_bit(near_bit, ours_x, theirs_x)
        leaf_ref[:, half:] = by_bit(near_bit, theirs_x, ours_x)
        rows_ref[:, :half] = by_bit(near_bit, ours[rows:], theirs[rows:])
        rows_ref[:, half:] = by_bit(near_bit, theirs[rows:], ours[rows:])

    leaf_x, separator_rows = stage(
        finish,
        [(rows, columns), (quarter, columns)],
        left,
        group_near,
        ours,
        base_keep,
        base_near,
    )
    return (leaf_x[None], separator_rows[None])


def solution(mesh):
    placed = (
        P("leaf", "sep", None),
        P("leaf", "sep", None),
        P("leaf", None, "sep"),
        P("leaf", None),
        P("leaf", None),
        P("leaf", "sep", None),
        P("leaf", None, None),
        P("leaf", None, None),
    )
    return jax.shard_map(
        per_device,
        mesh=mesh,
        in_specs=placed,
        out_specs=(P("leaf", "sep", None), P("leaf", "sep", None)),
        check_vma=False,
    )
```

time: 197 us -> 47.2 us (0.24)
  waiting for transfers between devices: 89.4 us -> 12.2 us
  blocking collectives: 47.3 us -> 0 us
  between operations: 15.2 us -> 0.89 us
  matrix products: 9.11 us -> 0 us
  Pallas kernels: 0 us -> 9.07 us
  local copies, waits for them, and re-layouts: 9.71 us -> 1.89 us
  starting transfers between devices: 25.6 us -> 22.9 us
    unnamed x4 -> x0, waiting for transfers between devices: 55.4 us -> none
    all_gather x7 -> x0, blocking collectives: 47.3 us -> none  [the longest x6 37.6 us: sep_rows(): return lax.all_gather(payload, 'sep', axis=0, tiled=True)]
    ppermute x10 -> x22, waiting for transfers between devices: 34 us -> 12.2 us  [the longest x20 9.29 us: swap(): return lax.ppermute(payload, axes, pairs)]
    dot_general x16 -> x0, matrix products: 9.11 us -> none  [the longest x7 4.26 us: product_first(): lax.dot_general(matrix, operand, (((0,), (0,)), ((), ())), precision=high...]
    pallas_call x0 -> x21, Pallas kernels: none -> 9.07 us  [stage(): pl.pallas_call(body, out_shape=[jax.ShapeDtypeStruct(shape, f32) if isins...]
    unnamed x25 -> x16, local copies, waits for them, and re-layouts: 8.01 us -> 1.89 us
    ppermute x10 -> x22, starting transfers between devices: 25.6 us -> 22.9 us  [the longest x20 20.3 us: swap(): return lax.ppermute(payload, axes, pairs)]
  transfers between devices with their start and end apart: 12 -> 22, of which waited for: 12 -> 12; matrix products, arithmetic and copies ran while one was open for 1% -> 0% of each run, Pallas kernels for 0% -> 17%
where the time goes in v3:
time: 47.2 us; the launch traced here: 47 us
  starting transfers between devices  22.9 us (49%)
  waiting for transfers between devices  12.2 us (26%)
  Pallas kernels  9.07 us (19%)
  local copies, waits for them, and re-layouts  1.89 us (4%)
  between operations  0.89 us (2%)
    ppermute x20, starting transfers between devices, swap(): return lax.ppermute(payload, axes, pairs)  20.3 us
    ppermute x20, waiting for transfers between devices, swap(): return lax.ppermute(payload, axes, pairs)  9.29 us
    pallas_call x21, Pallas kernels, stage(): pl.pallas_call(body, out_shape=[jax.ShapeDtypeStruct(shape, f32) if isins...  9.07 us
    ppermute x2, waiting for transfers between devices, quarter_swap(): return lax.ppermute(payload, axes, pairs)  2.92 us
    ppermute x2, starting transfers between devices, quarter_swap(): return lax.ppermute(payload, axes, pairs)  2.59 us
    unnamed x16, local copies, waits for them, and re-layouts  1.89 us
  transfers between devices with their start and end apart: 22, of which 12 were waited for; matrix products, arithmetic and copies ran while one was open for 0% of the time, Pallas kernels for 17%

profile of v3, /device:TPU:0, one launch (start us, length us, event | category | flops | bytes accessed | tf_op | source)
XLA Modules:
  0.0 47.0 jit_solution(8785316044120733530)
XLA Ops:
  0.6 0.5 %collective-permute-start = (f32[160,640]{1,0:T(8,128)}, f32[160,640]{1,0:T(8,128)S(1)}, u32[]{:S(2)}, u32[]{:S(2)}) collective-permute-start(f32[160,640]{1,0:T(8,128)} %bitcast.10), channel_id=1, source_target_pairs={{0,1},{1,0},{2,3},{3,2},{4,5},{5,4},{6,7},{7,6},{8,9},{9,8},{10,11... | collective-permute-start | bytes 1228808 | tf_op jit(solution)/shard_map/ppermute | solution.py:22
  1.2 0.1 collective-permute-start.1
  1.2 0.4 collective-permute-start.4
  1.7 1.3 %collective-permute-done.1.near_ref = f32[160,256]{1,0:T(8,128)S(1)} collective-permute-done((f32[160,256]{1,0:T(8,128)}, f32[160,256]{1,0:T(8,128)S(1)}, u32[]{:S(2)}, u32[]{:S(2)}) %collective-permute-start.1) | collective-permute-done | bytes 163872 | tf_op jit(solution)/shard_map/ppermute | solution.py:22
  3.0 0.9 %copy-done.4 = f32[1,160,256]{2,1,0:T(8,128)S(1)} copy-done((f32[1,160,256]{2,1,0:T(8,128)S(1)}, f32[1,160,256]{2,1,0:T(8,128)}, u32[]{:S(2)}) %copy-start.4) | copy-done | bytes 163864
  3.9 2.9 %collective-permute-start.3 = (f32[320,128]{1,0:T(8,128)S(1)}, f32[320,128]{1,0:T(8,128)S(1)}, u32[]{:S(2)}, u32[]{:S(2)}) collective-permute-start(f32[320,128]{1,0:T(8,128)S(1)} %shard_map.95.chip_ref), channel_id=1, source_target_pairs={{0,2},{1,3},{2,0},{3,1},{4,6},{5,7},{6,4},{7,5},{8,10},{9,11},{10,... | collective-permute-start | bytes 491528 | tf_op jit(solution)/shard_map/ppermute | solution.py:22
  6.9 0.9 %copy-done.2 = f32[1,256,256]{2,1,0:T(8,128)S(1)} copy-done((f32[1,256,256]{2,1,0:T(8,128)S(1)}, f32[1,256,256]{2,1,0:T(8,128)}, u32[]{:S(2)}) %copy-start.2) | copy-done | bytes 262168
  7.8 0.5 %shard_map.96.carry_ref.own_ref = f32[208,256]{1,0:T(8,128)S(1)} custom-call(f32[256,256]{1,0:T(8,128)S(1)} %bitcast.12, f32[256,256]{1,0:T(8,128)S(1)} %bitcast.13, s32[1,384]{1,0:T(1,128)S(1)} %copy-done.6, s32[1,3]{1,0:T(1,128)S(1)} %copy-done.7), custom_call_target="tpu_custom_call" | custom-call | tf_op jit(solution)/shard_map/pallas_call | solution.py:79
  8.3 1.6 %collective-permute-start.2 = (f32[208,256]{1,0:T(8,128)S(1)}, f32[208,256]{1,0:T(8,128)S(1)}, u32[]{:S(2)}, u32[]{:S(2)}) collective-permute-start(f32[208,256]{1,0:T(8,128)S(1)} %shard_map.96.carry_ref.own_ref), channel_id=1, source_target_pairs={{0,4},{1,5},{2,6},{3,7},{4,0},{5,1},{6,2},{7,3},{8,12},{9,13},{10,... | collective-permute-start | bytes 638984 | tf_op jit(solution)/shard_map/ppermute | solution.py:22
  9.9 1.2 %collective-permute-done.5.rows_near_ref = f32[64,256]{1,0:T(8,128)S(1)} collective-permute-done((f32[64,256]{1,0:T(8,128)S(1)}, f32[64,256]{1,0:T(8,128)S(1)}, u32[]{:S(2)}, u32[]{:S(2)}) %collective-permute-start.5) | collective-permute-done | bytes 65568 | tf_op jit(solution)/shard_map/ppermute | solution.py:22
  11.2 0.9 %shard_map.97 = (f32[320,128]{1,0:T(8,128)S(1)}, f32[320,640]{1,0:T(8,128)S(1)}, f32[320,320]{1,0:T(8,128)S(1)}, f32[320,320]{1,0:T(8,128)S(1)}, f32[320,384]{1,0:T(8,128)S(1)}, /*index=5*/f32[128,128]{1,0:T(8,128)S(1)}) custom-call(f32[160,640]{1,0:T(8,128)S(1)} %bitcast.11, f32[160,640]{1,0:T(8,128)S(1)} %collective-permute-done.inverse_near_ref, ...), custom_call_target="tpu_custom_call" | custom-call | tf_op jit(solution)/shard_map/pallas_call | solution.py:79
  12.1 0.7 %shard_map.98 = (f32[320,128]{1,0:T(8,128)S(1)}, f32[32,512]{1,0:T(8,128)S(1)}, f32[32,512]{1,0:T(8,128)S(1)}, f32[32,512]{1,0:T(8,128)S(1)}, f32[32,512]{1,0:T(8,128)S(1)}) custom-call(f32[320,128]{1,0:T(8,128)S(1)} %get-tuple-element.82.own_ref, f32[320,320]{1,0:T(8,128)S(1)} %get-tuple-element.83.inverse_ref, ...), custom_call_target="tpu_custom_call" | custom-call | tf_op jit(solution)/shard_map/pallas_call | solution.py:79
  12.9 1.1 %collective-permute-start.10 = (f32[32,512]{1,0:T(8,128)S(1)}, f32[32,512]{1,0:T(8,128)S(1)}, u32[]{:S(2)}, u32[]{:S(2)}) collective-permute-start(f32[32,512]{1,0:T(8,128)S(1)} %get-tuple-element.95), channel_id=1, source_target_pairs={{0,4},{1,5},{2,6},{3,7},{4,0},{5,1},{6,2},{7,3},{8,12},{9,13},{10,... | collective-permute-start | bytes 196616 | tf_op jit(solution)/shard_map/ppermute | solution.py:22
  13.9 1.4 %collective-permute-start.8 = (f32[32,512]{1,0:T(8,128)S(1)}, f32[32,512]{1,0:T(8,128)S(1)}, u32[]{:S(2)}, u32[]{:S(2)}) collective-permute-start(f32[32,512]{1,0:T(8,128)S(1)} %get-tuple-element.93), channel_id=1, source_target_pairs={{0,6},{1,7},{2,4},{3,5},{4,2},{5,3},{6,0},{7,1},{8,14},{9,15},{10,... | collective-permute-start | bytes 196616 | tf_op jit(solution)/shard_map/ppermute | solution.py:22
  15.4 1.1 %collective-permute-start.9 = (f32[32,512]{1,0:T(8,128)S(1)}, f32[32,512]{1,0:T(8,128)S(1)}, u32[]{:S(2)}, u32[]{:S(2)}) collective-permute-start(f32[32,512]{1,0:T(8,128)S(1)} %get-tuple-element.94), channel_id=1, source_target_pairs={{0,2},{1,3},{2,0},{3,1},{4,6},{5,7},{6,4},{7,5},{8,10},{9,11},{10,... | collective-permute-start | bytes 196616 | tf_op jit(solution)/shard_map/ppermute | solution.py:22
  16.5 1.3 %collective-permute-start.6 = (f32[200,256]{1,0:T(8,128)S(1)}, f32[200,256]{1,0:T(8,128)S(1)}, u32[]{:S(2)}, u32[]{:S(2)}) collective-permute-start(f32[200,256]{1,0:T(8,128)S(1)} %get-tuple-element.90.carry_ref), channel_id=1, source_target_pairs={{8,0},{9,1},{10,2},{11,3},{12,4},{13,5},{14,6},{15,7},{24,16},{25,... | collective-permute-start | bytes 614408 | tf_op jit(solution)/shard_map/ppermute | solution.py:34
  17.8 0.1 shard_map.100.hot_ref
  17.9 0.1 collective-permute-start.7
  18.0 1.1 %shard_map.101 = (f32[160,640]{1,0:T(8,128)S(1)}, f32[160,640]{1,0:T(8,128)S(1)}) custom-call(f32[320,640]{1,0:T(8,128)S(1)} %get-tuple-element.96.all_ref, f32[320,320]{1,0:T(8,128)S(1)} %get-tuple-element.97.mine_ref, f32[320,384]{1,0:T(8,128)S(1)} %get-tuple-element.85.update_ref, f32[320,128]{1,0:T(8,128)S(1)} %get-tuple-element.100.y_ref), custom_call_target="tpu_custom_call" | custom-call | tf_op jit(solution)/shard_map/pallas_call | solution.py:79
  19.0 0.1 collective-permute-done.8.both_ref
  19.1 0.6 %collective-permute-done.9.far_ref = f32[32,512]{1,0:T(8,128)S(1)} collective-permute-done((f32[32,512]{1,0:T(8,128)S(1)}, f32[32,512]{1,0:T(8,128)S(1)}, u32[]{:S(2)}, u32[]{:S(2)}) %collective-permute-start.9) | collective-permute-done | bytes 65568 | tf_op jit(solution)/shard_map/ppermute | solution.py:22
  19.7 0.3 shard_map.102
  20.0 0.4 shard_map.103.up_ref
  20.3 2.1 %collective-permute-start.12 = (f32[32,512]{1,0:T(8,128)S(1)}, f32[32,512]{1,0:T(8,128)S(1)}, u32[]{:S(2)}, u32[]{:S(2)}) collective-permute-start(f32[32,512]{1,0:T(8,128)S(1)} %shard_map.103.up_ref), channel_id=1, source_target_pairs={{0,8},{1,9},{2,10},{3,11},{4,12},{5,13},{6,14},{7,15},{8,0},{9,1},... | collective-permute-start | bytes 196616 | tf_op jit(solution)/shard_map/ppermute | solution.py:22
  22.5 2.9 %collective-permute-done.6.received_ref = f32[200,256]{1,0:T(8,128)S(1)} collective-permute-done((f32[200,256]{1,0:T(8,128)S(1)}, f32[200,256]{1,0:T(8,128)S(1)}, u32[]{:S(2)}, u32[]{:S(2)}) %collective-permute-start.6) | collective-permute-done | bytes 204832 | tf_op jit(solution)/shard_map/ppermute | solution.py:34
  25.4 0.1 collective-permute-start.13
  25.5 0.8 %shard_map.105.refs_0_ = f32[32,256]{1,0:T(8,128)S(1)} custom-call(f32[32,256]{1,0:T(8,128)S(1)} %get-tuple-element.117.residual_ref, f32[200,256]{1,0:T(8,128)S(1)} %get-tuple-element.91.half_ref.refs_2_, f32[200,256]{1,0:T(8,128)S(1)} %collective-permute-done.7.near_ref.refs_4_), custom_call_target="tpu_custom_call" | custom-call | tf_op jit(solution)/shard_map/pallas_call | solution.py:79
  26.3 1.3 %collective-permute-start.11 = (f32[72,256]{1,0:T(8,128)S(1)}, f32[72,256]{1,0:T(8,128)S(1)}, u32[]{:S(2)}, u32[]{:S(2)}) collective-permute-start(f32[72,256]{1,0:T(8,128)S(1)} %get-tuple-element.113.root_ref), channel_id=1, source_target_pairs={{16,24},{17,25},{18,26},{19,27},{20,28},{21,29},{22,30},{23,31},{8... | collective-permute-start | bytes 221192 | tf_op jit(solution)/shard_map/ppermute | solution.py:34
  27.6 1.3 %collective-permute-start.19 = (f32[160,640]{1,0:T(8,128)S(1)}, f32[160,640]{1,0:T(8,128)S(1)}, u32[]{:S(2)}, u32[]{:S(2)}) collective-permute-start(f32[160,640]{1,0:T(8,128)S(1)} %get-tuple-element.135), channel_id=1, source_target_pairs={{2,0},{3,1},{6,4},{7,5},{10,8},{11,9},{14,12},{15,13},{18,16},{19,... | collective-permute-start | bytes 1228808 | tf_op jit(solution)/shard_map/ppermute | solution.py:22
  29.0 0.4 shard_map.107.up_ref
  29.3 2.8 %collective-permute-start.15 = (f32[32,256]{1,0:T(8,128)S(1)}, f32[32,256]{1,0:T(8,128)S(1)}, u32[]{:S(2)}, u32[]{:S(2)}) collective-permute-start(f32[32,256]{1,0:T(8,128)S(1)} %shard_map.107.up_ref), channel_id=1, source_target_pairs={{0,16},{1,17},{2,18},{3,19},{4,20},{5,21},{6,22},{7,23},{8,24},{9,... | collective-permute-start | bytes 98312 | tf_op jit(solution)/shard_map/ppermute | solution.py:22
  32.1 0.8 %shard_map.108.refs_1_ = f32[32,256]{1,0:T(8,128)S(1)} custom-call(f32[32,256]{1,0:T(8,128)S(1)} %get-tuple-element.124.residual_ref, f32[200,256]{1,0:T(8,128)S(1)} %get-tuple-element.115.half_ref.refs_3_, f32[200,256]{1,0:T(8,128)S(1)} %collective-permute-done.13.near_ref.refs_5_), custom_call_target="tpu_custom_call" | custom-call | tf_op jit(solution)/shard_map/pallas_call | solution.py:79
  32.9 0.1 collective-permute-start.14
  33.0 1.1 %collective-permute-done.15.partner_ref = f32[32,256]{1,0:T(8,128)S(1)} collective-permute-done((f32[32,256]{1,0:T(8,128)S(1)}, f32[32,256]{1,0:T(8,128)S(1)}, u32[]{:S(2)}, u32[]{:S(2)}) %collective-permute-start.15) | collective-permute-done | bytes 32800 | tf_op jit(solution)/shard_map/ppermute | solution.py:22
  34.2 0.1 collective-permute-done.14.root_near_ref
  34.3 1.6 %shard_map.111 = (f32[32,512]{1,0:T(8,128)S(1)}, f32[32,512]{1,0:T(8,128)S(1)}, f32[32,512]{1,0:T(8,128)S(1)}, f32[32,512]{1,0:T(8,128)S(1)}) custom-call(f32[32,256]{1,0:T(8,128)S(1)} %shard_map.110.residual_ref, f32[72,256]{1,0:T(8,128)S(1)} %shard_map.109.root_ref, f32[72,256]{1,0:T(8,128)S(1)} %collective-permute-done.14.root_near_ref, ...), custom_call_target="tpu_custom_call" | custom-call | tf_op jit(solution)/shard_map/pallas_call | solution.py:79
  35.9 2.3 %collective-permute-start.16 = (f32[32,512]{1,0:T(8,128)S(1)}, f32[32,512]{1,0:T(8,128)S(1)}, u32[]{:S(2)}, u32[]{:S(2)}) collective-permute-start(f32[32,512]{1,0:T(8,128)S(1)} %get-tuple-element.131), channel_id=1, source_target_pairs={{0,6},{1,7},{2,4},{3,5},{4,2},{5,3},{6,0},{7,1},{8,14},{9,15},{10,... | collective-permute-start | bytes 196616 | tf_op jit(solution)/shard_map/ppermute | solution.py:22
  38.2 0.5 %collective-permute-start.17 = (f32[32,512]{1,0:T(8,128)S(1)}, f32[32,512]{1,0:T(8,128)S(1)}, u32[]{:S(2)}, u32[]{:S(2)}) collective-permute-start(f32[32,512]{1,0:T(8,128)S(1)} %get-tuple-element.132), channel_id=1, source_target_pairs={{0,2},{1,3},{2,0},{3,1},{4,6},{5,7},{6,4},{7,5},{8,10},{9,11},{10,... | collective-permute-start | bytes 196616 | tf_op jit(solution)/shard_map/ppermute | solution.py:22
  38.7 1.4 %collective-permute-start.18 = (f32[32,512]{1,0:T(8,128)S(1)}, f32[32,512]{1,0:T(8,128)S(1)}, u32[]{:S(2)}, u32[]{:S(2)}) collective-permute-start(f32[32,512]{1,0:T(8,128)S(1)} %get-tuple-element.133), channel_id=1, source_target_pairs={{0,4},{1,5},{2,6},{3,7},{4,0},{5,1},{6,2},{7,3},{8,12},{9,13},{10,... | collective-permute-start | bytes 196616 | tf_op jit(solution)/shard_map/ppermute | solution.py:22
  40.0 1.7 %collective-permute-done.19.far_ref = f32[160,640]{1,0:T(8,128)S(1)} collective-permute-done((f32[160,640]{1,0:T(8,128)S(1)}, f32[160,640]{1,0:T(8,128)S(1)}, u32[]{:S(2)}, u32[]{:S(2)}) %collective-permute-start.19) | collective-permute-done | bytes 409632 | tf_op jit(solution)/shard_map/ppermute | solution.py:22
  41.8 1.0 %collective-permute-done.16.refs_3_ = f32[32,512]{1,0:T(8,128)S(1)} collective-permute-done((f32[32,512]{1,0:T(8,128)S(1)}, f32[32,512]{1,0:T(8,128)S(1)}, u32[]{:S(2)}, u32[]{:S(2)}) %collective-permute-start.16) | collective-permute-done | bytes 65568 | tf_op jit(solution)/shard_map/ppermute | solution.py:22
  42.8 1.4 %collective-permute-done.17.refs_1_ = f32[32,512]{1,0:T(8,128)S(1)} collective-permute-done((f32[32,512]{1,0:T(8,128)S(1)}, f32[32,512]{1,0:T(8,128)S(1)}, u32[]{:S(2)}, u32[]{:S(2)}) %collective-permute-start.17) | collective-permute-done | bytes 65568 | tf_op jit(solution)/shard_map/ppermute | solution.py:22
  44.2 0.1 collective-permute-start.20
  44.3 0.5 %collective-permute-start.21 = (f32[160,128]{1,0:T(8,128)S(1)}, f32[160,128]{1,0:T(8,128)S(1)}, u32[]{:S(2)}, u32[]{:S(2)}) collective-permute-start(f32[160,128]{1,0:T(8,128)S(1)} %get-tuple-element.147), channel_id=1, source_target_pairs={{0,1},{1,0},{2,3},{3,2},{4,5},{5,4},{6,7},{7,6},{8,9},{9,8},{10,11... | collective-permute-start | bytes 245768 | tf_op jit(solution)/shard_map/ppermute | solution.py:22
  44.8 0.3 shard_map.114.ours_ref
  45.2 0.7 %collective-permute-done.20.group_ref = f32[128,512]{1,0:T(8,128)S(1)} collective-permute-done((f32[128,512]{1,0:T(8,128)S(1)}, f32[128,512]{1,0:T(8,128)S(1)}, u32[]{:S(2)}, u32[]{:S(2)}) %collective-permute-start.20) | collective-permute-done | bytes 262176 | tf_op jit(solution)/shard_map/ppermute | solution.py:22
  45.8 0.1 collective-permute-done.21.base_near_ref
  45.9 1.0 %shard_map.115 = (f32[160,256]{1,0:T(8,128)}, f32[64,256]{1,0:T(8,128)}) custom-call(f32[224,512]{1,0:T(8,128)S(1)} %get-tuple-element.139.left_ref, f32[128,512]{1,0:T(8,128)S(1)} %collective-permute-done.20.group_ref, f32[224,128]{1,0:T(8,128)S(1)} %shard_map.114.ours_ref, f32[160,128]{1,0:T(8,128)S(1)} %get-tuple-element.146.base_ref, ...), custom_call_target="tpu_custom_call" | custom-call | tf_op jit(solution)/shard_map/pallas_call | solution.py:79
  (33 shorter events, 0.3 us)
Async XLA Ops:
  0.6 6.2 %copy-start.1 = (f32[1,256,256]{2,1,0:T(8,128)S(1)}, f32[1,256,256]{2,1,0:T(8,128)}, u32[]{:S(2)}) copy-start(f32[1,256,256]{2,1,0:T(8,128)} %param.15) | copy-start | bytes 786436
  0.6 9.3 %collective-permute-start = (f32[160,640]{1,0:T(8,128)}, f32[160,640]{1,0:T(8,128)S(1)}, u32[]{:S(2)}, u32[]{:S(2)}) collective-permute-start(f32[160,640]{1,0:T(8,128)} %bitcast.10), channel_id=1, source_target_pairs={{0,1},{1,0},{2,3},{3,2},{4,5},{5,4},{6,7},{7,6},{8,9},{9,8},{10,11... | collective-permute-start | bytes 1228808 | tf_op jit(solution)/shard_map/ppermute | solution.py:22
  1.2 1.8 %collective-permute-start.1 = (f32[160,256]{1,0:T(8,128)}, f32[160,256]{1,0:T(8,128)S(1)}, u32[]{:S(2)}, u32[]{:S(2)}) collective-permute-start(f32[160,256]{1,0:T(8,128)} %bitcast.16), channel_id=1, source_target_pairs={{0,1},{1,0},{2,3},{3,2},{4,5},{5,4},{6,7},{7,6},{8,9},{9,8},{10,11... | collective-permute-start | bytes 491528 | tf_op jit(solution)/shard_map/ppermute | solution.py:22
  1.2 9.9 %collective-permute-start.4 = (f32[160,384]{1,0:T(8,128)}, f32[160,384]{1,0:T(8,128)S(1)}, u32[]{:S(2)}, u32[]{:S(2)}) collective-permute-start(f32[160,384]{1,0:T(8,128)} %bitcast.14), channel_id=1, source_target_pairs={{0,1},{1,0},{2,3},{3,2},{4,5},{5,4},{6,7},{7,6},{8,9},{9,8},{10,11... | collective-permute-start | bytes 737288 | tf_op jit(solution)/shard_map/ppermute | solution.py:22
  3.0 0.9 %copy-start.4 = (f32[1,160,256]{2,1,0:T(8,128)S(1)}, f32[1,160,256]{2,1,0:T(8,128)}, u32[]{:S(2)}) copy-start(f32[1,160,256]{2,1,0:T(8,128)} %param.8) | copy-start | bytes 491524
  3.9 3.0 %copy-start.6 = (s32[1,384]{1,0:T(1,128)S(1)}, s32[1,384]{1,0:T(1,128)}, u32[]{:S(2)}) copy-start(s32[1,384]{1,0:T(1,128)} %lists_ref.1) | copy-start | bytes 4612
  3.9 3.0 %copy-start.7 = (s32[1,3]{1,0:T(1,128)S(1)}, s32[1,3]{1,0:T(1,128)}, u32[]{:S(2)}) copy-start(s32[1,3]{1,0:T(1,128)} %counts_ref.1) | copy-start | bytes 40
  3.9 7.2 %copy-start = (f32[1,160,640]{2,1,0:T(8,128)S(1)}, f32[1,160,640]{2,1,0:T(8,128)}, u32[]{:S(2)}) copy-start(f32[1,160,640]{2,1,0:T(8,128)} %param.9) | copy-start | bytes 1228804
  3.9 8.2 %collective-permute-start.3 = (f32[320,128]{1,0:T(8,128)S(1)}, f32[320,128]{1,0:T(8,128)S(1)}, u32[]{:S(2)}, u32[]{:S(2)}) collective-permute-start(f32[320,128]{1,0:T(8,128)S(1)} %shard_map.95.chip_ref), channel_id=1, source_target_pairs={{0,2},{1,3},{2,0},{3,1},{4,6},{5,7},{6,4},{7,5},{8,10},{9,11},{10,... | collective-permute-start | bytes 491528 | tf_op jit(solution)/shard_map/ppermute | solution.py:22
  6.9 1.0 %copy-start.2 = (f32[1,256,256]{2,1,0:T(8,128)S(1)}, f32[1,256,256]{2,1,0:T(8,128)}, u32[]{:S(2)}) copy-start(f32[1,256,256]{2,1,0:T(8,128)} %param.14) | copy-start | bytes 786436
  7.8 2.1 %copy-start.5 = (f32[1,64,256]{2,1,0:T(8,128)S(1)}, f32[1,64,256]{2,1,0:T(8,128)}, u32[]{:S(2)}) copy-start(f32[1,64,256]{2,1,0:T(8,128)} %param.13) | copy-start | bytes 196612
  7.8 3.4 %copy-start.3 = (f32[1,384,160]{1,2,0:T(8,128)S(1)}, f32[1,384,160]{1,2,0:T(8,128)}, u32[]{:S(2)}) copy-start(f32[1,384,160]{1,2,0:T(8,128)} %param.10) | copy-start | bytes 737284
  8.3 8.1 %collective-permute-start.2 = (f32[208,256]{1,0:T(8,128)S(1)}, f32[208,256]{1,0:T(8,128)S(1)}, u32[]{:S(2)}, u32[]{:S(2)}) collective-permute-start(f32[208,256]{1,0:T(8,128)S(1)} %shard_map.96.carry_ref.own_ref), channel_id=1, source_target_pairs={{0,4},{1,5},{2,6},{3,7},{4,0},{5,1},{6,2},{7,3},{8,12},{9,13},{10,... | collective-permute-start | bytes 638984 | tf_op jit(solution)/shard_map/ppermute | solution.py:22
  9.9 1.3 %collective-permute-start.5 = (f32[64,256]{1,0:T(8,128)S(1)}, f32[64,256]{1,0:T(8,128)S(1)}, u32[]{:S(2)}, u32[]{:S(2)}) collective-permute-start(f32[64,256]{1,0:T(8,128)S(1)} %bitcast.18), channel_id=1, source_target_pairs={{0,1},{1,0},{2,3},{3,2},{4,5},{5,4},{6,7},{7,6},{8,9},{9,8},{10,11... | collective-permute-start | bytes 196616 | tf_op jit(solution)/shard_map/ppermute | solution.py:22
  12.9 6.1 %collective-permute-start.10 = (f32[32,512]{1,0:T(8,128)S(1)}, f32[32,512]{1,0:T(8,128)S(1)}, u32[]{:S(2)}, u32[]{:S(2)}) collective-permute-start(f32[32,512]{1,0:T(8,128)S(1)} %get-tuple-element.95), channel_id=1, source_target_pairs={{0,4},{1,5},{2,6},{3,7},{4,0},{5,1},{6,2},{7,3},{8,12},{9,13},{10,... | collective-permute-start | bytes 196616 | tf_op jit(solution)/shard_map/ppermute | solution.py:22
  13.9 5.2 %collective-permute-start.8 = (f32[32,512]{1,0:T(8,128)S(1)}, f32[32,512]{1,0:T(8,128)S(1)}, u32[]{:S(2)}, u32[]{:S(2)}) collective-permute-start(f32[32,512]{1,0:T(8,128)S(1)} %get-tuple-element.93), channel_id=1, source_target_pairs={{0,6},{1,7},{2,4},{3,5},{4,2},{5,3},{6,0},{7,1},{8,14},{9,15},{10,... | collective-permute-start | bytes 196616 | tf_op jit(solution)/shard_map/ppermute | solution.py:22
  15.4 4.3 %collective-permute-start.9 = (f32[32,512]{1,0:T(8,128)S(1)}, f32[32,512]{1,0:T(8,128)S(1)}, u32[]{:S(2)}, u32[]{:S(2)}) collective-permute-start(f32[32,512]{1,0:T(8,128)S(1)} %get-tuple-element.94), channel_id=1, source_target_pairs={{0,2},{1,3},{2,0},{3,1},{4,6},{5,7},{6,4},{7,5},{8,10},{9,11},{10,... | collective-permute-start | bytes 196616 | tf_op jit(solution)/shard_map/ppermute | solution.py:22
  16.5 8.9 %collective-permute-start.6 = (f32[200,256]{1,0:T(8,128)S(1)}, f32[200,256]{1,0:T(8,128)S(1)}, u32[]{:S(2)}, u32[]{:S(2)}) collective-permute-start(f32[200,256]{1,0:T(8,128)S(1)} %get-tuple-element.90.carry_ref), channel_id=1, source_target_pairs={{8,0},{9,1},{10,2},{11,3},{12,4},{13,5},{14,6},{15,7},{24,16},{25,... | collective-permute-start | bytes 614408 | tf_op jit(solution)/shard_map/ppermute | solution.py:34
  17.9 2.1 %collective-permute-start.7 = (f32[200,256]{1,0:T(8,128)S(1)}, f32[200,256]{1,0:T(8,128)S(1)}, u32[]{:S(2)}, u32[]{:S(2)}) collective-permute-start(f32[200,256]{1,0:T(8,128)S(1)} %get-tuple-element.91.half_ref.refs_2_), channel_id=1, source_target_pairs={{0,1},{1,0},{2,3},{3,2},{4,5},{5,4},{6,7},{7,6},{8,9},{9,8},{10,11... | collective-permute-start | bytes 614408 | tf_op jit(solution)/shard_map/ppermute | solution.py:22
  20.3 8.6 %collective-permute-start.12 = (f32[32,512]{1,0:T(8,128)S(1)}, f32[32,512]{1,0:T(8,128)S(1)}, u32[]{:S(2)}, u32[]{:S(2)}) collective-permute-start(f32[32,512]{1,0:T(8,128)S(1)} %shard_map.103.up_ref), channel_id=1, source_target_pairs={{0,8},{1,9},{2,10},{3,11},{4,12},{5,13},{6,14},{7,15},{8,0},{9,1},... | collective-permute-start | bytes 196616 | tf_op jit(solution)/shard_map/ppermute | solution.py:22
  25.4 3.5 %collective-permute-start.13 = (f32[200,256]{1,0:T(8,128)S(1)}, f32[200,256]{1,0:T(8,128)S(1)}, u32[]{:S(2)}, u32[]{:S(2)}) collective-permute-start(f32[200,256]{1,0:T(8,128)S(1)} %get-tuple-element.115.half_ref.refs_3_), channel_id=1, source_target_pairs={{0,1},{1,0},{2,3},{3,2},{4,5},{5,4},{6,7},{7,6},{8,9},{9,8},{10,11... | collective-permute-start | bytes 614408 | tf_op jit(solution)/shard_map/ppermute | solution.py:22
  26.3 6.6 %collective-permute-start.11 = (f32[72,256]{1,0:T(8,128)S(1)}, f32[72,256]{1,0:T(8,128)S(1)}, u32[]{:S(2)}, u32[]{:S(2)}) collective-permute-start(f32[72,256]{1,0:T(8,128)S(1)} %get-tuple-element.113.root_ref), channel_id=1, source_target_pairs={{16,24},{17,25},{18,26},{19,27},{20,28},{21,29},{22,30},{23,31},{8... | collective-permute-start | bytes 221192 | tf_op jit(solution)/shard_map/ppermute | solution.py:34
  27.6 14.2 %collective-permute-start.19 = (f32[160,640]{1,0:T(8,128)S(1)}, f32[160,640]{1,0:T(8,128)S(1)}, u32[]{:S(2)}, u32[]{:S(2)}) collective-permute-start(f32[160,640]{1,0:T(8,128)S(1)} %get-tuple-element.135), channel_id=1, source_target_pairs={{2,0},{3,1},{6,4},{7,5},{10,8},{11,9},{14,12},{15,13},{18,16},{19,... | collective-permute-start | bytes 1228808 | tf_op jit(solution)/shard_map/ppermute | solution.py:22
  29.3 4.9 %collective-permute-start.15 = (f32[32,256]{1,0:T(8,128)S(1)}, f32[32,256]{1,0:T(8,128)S(1)}, u32[]{:S(2)}, u32[]{:S(2)}) collective-permute-start(f32[32,256]{1,0:T(8,128)S(1)} %shard_map.107.up_ref), channel_id=1, source_target_pairs={{0,16},{1,17},{2,18},{3,19},{4,20},{5,21},{6,22},{7,23},{8,24},{9,... | collective-permute-start | bytes 98312 | tf_op jit(solution)/shard_map/ppermute | solution.py:22
  32.9 1.3 %collective-permute-start.14 = (f32[72,256]{1,0:T(8,128)S(1)}, f32[72,256]{1,0:T(8,128)S(1)}, u32[]{:S(2)}, u32[]{:S(2)}) collective-permute-start(f32[72,256]{1,0:T(8,128)S(1)} %shard_map.109.root_ref), channel_id=1, source_target_pairs={{0,1},{1,0},{2,3},{3,2},{4,5},{5,4},{6,7},{7,6},{8,9},{9,8},{10,11... | collective-permute-start | bytes 221192 | tf_op jit(solution)/shard_map/ppermute | solution.py:22
  35.9 6.9 %collective-permute-start.16 = (f32[32,512]{1,0:T(8,128)S(1)}, f32[32,512]{1,0:T(8,128)S(1)}, u32[]{:S(2)}, u32[]{:S(2)}) collective-permute-start(f32[32,512]{1,0:T(8,128)S(1)} %get-tuple-element.131), channel_id=1, source_target_pairs={{0,6},{1,7},{2,4},{3,5},{4,2},{5,3},{6,0},{7,1},{8,14},{9,15},{10,... | collective-permute-start | bytes 196616 | tf_op jit(solution)/shard_map/ppermute | solution.py:22
  38.2 6.0 %collective-permute-start.17 = (f32[32,512]{1,0:T(8,128)S(1)}, f32[32,512]{1,0:T(8,128)S(1)}, u32[]{:S(2)}, u32[]{:S(2)}) collective-permute-start(f32[32,512]{1,0:T(8,128)S(1)} %get-tuple-element.132), channel_id=1, source_target_pairs={{0,2},{1,3},{2,0},{3,1},{4,6},{5,7},{6,4},{7,5},{8,10},{9,11},{10,... | collective-permute-start | bytes 196616 | tf_op jit(solution)/shard_map/ppermute | solution.py:22
  38.7 5.5 %collective-permute-start.18 = (f32[32,512]{1,0:T(8,128)S(1)}, f32[32,512]{1,0:T(8,128)S(1)}, u32[]{:S(2)}, u32[]{:S(2)}) collective-permute-start(f32[32,512]{1,0:T(8,128)S(1)} %get-tuple-element.133), channel_id=1, source_target_pairs={{0,4},{1,5},{2,6},{3,7},{4,0},{5,1},{6,2},{7,3},{8,12},{9,13},{10,... | collective-permute-start | bytes 196616 | tf_op jit(solution)/shard_map/ppermute | solution.py:22
  44.2 1.6 %collective-permute-start.20 = (f32[128,512]{1,0:T(8,128)S(1)}, f32[128,512]{1,0:T(8,128)S(1)}, u32[]{:S(2)}, u32[]{:S(2)}) collective-permute-start(f32[128,512]{1,0:T(8,128)S(1)} %shard_map.113.group_ref), channel_id=1, source_target_pairs={{0,1},{1,0},{2,3},{3,2},{4,5},{5,4},{6,7},{7,6},{8,9},{9,8},{10,11... | collective-permute-start | bytes 786440 | tf_op jit(solution)/shard_map/ppermute | solution.py:22
  44.3 1.6 %collective-permute-start.21 = (f32[160,128]{1,0:T(8,128)S(1)}, f32[160,128]{1,0:T(8,128)S(1)}, u32[]{:S(2)}, u32[]{:S(2)}) collective-permute-start(f32[160,128]{1,0:T(8,128)S(1)} %get-tuple-element.147), channel_id=1, source_target_pairs={{0,1},{1,0},{2,3},{3,2},{4,5},{5,4},{6,7},{7,6},{8,9},{9,8},{10,11... | collective-permute-start | bytes 245768 | tf_op jit(solution)/shard_map/ppermute | solution.py:22

commit v4 on v3

--- a/solution.py
+++ b/solution.py
@@ -140,13 +140,18 @@
     inverse_near = swap(inverse, 0, 1)
     rows_near = swap(rows_source, 0, 1)
 
-    def chip_source(source_ref, near_ref, out_ref):
-        near_bit = place()[4]
-        own, other = source_ref[...], near_ref[...]
-        out_ref[at(near_bit, rows)] = by_bit(near_bit, own[:, :half], own[:, half:])
-        out_ref[at(1 - near_bit, rows)] = by_bit(near_bit, other[:, :half], other[:, half:])
-
-    (chip,) = stage(chip_source, [(2 * rows, half)], source, near)
+    def own_columns_of(source_ref, out_ref):
+        near_bit = place()[4]
+        out_ref[...] = by_bit(near_bit, source_ref[:, :half], source_ref[:, half:])
+
+    def chip_source(own_ref, near_ref, out_ref):
+        near_bit = place()[4]
+        out_ref[at(near_bit, rows)] = own_ref[...]
+        out_ref[at(1 - near_bit, rows)] = by_bit(near_bit, near_ref[:, :half], near_ref[:, half:])
+
+    (own_source,) = stage(own_columns_of, [(rows, half)], source)
+    near, rows_near, own_source = after(near, rows_near, own_source)
+    (chip,) = stage(chip_source, [(2 * rows, half)], own_source, near)
     far = swap(chip, 0, 2)
 
     def operators(coupling_ref, inverse_ref, lists_ref, counts_ref, out_ref, coupling, inverse, lists, counts, packed, sems):
@@ -370,36 +375,46 @@
         if out_ref.shape[1] > order:
             out_ref[:, order:] = slots_ref[:, order:]
 
-    def inverse_of(own, other, out_ref):
+    def blocks_of(own, other):
         near_bit = place()[4]
         row = lax.broadcasted_iota(jnp.int32, (middle, middle), 0)
         lane = lax.broadcasted_iota(jnp.int32, (middle, middle), 1)
         packed = jnp.concatenate([by_bit(near_bit, own, other), by_bit(near_bit, other, own)], 0)
         both = packed[:middle, :middle]
-        last = jnp.where(row > lane, jnp.transpose(both), 0.0)
-        out_ref[:middle, :middle] = jnp.where(row >= lane, both, 0.0)
-        out_ref[:middle, middle:] = jnp.zeros((middle, middle), f32)
-        out_ref[middle:, :middle] = packed[:middle, middle:]
-        out_ref[middle:, middle:] = jnp.where(row == lane, packed[middle : middle + 1, :middle], last)
-
-    def alone(residual_ref, half_ref, near_ref, out_ref, work):
-        inverse_of(half_ref[middle:], near_ref[middle:], work)
-        out_ref[...] = dot(dot(residual_ref[...], work[...], 1, 1), work[...])
+        last = jnp.where(row < lane, both, 0.0)
+        last = jnp.where(row == lane, packed[middle : middle + 1, :middle], last)
+        return jnp.where(row >= lane, both, 0.0), packed[:middle, middle:], last
+
+    def alone(residual_ref, half_ref, near_ref, out_ref, down_ref):
+        down_ref[...] = operator_of(half_ref, near_ref)
+        first, below, last = blocks_of(half_ref[middle:], near_ref[middle:])
+        one, two = residual_ref[:, :middle], residual_ref[:, middle:]
+        upper, lower = dot3(one, first, 1, 1), dot3(one, below, 1, 1) + dot3(two, last)
+        out_ref[:, :middle] = dot3(upper, first) + dot3(lower, below)
+        out_ref[:, middle:] = dot3(lower, last, 1, 1)
 
     def level_sum(up_ref, partner_ref, residual_ref, rest_ref):
         total = up_ref[...] + partner_ref[...]
         residual_ref[...] = total[:, :order]
         rest_ref[...] = total[:, order:]
 
-    partials = []
+    partials, downs = [], []
     halves_near[0], residual, slots = after(halves_near[0], residual, slots)
     (going_up,) = stage(
         push, [(block, (depth - 1) * order)], slots, residual, halves[0], halves_near[0]
     )
     for level in range(2, depth):
         partner = swap(going_up, 2 ** (level - 1), 0)
+        residuals[-1], going_up = after(residuals[-1], going_up)
+        partial, down = stage(
+            alone,
+            [(block, order), (order, order)],
+            residuals[-1],
+            halves[level - 2],
+            halves_near[level - 2],
+        )
         if level == depth - 1:
-            reached, going_up, far_sum = after(reached, going_up, far_sum)
+            reached, partial = after(reached, partial)
             new_half, root = stage(
                 last_forward, [(carried, order), (packed_rows, order)], carry, reached
             )
@@ -407,15 +422,7 @@
             from_far = swap(far_sum, 0, 2, lambda leaf, sep: sep // 2 == 1)
             halves_near.append(swap(new_half, 0, 1))
             by_root = quarter_swap(root, ((2, 3), (1, 0)))
-        residuals[-1], going_up, new_half = after(residuals[-1], going_up, halves[-1])
-        (partial,) = stage(
-            alone,
-            [(block, order)],
-            residuals[-1],
-            halves[level - 2],
-            halves_near[level - 2],
-            scratch=[(order, order)],
-        )
+        downs.append(down)
         partials.append(partial)
         partner, partial = after(partner, partial)
         residual, slots = stage(
@@ -423,7 +430,7 @@
             [(block, order), (block, (depth - level) * order)],
             going_up,
             partner,
-            cost=long,
+            cost=3 * medium,
         )
         residuals.append(residual)
         halves_near[level - 1], residual, slots = after(halves_near[level - 1], residual, slots)
@@ -438,15 +445,15 @@
     partner = swap(going_up, 2 ** (depth - 1), 0)
 
     residuals[-1], going_up = after(residuals[-1], going_up)
-    (partial,) = stage(
+    partial, down = stage(
         alone,
-        [(block, order)],
+        [(block, order), (order, order)],
         residuals[-1],
         halves[-1],
         halves_near[-1],
-        scratch=[(order, order)],
     )
     partials.append(partial)
+    downs.append(down)
     by_root, partial = after(by_root, partial)
     (root,) = stage(root_half, [(packed_rows, order)], root, by_root)
     root_near = swap(root, 0, 1)
@@ -460,14 +467,19 @@
 
     def way_down(residual_ref, root_ref, root_near_ref, hot_ref, *refs):
         leaf, _, odd, far_bit, _ = place()
-        partial_refs, half_refs = refs[: depth - 1], refs[depth - 1 : 2 * depth - 2]
-        near_refs, out_refs, work = refs[2 * depth - 2 : 3 * depth - 3], refs[3 * depth - 3 : -1], refs[-1]
-        inverse_of(root_ref[...], root_near_ref[...], work)
+        partial_refs, down_refs = refs[: depth - 1], refs[depth - 1 : 2 * depth - 2]
+        out_refs = refs[2 * depth - 2 :]
+        first, below, last = blocks_of(root_ref[...], root_near_ref[...])
+        one, two = residual_ref[:, :middle], residual_ref[:, middle:]
+        upper, lower = dot3(one, first, 1, 1), dot3(one, below, 1, 1) + dot3(two, last)
         solved = [None] * depth
-        solved[-1] = dot(dot(residual_ref[...], work[...], 1, 1), work[...])
+        solved[-1] = jnp.concatenate(
+            [dot3(upper, first) + dot3(lower, below), dot3(lower, last, 1, 1)], 1
+        )
         for level in range(depth - 1, 0, -1):
-            down = operator_of(half_refs[level - 1], near_refs[level - 1])
-            solved[level - 1] = partial_refs[level - 1][...] - dot(solved[level], down)
+            solved[level - 1] = partial_refs[level - 1][...] - dot3(
+                solved[level], down_refs[level - 1][...]
+            )
         even_solved = jnp.zeros_like(solved[0])
         for level in range(2, depth + 1):
             here = lax.rem(leaf - odd, 2**level) == 2 ** (level - 1)
@@ -495,9 +507,7 @@
         root_near,
         hots,
         *partials,
-        *halves,
-        *halves_near,
-        scratch=[(order, order)],
+        *downs,
     )
     both = swap(to_both, 1, 2)
     beyond = swap(to_far, 0, 2)

time: 47.2 us -> 43.3 us (0.917)
  waiting for transfers between devices: 12.2 us -> 9.89 us
  Pallas kernels: 9.07 us -> 7.89 us
  local copies, waits for them, and re-layouts: 1.89 us -> 0.95 us
  starting transfers between devices: 22.9 us -> 23.5 us
    ppermute x2, waiting for transfers between devices: 2.92 us -> 0.56 us  [quarter_swap(): return lax.ppermute(payload, axes, pairs)]
    pallas_call x21 -> x22, Pallas kernels: 9.07 us -> 7.89 us  [stage(): pl.pallas_call(body, out_shape=[jax.ShapeDtypeStruct(shape, f32) if isins...]
    unnamed x16, local copies, waits for them, and re-layouts: 1.89 us -> 0.95 us
    ppermute x20, starting transfers between devices: 20.3 us -> 20.9 us  [swap(): return lax.ppermute(payload, axes, pairs)]
  transfers between devices with their start and end apart: 22 -> 22, of which waited for: 12 -> 13; matrix products, arithmetic and copies ran while one was open for 0% -> 0% of each run, Pallas kernels for 17% -> 16%
where the time goes in v4:
time: 43.3 us; the launch traced here: 43.1 us
  starting transfers between devices  23.5 us (54%)
  waiting for transfers between devices  9.89 us (23%)
  Pallas kernels  7.89 us (18%)
  local copies, waits for them, and re-layouts  0.95 us (2%)
  between operations  0.9 us (2%)
    ppermute x20, starting transfers between devices, swap(): return lax.ppermute(payload, axes, pairs)  20.9 us
    ppermute x20, waiting for transfers between devices, swap(): return lax.ppermute(payload, axes, pairs)  9.33 us
    pallas_call x22, Pallas kernels, stage(): pl.pallas_call(body, out_shape=[jax.ShapeDtypeStruct(shape, f32) if isins...  7.89 us
    ppermute x2, starting transfers between devices, quarter_swap(): return lax.ppermute(payload, axes, pairs)  2.58 us
    unnamed x16, local copies, waits for them, and re-layouts  0.95 us
  transfers between devices with their start and end apart: 22, of which 13 were waited for; matrix products, arithmetic and copies ran while one was open for 0% of the time, Pallas kernels for 16%

profile of v4, /device:TPU:0, one launch (start us, length us, event | category | flops | bytes accessed | tf_op | source)
XLA Modules:
  0.0 43.1 jit_solution(17884264019117773969)
XLA Ops:
  0.6 0.5 %collective-permute-start = (f32[160,640]{1,0:T(8,128)}, f32[160,640]{1,0:T(8,128)S(1)}, u32[]{:S(2)}, u32[]{:S(2)}) collective-permute-start(f32[160,640]{1,0:T(8,128)} %bitcast.10), channel_id=1, source_target_pairs={{0,1},{1,0},{2,3},{3,2},{4,5},{5,4},{6,7},{7,6},{8,9},{9,8},{10,11... | collective-permute-start | bytes 1228808 | tf_op jit(solution)/shard_map/ppermute | solution.py:22
  1.1 0.1 collective-permute-start.1
  1.2 0.4 collective-permute-start.5
  1.7 0.1 collective-permute-start.2
  1.7 0.9 %copy-done.4 = f32[1,160,256]{2,1,0:T(8,128)S(1)} copy-done((f32[1,160,256]{2,1,0:T(8,128)S(1)}, f32[1,160,256]{2,1,0:T(8,128)}, u32[]{:S(2)}) %copy-start.4) | copy-done | bytes 163864
  2.7 0.7 %collective-permute-done.2.rows_near_ref = f32[64,256]{1,0:T(8,128)S(1)} collective-permute-done((f32[64,256]{1,0:T(8,128)}, f32[64,256]{1,0:T(8,128)S(1)}, u32[]{:S(2)}, u32[]{:S(2)}) %collective-permute-start.2) | collective-permute-done | bytes 65568 | tf_op jit(solution)/shard_map/ppermute | solution.py:22
  3.5 2.9 %collective-permute-start.4 = (f32[320,128]{1,0:T(8,128)S(1)}, f32[320,128]{1,0:T(8,128)S(1)}, u32[]{:S(2)}, u32[]{:S(2)}) collective-permute-start(f32[320,128]{1,0:T(8,128)S(1)} %shard_map.96.chip_ref), channel_id=1, source_target_pairs={{0,2},{1,3},{2,0},{3,1},{4,6},{5,7},{6,4},{7,5},{8,10},{9,11},{10,... | collective-permute-start | bytes 491528 | tf_op jit(solution)/shard_map/ppermute | solution.py:22
  6.4 0.5 %shard_map.97.carry_ref.own_ref = f32[208,256]{1,0:T(8,128)S(1)} custom-call(f32[256,256]{1,0:T(8,128)S(1)} %bitcast.12, f32[256,256]{1,0:T(8,128)S(1)} %bitcast.13, s32[1,384]{1,0:T(1,128)S(1)} %copy-done.6, s32[1,3]{1,0:T(1,128)S(1)} %copy-done.7), custom_call_target="tpu_custom_call" | custom-call | tf_op jit(solution)/shard_map/pallas_call | solution.py:79
  6.9 1.6 %collective-permute-start.3 = (f32[208,256]{1,0:T(8,128)S(1)}, f32[208,256]{1,0:T(8,128)S(1)}, u32[]{:S(2)}, u32[]{:S(2)}) collective-permute-start(f32[208,256]{1,0:T(8,128)S(1)} %shard_map.97.carry_ref.own_ref), channel_id=1, source_target_pairs={{0,4},{1,5},{2,6},{3,7},{4,0},{5,1},{6,2},{7,3},{8,12},{9,13},{10,... | collective-permute-start | bytes 638984 | tf_op jit(solution)/shard_map/ppermute | solution.py:22
  8.6 0.9 %shard_map.98 = (f32[320,128]{1,0:T(8,128)S(1)}, f32[320,640]{1,0:T(8,128)S(1)}, f32[320,320]{1,0:T(8,128)S(1)}, f32[320,320]{1,0:T(8,128)S(1)}, f32[320,384]{1,0:T(8,128)S(1)}, /*index=5*/f32[128,128]{1,0:T(8,128)S(1)}) custom-call(f32[160,640]{1,0:T(8,128)S(1)} %bitcast.11, f32[160,640]{1,0:T(8,128)S(1)} %collective-permute-done.inverse_near_ref, ...), custom_call_target="tpu_custom_call" | custom-call | tf_op jit(solution)/shard_map/pallas_call | solution.py:79
  9.5 1.4 %collective-permute-done.4.far_ref = f32[320,128]{1,0:T(8,128)S(1)} collective-permute-done((f32[320,128]{1,0:T(8,128)S(1)}, f32[320,128]{1,0:T(8,128)S(1)}, u32[]{:S(2)}, u32[]{:S(2)}) %collective-permute-start.4) | collective-permute-done | bytes 163872 | tf_op jit(solution)/shard_map/ppermute | solution.py:22
  10.9 0.7 %shard_map.99 = (f32[320,128]{1,0:T(8,128)S(1)}, f32[32,512]{1,0:T(8,128)S(1)}, f32[32,512]{1,0:T(8,128)S(1)}, f32[32,512]{1,0:T(8,128)S(1)}, f32[32,512]{1,0:T(8,128)S(1)}) custom-call(f32[320,128]{1,0:T(8,128)S(1)} %get-tuple-element.91.own_ref, f32[320,320]{1,0:T(8,128)S(1)} %get-tuple-element.92.inverse_ref, ...), custom_call_target="tpu_custom_call" | custom-call | tf_op jit(solution)/shard_map/pallas_call | solution.py:79
  11.6 2.8 %collective-permute-start.7 = (f32[32,512]{1,0:T(8,128)S(1)}, f32[32,512]{1,0:T(8,128)S(1)}, u32[]{:S(2)}, u32[]{:S(2)}) collective-permute-start(f32[32,512]{1,0:T(8,128)S(1)} %get-tuple-element.101), channel_id=1, source_target_pairs={{0,6},{1,7},{2,4},{3,5},{4,2},{5,3},{6,0},{7,1},{8,14},{9,15},{10,... | collective-permute-start | bytes 196616 | tf_op jit(solution)/shard_map/ppermute | solution.py:22
  14.4 0.5 %collective-permute-start.8 = (f32[32,512]{1,0:T(8,128)S(1)}, f32[32,512]{1,0:T(8,128)S(1)}, u32[]{:S(2)}, u32[]{:S(2)}) collective-permute-start(f32[32,512]{1,0:T(8,128)S(1)} %get-tuple-element.102), channel_id=1, source_target_pairs={{0,2},{1,3},{2,0},{3,1},{4,6},{5,7},{6,4},{7,5},{8,10},{9,11},{10,... | collective-permute-start | bytes 196616 | tf_op jit(solution)/shard_map/ppermute | solution.py:22
  14.9 0.3 collective-permute-start.9
  15.2 1.3 %collective-permute-start.6 = (f32[200,256]{1,0:T(8,128)S(1)}, f32[200,256]{1,0:T(8,128)S(1)}, u32[]{:S(2)}, u32[]{:S(2)}) collective-permute-start(f32[200,256]{1,0:T(8,128)S(1)} %get-tuple-element.99.carry_ref), channel_id=1, source_target_pairs={{8,0},{9,1},{10,2},{11,3},{12,4},{13,5},{14,6},{15,7},{24,16},{25,... | collective-permute-start | bytes 614408 | tf_op jit(solution)/shard_map/ppermute | solution.py:34
  16.5 0.1 shard_map.101.hot_ref
  16.7 1.1 %shard_map.102 = (f32[160,640]{1,0:T(8,128)S(1)}, f32[160,640]{1,0:T(8,128)S(1)}) custom-call(f32[320,640]{1,0:T(8,128)S(1)} %get-tuple-element.104.all_ref, f32[320,320]{1,0:T(8,128)S(1)} %get-tuple-element.105.mine_ref, f32[320,384]{1,0:T(8,128)S(1)} %get-tuple-element.94.update_ref, f32[320,128]{1,0:T(8,128)S(1)} %get-tuple-element.108.y_ref), custom_call_target="tpu_custom_call" | custom-call | tf_op jit(solution)/shard_map/pallas_call | solution.py:79
  17.8 0.9 %collective-permute-done.8.far_ref = f32[32,512]{1,0:T(8,128)S(1)} collective-permute-done((f32[32,512]{1,0:T(8,128)S(1)}, f32[32,512]{1,0:T(8,128)S(1)}, u32[]{:S(2)}, u32[]{:S(2)}) %collective-permute-start.8) | collective-permute-done | bytes 65568 | tf_op jit(solution)/shard_map/ppermute | solution.py:22
  18.6 0.5 %collective-permute-done.9.odd_ref = f32[32,512]{1,0:T(8,128)S(1)} collective-permute-done((f32[32,512]{1,0:T(8,128)S(1)}, f32[32,512]{1,0:T(8,128)S(1)}, u32[]{:S(2)}, u32[]{:S(2)}) %collective-permute-start.9) | collective-permute-done | bytes 65568 | tf_op jit(solution)/shard_map/ppermute | solution.py:22
  19.2 0.3 shard_map.103
  19.5 0.4 shard_map.104.up_ref
  19.8 1.6 %collective-permute-start.12 = (f32[32,512]{1,0:T(8,128)S(1)}, f32[32,512]{1,0:T(8,128)S(1)}, u32[]{:S(2)}, u32[]{:S(2)}) collective-permute-start(f32[32,512]{1,0:T(8,128)S(1)} %shard_map.104.up_ref), channel_id=1, source_target_pairs={{0,8},{1,9},{2,10},{3,11},{4,12},{5,13},{6,14},{7,15},{8,0},{9,1},... | collective-permute-start | bytes 196616 | tf_op jit(solution)/shard_map/ppermute | solution.py:22
  21.5 1.3 %collective-permute-start.19 = (f32[160,640]{1,0:T(8,128)S(1)}, f32[160,640]{1,0:T(8,128)S(1)}, u32[]{:S(2)}, u32[]{:S(2)}) collective-permute-start(f32[160,640]{1,0:T(8,128)S(1)} %get-tuple-element.147), channel_id=1, source_target_pairs={{2,0},{3,1},{6,4},{7,5},{10,8},{11,9},{14,12},{15,13},{18,16},{19,... | collective-permute-start | bytes 1228808 | tf_op jit(solution)/shard_map/ppermute | solution.py:22
  22.8 0.5 %shard_map.105 = (f32[32,256]{1,0:T(8,128)S(1)}, f32[256,256]{1,0:T(8,128)S(1)}) custom-call(f32[32,256]{1,0:T(8,128)S(1)} %get-tuple-element.120.residual_ref, f32[200,256]{1,0:T(8,128)S(1)} %get-tuple-element.115.half_ref, f32[200,256]{1,0:T(8,128)S(1)} %collective-permute-done.10.near_ref), custom_call_target="tpu_custom_call" | custom-call | tf_op jit(solution)/shard_map/pallas_call | solution.py:79
  23.3 0.1 collective-permute-start.13
  23.4 1.3 %collective-permute-start.11 = (f32[72,256]{1,0:T(8,128)S(1)}, f32[72,256]{1,0:T(8,128)S(1)}, u32[]{:S(2)}, u32[]{:S(2)}) collective-permute-start(f32[72,256]{1,0:T(8,128)S(1)} %get-tuple-element.123.root_ref), channel_id=1, source_target_pairs={{16,24},{17,25},{18,26},{19,27},{20,28},{21,29},{22,30},{23,31},{8... | collective-permute-start | bytes 221192 | tf_op jit(solution)/shard_map/ppermute | solution.py:34
  24.7 0.1 collective-permute-done.13.near_ref
  24.8 0.3 shard_map.108.up_ref
  25.2 3.8 %collective-permute-start.15 = (f32[32,256]{1,0:T(8,128)S(1)}, f32[32,256]{1,0:T(8,128)S(1)}, u32[]{:S(2)}, u32[]{:S(2)}) collective-permute-start(f32[32,256]{1,0:T(8,128)S(1)} %shard_map.108.up_ref), channel_id=1, source_target_pairs={{0,16},{1,17},{2,18},{3,19},{4,20},{5,21},{6,22},{7,23},{8,24},{9,... | collective-permute-start | bytes 98312 | tf_op jit(solution)/shard_map/ppermute | solution.py:22
  28.9 0.5 %shard_map.109 = (f32[32,256]{1,0:T(8,128)S(1)}, f32[256,256]{1,0:T(8,128)S(1)}) custom-call(f32[32,256]{1,0:T(8,128)S(1)} %get-tuple-element.133.residual_ref, f32[200,256]{1,0:T(8,128)S(1)} %get-tuple-element.128.half_ref, f32[200,256]{1,0:T(8,128)S(1)} %collective-permute-done.13.near_ref), custom_call_target="tpu_custom_call" | custom-call | tf_op jit(solution)/shard_map/pallas_call | solution.py:79
  29.4 0.6 %collective-permute-done.11.received_ref = f32[72,256]{1,0:T(8,128)S(1)} collective-permute-done((f32[72,256]{1,0:T(8,128)S(1)}, f32[72,256]{1,0:T(8,128)S(1)}, u32[]{:S(2)}, u32[]{:S(2)}) %collective-permute-start.11) | collective-permute-done | bytes 73760 | tf_op jit(solution)/shard_map/ppermute | solution.py:34
  29.9 0.1 collective-permute-start.14
  30.0 0.8 %collective-permute-done.15.partner_ref = f32[32,256]{1,0:T(8,128)S(1)} collective-permute-done((f32[32,256]{1,0:T(8,128)S(1)}, f32[32,256]{1,0:T(8,128)S(1)}, u32[]{:S(2)}, u32[]{:S(2)}) %collective-permute-start.15) | collective-permute-done | bytes 32800 | tf_op jit(solution)/shard_map/ppermute | solution.py:22
  30.8 0.5 %collective-permute-done.14.root_near_ref = f32[72,256]{1,0:T(8,128)S(1)} collective-permute-done((f32[72,256]{1,0:T(8,128)S(1)}, f32[72,256]{1,0:T(8,128)S(1)}, u32[]{:S(2)}, u32[]{:S(2)}) %collective-permute-start.14) | collective-permute-done | bytes 73760 | tf_op jit(solution)/shard_map/ppermute | solution.py:22
  31.3 1.0 %shard_map.112 = (f32[32,512]{1,0:T(8,128)S(1)}, f32[32,512]{1,0:T(8,128)S(1)}, f32[32,512]{1,0:T(8,128)S(1)}, f32[32,512]{1,0:T(8,128)S(1)}) custom-call(f32[32,256]{1,0:T(8,128)S(1)} %shard_map.111.residual_ref, f32[72,256]{1,0:T(8,128)S(1)} %shard_map.110.root_ref, f32[72,256]{1,0:T(8,128)S(1)} %collective-permute-done.14.root_near_ref, ...), custom_call_target="tpu_custom_call" | custom-call | tf_op jit(solution)/shard_map/pallas_call | solution.py:79
  32.3 3.7 %collective-permute-start.16 = (f32[32,512]{1,0:T(8,128)S(1)}, f32[32,512]{1,0:T(8,128)S(1)}, u32[]{:S(2)}, u32[]{:S(2)}) collective-permute-start(f32[32,512]{1,0:T(8,128)S(1)} %get-tuple-element.143), channel_id=1, source_target_pairs={{0,6},{1,7},{2,4},{3,5},{4,2},{5,3},{6,0},{7,1},{8,14},{9,15},{10,... | collective-permute-start | bytes 196616 | tf_op jit(solution)/shard_map/ppermute | solution.py:22
  36.0 0.1 collective-permute-start.17
  36.1 0.5 %collective-permute-start.18 = (f32[32,512]{1,0:T(8,128)S(1)}, f32[32,512]{1,0:T(8,128)S(1)}, u32[]{:S(2)}, u32[]{:S(2)}) collective-permute-start(f32[32,512]{1,0:T(8,128)S(1)} %get-tuple-element.145), channel_id=1, source_target_pairs={{0,4},{1,5},{2,6},{3,7},{4,0},{5,1},{6,2},{7,3},{8,12},{9,13},{10,... | collective-permute-start | bytes 196616 | tf_op jit(solution)/shard_map/ppermute | solution.py:22
  36.7 1.7 %collective-permute-done.16.refs_3_ = f32[32,512]{1,0:T(8,128)S(1)} collective-permute-done((f32[32,512]{1,0:T(8,128)S(1)}, f32[32,512]{1,0:T(8,128)S(1)}, u32[]{:S(2)}, u32[]{:S(2)}) %collective-permute-start.16) | collective-permute-done | bytes 65568 | tf_op jit(solution)/shard_map/ppermute | solution.py:22
  38.4 1.9 %collective-permute-done.17.refs_1_ = f32[32,512]{1,0:T(8,128)S(1)} collective-permute-done((f32[32,512]{1,0:T(8,128)S(1)}, f32[32,512]{1,0:T(8,128)S(1)}, u32[]{:S(2)}, u32[]{:S(2)}) %collective-permute-start.17) | collective-permute-done | bytes 65568 | tf_op jit(solution)/shard_map/ppermute | solution.py:22
  40.2 0.1 collective-permute-done.18.refs_2_
  40.4 0.1 collective-permute-start.20
  40.5 0.5 %collective-permute-start.21 = (f32[160,128]{1,0:T(8,128)S(1)}, f32[160,128]{1,0:T(8,128)S(1)}, u32[]{:S(2)}, u32[]{:S(2)}) collective-permute-start(f32[160,128]{1,0:T(8,128)S(1)} %get-tuple-element.159), channel_id=1, source_target_pairs={{0,1},{1,0},{2,3},{3,2},{4,5},{5,4},{6,7},{7,6},{8,9},{9,8},{10,11... | collective-permute-start | bytes 245768 | tf_op jit(solution)/shard_map/ppermute | solution.py:22
  41.0 0.4 shard_map.115.ours_ref
  41.3 0.7 %collective-permute-done.20.group_ref = f32[128,512]{1,0:T(8,128)S(1)} collective-permute-done((f32[128,512]{1,0:T(8,128)S(1)}, f32[128,512]{1,0:T(8,128)S(1)}, u32[]{:S(2)}, u32[]{:S(2)}) %collective-permute-start.20) | collective-permute-done | bytes 262176 | tf_op jit(solution)/shard_map/ppermute | solution.py:22
  42.0 0.1 collective-permute-done.21.base_near_ref
  42.1 1.0 %shard_map.116 = (f32[160,256]{1,0:T(8,128)}, f32[64,256]{1,0:T(8,128)}) custom-call(f32[224,512]{1,0:T(8,128)S(1)} %get-tuple-element.151.left_ref, f32[128,512]{1,0:T(8,128)S(1)} %collective-permute-done.20.group_ref, f32[224,128]{1,0:T(8,128)S(1)} %shard_map.115.ours_ref, f32[160,128]{1,0:T(8,128)S(1)} %get-tuple-element.158.base_ref, ...), custom_call_target="tpu_custom_call" | custom-call | tf_op jit(solution)/shard_map/pallas_call | solution.py:79
  (34 shorter events, 0.4 us)
Async XLA Ops:
  0.6 7.9 %collective-permute-start = (f32[160,640]{1,0:T(8,128)}, f32[160,640]{1,0:T(8,128)S(1)}, u32[]{:S(2)}, u32[]{:S(2)}) collective-permute-start(f32[160,640]{1,0:T(8,128)} %bitcast.10), channel_id=1, source_target_pairs={{0,1},{1,0},{2,3},{3,2},{4,5},{5,4},{6,7},{7,6},{8,9},{9,8},{10,11... | collective-permute-start | bytes 1228808 | tf_op jit(solution)/shard_map/ppermute | solution.py:22
  1.1 2.3 %collective-permute-start.1 = (f32[160,256]{1,0:T(8,128)}, f32[160,256]{1,0:T(8,128)S(1)}, u32[]{:S(2)}, u32[]{:S(2)}) collective-permute-start(f32[160,256]{1,0:T(8,128)} %bitcast.16), channel_id=1, source_target_pairs={{0,1},{1,0},{2,3},{3,2},{4,5},{5,4},{6,7},{7,6},{8,9},{9,8},{10,11... | collective-permute-start | bytes 491528 | tf_op jit(solution)/shard_map/ppermute | solution.py:22
  1.2 7.3 %collective-permute-start.5 = (f32[160,384]{1,0:T(8,128)}, f32[160,384]{1,0:T(8,128)S(1)}, u32[]{:S(2)}, u32[]{:S(2)}) collective-permute-start(f32[160,384]{1,0:T(8,128)} %bitcast.14), channel_id=1, source_target_pairs={{0,1},{1,0},{2,3},{3,2},{4,5},{5,4},{6,7},{7,6},{8,9},{9,8},{10,11... | collective-permute-start | bytes 737288 | tf_op jit(solution)/shard_map/ppermute | solution.py:22
  1.7 1.8 %collective-permute-start.2 = (f32[64,256]{1,0:T(8,128)}, f32[64,256]{1,0:T(8,128)S(1)}, u32[]{:S(2)}, u32[]{:S(2)}) collective-permute-start(f32[64,256]{1,0:T(8,128)} %bitcast.18), channel_id=1, source_target_pairs={{0,1},{1,0},{2,3},{3,2},{4,5},{5,4},{6,7},{7,6},{8,9},{9,8},{10,11... | collective-permute-start | bytes 196616 | tf_op jit(solution)/shard_map/ppermute | solution.py:22
  1.7 0.9 %copy-start.4 = (f32[1,160,256]{2,1,0:T(8,128)S(1)}, f32[1,160,256]{2,1,0:T(8,128)}, u32[]{:S(2)}) copy-start(f32[1,160,256]{2,1,0:T(8,128)} %param.8) | copy-start | bytes 491524
  2.7 3.7 %copy-start.2 = (f32[1,256,256]{2,1,0:T(8,128)S(1)}, f32[1,256,256]{2,1,0:T(8,128)}, u32[]{:S(2)}) copy-start(f32[1,256,256]{2,1,0:T(8,128)} %param.14) | copy-start | bytes 786436
  2.7 3.7 %copy-start.1 = (f32[1,256,256]{2,1,0:T(8,128)S(1)}, f32[1,256,256]{2,1,0:T(8,128)}, u32[]{:S(2)}) copy-start(f32[1,256,256]{2,1,0:T(8,128)} %param.15) | copy-start | bytes 786436
  3.4 3.0 %copy-start.6 = (s32[1,384]{1,0:T(1,128)S(1)}, s32[1,384]{1,0:T(1,128)}, u32[]{:S(2)}) copy-start(s32[1,384]{1,0:T(1,128)} %lists_ref.1) | copy-start | bytes 4612
  3.4 3.0 %copy-start.7 = (s32[1,3]{1,0:T(1,128)S(1)}, s32[1,3]{1,0:T(1,128)}, u32[]{:S(2)}) copy-start(s32[1,3]{1,0:T(1,128)} %counts_ref.1) | copy-start | bytes 40
  3.4 5.1 %copy-start = (f32[1,160,640]{2,1,0:T(8,128)S(1)}, f32[1,160,640]{2,1,0:T(8,128)}, u32[]{:S(2)}) copy-start(f32[1,160,640]{2,1,0:T(8,128)} %param.9) | copy-start | bytes 1228804
  3.5 7.4 %collective-permute-start.4 = (f32[320,128]{1,0:T(8,128)S(1)}, f32[320,128]{1,0:T(8,128)S(1)}, u32[]{:S(2)}, u32[]{:S(2)}) collective-permute-start(f32[320,128]{1,0:T(8,128)S(1)} %shard_map.96.chip_ref), channel_id=1, source_target_pairs={{0,2},{1,3},{2,0},{3,1},{4,6},{5,7},{6,4},{7,5},{8,10},{9,11},{10,... | collective-permute-start | bytes 491528 | tf_op jit(solution)/shard_map/ppermute | solution.py:22
  6.4 2.2 %copy-start.3 = (f32[1,384,160]{1,2,0:T(8,128)S(1)}, f32[1,384,160]{1,2,0:T(8,128)}, u32[]{:S(2)}) copy-start(f32[1,384,160]{1,2,0:T(8,128)} %param.10) | copy-start | bytes 737284
  6.4 2.2 %copy-start.5 = (f32[1,64,256]{2,1,0:T(8,128)S(1)}, f32[1,64,256]{2,1,0:T(8,128)}, u32[]{:S(2)}) copy-start(f32[1,64,256]{2,1,0:T(8,128)} %param.13) | copy-start | bytes 196612
  6.9 8.2 %collective-permute-start.3 = (f32[208,256]{1,0:T(8,128)S(1)}, f32[208,256]{1,0:T(8,128)S(1)}, u32[]{:S(2)}, u32[]{:S(2)}) collective-permute-start(f32[208,256]{1,0:T(8,128)S(1)} %shard_map.97.carry_ref.own_ref), channel_id=1, source_target_pairs={{0,4},{1,5},{2,6},{3,7},{4,0},{5,1},{6,2},{7,3},{8,12},{9,13},{10,... | collective-permute-start | bytes 638984 | tf_op jit(solution)/shard_map/ppermute | solution.py:22
  11.6 6.1 %collective-permute-start.7 = (f32[32,512]{1,0:T(8,128)S(1)}, f32[32,512]{1,0:T(8,128)S(1)}, u32[]{:S(2)}, u32[]{:S(2)}) collective-permute-start(f32[32,512]{1,0:T(8,128)S(1)} %get-tuple-element.101), channel_id=1, source_target_pairs={{0,6},{1,7},{2,4},{3,5},{4,2},{5,3},{6,0},{7,1},{8,14},{9,15},{10,... | collective-permute-start | bytes 196616 | tf_op jit(solution)/shard_map/ppermute | solution.py:22
  14.4 4.3 %collective-permute-start.8 = (f32[32,512]{1,0:T(8,128)S(1)}, f32[32,512]{1,0:T(8,128)S(1)}, u32[]{:S(2)}, u32[]{:S(2)}) collective-permute-start(f32[32,512]{1,0:T(8,128)S(1)} %get-tuple-element.102), channel_id=1, source_target_pairs={{0,2},{1,3},{2,0},{3,1},{4,6},{5,7},{6,4},{7,5},{8,10},{9,11},{10,... | collective-permute-start | bytes 196616 | tf_op jit(solution)/shard_map/ppermute | solution.py:22
  14.9 4.3 %collective-permute-start.9 = (f32[32,512]{1,0:T(8,128)S(1)}, f32[32,512]{1,0:T(8,128)S(1)}, u32[]{:S(2)}, u32[]{:S(2)}) collective-permute-start(f32[32,512]{1,0:T(8,128)S(1)} %get-tuple-element.103), channel_id=1, source_target_pairs={{0,4},{1,5},{2,6},{3,7},{4,0},{5,1},{6,2},{7,3},{8,12},{9,13},{10,... | collective-permute-start | bytes 196616 | tf_op jit(solution)/shard_map/ppermute | solution.py:22
  15.2 8.0 %collective-permute-start.6 = (f32[200,256]{1,0:T(8,128)S(1)}, f32[200,256]{1,0:T(8,128)S(1)}, u32[]{:S(2)}, u32[]{:S(2)}) collective-permute-start(f32[200,256]{1,0:T(8,128)S(1)} %get-tuple-element.99.carry_ref), channel_id=1, source_target_pairs={{8,0},{9,1},{10,2},{11,3},{12,4},{13,5},{14,6},{15,7},{24,16},{25,... | collective-permute-start | bytes 614408 | tf_op jit(solution)/shard_map/ppermute | solution.py:34
  16.6 2.8 %collective-permute-start.10 = (f32[200,256]{1,0:T(8,128)S(1)}, f32[200,256]{1,0:T(8,128)S(1)}, u32[]{:S(2)}, u32[]{:S(2)}) collective-permute-start(f32[200,256]{1,0:T(8,128)S(1)} %get-tuple-element.115.half_ref), channel_id=1, source_target_pairs={{0,1},{1,0},{2,3},{3,2},{4,5},{5,4},{6,7},{7,6},{8,9},{9,8},{10,11... | collective-permute-start | bytes 614408 | tf_op jit(solution)/shard_map/ppermute | solution.py:22
  19.8 4.8 %collective-permute-start.12 = (f32[32,512]{1,0:T(8,128)S(1)}, f32[32,512]{1,0:T(8,128)S(1)}, u32[]{:S(2)}, u32[]{:S(2)}) collective-permute-start(f32[32,512]{1,0:T(8,128)S(1)} %shard_map.104.up_ref), channel_id=1, source_target_pairs={{0,8},{1,9},{2,10},{3,11},{4,12},{5,13},{6,14},{7,15},{8,0},{9,1},... | collective-permute-start | bytes 196616 | tf_op jit(solution)/shard_map/ppermute | solution.py:22
  21.5 15.1 %collective-permute-start.19 = (f32[160,640]{1,0:T(8,128)S(1)}, f32[160,640]{1,0:T(8,128)S(1)}, u32[]{:S(2)}, u32[]{:S(2)}) collective-permute-start(f32[160,640]{1,0:T(8,128)S(1)} %get-tuple-element.147), channel_id=1, source_target_pairs={{2,0},{3,1},{6,4},{7,5},{10,8},{11,9},{14,12},{15,13},{18,16},{19,... | collective-permute-start | bytes 1228808 | tf_op jit(solution)/shard_map/ppermute | solution.py:22
  23.3 1.5 %collective-permute-start.13 = (f32[200,256]{1,0:T(8,128)S(1)}, f32[200,256]{1,0:T(8,128)S(1)}, u32[]{:S(2)}, u32[]{:S(2)}) collective-permute-start(f32[200,256]{1,0:T(8,128)S(1)} %get-tuple-element.128.half_ref), channel_id=1, source_target_pairs={{0,1},{1,0},{2,3},{3,2},{4,5},{5,4},{6,7},{7,6},{8,9},{9,8},{10,11... | collective-permute-start | bytes 614408 | tf_op jit(solution)/shard_map/ppermute | solution.py:22
  23.4 6.6 %collective-permute-start.11 = (f32[72,256]{1,0:T(8,128)S(1)}, f32[72,256]{1,0:T(8,128)S(1)}, u32[]{:S(2)}, u32[]{:S(2)}) collective-permute-start(f32[72,256]{1,0:T(8,128)S(1)} %get-tuple-element.123.root_ref), channel_id=1, source_target_pairs={{16,24},{17,25},{18,26},{19,27},{20,28},{21,29},{22,30},{23,31},{8... | collective-permute-start | bytes 221192 | tf_op jit(solution)/shard_map/ppermute | solution.py:34
  25.2 5.7 %collective-permute-start.15 = (f32[32,256]{1,0:T(8,128)S(1)}, f32[32,256]{1,0:T(8,128)S(1)}, u32[]{:S(2)}, u32[]{:S(2)}) collective-permute-start(f32[32,256]{1,0:T(8,128)S(1)} %shard_map.108.up_ref), channel_id=1, source_target_pairs={{0,16},{1,17},{2,18},{3,19},{4,20},{5,21},{6,22},{7,23},{8,24},{9,... | collective-permute-start | bytes 98312 | tf_op jit(solution)/shard_map/ppermute | solution.py:22
  29.9 1.3 %collective-permute-start.14 = (f32[72,256]{1,0:T(8,128)S(1)}, f32[72,256]{1,0:T(8,128)S(1)}, u32[]{:S(2)}, u32[]{:S(2)}) collective-permute-start(f32[72,256]{1,0:T(8,128)S(1)} %shard_map.110.root_ref), channel_id=1, source_target_pairs={{0,1},{1,0},{2,3},{3,2},{4,5},{5,4},{6,7},{7,6},{8,9},{9,8},{10,11... | collective-permute-start | bytes 221192 | tf_op jit(solution)/shard_map/ppermute | solution.py:22
  32.3 6.1 %collective-permute-start.16 = (f32[32,512]{1,0:T(8,128)S(1)}, f32[32,512]{1,0:T(8,128)S(1)}, u32[]{:S(2)}, u32[]{:S(2)}) collective-permute-start(f32[32,512]{1,0:T(8,128)S(1)} %get-tuple-element.143), channel_id=1, source_target_pairs={{0,6},{1,7},{2,4},{3,5},{4,2},{5,3},{6,0},{7,1},{8,14},{9,15},{10,... | collective-permute-start | bytes 196616 | tf_op jit(solution)/shard_map/ppermute | solution.py:22
  36.0 4.3 %collective-permute-start.17 = (f32[32,512]{1,0:T(8,128)S(1)}, f32[32,512]{1,0:T(8,128)S(1)}, u32[]{:S(2)}, u32[]{:S(2)}) collective-permute-start(f32[32,512]{1,0:T(8,128)S(1)} %get-tuple-element.144), channel_id=1, source_target_pairs={{0,2},{1,3},{2,0},{3,1},{4,6},{5,7},{6,4},{7,5},{8,10},{9,11},{10,... | collective-permute-start | bytes 196616 | tf_op jit(solution)/shard_map/ppermute | solution.py:22
  36.1 4.3 %collective-permute-start.18 = (f32[32,512]{1,0:T(8,128)S(1)}, f32[32,512]{1,0:T(8,128)S(1)}, u32[]{:S(2)}, u32[]{:S(2)}) collective-permute-start(f32[32,512]{1,0:T(8,128)S(1)} %get-tuple-element.145), channel_id=1, source_target_pairs={{0,4},{1,5},{2,6},{3,7},{4,0},{5,1},{6,2},{7,3},{8,12},{9,13},{10,... | collective-permute-start | bytes 196616 | tf_op jit(solution)/shard_map/ppermute | solution.py:22
  40.4 1.6 %collective-permute-start.20 = (f32[128,512]{1,0:T(8,128)S(1)}, f32[128,512]{1,0:T(8,128)S(1)}, u32[]{:S(2)}, u32[]{:S(2)}) collective-permute-start(f32[128,512]{1,0:T(8,128)S(1)} %shard_map.114.group_ref), channel_id=1, source_target_pairs={{0,1},{1,0},{2,3},{3,2},{4,5},{5,4},{6,7},{7,6},{8,9},{9,8},{10,11... | collective-permute-start | bytes 786440 | tf_op jit(solution)/shard_map/ppermute | solution.py:22
  40.5 1.6 %collective-permute-start.21 = (f32[160,128]{1,0:T(8,128)S(1)}, f32[160,128]{1,0:T(8,128)S(1)}, u32[]{:S(2)}, u32[]{:S(2)}) collective-permute-start(f32[160,128]{1,0:T(8,128)S(1)} %get-tuple-element.159), channel_id=1, source_target_pairs={{0,1},{1,0},{2,3},{3,2},{4,5},{5,4},{6,7},{7,6},{8,9},{9,8},{10,11... | collective-permute-start | bytes 245768 | tf_op jit(solution)/shard_map/ppermute | solution.py:22

commit v5 on v4

--- a/solution.py
+++ b/solution.py
@@ -150,7 +150,7 @@
         out_ref[at(1 - near_bit, rows)] = by_bit(near_bit, near_ref[:, :half], near_ref[:, half:])
 
     (own_source,) = stage(own_columns_of, [(rows, half)], source)
-    near, rows_near, own_source = after(near, rows_near, own_source)
+    near, own_source = after(near, own_source)
     (chip,) = stage(chip_source, [(2 * rows, half)], own_source, near)
     far = swap(chip, 0, 2)
 
@@ -220,7 +220,7 @@
         )
 
     received = swap(payload, 1, 0)
-    inverse_near, payload = after(inverse_near, payload)
+    inverse_near, rows_near, payload = after(inverse_near, rows_near, payload)
     own_y, inverse_all, inverse_far, inverse_mine, update_all, turned = stage(
         own_part,
         [(2 * rows, half), (2 * rows, size), (2 * rows, 2 * rows), (2 * rows, 2 * rows), (2 * rows, updates), (half, 2 * quarter)],
@@ -370,7 +370,7 @@
         return jnp.concatenate([by_bit(near_bit, own, other), by_bit(near_bit, other, own)], 0)
 
     def push(slots_ref, residual_ref, half_ref, near_ref, out_ref):
-        taken = dot(residual_ref[...], operator_of(half_ref, near_ref), 1, 1)
+        taken = dot3(residual_ref[...], operator_of(half_ref, near_ref), 1, 1)
         out_ref[:, :order] = slots_ref[:, :order] - taken
         if out_ref.shape[1] > order:
             out_ref[:, order:] = slots_ref[:, order:]
@@ -405,26 +405,15 @@
     )
     for level in range(2, depth):
         partner = swap(going_up, 2 ** (level - 1), 0)
-        residuals[-1], going_up = after(residuals[-1], going_up)
-        partial, down = stage(
-            alone,
-            [(block, order), (order, order)],
-            residuals[-1],
-            halves[level - 2],
-            halves_near[level - 2],
-        )
         if level == depth - 1:
-            reached, partial = after(reached, partial)
+            reached, going_up = after(reached, going_up)
             new_half, root = stage(
                 last_forward, [(carried, order), (packed_rows, order)], carry, reached
             )
             halves.append(new_half)
             from_far = swap(far_sum, 0, 2, lambda leaf, sep: sep // 2 == 1)
             halves_near.append(swap(new_half, 0, 1))
-            by_root = quarter_swap(root, ((2, 3), (1, 0)))
-        downs.append(down)
-        partials.append(partial)
-        partner, partial = after(partner, partial)
+            by_root = swap(root, leaves // 4, 0)
         residual, slots = stage(
             level_sum,
             [(block, order), (block, (depth - level) * order)],
@@ -444,16 +433,17 @@
         )
     partner = swap(going_up, 2 ** (depth - 1), 0)
 
-    residuals[-1], going_up = after(residuals[-1], going_up)
-    partial, down = stage(
-        alone,
-        [(block, order), (order, order)],
-        residuals[-1],
-        halves[-1],
-        halves_near[-1],
-    )
-    partials.append(partial)
-    downs.append(down)
+    for level in range(1, depth):
+        residual, going_up = after(residuals[level - 1], going_up)
+        partial, down = stage(
+            alone,
+            [(block, order), (order, order)],
+            residual,
+            halves[level - 1],
+            halves_near[level - 1],
+        )
+        partials.append(partial)
+        downs.append(down)
     by_root, partial = after(by_root, partial)
     (root,) = stage(root_half, [(packed_rows, order)], root, by_root)
     root_near = swap(root, 0, 1)

time: 43.3 us -> 41.4 us (0.956)
  starting transfers between devices: 23.5 us -> 21 us
  waiting for transfers between devices: 9.89 us -> 10.8 us
    ppermute x2 -> x1, starting transfers between devices: 2.58 us -> 1.29 us  [quarter_swap(): return lax.ppermute(payload, axes, pairs)]
    ppermute x20 -> x21, starting transfers between devices: 20.9 us -> 19.7 us  [swap(): return lax.ppermute(payload, axes, pairs)]
    ppermute x2 -> x1, waiting for transfers between devices: 0.56 us -> 1.43 us  [quarter_swap(): return lax.ppermute(payload, axes, pairs)]
    ppermute x20 -> x21, waiting for transfers between devices: 9.33 us -> 9.35 us  [swap(): return lax.ppermute(payload, axes, pairs)]
where the time goes in v5:
time: 41.4 us; the launch traced here: 41.2 us
  starting transfers between devices  21 us (51%)
  waiting for transfers between devices  10.8 us (26%)
  Pallas kernels  7.66 us (19%)
  local copies, waits for them, and re-layouts  0.95 us (2%)
  between operations  0.87 us (2%)
    ppermute x21, starting transfers between devices, swap(): return lax.ppermute(payload, axes, pairs)  19.7 us
    ppermute x21, waiting for transfers between devices, swap(): return lax.ppermute(payload, axes, pairs)  9.35 us
    pallas_call x22, Pallas kernels, stage(): pl.pallas_call(body, out_shape=[jax.ShapeDtypeStruct(shape, f32) if isins...  7.66 us
    ppermute x1, waiting for transfers between devices, quarter_swap(): return lax.ppermute(payload, axes, pairs)  1.43 us
    ppermute x1, starting transfers between devices, quarter_swap(): return lax.ppermute(payload, axes, pairs)  1.29 us
    unnamed x16, local copies, waits for them, and re-layouts  0.95 us
  transfers between devices with their start and end apart: 22, of which 13 were waited for; matrix products, arithmetic and copies ran while one was open for 0% of the time, Pallas kernels for 16%

profile of v5, /device:TPU:0, one launch (start us, length us, event | category | flops | bytes accessed | tf_op | source)
XLA Modules:
  0.0 41.2 jit_solution(492650041142620013)
XLA Ops:
  0.6 0.5 %collective-permute-start = (f32[160,640]{1,0:T(8,128)}, f32[160,640]{1,0:T(8,128)S(1)}, u32[]{:S(2)}, u32[]{:S(2)}) collective-permute-start(f32[160,640]{1,0:T(8,128)} %bitcast.10), channel_id=1, source_target_pairs={{0,1},{1,0},{2,3},{3,2},{4,5},{5,4},{6,7},{7,6},{8,9},{9,8},{10,11... | collective-permute-start | bytes 1228808 | tf_op jit(solution)/shard_map/ppermute | solution.py:22
  1.1 0.1 collective-permute-start.2
  1.2 0.4 %collective-permute-start.5 = (f32[160,384]{1,0:T(8,128)}, f32[160,384]{1,0:T(8,128)S(1)}, u32[]{:S(2)}, u32[]{:S(2)}) collective-permute-start(f32[160,384]{1,0:T(8,128)} %bitcast.14), channel_id=1, source_target_pairs={{0,1},{1,0},{2,3},{3,2},{4,5},{5,4},{6,7},{7,6},{8,9},{9,8},{10,11... | collective-permute-start | bytes 737288 | tf_op jit(solution)/shard_map/ppermute | solution.py:22
  1.7 0.9 %copy-done.4 = f32[1,160,256]{2,1,0:T(8,128)S(1)} copy-done((f32[1,160,256]{2,1,0:T(8,128)S(1)}, f32[1,160,256]{2,1,0:T(8,128)}, u32[]{:S(2)}) %copy-start.4) | copy-done | bytes 163864
  2.6 0.4 collective-permute-done.2.near_ref
  3.0 2.9 %collective-permute-start.4 = (f32[320,128]{1,0:T(8,128)S(1)}, f32[320,128]{1,0:T(8,128)S(1)}, u32[]{:S(2)}, u32[]{:S(2)}) collective-permute-start(f32[320,128]{1,0:T(8,128)S(1)} %shard_map.96.chip_ref), channel_id=1, source_target_pairs={{0,2},{1,3},{2,0},{3,1},{4,6},{5,7},{6,4},{7,5},{8,10},{9,11},{10,... | collective-permute-start | bytes 491528 | tf_op jit(solution)/shard_map/ppermute | solution.py:22
  6.0 0.5 %shard_map.97.carry_ref.own_ref = f32[208,256]{1,0:T(8,128)S(1)} custom-call(f32[256,256]{1,0:T(8,128)S(1)} %bitcast.12, f32[256,256]{1,0:T(8,128)S(1)} %bitcast.13, s32[1,384]{1,0:T(1,128)S(1)} %copy-done.6, s32[1,3]{1,0:T(1,128)S(1)} %copy-done.7), custom_call_target="tpu_custom_call" | custom-call | tf_op jit(solution)/shard_map/pallas_call | solution.py:79
  6.5 1.6 %collective-permute-start.3 = (f32[208,256]{1,0:T(8,128)S(1)}, f32[208,256]{1,0:T(8,128)S(1)}, u32[]{:S(2)}, u32[]{:S(2)}) collective-permute-start(f32[208,256]{1,0:T(8,128)S(1)} %shard_map.97.carry_ref.own_ref), channel_id=1, source_target_pairs={{0,4},{1,5},{2,6},{3,7},{4,0},{5,1},{6,2},{7,3},{8,12},{9,13},{10,... | collective-permute-start | bytes 638984 | tf_op jit(solution)/shard_map/ppermute | solution.py:22
  8.1 1.3 %collective-permute-done.1.rows_near_ref = f32[64,256]{1,0:T(8,128)S(1)} collective-permute-done((f32[64,256]{1,0:T(8,128)S(1)}, f32[64,256]{1,0:T(8,128)S(1)}, u32[]{:S(2)}, u32[]{:S(2)}) %collective-permute-start.1) | collective-permute-done | bytes 65568 | tf_op jit(solution)/shard_map/ppermute | solution.py:22
  9.4 0.9 %shard_map.98 = (f32[320,128]{1,0:T(8,128)S(1)}, f32[320,640]{1,0:T(8,128)S(1)}, f32[320,320]{1,0:T(8,128)S(1)}, f32[320,320]{1,0:T(8,128)S(1)}, f32[320,384]{1,0:T(8,128)S(1)}, /*index=5*/f32[128,128]{1,0:T(8,128)S(1)}) custom-call(f32[160,640]{1,0:T(8,128)S(1)} %bitcast.11, f32[160,640]{1,0:T(8,128)S(1)} %collective-permute-done.inverse_near_ref, ...), custom_call_target="tpu_custom_call" | custom-call | tf_op jit(solution)/shard_map/pallas_call | solution.py:79
  10.3 0.1 collective-permute-done.4.far_ref
  10.4 0.7 %shard_map.99 = (f32[320,128]{1,0:T(8,128)S(1)}, f32[32,512]{1,0:T(8,128)S(1)}, f32[32,512]{1,0:T(8,128)S(1)}, f32[32,512]{1,0:T(8,128)S(1)}, f32[32,512]{1,0:T(8,128)S(1)}) custom-call(f32[320,128]{1,0:T(8,128)S(1)} %get-tuple-element.90.own_ref, f32[320,320]{1,0:T(8,128)S(1)} %get-tuple-element.91.inverse_ref, ...), custom_call_target="tpu_custom_call" | custom-call | tf_op jit(solution)/shard_map/pallas_call | solution.py:79
  11.2 1.8 %collective-permute-start.10 = (f32[32,512]{1,0:T(8,128)S(1)}, f32[32,512]{1,0:T(8,128)S(1)}, u32[]{:S(2)}, u32[]{:S(2)}) collective-permute-start(f32[32,512]{1,0:T(8,128)S(1)} %get-tuple-element.103), channel_id=1, source_target_pairs={{0,4},{1,5},{2,6},{3,7},{4,0},{5,1},{6,2},{7,3},{8,12},{9,13},{10,... | collective-permute-start | bytes 196616 | tf_op jit(solution)/shard_map/ppermute | solution.py:22
  13.0 1.4 %collective-permute-start.8 = (f32[32,512]{1,0:T(8,128)S(1)}, f32[32,512]{1,0:T(8,128)S(1)}, u32[]{:S(2)}, u32[]{:S(2)}) collective-permute-start(f32[32,512]{1,0:T(8,128)S(1)} %get-tuple-element.101), channel_id=1, source_target_pairs={{0,6},{1,7},{2,4},{3,5},{4,2},{5,3},{6,0},{7,1},{8,14},{9,15},{10,... | collective-permute-start | bytes 196616 | tf_op jit(solution)/shard_map/ppermute | solution.py:22
  14.5 0.3 collective-permute-start.9
  14.8 1.3 %collective-permute-start.6 = (f32[200,256]{1,0:T(8,128)S(1)}, f32[200,256]{1,0:T(8,128)S(1)}, u32[]{:S(2)}, u32[]{:S(2)}) collective-permute-start(f32[200,256]{1,0:T(8,128)S(1)} %get-tuple-element.98.carry_ref), channel_id=1, source_target_pairs={{8,0},{9,1},{10,2},{11,3},{12,4},{13,5},{14,6},{15,7},{24,16},{25,... | collective-permute-start | bytes 614408 | tf_op jit(solution)/shard_map/ppermute | solution.py:34
  16.1 0.1 shard_map.101.hot_ref
  16.2 0.1 collective-permute-start.7
  16.3 1.1 %shard_map.102 = (f32[160,640]{1,0:T(8,128)S(1)}, f32[160,640]{1,0:T(8,128)S(1)}) custom-call(f32[320,640]{1,0:T(8,128)S(1)} %get-tuple-element.104.all_ref, f32[320,320]{1,0:T(8,128)S(1)} %get-tuple-element.105.mine_ref, f32[320,384]{1,0:T(8,128)S(1)} %get-tuple-element.93.update_ref, f32[320,128]{1,0:T(8,128)S(1)} %get-tuple-element.108.y_ref), custom_call_target="tpu_custom_call" | custom-call | tf_op jit(solution)/shard_map/pallas_call | solution.py:79
  17.3 0.8 %collective-permute-done.8.both_ref = f32[32,512]{1,0:T(8,128)S(1)} collective-permute-done((f32[32,512]{1,0:T(8,128)S(1)}, f32[32,512]{1,0:T(8,128)S(1)}, u32[]{:S(2)}, u32[]{:S(2)}) %collective-permute-start.8) | collective-permute-done | bytes 65568 | tf_op jit(solution)/shard_map/ppermute | solution.py:22
  18.2 0.5 %collective-permute-done.9.far_ref = f32[32,512]{1,0:T(8,128)S(1)} collective-permute-done((f32[32,512]{1,0:T(8,128)S(1)}, f32[32,512]{1,0:T(8,128)S(1)}, u32[]{:S(2)}, u32[]{:S(2)}) %collective-permute-start.9) | collective-permute-done | bytes 65568 | tf_op jit(solution)/shard_map/ppermute | solution.py:22
  18.7 0.3 shard_map.103
  19.0 0.2 shard_map.104.up_ref
  19.2 1.6 %collective-permute-start.12 = (f32[32,512]{1,0:T(8,128)S(1)}, f32[32,512]{1,0:T(8,128)S(1)}, u32[]{:S(2)}, u32[]{:S(2)}) collective-permute-start(f32[32,512]{1,0:T(8,128)S(1)} %shard_map.104.up_ref), channel_id=1, source_target_pairs={{0,8},{1,9},{2,10},{3,11},{4,12},{5,13},{6,14},{7,15},{8,0},{9,1},... | collective-permute-start | bytes 196616 | tf_op jit(solution)/shard_map/ppermute | solution.py:22
  20.9 1.3 %collective-permute-start.19 = (f32[160,640]{1,0:T(8,128)S(1)}, f32[160,640]{1,0:T(8,128)S(1)}, u32[]{:S(2)}, u32[]{:S(2)}) collective-permute-start(f32[160,640]{1,0:T(8,128)S(1)} %get-tuple-element.145), channel_id=1, source_target_pairs={{2,0},{3,1},{6,4},{7,5},{10,8},{11,9},{14,12},{15,13},{18,16},{19,... | collective-permute-start | bytes 1228808 | tf_op jit(solution)/shard_map/ppermute | solution.py:22
  22.2 1.4 %collective-permute-done.6.received_ref = f32[200,256]{1,0:T(8,128)S(1)} collective-permute-done((f32[200,256]{1,0:T(8,128)S(1)}, f32[200,256]{1,0:T(8,128)S(1)}, u32[]{:S(2)}, u32[]{:S(2)}) %collective-permute-start.6) | collective-permute-done | bytes 204832 | tf_op jit(solution)/shard_map/ppermute | solution.py:34
  23.6 0.1 collective-permute-start.13
  23.7 0.9 %collective-permute-start.11 = (f32[72,256]{1,0:T(8,128)S(1)}, f32[72,256]{1,0:T(8,128)S(1)}, u32[]{:S(2)}, u32[]{:S(2)}) collective-permute-start(f32[72,256]{1,0:T(8,128)S(1)} %get-tuple-element.120.root_ref), channel_id=1, source_target_pairs={{0,8},{1,9},{2,10},{3,11},{4,12},{5,13},{6,14},{7,15},{8,0},{9,1},... | collective-permute-start | bytes 221192 | tf_op jit(solution)/shard_map/ppermute | solution.py:22
  24.7 0.5 %collective-permute-done.13.near_ref = f32[200,256]{1,0:T(8,128)S(1)} collective-permute-done((f32[200,256]{1,0:T(8,128)S(1)}, f32[200,256]{1,0:T(8,128)S(1)}, u32[]{:S(2)}, u32[]{:S(2)}) %collective-permute-start.13) | collective-permute-done | bytes 204832 | tf_op jit(solution)/shard_map/ppermute | solution.py:22
  25.1 0.2 shard_map.107.up_ref
  25.4 2.4 %collective-permute-start.15 = (f32[32,256]{1,0:T(8,128)S(1)}, f32[32,256]{1,0:T(8,128)S(1)}, u32[]{:S(2)}, u32[]{:S(2)}) collective-permute-start(f32[32,256]{1,0:T(8,128)S(1)} %shard_map.107.up_ref), channel_id=1, source_target_pairs={{0,16},{1,17},{2,18},{3,19},{4,20},{5,21},{6,22},{7,23},{8,24},{9,... | collective-permute-start | bytes 98312 | tf_op jit(solution)/shard_map/ppermute | solution.py:22
  27.8 0.5 %shard_map.111 = (f32[32,256]{1,0:T(8,128)S(1)}, f32[256,256]{1,0:T(8,128)S(1)}) custom-call(f32[32,256]{1,0:T(8,128)S(1)} %get-tuple-element.137.residual_ref, f32[200,256]{1,0:T(8,128)S(1)} %get-tuple-element.99.half_ref, f32[200,256]{1,0:T(8,128)S(1)} %collective-permute-done.7.near_ref), custom_call_target="tpu_custom_call" | custom-call | tf_op jit(solution)/shard_map/pallas_call | solution.py:79
  28.2 0.5 %shard_map.108 = (f32[32,256]{1,0:T(8,128)S(1)}, f32[256,256]{1,0:T(8,128)S(1)}) custom-call(f32[32,256]{1,0:T(8,128)S(1)} %get-tuple-element.129.residual_ref, f32[200,256]{1,0:T(8,128)S(1)} %get-tuple-element.123.half_ref, f32[200,256]{1,0:T(8,128)S(1)} %collective-permute-done.13.near_ref), custom_call_target="tpu_custom_call" | custom-call | tf_op jit(solution)/shard_map/pallas_call | solution.py:79
  28.8 0.1 collective-permute-start.14
  28.9 1.7 %collective-permute-done.15.partner_ref = f32[32,256]{1,0:T(8,128)S(1)} collective-permute-done((f32[32,256]{1,0:T(8,128)S(1)}, f32[32,256]{1,0:T(8,128)S(1)}, u32[]{:S(2)}, u32[]{:S(2)}) %collective-permute-start.15) | collective-permute-done | bytes 32800 | tf_op jit(solution)/shard_map/ppermute | solution.py:22
  30.5 1.0 %shard_map.112 = (f32[32,512]{1,0:T(8,128)S(1)}, f32[32,512]{1,0:T(8,128)S(1)}, f32[32,512]{1,0:T(8,128)S(1)}, f32[32,512]{1,0:T(8,128)S(1)}) custom-call(f32[32,256]{1,0:T(8,128)S(1)} %shard_map.110.residual_ref, f32[72,256]{1,0:T(8,128)S(1)} %shard_map.109.root_ref, f32[72,256]{1,0:T(8,128)S(1)} %collective-permute-done.14.root_near_ref, ...), custom_call_target="tpu_custom_call" | custom-call | tf_op jit(solution)/shard_map/pallas_call | solution.py:79
  31.6 2.3 %collective-permute-start.16 = (f32[32,512]{1,0:T(8,128)S(1)}, f32[32,512]{1,0:T(8,128)S(1)}, u32[]{:S(2)}, u32[]{:S(2)}) collective-permute-start(f32[32,512]{1,0:T(8,128)S(1)} %get-tuple-element.141), channel_id=1, source_target_pairs={{0,6},{1,7},{2,4},{3,5},{4,2},{5,3},{6,0},{7,1},{8,14},{9,15},{10,... | collective-permute-start | bytes 196616 | tf_op jit(solution)/shard_map/ppermute | solution.py:22
  33.9 0.3 collective-permute-start.17
  34.2 0.9 %collective-permute-start.18 = (f32[32,512]{1,0:T(8,128)S(1)}, f32[32,512]{1,0:T(8,128)S(1)}, u32[]{:S(2)}, u32[]{:S(2)}) collective-permute-start(f32[32,512]{1,0:T(8,128)S(1)} %get-tuple-element.143), channel_id=1, source_target_pairs={{0,4},{1,5},{2,6},{3,7},{4,0},{5,1},{6,2},{7,3},{8,12},{9,13},{10,... | collective-permute-start | bytes 196616 | tf_op jit(solution)/shard_map/ppermute | solution.py:22
  35.2 2.3 %collective-permute-done.16.refs_3_ = f32[32,512]{1,0:T(8,128)S(1)} collective-permute-done((f32[32,512]{1,0:T(8,128)S(1)}, f32[32,512]{1,0:T(8,128)S(1)}, u32[]{:S(2)}, u32[]{:S(2)}) %collective-permute-start.16) | collective-permute-done | bytes 65568 | tf_op jit(solution)/shard_map/ppermute | solution.py:22
  37.5 0.6 %collective-permute-done.17.refs_1_ = f32[32,512]{1,0:T(8,128)S(1)} collective-permute-done((f32[32,512]{1,0:T(8,128)S(1)}, f32[32,512]{1,0:T(8,128)S(1)}, u32[]{:S(2)}, u32[]{:S(2)}) %collective-permute-start.17) | collective-permute-done | bytes 65568 | tf_op jit(solution)/shard_map/ppermute | solution.py:22
  38.1 0.3 collective-permute-done.18.refs_2_
  38.5 0.1 collective-permute-start.20
  38.6 0.5 %collective-permute-start.21 = (f32[160,128]{1,0:T(8,128)S(1)}, f32[160,128]{1,0:T(8,128)S(1)}, u32[]{:S(2)}, u32[]{:S(2)}) collective-permute-start(f32[160,128]{1,0:T(8,128)S(1)} %get-tuple-element.157), channel_id=1, source_target_pairs={{0,1},{1,0},{2,3},{3,2},{4,5},{5,4},{6,7},{7,6},{8,9},{9,8},{10,11... | collective-permute-start | bytes 245768 | tf_op jit(solution)/shard_map/ppermute | solution.py:22
  39.1 0.3 shard_map.115.ours_ref
  39.4 0.7 %collective-permute-done.20.group_ref = f32[128,512]{1,0:T(8,128)S(1)} collective-permute-done((f32[128,512]{1,0:T(8,128)S(1)}, f32[128,512]{1,0:T(8,128)S(1)}, u32[]{:S(2)}, u32[]{:S(2)}) %collective-permute-start.20) | collective-permute-done | bytes 262176 | tf_op jit(solution)/shard_map/ppermute | solution.py:22
  40.1 0.1 collective-permute-done.21.base_near_ref
  40.2 1.0 %shard_map.116 = (f32[160,256]{1,0:T(8,128)}, f32[64,256]{1,0:T(8,128)}) custom-call(f32[224,512]{1,0:T(8,128)S(1)} %get-tuple-element.149.left_ref, f32[128,512]{1,0:T(8,128)S(1)} %collective-permute-done.20.group_ref, f32[224,128]{1,0:T(8,128)S(1)} %shard_map.115.ours_ref, f32[160,128]{1,0:T(8,128)S(1)} %get-tuple-element.156.base_ref, ...), custom_call_target="tpu_custom_call" | custom-call | tf_op jit(solution)/shard_map/pallas_call | solution.py:79
  (34 shorter events, 0.3 us)
Async XLA Ops:
  0.6 8.7 %collective-permute-start = (f32[160,640]{1,0:T(8,128)}, f32[160,640]{1,0:T(8,128)S(1)}, u32[]{:S(2)}, u32[]{:S(2)}) collective-permute-start(f32[160,640]{1,0:T(8,128)} %bitcast.10), channel_id=1, source_target_pairs={{0,1},{1,0},{2,3},{3,2},{4,5},{5,4},{6,7},{7,6},{8,9},{9,8},{10,11... | collective-permute-start | bytes 1228808 | tf_op jit(solution)/shard_map/ppermute | solution.py:22
  1.1 1.8 %collective-permute-start.2 = (f32[160,256]{1,0:T(8,128)}, f32[160,256]{1,0:T(8,128)S(1)}, u32[]{:S(2)}, u32[]{:S(2)}) collective-permute-start(f32[160,256]{1,0:T(8,128)} %bitcast.16), channel_id=1, source_target_pairs={{0,1},{1,0},{2,3},{3,2},{4,5},{5,4},{6,7},{7,6},{8,9},{9,8},{10,11... | collective-permute-start | bytes 491528 | tf_op jit(solution)/shard_map/ppermute | solution.py:22
  1.2 8.1 %collective-permute-start.5 = (f32[160,384]{1,0:T(8,128)}, f32[160,384]{1,0:T(8,128)S(1)}, u32[]{:S(2)}, u32[]{:S(2)}) collective-permute-start(f32[160,384]{1,0:T(8,128)} %bitcast.14), channel_id=1, source_target_pairs={{0,1},{1,0},{2,3},{3,2},{4,5},{5,4},{6,7},{7,6},{8,9},{9,8},{10,11... | collective-permute-start | bytes 737288 | tf_op jit(solution)/shard_map/ppermute | solution.py:22
  1.7 0.9 %copy-start.4 = (f32[1,160,256]{2,1,0:T(8,128)S(1)}, f32[1,160,256]{2,1,0:T(8,128)}, u32[]{:S(2)}) copy-start(f32[1,160,256]{2,1,0:T(8,128)} %param.8) | copy-start | bytes 491524
  2.6 3.4 %copy-start.2 = (f32[1,256,256]{2,1,0:T(8,128)S(1)}, f32[1,256,256]{2,1,0:T(8,128)}, u32[]{:S(2)}) copy-start(f32[1,256,256]{2,1,0:T(8,128)} %param.14) | copy-start | bytes 786436
  2.6 3.3 %copy-start.1 = (f32[1,256,256]{2,1,0:T(8,128)S(1)}, f32[1,256,256]{2,1,0:T(8,128)}, u32[]{:S(2)}) copy-start(f32[1,256,256]{2,1,0:T(8,128)} %param.15) | copy-start | bytes 786436
  3.0 3.0 %copy-start.6 = (s32[1,384]{1,0:T(1,128)S(1)}, s32[1,384]{1,0:T(1,128)}, u32[]{:S(2)}) copy-start(s32[1,384]{1,0:T(1,128)} %lists_ref.1) | copy-start | bytes 4612
  3.0 3.0 %copy-start.7 = (s32[1,3]{1,0:T(1,128)S(1)}, s32[1,3]{1,0:T(1,128)}, u32[]{:S(2)}) copy-start(s32[1,3]{1,0:T(1,128)} %counts_ref.1) | copy-start | bytes 40
  3.0 6.4 %copy-start = (f32[1,160,640]{2,1,0:T(8,128)S(1)}, f32[1,160,640]{2,1,0:T(8,128)}, u32[]{:S(2)}) copy-start(f32[1,160,640]{2,1,0:T(8,128)} %param.9) | copy-start | bytes 1228804
  3.0 7.4 %collective-permute-start.4 = (f32[320,128]{1,0:T(8,128)S(1)}, f32[320,128]{1,0:T(8,128)S(1)}, u32[]{:S(2)}, u32[]{:S(2)}) collective-permute-start(f32[320,128]{1,0:T(8,128)S(1)} %shard_map.96.chip_ref), channel_id=1, source_target_pairs={{0,2},{1,3},{2,0},{3,1},{4,6},{5,7},{6,4},{7,5},{8,10},{9,11},{10,... | collective-permute-start | bytes 491528 | tf_op jit(solution)/shard_map/ppermute | solution.py:22
  5.9 2.1 %copy-start.5 = (f32[1,64,256]{2,1,0:T(8,128)S(1)}, f32[1,64,256]{2,1,0:T(8,128)}, u32[]{:S(2)}) copy-start(f32[1,64,256]{2,1,0:T(8,128)} %param.13) | copy-start | bytes 196612
  6.0 3.4 %copy-start.3 = (f32[1,384,160]{1,2,0:T(8,128)S(1)}, f32[1,384,160]{1,2,0:T(8,128)}, u32[]{:S(2)}) copy-start(f32[1,384,160]{1,2,0:T(8,128)} %param.10) | copy-start | bytes 737284
  6.5 8.2 %collective-permute-start.3 = (f32[208,256]{1,0:T(8,128)S(1)}, f32[208,256]{1,0:T(8,128)S(1)}, u32[]{:S(2)}, u32[]{:S(2)}) collective-permute-start(f32[208,256]{1,0:T(8,128)S(1)} %shard_map.97.carry_ref.own_ref), channel_id=1, source_target_pairs={{0,4},{1,5},{2,6},{3,7},{4,0},{5,1},{6,2},{7,3},{8,12},{9,13},{10,... | collective-permute-start | bytes 638984 | tf_op jit(solution)/shard_map/ppermute | solution.py:22
  8.1 1.3 %collective-permute-start.1 = (f32[64,256]{1,0:T(8,128)S(1)}, f32[64,256]{1,0:T(8,128)S(1)}, u32[]{:S(2)}, u32[]{:S(2)}) collective-permute-start(f32[64,256]{1,0:T(8,128)S(1)} %bitcast.18), channel_id=1, source_target_pairs={{0,1},{1,0},{2,3},{3,2},{4,5},{5,4},{6,7},{7,6},{8,9},{9,8},{10,11... | collective-permute-start | bytes 196616 | tf_op jit(solution)/shard_map/ppermute | solution.py:22
  11.2 6.1 %collective-permute-start.10 = (f32[32,512]{1,0:T(8,128)S(1)}, f32[32,512]{1,0:T(8,128)S(1)}, u32[]{:S(2)}, u32[]{:S(2)}) collective-permute-start(f32[32,512]{1,0:T(8,128)S(1)} %get-tuple-element.103), channel_id=1, source_target_pairs={{0,4},{1,5},{2,6},{3,7},{4,0},{5,1},{6,2},{7,3},{8,12},{9,13},{10,... | collective-permute-start | bytes 196616 | tf_op jit(solution)/shard_map/ppermute | solution.py:22
  13.0 5.2 %collective-permute-start.8 = (f32[32,512]{1,0:T(8,128)S(1)}, f32[32,512]{1,0:T(8,128)S(1)}, u32[]{:S(2)}, u32[]{:S(2)}) collective-permute-start(f32[32,512]{1,0:T(8,128)S(1)} %get-tuple-element.101), channel_id=1, source_target_pairs={{0,6},{1,7},{2,4},{3,5},{4,2},{5,3},{6,0},{7,1},{8,14},{9,15},{10,... | collective-permute-start | bytes 196616 | tf_op jit(solution)/shard_map/ppermute | solution.py:22
  14.5 4.3 %collective-permute-start.9 = (f32[32,512]{1,0:T(8,128)S(1)}, f32[32,512]{1,0:T(8,128)S(1)}, u32[]{:S(2)}, u32[]{:S(2)}) collective-permute-start(f32[32,512]{1,0:T(8,128)S(1)} %get-tuple-element.102), channel_id=1, source_target_pairs={{0,2},{1,3},{2,0},{3,1},{4,6},{5,7},{6,4},{7,5},{8,10},{9,11},{10,... | collective-permute-start | bytes 196616 | tf_op jit(solution)/shard_map/ppermute | solution.py:22
  14.8 8.8 %collective-permute-start.6 = (f32[200,256]{1,0:T(8,128)S(1)}, f32[200,256]{1,0:T(8,128)S(1)}, u32[]{:S(2)}, u32[]{:S(2)}) collective-permute-start(f32[200,256]{1,0:T(8,128)S(1)} %get-tuple-element.98.carry_ref), channel_id=1, source_target_pairs={{8,0},{9,1},{10,2},{11,3},{12,4},{13,5},{14,6},{15,7},{24,16},{25,... | collective-permute-start | bytes 614408 | tf_op jit(solution)/shard_map/ppermute | solution.py:34
  16.2 2.8 %collective-permute-start.7 = (f32[200,256]{1,0:T(8,128)S(1)}, f32[200,256]{1,0:T(8,128)S(1)}, u32[]{:S(2)}, u32[]{:S(2)}) collective-permute-start(f32[200,256]{1,0:T(8,128)S(1)} %get-tuple-element.99.half_ref), channel_id=1, source_target_pairs={{0,1},{1,0},{2,3},{3,2},{4,5},{5,4},{6,7},{7,6},{8,9},{9,8},{10,11... | collective-permute-start | bytes 614408 | tf_op jit(solution)/shard_map/ppermute | solution.py:22
  19.2 5.4 %collective-permute-start.12 = (f32[32,512]{1,0:T(8,128)S(1)}, f32[32,512]{1,0:T(8,128)S(1)}, u32[]{:S(2)}, u32[]{:S(2)}) collective-permute-start(f32[32,512]{1,0:T(8,128)S(1)} %shard_map.104.up_ref), channel_id=1, source_target_pairs={{0,8},{1,9},{2,10},{3,11},{4,12},{5,13},{6,14},{7,15},{8,0},{9,1},... | collective-permute-start | bytes 196616 | tf_op jit(solution)/shard_map/ppermute | solution.py:22
  20.9 14.2 %collective-permute-start.19 = (f32[160,640]{1,0:T(8,128)S(1)}, f32[160,640]{1,0:T(8,128)S(1)}, u32[]{:S(2)}, u32[]{:S(2)}) collective-permute-start(f32[160,640]{1,0:T(8,128)S(1)} %get-tuple-element.145), channel_id=1, source_target_pairs={{2,0},{3,1},{6,4},{7,5},{10,8},{11,9},{14,12},{15,13},{18,16},{19,... | collective-permute-start | bytes 1228808 | tf_op jit(solution)/shard_map/ppermute | solution.py:22
  23.6 1.5 %collective-permute-start.13 = (f32[200,256]{1,0:T(8,128)S(1)}, f32[200,256]{1,0:T(8,128)S(1)}, u32[]{:S(2)}, u32[]{:S(2)}) collective-permute-start(f32[200,256]{1,0:T(8,128)S(1)} %get-tuple-element.123.half_ref), channel_id=1, source_target_pairs={{0,1},{1,0},{2,3},{3,2},{4,5},{5,4},{6,7},{7,6},{8,9},{9,8},{10,11... | collective-permute-start | bytes 614408 | tf_op jit(solution)/shard_map/ppermute | solution.py:22
  23.7 5.0 %collective-permute-start.11 = (f32[72,256]{1,0:T(8,128)S(1)}, f32[72,256]{1,0:T(8,128)S(1)}, u32[]{:S(2)}, u32[]{:S(2)}) collective-permute-start(f32[72,256]{1,0:T(8,128)S(1)} %get-tuple-element.120.root_ref), channel_id=1, source_target_pairs={{0,8},{1,9},{2,10},{3,11},{4,12},{5,13},{6,14},{7,15},{8,0},{9,1},... | collective-permute-start | bytes 221192 | tf_op jit(solution)/shard_map/ppermute | solution.py:22
  25.4 5.1 %collective-permute-start.15 = (f32[32,256]{1,0:T(8,128)S(1)}, f32[32,256]{1,0:T(8,128)S(1)}, u32[]{:S(2)}, u32[]{:S(2)}) collective-permute-start(f32[32,256]{1,0:T(8,128)S(1)} %shard_map.107.up_ref), channel_id=1, source_target_pairs={{0,16},{1,17},{2,18},{3,19},{4,20},{5,21},{6,22},{7,23},{8,24},{9,... | collective-permute-start | bytes 98312 | tf_op jit(solution)/shard_map/ppermute | solution.py:22
  28.8 1.8 %collective-permute-start.14 = (f32[72,256]{1,0:T(8,128)S(1)}, f32[72,256]{1,0:T(8,128)S(1)}, u32[]{:S(2)}, u32[]{:S(2)}) collective-permute-start(f32[72,256]{1,0:T(8,128)S(1)} %shard_map.109.root_ref), channel_id=1, source_target_pairs={{0,1},{1,0},{2,3},{3,2},{4,5},{5,4},{6,7},{7,6},{8,9},{9,8},{10,11... | collective-permute-start | bytes 221192 | tf_op jit(solution)/shard_map/ppermute | solution.py:22
  31.6 6.0 %collective-permute-start.16 = (f32[32,512]{1,0:T(8,128)S(1)}, f32[32,512]{1,0:T(8,128)S(1)}, u32[]{:S(2)}, u32[]{:S(2)}) collective-permute-start(f32[32,512]{1,0:T(8,128)S(1)} %get-tuple-element.141), channel_id=1, source_target_pairs={{0,6},{1,7},{2,4},{3,5},{4,2},{5,3},{6,0},{7,1},{8,14},{9,15},{10,... | collective-permute-start | bytes 196616 | tf_op jit(solution)/shard_map/ppermute | solution.py:22
  33.9 4.3 %collective-permute-start.17 = (f32[32,512]{1,0:T(8,128)S(1)}, f32[32,512]{1,0:T(8,128)S(1)}, u32[]{:S(2)}, u32[]{:S(2)}) collective-permute-start(f32[32,512]{1,0:T(8,128)S(1)} %get-tuple-element.142), channel_id=1, source_target_pairs={{0,2},{1,3},{2,0},{3,1},{4,6},{5,7},{6,4},{7,5},{8,10},{9,11},{10,... | collective-permute-start | bytes 196616 | tf_op jit(solution)/shard_map/ppermute | solution.py:22
  34.2 4.3 %collective-permute-start.18 = (f32[32,512]{1,0:T(8,128)S(1)}, f32[32,512]{1,0:T(8,128)S(1)}, u32[]{:S(2)}, u32[]{:S(2)}) collective-permute-start(f32[32,512]{1,0:T(8,128)S(1)} %get-tuple-element.143), channel_id=1, source_target_pairs={{0,4},{1,5},{2,6},{3,7},{4,0},{5,1},{6,2},{7,3},{8,12},{9,13},{10,... | collective-permute-start | bytes 196616 | tf_op jit(solution)/shard_map/ppermute | solution.py:22
  38.5 1.6 %collective-permute-start.20 = (f32[128,512]{1,0:T(8,128)S(1)}, f32[128,512]{1,0:T(8,128)S(1)}, u32[]{:S(2)}, u32[]{:S(2)}) collective-permute-start(f32[128,512]{1,0:T(8,128)S(1)} %shard_map.114.group_ref), channel_id=1, source_target_pairs={{0,1},{1,0},{2,3},{3,2},{4,5},{5,4},{6,7},{7,6},{8,9},{9,8},{10,11... | collective-permute-start | bytes 786440 | tf_op jit(solution)/shard_map/ppermute | solution.py:22
  38.6 1.6 %collective-permute-start.21 = (f32[160,128]{1,0:T(8,128)S(1)}, f32[160,128]{1,0:T(8,128)S(1)}, u32[]{:S(2)}, u32[]{:S(2)}) collective-permute-start(f32[160,128]{1,0:T(8,128)S(1)} %get-tuple-element.157), channel_id=1, source_target_pairs={{0,1},{1,0},{2,3},{3,2},{4,5},{5,4},{6,7},{7,6},{8,9},{9,8},{10,11... | collective-permute-start | bytes 245768 | tf_op jit(solution)/shard_map/ppermute | solution.py:22

commit v6 on v5

--- a/solution.py
+++ b/solution.py
@@ -154,15 +154,9 @@
     (chip,) = stage(chip_source, [(2 * rows, half)], own_source, near)
     far = swap(chip, 0, 2)
 
-    def operators(coupling_ref, inverse_ref, lists_ref, counts_ref, out_ref, coupling, inverse, lists, counts, packed, sems):
-        near_bit = place()[4]
-        pairs = ((coupling_ref.at[at(near_bit, middle)], coupling), (inverse_ref, inverse), (lists_ref, lists), (counts_ref, counts))
-        copies = [pltpu.make_async_copy(src, dst, sems.at[index]) for index, (src, dst) in enumerate(pairs)]
-        for copy in copies:
-            copy.start()
-        for copy in copies:
-            copy.wait()
-        out_ref[:middle] = dot(coupling[...], inverse[...])
+    def operators(coupling_ref, inverse, lists, out_ref, packed):
+        near_bit = place()[4]
+        out_ref[:middle] = dot(coupling_ref[at(near_bit, middle)], inverse[...])
         row = lax.broadcasted_iota(jnp.int32, (middle, middle), 0)
         lane = lax.broadcasted_iota(jnp.int32, (middle, middle), 1)
         last = inverse[middle:, middle:]
@@ -175,26 +169,19 @@
         slot = lax.broadcasted_iota(jnp.int32, (1, capacity), 1)
         for level in range(depth):
             names = lists[:, level * capacity : (level + 1) * capacity]
-            live = slot < counts[:, level : level + 1]
+            live = slot < lists[:, updates + level : updates + level + 1]
             out_ref[carried + level : carried + level + 1, :capacity] = jnp.where(live, names, -1).astype(f32)
 
     chip, coupling, own_inverse = after(chip, separator_coupling[0], separator_inverse[0])
+    names_and_counts = jnp.concatenate([row_lists, row_counts], 1)
     (payload,) = stage(
         operators,
         [(carried + list_rows, order)],
         coupling,
         own_inverse,
-        row_lists,
-        row_counts,
-        scratch=[
-            (middle, order),
-            (order, order),
-            pltpu.VMEM(row_lists.shape, jnp.int32),
-            pltpu.VMEM(row_counts.shape, jnp.int32),
-            (2 * packed_rows, order),
-            pltpu.SemaphoreType.DMA((4,)),
-        ],
-        space=pltpu.HBM,
+        names_and_counts,
+        scratch=[(2 * packed_rows, order)],
+        cost=3 * medium,
     )
 
     def own_part(inverse_ref, inverse_near_ref, update_ref, update_near_ref, rows_ref, rows_near_ref, chip_ref, y_ref, all_ref, far_ref, mine_ref, update_out_ref, turned_ref):

time: 41.4 us -> 41.2 us (level)
    ppermute x21, waiting for transfers between devices: 9.35 us -> 9.85 us  [swap(): return lax.ppermute(payload, axes, pairs)]
  transfers between devices with their start and end apart: 22 -> 22, of which waited for: 13 -> 12; matrix products, arithmetic and copies ran while one was open for 0% -> 0% of each run, Pallas kernels for 16% -> 15%
where the time goes in v6:
time: 41.2 us; the launch traced here: 41 us
  starting transfers between devices  20.7 us (50%)
  waiting for transfers between devices  11 us (27%)
  Pallas kernels  7.41 us (18%)
  local copies, waits for them, and re-layouts  0.95 us (2%)
  between operations  0.89 us (2%)
    ppermute x21, starting transfers between devices, swap(): return lax.ppermute(payload, axes, pairs)  19.4 us
    ppermute x21, waiting for transfers between devices, swap(): return lax.ppermute(payload, axes, pairs)  9.85 us
    pallas_call x22, Pallas kernels, stage(): pl.pallas_call(body, out_shape=[jax.ShapeDtypeStruct(shape, f32) if isins...  7.41 us
    ppermute x1, starting transfers between devices, quarter_swap(): return lax.ppermute(payload, axes, pairs)  1.29 us
    ppermute x1, waiting for transfers between devices, quarter_swap(): return lax.ppermute(payload, axes, pairs)  1.18 us
    unnamed x16, local copies, waits for them, and re-layouts  0.95 us
  transfers between devices with their start and end apart: 22, of which 12 were waited for; matrix products, arithmetic and copies ran while one was open for 0% of the time, Pallas kernels for 15%

profile of v6, /device:TPU:0, one launch (start us, length us, event | category | flops | bytes accessed | tf_op | source)
XLA Modules:
  0.0 41.0 jit_solution(1051435798639201167)
XLA Ops:
  0.6 0.5 %collective-permute-start.2 = (f32[160,256]{1,0:T(8,128)}, f32[160,256]{1,0:T(8,128)S(1)}, u32[]{:S(2)}, u32[]{:S(2)}) collective-permute-start(f32[160,256]{1,0:T(8,128)} %bitcast.14), channel_id=1, source_target_pairs={{0,1},{1,0},{2,3},{3,2},{4,5},{5,4},{6,7},{7,6},{8,9},{9,8},{10,11... | collective-permute-start | bytes 491528 | tf_op jit(solution)/shard_map/ppermute | solution.py:22
  1.2 0.1 collective-permute-start
  1.2 0.4 %collective-permute-start.5 = (f32[160,384]{1,0:T(8,128)}, f32[160,384]{1,0:T(8,128)S(1)}, u32[]{:S(2)}, u32[]{:S(2)}) collective-permute-start(f32[160,384]{1,0:T(8,128)} %bitcast.12), channel_id=1, source_target_pairs={{0,1},{1,0},{2,3},{3,2},{4,5},{5,4},{6,7},{7,6},{8,9},{9,8},{10,11... | collective-permute-start | bytes 737288 | tf_op jit(solution)/shard_map/ppermute | solution.py:22
  1.7 0.9 %copy-done.2 = f32[1,160,256]{2,1,0:T(8,128)S(1)} copy-done((f32[1,160,256]{2,1,0:T(8,128)S(1)}, f32[1,160,256]{2,1,0:T(8,128)}, u32[]{:S(2)}) %copy-start.2) | copy-done | bytes 163864
  2.7 2.6 %collective-permute-start.4 = (f32[320,128]{1,0:T(8,128)S(1)}, f32[320,128]{1,0:T(8,128)S(1)}, u32[]{:S(2)}, u32[]{:S(2)}) collective-permute-start(f32[320,128]{1,0:T(8,128)S(1)} %shard_map.96.chip_ref), channel_id=1, source_target_pairs={{0,2},{1,3},{2,0},{3,1},{4,6},{5,7},{6,4},{7,5},{8,10},{9,11},{10,... | collective-permute-start | bytes 491528 | tf_op jit(solution)/shard_map/ppermute | solution.py:22
  5.4 0.3 shard_map.97.carry_ref.own_ref
  5.6 1.6 %collective-permute-start.3 = (f32[208,256]{1,0:T(8,128)S(1)}, f32[208,256]{1,0:T(8,128)S(1)}, u32[]{:S(2)}, u32[]{:S(2)}) collective-permute-start(f32[208,256]{1,0:T(8,128)S(1)} %shard_map.97.carry_ref.own_ref), channel_id=1, source_target_pairs={{0,4},{1,5},{2,6},{3,7},{4,0},{5,1},{6,2},{7,3},{8,12},{9,13},{10,... | collective-permute-start | bytes 638984 | tf_op jit(solution)/shard_map/ppermute | solution.py:22
  7.2 1.3 %collective-permute-done.1.rows_near_ref = f32[64,256]{1,0:T(8,128)S(1)} collective-permute-done((f32[64,256]{1,0:T(8,128)S(1)}, f32[64,256]{1,0:T(8,128)S(1)}, u32[]{:S(2)}, u32[]{:S(2)}) %collective-permute-start.1) | collective-permute-done | bytes 65568 | tf_op jit(solution)/shard_map/ppermute | solution.py:22
  8.5 0.9 %shard_map.98 = (f32[320,128]{1,0:T(8,128)S(1)}, f32[320,640]{1,0:T(8,128)S(1)}, f32[320,320]{1,0:T(8,128)S(1)}, f32[320,320]{1,0:T(8,128)S(1)}, f32[320,384]{1,0:T(8,128)S(1)}, /*index=5*/f32[128,128]{1,0:T(8,128)S(1)}) custom-call(f32[160,640]{1,0:T(8,128)S(1)} %bitcast.11, f32[160,640]{1,0:T(8,128)S(1)} %collective-permute-done.inverse_near_ref, ...), custom_call_target="tpu_custom_call" | custom-call | tf_op jit(solution)/shard_map/pallas_call | solution.py:79
  9.5 0.7 %collective-permute-done.4.far_ref = f32[320,128]{1,0:T(8,128)S(1)} collective-permute-done((f32[320,128]{1,0:T(8,128)S(1)}, f32[320,128]{1,0:T(8,128)S(1)}, u32[]{:S(2)}, u32[]{:S(2)}) %collective-permute-start.4) | collective-permute-done | bytes 163872 | tf_op jit(solution)/shard_map/ppermute | solution.py:22
  10.1 0.7 %shard_map.99 = (f32[320,128]{1,0:T(8,128)S(1)}, f32[32,512]{1,0:T(8,128)S(1)}, f32[32,512]{1,0:T(8,128)S(1)}, f32[32,512]{1,0:T(8,128)S(1)}, f32[32,512]{1,0:T(8,128)S(1)}) custom-call(f32[320,128]{1,0:T(8,128)S(1)} %get-tuple-element.90.own_ref, f32[320,320]{1,0:T(8,128)S(1)} %get-tuple-element.91.inverse_ref, ...), custom_call_target="tpu_custom_call" | custom-call | tf_op jit(solution)/shard_map/pallas_call | solution.py:79
  10.9 1.9 %collective-permute-start.10 = (f32[32,512]{1,0:T(8,128)S(1)}, f32[32,512]{1,0:T(8,128)S(1)}, u32[]{:S(2)}, u32[]{:S(2)}) collective-permute-start(f32[32,512]{1,0:T(8,128)S(1)} %get-tuple-element.103), channel_id=1, source_target_pairs={{0,4},{1,5},{2,6},{3,7},{4,0},{5,1},{6,2},{7,3},{8,12},{9,13},{10,... | collective-permute-start | bytes 196616 | tf_op jit(solution)/shard_map/ppermute | solution.py:22
  12.7 1.4 %collective-permute-start.8 = (f32[32,512]{1,0:T(8,128)S(1)}, f32[32,512]{1,0:T(8,128)S(1)}, u32[]{:S(2)}, u32[]{:S(2)}) collective-permute-start(f32[32,512]{1,0:T(8,128)S(1)} %get-tuple-element.101), channel_id=1, source_target_pairs={{0,6},{1,7},{2,4},{3,5},{4,2},{5,3},{6,0},{7,1},{8,14},{9,15},{10,... | collective-permute-start | bytes 196616 | tf_op jit(solution)/shard_map/ppermute | solution.py:22
  14.2 0.3 collective-permute-start.9
  14.5 1.3 %collective-permute-start.6 = (f32[200,256]{1,0:T(8,128)S(1)}, f32[200,256]{1,0:T(8,128)S(1)}, u32[]{:S(2)}, u32[]{:S(2)}) collective-permute-start(f32[200,256]{1,0:T(8,128)S(1)} %get-tuple-element.98.carry_ref), channel_id=1, source_target_pairs={{8,0},{9,1},{10,2},{11,3},{12,4},{13,5},{14,6},{15,7},{24,16},{25,... | collective-permute-start | bytes 614408 | tf_op jit(solution)/shard_map/ppermute | solution.py:34
  15.8 0.1 shard_map.101.hot_ref
  15.9 0.1 collective-permute-start.7
  15.9 1.1 %shard_map.102 = (f32[160,640]{1,0:T(8,128)S(1)}, f32[160,640]{1,0:T(8,128)S(1)}) custom-call(f32[320,640]{1,0:T(8,128)S(1)} %get-tuple-element.104.all_ref, f32[320,320]{1,0:T(8,128)S(1)} %get-tuple-element.105.mine_ref, f32[320,384]{1,0:T(8,128)S(1)} %get-tuple-element.93.update_ref, f32[320,128]{1,0:T(8,128)S(1)} %get-tuple-element.108.y_ref), custom_call_target="tpu_custom_call" | custom-call | tf_op jit(solution)/shard_map/pallas_call | solution.py:79
  17.0 1.2 %collective-permute-done.8.both_ref = f32[32,512]{1,0:T(8,128)S(1)} collective-permute-done((f32[32,512]{1,0:T(8,128)S(1)}, f32[32,512]{1,0:T(8,128)S(1)}, u32[]{:S(2)}, u32[]{:S(2)}) %collective-permute-start.8) | collective-permute-done | bytes 65568 | tf_op jit(solution)/shard_map/ppermute | solution.py:22
  18.2 0.2 collective-permute-done.9.far_ref
  18.4 0.3 shard_map.103
  18.7 0.2 shard_map.104.up_ref
  18.9 1.6 %collective-permute-start.12 = (f32[32,512]{1,0:T(8,128)S(1)}, f32[32,512]{1,0:T(8,128)S(1)}, u32[]{:S(2)}, u32[]{:S(2)}) collective-permute-start(f32[32,512]{1,0:T(8,128)S(1)} %shard_map.104.up_ref), channel_id=1, source_target_pairs={{0,8},{1,9},{2,10},{3,11},{4,12},{5,13},{6,14},{7,15},{8,0},{9,1},... | collective-permute-start | bytes 196616 | tf_op jit(solution)/shard_map/ppermute | solution.py:22
  20.6 1.3 %collective-permute-start.19 = (f32[160,640]{1,0:T(8,128)S(1)}, f32[160,640]{1,0:T(8,128)S(1)}, u32[]{:S(2)}, u32[]{:S(2)}) collective-permute-start(f32[160,640]{1,0:T(8,128)S(1)} %get-tuple-element.145), channel_id=1, source_target_pairs={{2,0},{3,1},{6,4},{7,5},{10,8},{11,9},{14,12},{15,13},{18,16},{19,... | collective-permute-start | bytes 1228808 | tf_op jit(solution)/shard_map/ppermute | solution.py:22
  21.9 1.2 %collective-permute-done.6.received_ref = f32[200,256]{1,0:T(8,128)S(1)} collective-permute-done((f32[200,256]{1,0:T(8,128)S(1)}, f32[200,256]{1,0:T(8,128)S(1)}, u32[]{:S(2)}, u32[]{:S(2)}) %collective-permute-start.6) | collective-permute-done | bytes 204832 | tf_op jit(solution)/shard_map/ppermute | solution.py:34
  23.1 0.1 collective-permute-start.13
  23.2 1.0 %collective-permute-start.11 = (f32[72,256]{1,0:T(8,128)S(1)}, f32[72,256]{1,0:T(8,128)S(1)}, u32[]{:S(2)}, u32[]{:S(2)}) collective-permute-start(f32[72,256]{1,0:T(8,128)S(1)} %get-tuple-element.120.root_ref), channel_id=1, source_target_pairs={{0,8},{1,9},{2,10},{3,11},{4,12},{5,13},{6,14},{7,15},{8,0},{9,1},... | collective-permute-start | bytes 221192 | tf_op jit(solution)/shard_map/ppermute | solution.py:22
  24.2 0.4 collective-permute-done.13.near_ref
  24.6 0.2 shard_map.107.up_ref
  24.8 2.3 %collective-permute-start.15 = (f32[32,256]{1,0:T(8,128)S(1)}, f32[32,256]{1,0:T(8,128)S(1)}, u32[]{:S(2)}, u32[]{:S(2)}) collective-permute-start(f32[32,256]{1,0:T(8,128)S(1)} %shard_map.107.up_ref), channel_id=1, source_target_pairs={{0,16},{1,17},{2,18},{3,19},{4,20},{5,21},{6,22},{7,23},{8,24},{9,... | collective-permute-start | bytes 98312 | tf_op jit(solution)/shard_map/ppermute | solution.py:22
  27.2 0.5 %shard_map.111 = (f32[32,256]{1,0:T(8,128)S(1)}, f32[256,256]{1,0:T(8,128)S(1)}) custom-call(f32[32,256]{1,0:T(8,128)S(1)} %get-tuple-element.137.residual_ref, f32[200,256]{1,0:T(8,128)S(1)} %get-tuple-element.99.half_ref, f32[200,256]{1,0:T(8,128)S(1)} %collective-permute-done.7.near_ref), custom_call_target="tpu_custom_call" | custom-call | tf_op jit(solution)/shard_map/pallas_call | solution.py:79
  27.6 0.5 %shard_map.108 = (f32[32,256]{1,0:T(8,128)S(1)}, f32[256,256]{1,0:T(8,128)S(1)}) custom-call(f32[32,256]{1,0:T(8,128)S(1)} %get-tuple-element.129.residual_ref, f32[200,256]{1,0:T(8,128)S(1)} %get-tuple-element.123.half_ref, f32[200,256]{1,0:T(8,128)S(1)} %collective-permute-done.13.near_ref), custom_call_target="tpu_custom_call" | custom-call | tf_op jit(solution)/shard_map/pallas_call | solution.py:79
  28.2 0.1 collective-permute-start.14
  28.2 1.7 %collective-permute-done.15.partner_ref = f32[32,256]{1,0:T(8,128)S(1)} collective-permute-done((f32[32,256]{1,0:T(8,128)S(1)}, f32[32,256]{1,0:T(8,128)S(1)}, u32[]{:S(2)}, u32[]{:S(2)}) %collective-permute-start.15) | collective-permute-done | bytes 32800 | tf_op jit(solution)/shard_map/ppermute | solution.py:22
  30.0 1.0 %shard_map.112 = (f32[32,512]{1,0:T(8,128)S(1)}, f32[32,512]{1,0:T(8,128)S(1)}, f32[32,512]{1,0:T(8,128)S(1)}, f32[32,512]{1,0:T(8,128)S(1)}) custom-call(f32[32,256]{1,0:T(8,128)S(1)} %shard_map.110.residual_ref, f32[72,256]{1,0:T(8,128)S(1)} %shard_map.109.root_ref, f32[72,256]{1,0:T(8,128)S(1)} %collective-permute-done.14.root_near_ref, ...), custom_call_target="tpu_custom_call" | custom-call | tf_op jit(solution)/shard_map/pallas_call | solution.py:79
  31.0 2.6 %collective-permute-start.16 = (f32[32,512]{1,0:T(8,128)S(1)}, f32[32,512]{1,0:T(8,128)S(1)}, u32[]{:S(2)}, u32[]{:S(2)}) collective-permute-start(f32[32,512]{1,0:T(8,128)S(1)} %get-tuple-element.141), channel_id=1, source_target_pairs={{0,6},{1,7},{2,4},{3,5},{4,2},{5,3},{6,0},{7,1},{8,14},{9,15},{10,... | collective-permute-start | bytes 196616 | tf_op jit(solution)/shard_map/ppermute | solution.py:22
  33.6 0.4 collective-permute-start.17
  34.0 0.6 %collective-permute-start.18 = (f32[32,512]{1,0:T(8,128)S(1)}, f32[32,512]{1,0:T(8,128)S(1)}, u32[]{:S(2)}, u32[]{:S(2)}) collective-permute-start(f32[32,512]{1,0:T(8,128)S(1)} %get-tuple-element.143), channel_id=1, source_target_pairs={{0,4},{1,5},{2,6},{3,7},{4,0},{5,1},{6,2},{7,3},{8,12},{9,13},{10,... | collective-permute-start | bytes 196616 | tf_op jit(solution)/shard_map/ppermute | solution.py:22
  34.5 0.1 shard_map.113
  34.6 2.3 %collective-permute-done.16.refs_3_ = f32[32,512]{1,0:T(8,128)S(1)} collective-permute-done((f32[32,512]{1,0:T(8,128)S(1)}, f32[32,512]{1,0:T(8,128)S(1)}, u32[]{:S(2)}, u32[]{:S(2)}) %collective-permute-start.16) | collective-permute-done | bytes 65568 | tf_op jit(solution)/shard_map/ppermute | solution.py:22
  36.9 0.9 %collective-permute-done.17.refs_1_ = f32[32,512]{1,0:T(8,128)S(1)} collective-permute-done((f32[32,512]{1,0:T(8,128)S(1)}, f32[32,512]{1,0:T(8,128)S(1)}, u32[]{:S(2)}, u32[]{:S(2)}) %collective-permute-start.17) | collective-permute-done | bytes 65568 | tf_op jit(solution)/shard_map/ppermute | solution.py:22
  37.8 0.4 collective-permute-done.18.refs_2_
  38.3 0.1 collective-permute-start.20
  38.3 0.5 %collective-permute-start.21 = (f32[160,128]{1,0:T(8,128)S(1)}, f32[160,128]{1,0:T(8,128)S(1)}, u32[]{:S(2)}, u32[]{:S(2)}) collective-permute-start(f32[160,128]{1,0:T(8,128)S(1)} %get-tuple-element.157), channel_id=1, source_target_pairs={{0,1},{1,0},{2,3},{3,2},{4,5},{5,4},{6,7},{7,6},{8,9},{9,8},{10,11... | collective-permute-start | bytes 245768 | tf_op jit(solution)/shard_map/ppermute | solution.py:22
  38.8 0.4 shard_map.115.ours_ref
  39.2 0.7 %collective-permute-done.20.group_ref = f32[128,512]{1,0:T(8,128)S(1)} collective-permute-done((f32[128,512]{1,0:T(8,128)S(1)}, f32[128,512]{1,0:T(8,128)S(1)}, u32[]{:S(2)}, u32[]{:S(2)}) %collective-permute-start.20) | collective-permute-done | bytes 262176 | tf_op jit(solution)/shard_map/ppermute | solution.py:22
  39.9 0.1 collective-permute-done.21.base_near_ref
  40.0 1.0 %shard_map.116 = (f32[160,256]{1,0:T(8,128)}, f32[64,256]{1,0:T(8,128)}) custom-call(f32[224,512]{1,0:T(8,128)S(1)} %get-tuple-element.149.left_ref, f32[128,512]{1,0:T(8,128)S(1)} %collective-permute-done.20.group_ref, f32[224,128]{1,0:T(8,128)S(1)} %shard_map.115.ours_ref, f32[160,128]{1,0:T(8,128)S(1)} %get-tuple-element.156.base_ref, ...), custom_call_target="tpu_custom_call" | custom-call | tf_op jit(solution)/shard_map/pallas_call | solution.py:79
  (35 shorter events, 0.3 us)
Async XLA Ops:
  0.6 2.0 %copy-start.7 = (s32[1,3]{1,0:T(1,128)S(1)}, s32[1,3]{1,0:T(1,128)}, u32[]{:S(2)}) copy-start(s32[1,3]{1,0:T(1,128)} %param.12) | copy-start | bytes 40
  0.6 2.0 %collective-permute-start.2 = (f32[160,256]{1,0:T(8,128)}, f32[160,256]{1,0:T(8,128)S(1)}, u32[]{:S(2)}, u32[]{:S(2)}) collective-permute-start(f32[160,256]{1,0:T(8,128)} %bitcast.14), channel_id=1, source_target_pairs={{0,1},{1,0},{2,3},{3,2},{4,5},{5,4},{6,7},{7,6},{8,9},{9,8},{10,11... | collective-permute-start | bytes 491528 | tf_op jit(solution)/shard_map/ppermute | solution.py:22
  1.2 7.3 %collective-permute-start = (f32[160,640]{1,0:T(8,128)}, f32[160,640]{1,0:T(8,128)S(1)}, u32[]{:S(2)}, u32[]{:S(2)}) collective-permute-start(f32[160,640]{1,0:T(8,128)} %bitcast.10), channel_id=1, source_target_pairs={{0,1},{1,0},{2,3},{3,2},{4,5},{5,4},{6,7},{7,6},{8,9},{9,8},{10,11... | collective-permute-start | bytes 1228808 | tf_op jit(solution)/shard_map/ppermute | solution.py:22
  1.2 1.4 %copy-start.6 = (s32[1,384]{1,0:T(1,128)S(1)}, s32[1,384]{1,0:T(1,128)}, u32[]{:S(2)}) copy-start(s32[1,384]{1,0:T(1,128)} %param.11) | copy-start | bytes 4612
  1.2 7.3 %collective-permute-start.5 = (f32[160,384]{1,0:T(8,128)}, f32[160,384]{1,0:T(8,128)S(1)}, u32[]{:S(2)}, u32[]{:S(2)}) collective-permute-start(f32[160,384]{1,0:T(8,128)} %bitcast.12), channel_id=1, source_target_pairs={{0,1},{1,0},{2,3},{3,2},{4,5},{5,4},{6,7},{7,6},{8,9},{9,8},{10,11... | collective-permute-start | bytes 737288 | tf_op jit(solution)/shard_map/ppermute | solution.py:22
  1.7 0.9 %copy-start.2 = (f32[1,160,256]{2,1,0:T(8,128)S(1)}, f32[1,160,256]{2,1,0:T(8,128)}, u32[]{:S(2)}) copy-start(f32[1,160,256]{2,1,0:T(8,128)} %param.8) | copy-start | bytes 491524
  2.6 2.8 %copy-start.5 = (f32[1,256,256]{2,1,0:T(8,128)S(1)}, f32[1,256,256]{2,1,0:T(8,128)}, u32[]{:S(2)}) copy-start(f32[1,256,256]{2,1,0:T(8,128)} %param.14) | copy-start | bytes 786436
  2.6 2.7 %copy-start.4 = (f32[1,256,256]{2,1,0:T(8,128)S(1)}, f32[1,256,256]{2,1,0:T(8,128)}, u32[]{:S(2)}) copy-start(f32[1,256,256]{2,1,0:T(8,128)} %param.15) | copy-start | bytes 786436
  2.7 7.4 %collective-permute-start.4 = (f32[320,128]{1,0:T(8,128)S(1)}, f32[320,128]{1,0:T(8,128)S(1)}, u32[]{:S(2)}, u32[]{:S(2)}) collective-permute-start(f32[320,128]{1,0:T(8,128)S(1)} %shard_map.96.chip_ref), channel_id=1, source_target_pairs={{0,2},{1,3},{2,0},{3,1},{4,6},{5,7},{6,4},{7,5},{8,10},{9,11},{10,... | collective-permute-start | bytes 491528 | tf_op jit(solution)/shard_map/ppermute | solution.py:22
  5.3 1.9 %copy-start.3 = (f32[1,64,256]{2,1,0:T(8,128)S(1)}, f32[1,64,256]{2,1,0:T(8,128)}, u32[]{:S(2)}) copy-start(f32[1,64,256]{2,1,0:T(8,128)} %param.13) | copy-start | bytes 196612
  5.3 3.2 %copy-start = (f32[1,160,640]{2,1,0:T(8,128)S(1)}, f32[1,160,640]{2,1,0:T(8,128)}, u32[]{:S(2)}) copy-start(f32[1,160,640]{2,1,0:T(8,128)} %param.9) | copy-start | bytes 1228804
  5.4 3.2 %copy-start.1 = (f32[1,384,160]{1,2,0:T(8,128)S(1)}, f32[1,384,160]{1,2,0:T(8,128)}, u32[]{:S(2)}) copy-start(f32[1,384,160]{1,2,0:T(8,128)} %param.10) | copy-start | bytes 737284
  5.6 8.8 %collective-permute-start.3 = (f32[208,256]{1,0:T(8,128)S(1)}, f32[208,256]{1,0:T(8,128)S(1)}, u32[]{:S(2)}, u32[]{:S(2)}) collective-permute-start(f32[208,256]{1,0:T(8,128)S(1)} %shard_map.97.carry_ref.own_ref), channel_id=1, source_target_pairs={{0,4},{1,5},{2,6},{3,7},{4,0},{5,1},{6,2},{7,3},{8,12},{9,13},{10,... | collective-permute-start | bytes 638984 | tf_op jit(solution)/shard_map/ppermute | solution.py:22
  7.2 1.3 %collective-permute-start.1 = (f32[64,256]{1,0:T(8,128)S(1)}, f32[64,256]{1,0:T(8,128)S(1)}, u32[]{:S(2)}, u32[]{:S(2)}) collective-permute-start(f32[64,256]{1,0:T(8,128)S(1)} %bitcast.16), channel_id=1, source_target_pairs={{0,1},{1,0},{2,3},{3,2},{4,5},{5,4},{6,7},{7,6},{8,9},{9,8},{10,11... | collective-permute-start | bytes 196616 | tf_op jit(solution)/shard_map/ppermute | solution.py:22
  10.9 6.2 %collective-permute-start.10 = (f32[32,512]{1,0:T(8,128)S(1)}, f32[32,512]{1,0:T(8,128)S(1)}, u32[]{:S(2)}, u32[]{:S(2)}) collective-permute-start(f32[32,512]{1,0:T(8,128)S(1)} %get-tuple-element.103), channel_id=1, source_target_pairs={{0,4},{1,5},{2,6},{3,7},{4,0},{5,1},{6,2},{7,3},{8,12},{9,13},{10,... | collective-permute-start | bytes 196616 | tf_op jit(solution)/shard_map/ppermute | solution.py:22
  12.7 5.5 %collective-permute-start.8 = (f32[32,512]{1,0:T(8,128)S(1)}, f32[32,512]{1,0:T(8,128)S(1)}, u32[]{:S(2)}, u32[]{:S(2)}) collective-permute-start(f32[32,512]{1,0:T(8,128)S(1)} %get-tuple-element.101), channel_id=1, source_target_pairs={{0,6},{1,7},{2,4},{3,5},{4,2},{5,3},{6,0},{7,1},{8,14},{9,15},{10,... | collective-permute-start | bytes 196616 | tf_op jit(solution)/shard_map/ppermute | solution.py:22
  14.2 4.3 %collective-permute-start.9 = (f32[32,512]{1,0:T(8,128)S(1)}, f32[32,512]{1,0:T(8,128)S(1)}, u32[]{:S(2)}, u32[]{:S(2)}) collective-permute-start(f32[32,512]{1,0:T(8,128)S(1)} %get-tuple-element.102), channel_id=1, source_target_pairs={{0,2},{1,3},{2,0},{3,1},{4,6},{5,7},{6,4},{7,5},{8,10},{9,11},{10,... | collective-permute-start | bytes 196616 | tf_op jit(solution)/shard_map/ppermute | solution.py:22
  14.5 8.6 %collective-permute-start.6 = (f32[200,256]{1,0:T(8,128)S(1)}, f32[200,256]{1,0:T(8,128)S(1)}, u32[]{:S(2)}, u32[]{:S(2)}) collective-permute-start(f32[200,256]{1,0:T(8,128)S(1)} %get-tuple-element.98.carry_ref), channel_id=1, source_target_pairs={{8,0},{9,1},{10,2},{11,3},{12,4},{13,5},{14,6},{15,7},{24,16},{25,... | collective-permute-start | bytes 614408 | tf_op jit(solution)/shard_map/ppermute | solution.py:34
  15.9 2.8 %collective-permute-start.7 = (f32[200,256]{1,0:T(8,128)S(1)}, f32[200,256]{1,0:T(8,128)S(1)}, u32[]{:S(2)}, u32[]{:S(2)}) collective-permute-start(f32[200,256]{1,0:T(8,128)S(1)} %get-tuple-element.99.half_ref), channel_id=1, source_target_pairs={{0,1},{1,0},{2,3},{3,2},{4,5},{5,4},{6,7},{7,6},{8,9},{9,8},{10,11... | collective-permute-start | bytes 614408 | tf_op jit(solution)/shard_map/ppermute | solution.py:22
  18.9 5.3 %collective-permute-start.12 = (f32[32,512]{1,0:T(8,128)S(1)}, f32[32,512]{1,0:T(8,128)S(1)}, u32[]{:S(2)}, u32[]{:S(2)}) collective-permute-start(f32[32,512]{1,0:T(8,128)S(1)} %shard_map.104.up_ref), channel_id=1, source_target_pairs={{0,8},{1,9},{2,10},{3,11},{4,12},{5,13},{6,14},{7,15},{8,0},{9,1},... | collective-permute-start | bytes 196616 | tf_op jit(solution)/shard_map/ppermute | solution.py:22
  20.6 14.0 %collective-permute-start.19 = (f32[160,640]{1,0:T(8,128)S(1)}, f32[160,640]{1,0:T(8,128)S(1)}, u32[]{:S(2)}, u32[]{:S(2)}) collective-permute-start(f32[160,640]{1,0:T(8,128)S(1)} %get-tuple-element.145), channel_id=1, source_target_pairs={{2,0},{3,1},{6,4},{7,5},{10,8},{11,9},{14,12},{15,13},{18,16},{19,... | collective-permute-start | bytes 1228808 | tf_op jit(solution)/shard_map/ppermute | solution.py:22
  23.1 1.5 %collective-permute-start.13 = (f32[200,256]{1,0:T(8,128)S(1)}, f32[200,256]{1,0:T(8,128)S(1)}, u32[]{:S(2)}, u32[]{:S(2)}) collective-permute-start(f32[200,256]{1,0:T(8,128)S(1)} %get-tuple-element.123.half_ref), channel_id=1, source_target_pairs={{0,1},{1,0},{2,3},{3,2},{4,5},{5,4},{6,7},{7,6},{8,9},{9,8},{10,11... | collective-permute-start | bytes 614408 | tf_op jit(solution)/shard_map/ppermute | solution.py:22
  23.2 4.9 %collective-permute-start.11 = (f32[72,256]{1,0:T(8,128)S(1)}, f32[72,256]{1,0:T(8,128)S(1)}, u32[]{:S(2)}, u32[]{:S(2)}) collective-permute-start(f32[72,256]{1,0:T(8,128)S(1)} %get-tuple-element.120.root_ref), channel_id=1, source_target_pairs={{0,8},{1,9},{2,10},{3,11},{4,12},{5,13},{6,14},{7,15},{8,0},{9,1},... | collective-permute-start | bytes 221192 | tf_op jit(solution)/shard_map/ppermute | solution.py:22
  24.8 5.1 %collective-permute-start.15 = (f32[32,256]{1,0:T(8,128)S(1)}, f32[32,256]{1,0:T(8,128)S(1)}, u32[]{:S(2)}, u32[]{:S(2)}) collective-permute-start(f32[32,256]{1,0:T(8,128)S(1)} %shard_map.107.up_ref), channel_id=1, source_target_pairs={{0,16},{1,17},{2,18},{3,19},{4,20},{5,21},{6,22},{7,23},{8,24},{9,... | collective-permute-start | bytes 98312 | tf_op jit(solution)/shard_map/ppermute | solution.py:22
  28.2 1.8 %collective-permute-start.14 = (f32[72,256]{1,0:T(8,128)S(1)}, f32[72,256]{1,0:T(8,128)S(1)}, u32[]{:S(2)}, u32[]{:S(2)}) collective-permute-start(f32[72,256]{1,0:T(8,128)S(1)} %shard_map.109.root_ref), channel_id=1, source_target_pairs={{0,1},{1,0},{2,3},{3,2},{4,5},{5,4},{6,7},{7,6},{8,9},{9,8},{10,11... | collective-permute-start | bytes 221192 | tf_op jit(solution)/shard_map/ppermute | solution.py:22
  31.0 5.9 %collective-permute-start.16 = (f32[32,512]{1,0:T(8,128)S(1)}, f32[32,512]{1,0:T(8,128)S(1)}, u32[]{:S(2)}, u32[]{:S(2)}) collective-permute-start(f32[32,512]{1,0:T(8,128)S(1)} %get-tuple-element.141), channel_id=1, source_target_pairs={{0,6},{1,7},{2,4},{3,5},{4,2},{5,3},{6,0},{7,1},{8,14},{9,15},{10,... | collective-permute-start | bytes 196616 | tf_op jit(solution)/shard_map/ppermute | solution.py:22
  33.6 4.3 %collective-permute-start.17 = (f32[32,512]{1,0:T(8,128)S(1)}, f32[32,512]{1,0:T(8,128)S(1)}, u32[]{:S(2)}, u32[]{:S(2)}) collective-permute-start(f32[32,512]{1,0:T(8,128)S(1)} %get-tuple-element.142), channel_id=1, source_target_pairs={{0,2},{1,3},{2,0},{3,1},{4,6},{5,7},{6,4},{7,5},{8,10},{9,11},{10,... | collective-permute-start | bytes 196616 | tf_op jit(solution)/shard_map/ppermute | solution.py:22
  34.0 4.3 %collective-permute-start.18 = (f32[32,512]{1,0:T(8,128)S(1)}, f32[32,512]{1,0:T(8,128)S(1)}, u32[]{:S(2)}, u32[]{:S(2)}) collective-permute-start(f32[32,512]{1,0:T(8,128)S(1)} %get-tuple-element.143), channel_id=1, source_target_pairs={{0,4},{1,5},{2,6},{3,7},{4,0},{5,1},{6,2},{7,3},{8,12},{9,13},{10,... | collective-permute-start | bytes 196616 | tf_op jit(solution)/shard_map/ppermute | solution.py:22
  38.3 1.6 %collective-permute-start.20 = (f32[128,512]{1,0:T(8,128)S(1)}, f32[128,512]{1,0:T(8,128)S(1)}, u32[]{:S(2)}, u32[]{:S(2)}) collective-permute-start(f32[128,512]{1,0:T(8,128)S(1)} %shard_map.114.group_ref), channel_id=1, source_target_pairs={{0,1},{1,0},{2,3},{3,2},{4,5},{5,4},{6,7},{7,6},{8,9},{9,8},{10,11... | collective-permute-start | bytes 786440 | tf_op jit(solution)/shard_map/ppermute | solution.py:22
  38.3 1.6 %collective-permute-start.21 = (f32[160,128]{1,0:T(8,128)S(1)}, f32[160,128]{1,0:T(8,128)S(1)}, u32[]{:S(2)}, u32[]{:S(2)}) collective-permute-start(f32[160,128]{1,0:T(8,128)S(1)} %get-tuple-element.157), channel_id=1, source_target_pairs={{0,1},{1,0},{2,3},{3,2},{4,5},{5,4},{6,7},{7,6},{8,9},{9,8},{10,11... | collective-permute-start | bytes 245768 | tf_op jit(solution)/shard_map/ppermute | solution.py:22

commit v7 on v6

--- a/solution.py
+++ b/solution.py
@@ -66,13 +66,9 @@
 
 
 def hot_dot(left, right, right_dim):
-    high = left.astype(bf16)
-    rest = left - high.astype(f32)
-    middle = rest.astype(bf16)
-    low = (rest - middle.astype(f32)).astype(bf16)
-    out = product(jnp.concatenate([high, middle, low], 0), right, 1, right_dim)
-    size = left.shape[0]
-    return out[:size] + (out[size : 2 * size] + out[2 * size :])
+    high, low = pieces_of(left)
+    out = product(jnp.concatenate([high, low], 0), right, 1, right_dim)
+    return out[: left.shape[0]] + out[left.shape[0] :]
 
 
 def stage(body, shapes, *operands, scratch=(), space=pltpu.VMEM, cost=brief):
@@ -154,14 +150,15 @@
     (chip,) = stage(chip_source, [(2 * rows, half)], own_source, near)
     far = swap(chip, 0, 2)
 
-    def operators(coupling_ref, inverse, lists, out_ref, packed):
+    def operators(coupling_ref, inverse, lists, out_ref, packed, square):
         near_bit = place()[4]
         out_ref[:middle] = dot(coupling_ref[at(near_bit, middle)], inverse[...])
+        square[...] = dot(inverse[...], inverse[...], 0, 0)
         row = lax.broadcasted_iota(jnp.int32, (middle, middle), 0)
         lane = lax.broadcasted_iota(jnp.int32, (middle, middle), 1)
-        last = inverse[middle:, middle:]
-        packed[:middle, :middle] = jnp.where(row >= lane, inverse[:middle, :middle], jnp.transpose(last))
-        packed[:middle, middle:] = inverse[middle:, :middle]
+        last = square[middle:, middle:]
+        packed[:middle, :middle] = jnp.where(row >= lane, square[:middle, :middle], last)
+        packed[:middle, middle:] = square[middle:, :middle]
         packed[middle:] = jnp.zeros((2 * packed_rows - middle, order), f32)
         packed[middle : middle + 1, :middle] = jnp.sum(jnp.where(row == lane, last, 0.0), 0, keepdims=True)
         out_ref[middle:carried] = packed[at(near_bit, packed_rows)]
@@ -180,7 +177,7 @@
         coupling,
         own_inverse,
         names_and_counts,
-        scratch=[(2 * packed_rows, order)],
+        scratch=[(2 * packed_rows, order), (order, order)],
         cost=3 * medium,
     )
 
@@ -362,23 +359,41 @@
         if out_ref.shape[1] > order:
             out_ref[:, order:] = slots_ref[:, order:]
 
-    def blocks_of(own, other):
+    def squared(residual, own, other):
         near_bit = place()[4]
         row = lax.broadcasted_iota(jnp.int32, (middle, middle), 0)
         lane = lax.broadcasted_iota(jnp.int32, (middle, middle), 1)
         packed = jnp.concatenate([by_bit(near_bit, own, other), by_bit(near_bit, other, own)], 0)
-        both = packed[:middle, :middle]
-        last = jnp.where(row < lane, both, 0.0)
-        last = jnp.where(row == lane, packed[middle : middle + 1, :middle], last)
-        return jnp.where(row >= lane, both, 0.0), packed[:middle, middle:], last
+        both, below = packed[:middle, :middle], packed[:middle, middle:]
+        lower, upper = jnp.where(row > lane, both, 0.0), jnp.where(row < lane, both, 0.0)
+        first = jnp.where(row >= lane, both, 0.0)
+        last = jnp.where(row == lane, packed[middle : middle + 1, :middle], upper)
+        one, two = residual[:, :middle], residual[:, middle:]
+        return jnp.concatenate(
+            [
+                dot3(one, first) + dot3(one, lower, 1, 1) + dot3(two, below),
+                dot3(one, below, 1, 1) + dot3(two, last) + dot3(two, upper, 1, 1),
+            ],
+            1,
+        )
 
     def alone(residual_ref, half_ref, near_ref, out_ref, down_ref):
         down_ref[...] = operator_of(half_ref, near_ref)
-        first, below, last = blocks_of(half_ref[middle:], near_ref[middle:])
-        one, two = residual_ref[:, :middle], residual_ref[:, middle:]
-        upper, lower = dot3(one, first, 1, 1), dot3(one, below, 1, 1) + dot3(two, last)
-        out_ref[:, :middle] = dot3(upper, first) + dot3(lower, below)
-        out_ref[:, middle:] = dot3(lower, last, 1, 1)
+        out_ref[...] = squared(residual_ref[...], half_ref[middle:], near_ref[middle:])
+
+    def below_root(*refs):
+        count = depth - 1
+        partial_refs, down_refs = refs[:count], refs[count : 2 * count]
+        base_ref, high_ref, low_ref = refs[2 * count :]
+        base, taken = partial_refs[-1][...], -down_refs[-1][...]
+        for level in range(depth - 1, 0, -1):
+            if level < depth - 1:
+                down = down_refs[level - 1][...]
+                base = partial_refs[level - 1][...] - dot3(base, down)
+                taken = -dot3(taken, down)
+            part = slice((level - 1) * order, level * order)
+            base_ref[:, part] = base
+            high_ref[:, part], low_ref[:, part] = pieces_of(taken)
 
     def level_sum(up_ref, partner_ref, residual_ref, rest_ref):
         total = up_ref[...] + partner_ref[...]
@@ -434,7 +449,12 @@
     by_root, partial = after(by_root, partial)
     (root,) = stage(root_half, [(packed_rows, order)], root, by_root)
     root_near = swap(root, 0, 1)
-    partner, root = after(partner, root)
+    partials[-1], root = after(partials[-1], root)
+    pieces = jax.ShapeDtypeStruct((order, (depth - 1) * order), bf16)
+    base, taken_high, taken_low = stage(
+        below_root, [(block, (depth - 1) * order), pieces, pieces], *partials, *downs
+    )
+    partner, root, base = after(partner, root, base)
 
     def root_sum(up_ref, partner_ref, out_ref):
         out_ref[...] = up_ref[...] + partner_ref[...]
@@ -442,21 +462,15 @@
     (residual,) = stage(root_sum, [(block, order)], going_up, partner, cost=medium)
     root_near, residual = after(root_near, residual)
 
-    def way_down(residual_ref, root_ref, root_near_ref, hot_ref, *refs):
+    def way_down(residual_ref, root_ref, root_near_ref, hot_ref, base_ref, high_ref, low_ref, *out_refs):
         leaf, _, odd, far_bit, _ = place()
-        partial_refs, down_refs = refs[: depth - 1], refs[depth - 1 : 2 * depth - 2]
-        out_refs = refs[2 * depth - 2 :]
-        first, below, last = blocks_of(root_ref[...], root_near_ref[...])
-        one, two = residual_ref[:, :middle], residual_ref[:, middle:]
-        upper, lower = dot3(one, first, 1, 1), dot3(one, below, 1, 1) + dot3(two, last)
-        solved = [None] * depth
-        solved[-1] = jnp.concatenate(
-            [dot3(upper, first) + dot3(lower, below), dot3(lower, last, 1, 1)], 1
-        )
-        for level in range(depth - 1, 0, -1):
-            solved[level - 1] = partial_refs[level - 1][...] - dot3(
-                solved[level], down_refs[level - 1][...]
-            )
+        top = squared(residual_ref[...], root_ref[...], root_near_ref[...])
+        high, low = pieces_of(top)
+        large = product(jnp.concatenate([high, low], 0), high_ref[...], 1, 0)
+        small = large[block:] + product(high, low_ref[...], 1, 0)
+        under = base_ref[...] + (large[:block] + small)
+        solved = [under[:, level * order : (level + 1) * order] for level in range(depth - 1)]
+        solved.append(top)
         even_solved = jnp.zeros_like(solved[0])
         for level in range(2, depth + 1):
             here = lax.rem(leaf - odd, 2**level) == 2 ** (level - 1)
@@ -483,8 +497,9 @@
         root,
         root_near,
         hots,
-        *partials,
-        *downs,
+        base,
+        taken_high,
+        taken_low,
     )
     both = swap(to_both, 1, 2)
     beyond = swap(to_far, 0, 2)

time: 41.2 us -> 40.9 us (level)
    pallas_call x22 -> x23, Pallas kernels: 7.41 us -> 7.52 us  [stage(): pl.pallas_call(body, out_shape=[jax.ShapeDtypeStruct(shape, f32) if isins...]
  transfers between devices with their start and end apart: 22 -> 22, of which waited for: 12 -> 13; matrix products, arithmetic and copies ran while one was open for 0% -> 0% of each run, Pallas kernels for 15% -> 16%
where the time goes in v7:
time: 40.9 us; the launch traced here: 40.7 us
  starting transfers between devices  20.7 us (51%)
  waiting for transfers between devices  10.6 us (26%)
  Pallas kernels  7.52 us (18%)
  local copies, waits for them, and re-layouts  0.95 us (2%)
  between operations  0.9 us (2%)
    ppermute x21, starting transfers between devices, swap(): return lax.ppermute(payload, axes, pairs)  19.4 us
    ppermute x21, waiting for transfers between devices, swap(): return lax.ppermute(payload, axes, pairs)  9.44 us
    pallas_call x23, Pallas kernels, stage(): pl.pallas_call(body, out_shape=[jax.ShapeDtypeStruct(shape, f32) if isins...  7.52 us
    ppermute x1, starting transfers between devices, quarter_swap(): return lax.ppermute(payload, axes, pairs)  1.29 us
    ppermute x1, waiting for transfers between devices, quarter_swap(): return lax.ppermute(payload, axes, pairs)  1.18 us
    unnamed x16, local copies, waits for them, and re-layouts  0.95 us
  transfers between devices with their start and end apart: 22, of which 13 were waited for; matrix products, arithmetic and copies ran while one was open for 0% of the time, Pallas kernels for 16%

profile of v7, /device:TPU:0, one launch (start us, length us, event | category | flops | bytes accessed | tf_op | source)
XLA Modules:
  0.0 40.7 jit_solution(1977093573325263946)
XLA Ops:
  0.6 0.5 %collective-permute-start.2 = (f32[160,256]{1,0:T(8,128)}, f32[160,256]{1,0:T(8,128)S(1)}, u32[]{:S(2)}, u32[]{:S(2)}) collective-permute-start(f32[160,256]{1,0:T(8,128)} %bitcast.14), channel_id=1, source_target_pairs={{0,1},{1,0},{2,3},{3,2},{4,5},{5,4},{6,7},{7,6},{8,9},{9,8},{10,11... | collective-permute-start | bytes 491528 | tf_op jit(solution)/shard_map/ppermute | solution.py:22
  1.2 0.1 collective-permute-start
  1.2 0.4 %collective-permute-start.5 = (f32[160,384]{1,0:T(8,128)}, f32[160,384]{1,0:T(8,128)S(1)}, u32[]{:S(2)}, u32[]{:S(2)}) collective-permute-start(f32[160,384]{1,0:T(8,128)} %bitcast.12), channel_id=1, source_target_pairs={{0,1},{1,0},{2,3},{3,2},{4,5},{5,4},{6,7},{7,6},{8,9},{9,8},{10,11... | collective-permute-start | bytes 737288 | tf_op jit(solution)/shard_map/ppermute | solution.py:22
  1.7 0.9 %copy-done.2 = f32[1,160,256]{2,1,0:T(8,128)S(1)} copy-done((f32[1,160,256]{2,1,0:T(8,128)S(1)}, f32[1,160,256]{2,1,0:T(8,128)}, u32[]{:S(2)}) %copy-start.2) | copy-done | bytes 163864
  2.7 2.6 %collective-permute-start.4 = (f32[320,128]{1,0:T(8,128)S(1)}, f32[320,128]{1,0:T(8,128)S(1)}, u32[]{:S(2)}, u32[]{:S(2)}) collective-permute-start(f32[320,128]{1,0:T(8,128)S(1)} %shard_map.96.chip_ref), channel_id=1, source_target_pairs={{0,2},{1,3},{2,0},{3,1},{4,6},{5,7},{6,4},{7,5},{8,10},{9,11},{10,... | collective-permute-start | bytes 491528 | tf_op jit(solution)/shard_map/ppermute | solution.py:22
  5.4 0.6 %shard_map.97.carry_ref.own_ref = f32[208,256]{1,0:T(8,128)S(1)} custom-call(f32[256,256]{1,0:T(8,128)S(1)} %bitcast.18, f32[256,256]{1,0:T(8,128)S(1)} %bitcast.19, s32[1,387]{1,0:T(1,128)S(1)} %pad_add_fusion.lists), custom_call_target="tpu_custom_call" | custom-call | flops 3000000000 | tf_op jit(solution)/shard_map/pallas_call | solution.py:75
  5.9 1.6 %collective-permute-start.3 = (f32[208,256]{1,0:T(8,128)S(1)}, f32[208,256]{1,0:T(8,128)S(1)}, u32[]{:S(2)}, u32[]{:S(2)}) collective-permute-start(f32[208,256]{1,0:T(8,128)S(1)} %shard_map.97.carry_ref.own_ref), channel_id=1, source_target_pairs={{0,4},{1,5},{2,6},{3,7},{4,0},{5,1},{6,2},{7,3},{8,12},{9,13},{10,... | collective-permute-start | bytes 638984 | tf_op jit(solution)/shard_map/ppermute | solution.py:22
  7.5 1.3 %collective-permute-done.1.rows_near_ref = f32[64,256]{1,0:T(8,128)S(1)} collective-permute-done((f32[64,256]{1,0:T(8,128)S(1)}, f32[64,256]{1,0:T(8,128)S(1)}, u32[]{:S(2)}, u32[]{:S(2)}) %collective-permute-start.1) | collective-permute-done | bytes 65568 | tf_op jit(solution)/shard_map/ppermute | solution.py:22
  8.8 0.9 %shard_map.98 = (f32[320,128]{1,0:T(8,128)S(1)}, f32[320,640]{1,0:T(8,128)S(1)}, f32[320,320]{1,0:T(8,128)S(1)}, f32[320,320]{1,0:T(8,128)S(1)}, f32[320,384]{1,0:T(8,128)S(1)}, /*index=5*/f32[128,128]{1,0:T(8,128)S(1)}) custom-call(f32[160,640]{1,0:T(8,128)S(1)} %bitcast.11, f32[160,640]{1,0:T(8,128)S(1)} %collective-permute-done.inverse_near_ref, ...), custom_call_target="tpu_custom_call" | custom-call | tf_op jit(solution)/shard_map/pallas_call | solution.py:75
  9.7 0.4 collective-permute-done.4.far_ref
  10.1 0.7 %shard_map.99 = (f32[320,128]{1,0:T(8,128)S(1)}, f32[32,512]{1,0:T(8,128)S(1)}, f32[32,512]{1,0:T(8,128)S(1)}, f32[32,512]{1,0:T(8,128)S(1)}, f32[32,512]{1,0:T(8,128)S(1)}) custom-call(f32[320,128]{1,0:T(8,128)S(1)} %get-tuple-element.96.own_ref, f32[320,320]{1,0:T(8,128)S(1)} %get-tuple-element.97.inverse_ref, ...), custom_call_target="tpu_custom_call" | custom-call | tf_op jit(solution)/shard_map/pallas_call | solution.py:75
  10.9 1.9 %collective-permute-start.10 = (f32[32,512]{1,0:T(8,128)S(1)}, f32[32,512]{1,0:T(8,128)S(1)}, u32[]{:S(2)}, u32[]{:S(2)}) collective-permute-start(f32[32,512]{1,0:T(8,128)S(1)} %get-tuple-element.109), channel_id=1, source_target_pairs={{0,4},{1,5},{2,6},{3,7},{4,0},{5,1},{6,2},{7,3},{8,12},{9,13},{10,... | collective-permute-start | bytes 196616 | tf_op jit(solution)/shard_map/ppermute | solution.py:22
  12.7 1.4 %collective-permute-start.8 = (f32[32,512]{1,0:T(8,128)S(1)}, f32[32,512]{1,0:T(8,128)S(1)}, u32[]{:S(2)}, u32[]{:S(2)}) collective-permute-start(f32[32,512]{1,0:T(8,128)S(1)} %get-tuple-element.107), channel_id=1, source_target_pairs={{0,6},{1,7},{2,4},{3,5},{4,2},{5,3},{6,0},{7,1},{8,14},{9,15},{10,... | collective-permute-start | bytes 196616 | tf_op jit(solution)/shard_map/ppermute | solution.py:22
  14.2 0.3 collective-permute-start.9
  14.5 1.3 %collective-permute-start.6 = (f32[200,256]{1,0:T(8,128)S(1)}, f32[200,256]{1,0:T(8,128)S(1)}, u32[]{:S(2)}, u32[]{:S(2)}) collective-permute-start(f32[200,256]{1,0:T(8,128)S(1)} %get-tuple-element.104.carry_ref), channel_id=1, source_target_pairs={{8,0},{9,1},{10,2},{11,3},{12,4},{13,5},{14,6},{15,7},{24,16},{25,... | collective-permute-start | bytes 614408 | tf_op jit(solution)/shard_map/ppermute | solution.py:34
  15.8 0.1 shard_map.101.hot_ref
  15.9 0.1 collective-permute-start.7
  15.9 1.1 %shard_map.102 = (f32[160,640]{1,0:T(8,128)S(1)}, f32[160,640]{1,0:T(8,128)S(1)}) custom-call(f32[320,640]{1,0:T(8,128)S(1)} %get-tuple-element.110.all_ref, f32[320,320]{1,0:T(8,128)S(1)} %get-tuple-element.111.mine_ref, f32[320,384]{1,0:T(8,128)S(1)} %get-tuple-element.99.update_ref, f32[320,128]{1,0:T(8,128)S(1)} %get-tuple-element.114.y_ref), custom_call_target="tpu_custom_call" | custom-call | tf_op jit(solution)/shard_map/pallas_call | solution.py:75
  17.0 1.2 %collective-permute-done.8.both_ref = f32[32,512]{1,0:T(8,128)S(1)} collective-permute-done((f32[32,512]{1,0:T(8,128)S(1)}, f32[32,512]{1,0:T(8,128)S(1)}, u32[]{:S(2)}, u32[]{:S(2)}) %collective-permute-start.8) | collective-permute-done | bytes 65568 | tf_op jit(solution)/shard_map/ppermute | solution.py:22
  18.2 0.2 collective-permute-done.9.far_ref
  18.4 0.3 shard_map.103
  18.7 0.2 shard_map.104.up_ref
  18.9 1.6 %collective-permute-start.12 = (f32[32,512]{1,0:T(8,128)S(1)}, f32[32,512]{1,0:T(8,128)S(1)}, u32[]{:S(2)}, u32[]{:S(2)}) collective-permute-start(f32[32,512]{1,0:T(8,128)S(1)} %shard_map.104.up_ref), channel_id=1, source_target_pairs={{0,8},{1,9},{2,10},{3,11},{4,12},{5,13},{6,14},{7,15},{8,0},{9,1},... | collective-permute-start | bytes 196616 | tf_op jit(solution)/shard_map/ppermute | solution.py:22
  20.6 1.3 %collective-permute-start.19 = (f32[160,640]{1,0:T(8,128)S(1)}, f32[160,640]{1,0:T(8,128)S(1)}, u32[]{:S(2)}, u32[]{:S(2)}) collective-permute-start(f32[160,640]{1,0:T(8,128)S(1)} %get-tuple-element.157), channel_id=1, source_target_pairs={{2,0},{3,1},{6,4},{7,5},{10,8},{11,9},{14,12},{15,13},{18,16},{19,... | collective-permute-start | bytes 1228808 | tf_op jit(solution)/shard_map/ppermute | solution.py:22
  21.9 1.2 %collective-permute-done.6.received_ref = f32[200,256]{1,0:T(8,128)S(1)} collective-permute-done((f32[200,256]{1,0:T(8,128)S(1)}, f32[200,256]{1,0:T(8,128)S(1)}, u32[]{:S(2)}, u32[]{:S(2)}) %collective-permute-start.6) | collective-permute-done | bytes 204832 | tf_op jit(solution)/shard_map/ppermute | solution.py:34
  23.1 0.1 collective-permute-start.13
  23.2 1.0 %collective-permute-start.11 = (f32[72,256]{1,0:T(8,128)S(1)}, f32[72,256]{1,0:T(8,128)S(1)}, u32[]{:S(2)}, u32[]{:S(2)}) collective-permute-start(f32[72,256]{1,0:T(8,128)S(1)} %get-tuple-element.126.root_ref), channel_id=1, source_target_pairs={{0,8},{1,9},{2,10},{3,11},{4,12},{5,13},{6,14},{7,15},{8,0},{9,1},... | collective-permute-start | bytes 221192 | tf_op jit(solution)/shard_map/ppermute | solution.py:22
  24.2 0.4 collective-permute-done.13.near_ref
  24.6 0.2 shard_map.107.up_ref
  24.8 2.3 %collective-permute-start.15 = (f32[32,256]{1,0:T(8,128)S(1)}, f32[32,256]{1,0:T(8,128)S(1)}, u32[]{:S(2)}, u32[]{:S(2)}) collective-permute-start(f32[32,256]{1,0:T(8,128)S(1)} %shard_map.107.up_ref), channel_id=1, source_target_pairs={{0,16},{1,17},{2,18},{3,19},{4,20},{5,21},{6,22},{7,23},{8,24},{9,... | collective-permute-start | bytes 98312 | tf_op jit(solution)/shard_map/ppermute | solution.py:22
  27.2 0.4 shard_map.108
  27.5 0.3 collective-permute-done.11.received_ref
  27.9 0.1 collective-permute-start.14
  27.9 0.4 shard_map.110
  28.3 0.4 shard_map.111
  28.7 1.3 %collective-permute-done.15.partner_ref = f32[32,256]{1,0:T(8,128)S(1)} collective-permute-done((f32[32,256]{1,0:T(8,128)S(1)}, f32[32,256]{1,0:T(8,128)S(1)}, u32[]{:S(2)}, u32[]{:S(2)}) %collective-permute-start.15) | collective-permute-done | bytes 32800 | tf_op jit(solution)/shard_map/ppermute | solution.py:22
  30.0 0.7 %shard_map.113 = (f32[32,512]{1,0:T(8,128)S(1)}, f32[32,512]{1,0:T(8,128)S(1)}, f32[32,512]{1,0:T(8,128)S(1)}, f32[32,512]{1,0:T(8,128)S(1)}) custom-call(f32[32,256]{1,0:T(8,128)S(1)} %shard_map.112.residual_ref, f32[72,256]{1,0:T(8,128)S(1)} %shard_map.109.root_ref, f32[72,256]{1,0:T(8,128)S(1)} %collective-permute-done.14.root_near_ref, ...), custom_call_target="tpu_custom_call" | custom-call | tf_op jit(solution)/shard_map/pallas_call | solution.py:75
  30.7 2.6 %collective-permute-start.16 = (f32[32,512]{1,0:T(8,128)S(1)}, f32[32,512]{1,0:T(8,128)S(1)}, u32[]{:S(2)}, u32[]{:S(2)}) collective-permute-start(f32[32,512]{1,0:T(8,128)S(1)} %get-tuple-element.153), channel_id=1, source_target_pairs={{0,6},{1,7},{2,4},{3,5},{4,2},{5,3},{6,0},{7,1},{8,14},{9,15},{10,... | collective-permute-start | bytes 196616 | tf_op jit(solution)/shard_map/ppermute | solution.py:22
  33.3 0.4 collective-permute-start.17
  33.7 0.6 %collective-permute-start.18 = (f32[32,512]{1,0:T(8,128)S(1)}, f32[32,512]{1,0:T(8,128)S(1)}, u32[]{:S(2)}, u32[]{:S(2)}) collective-permute-start(f32[32,512]{1,0:T(8,128)S(1)} %get-tuple-element.155), channel_id=1, source_target_pairs={{0,4},{1,5},{2,6},{3,7},{4,0},{5,1},{6,2},{7,3},{8,12},{9,13},{10,... | collective-permute-start | bytes 196616 | tf_op jit(solution)/shard_map/ppermute | solution.py:22
  34.3 2.8 %collective-permute-done.16.refs_3_ = f32[32,512]{1,0:T(8,128)S(1)} collective-permute-done((f32[32,512]{1,0:T(8,128)S(1)}, f32[32,512]{1,0:T(8,128)S(1)}, u32[]{:S(2)}, u32[]{:S(2)}) %collective-permute-start.16) | collective-permute-done | bytes 65568 | tf_op jit(solution)/shard_map/ppermute | solution.py:22
  37.1 0.5 %collective-permute-done.17.refs_1_ = f32[32,512]{1,0:T(8,128)S(1)} collective-permute-done((f32[32,512]{1,0:T(8,128)S(1)}, f32[32,512]{1,0:T(8,128)S(1)}, u32[]{:S(2)}, u32[]{:S(2)}) %collective-permute-start.17) | collective-permute-done | bytes 65568 | tf_op jit(solution)/shard_map/ppermute | solution.py:22
  37.6 0.4 collective-permute-done.18.refs_2_
  38.1 0.5 %collective-permute-start.21 = (f32[160,128]{1,0:T(8,128)S(1)}, f32[160,128]{1,0:T(8,128)S(1)}, u32[]{:S(2)}, u32[]{:S(2)}) collective-permute-start(f32[160,128]{1,0:T(8,128)S(1)} %get-tuple-element.169), channel_id=1, source_target_pairs={{0,1},{1,0},{2,3},{3,2},{4,5},{5,4},{6,7},{7,6},{8,9},{9,8},{10,11... | collective-permute-start | bytes 245768 | tf_op jit(solution)/shard_map/ppermute | solution.py:22
  38.6 0.4 shard_map.116.ours_ref
  38.9 0.7 %collective-permute-done.20.group_ref = f32[128,512]{1,0:T(8,128)S(1)} collective-permute-done((f32[128,512]{1,0:T(8,128)S(1)}, f32[128,512]{1,0:T(8,128)S(1)}, u32[]{:S(2)}, u32[]{:S(2)}) %collective-permute-start.20) | collective-permute-done | bytes 262176 | tf_op jit(solution)/shard_map/ppermute | solution.py:22
  39.6 0.1 collective-permute-done.21.base_near_ref
  39.7 1.0 %shard_map.117 = (f32[160,256]{1,0:T(8,128)}, f32[64,256]{1,0:T(8,128)}) custom-call(f32[224,512]{1,0:T(8,128)S(1)} %get-tuple-element.161.left_ref, f32[128,512]{1,0:T(8,128)S(1)} %collective-permute-done.20.group_ref, f32[224,128]{1,0:T(8,128)S(1)} %shard_map.116.ours_ref, f32[160,128]{1,0:T(8,128)S(1)} %get-tuple-element.168.base_ref, ...), custom_call_target="tpu_custom_call" | custom-call | tf_op jit(solution)/shard_map/pallas_call | solution.py:75
  (36 shorter events, 0.4 us)
Async XLA Ops:
  0.6 2.0 %copy-start.7 = (s32[1,3]{1,0:T(1,128)S(1)}, s32[1,3]{1,0:T(1,128)}, u32[]{:S(2)}) copy-start(s32[1,3]{1,0:T(1,128)} %param.12) | copy-start | bytes 40
  0.6 2.0 %collective-permute-start.2 = (f32[160,256]{1,0:T(8,128)}, f32[160,256]{1,0:T(8,128)S(1)}, u32[]{:S(2)}, u32[]{:S(2)}) collective-permute-start(f32[160,256]{1,0:T(8,128)} %bitcast.14), channel_id=1, source_target_pairs={{0,1},{1,0},{2,3},{3,2},{4,5},{5,4},{6,7},{7,6},{8,9},{9,8},{10,11... | collective-permute-start | bytes 491528 | tf_op jit(solution)/shard_map/ppermute | solution.py:22
  1.2 7.6 %collective-permute-start = (f32[160,640]{1,0:T(8,128)}, f32[160,640]{1,0:T(8,128)S(1)}, u32[]{:S(2)}, u32[]{:S(2)}) collective-permute-start(f32[160,640]{1,0:T(8,128)} %bitcast.10), channel_id=1, source_target_pairs={{0,1},{1,0},{2,3},{3,2},{4,5},{5,4},{6,7},{7,6},{8,9},{9,8},{10,11... | collective-permute-start | bytes 1228808 | tf_op jit(solution)/shard_map/ppermute | solution.py:22
  1.2 1.4 %copy-start.6 = (s32[1,384]{1,0:T(1,128)S(1)}, s32[1,384]{1,0:T(1,128)}, u32[]{:S(2)}) copy-start(s32[1,384]{1,0:T(1,128)} %param.11) | copy-start | bytes 4612
  1.2 7.5 %collective-permute-start.5 = (f32[160,384]{1,0:T(8,128)}, f32[160,384]{1,0:T(8,128)S(1)}, u32[]{:S(2)}, u32[]{:S(2)}) collective-permute-start(f32[160,384]{1,0:T(8,128)} %bitcast.12), channel_id=1, source_target_pairs={{0,1},{1,0},{2,3},{3,2},{4,5},{5,4},{6,7},{7,6},{8,9},{9,8},{10,11... | collective-permute-start | bytes 737288 | tf_op jit(solution)/shard_map/ppermute | solution.py:22
  1.7 0.9 %copy-start.2 = (f32[1,160,256]{2,1,0:T(8,128)S(1)}, f32[1,160,256]{2,1,0:T(8,128)}, u32[]{:S(2)}) copy-start(f32[1,160,256]{2,1,0:T(8,128)} %param.8) | copy-start | bytes 491524
  2.6 2.8 %copy-start.5 = (f32[1,256,256]{2,1,0:T(8,128)S(1)}, f32[1,256,256]{2,1,0:T(8,128)}, u32[]{:S(2)}) copy-start(f32[1,256,256]{2,1,0:T(8,128)} %param.14) | copy-start | bytes 786436
  2.6 2.7 %copy-start.4 = (f32[1,256,256]{2,1,0:T(8,128)S(1)}, f32[1,256,256]{2,1,0:T(8,128)}, u32[]{:S(2)}) copy-start(f32[1,256,256]{2,1,0:T(8,128)} %param.15) | copy-start | bytes 786436
  2.7 7.4 %collective-permute-start.4 = (f32[320,128]{1,0:T(8,128)S(1)}, f32[320,128]{1,0:T(8,128)S(1)}, u32[]{:S(2)}, u32[]{:S(2)}) collective-permute-start(f32[320,128]{1,0:T(8,128)S(1)} %shard_map.96.chip_ref), channel_id=1, source_target_pairs={{0,2},{1,3},{2,0},{3,1},{4,6},{5,7},{6,4},{7,5},{8,10},{9,11},{10,... | collective-permute-start | bytes 491528 | tf_op jit(solution)/shard_map/ppermute | solution.py:22
  5.3 2.2 %copy-start.3 = (f32[1,64,256]{2,1,0:T(8,128)S(1)}, f32[1,64,256]{2,1,0:T(8,128)}, u32[]{:S(2)}) copy-start(f32[1,64,256]{2,1,0:T(8,128)} %param.13) | copy-start | bytes 196612
  5.3 3.4 %copy-start = (f32[1,160,640]{2,1,0:T(8,128)S(1)}, f32[1,160,640]{2,1,0:T(8,128)}, u32[]{:S(2)}) copy-start(f32[1,160,640]{2,1,0:T(8,128)} %param.9) | copy-start | bytes 1228804
  5.4 3.4 %copy-start.1 = (f32[1,384,160]{1,2,0:T(8,128)S(1)}, f32[1,384,160]{1,2,0:T(8,128)}, u32[]{:S(2)}) copy-start(f32[1,384,160]{1,2,0:T(8,128)} %param.10) | copy-start | bytes 737284
  5.9 8.5 %collective-permute-start.3 = (f32[208,256]{1,0:T(8,128)S(1)}, f32[208,256]{1,0:T(8,128)S(1)}, u32[]{:S(2)}, u32[]{:S(2)}) collective-permute-start(f32[208,256]{1,0:T(8,128)S(1)} %shard_map.97.carry_ref.own_ref), channel_id=1, source_target_pairs={{0,4},{1,5},{2,6},{3,7},{4,0},{5,1},{6,2},{7,3},{8,12},{9,13},{10,... | collective-permute-start | bytes 638984 | tf_op jit(solution)/shard_map/ppermute | solution.py:22
  7.5 1.3 %collective-permute-start.1 = (f32[64,256]{1,0:T(8,128)S(1)}, f32[64,256]{1,0:T(8,128)S(1)}, u32[]{:S(2)}, u32[]{:S(2)}) collective-permute-start(f32[64,256]{1,0:T(8,128)S(1)} %bitcast.16), channel_id=1, source_target_pairs={{0,1},{1,0},{2,3},{3,2},{4,5},{5,4},{6,7},{7,6},{8,9},{9,8},{10,11... | collective-permute-start | bytes 196616 | tf_op jit(solution)/shard_map/ppermute | solution.py:22
  10.9 6.2 %collective-permute-start.10 = (f32[32,512]{1,0:T(8,128)S(1)}, f32[32,512]{1,0:T(8,128)S(1)}, u32[]{:S(2)}, u32[]{:S(2)}) collective-permute-start(f32[32,512]{1,0:T(8,128)S(1)} %get-tuple-element.109), channel_id=1, source_target_pairs={{0,4},{1,5},{2,6},{3,7},{4,0},{5,1},{6,2},{7,3},{8,12},{9,13},{10,... | collective-permute-start | bytes 196616 | tf_op jit(solution)/shard_map/ppermute | solution.py:22
  12.7 5.5 %collective-permute-start.8 = (f32[32,512]{1,0:T(8,128)S(1)}, f32[32,512]{1,0:T(8,128)S(1)}, u32[]{:S(2)}, u32[]{:S(2)}) collective-permute-start(f32[32,512]{1,0:T(8,128)S(1)} %get-tuple-element.107), channel_id=1, source_target_pairs={{0,6},{1,7},{2,4},{3,5},{4,2},{5,3},{6,0},{7,1},{8,14},{9,15},{10,... | collective-permute-start | bytes 196616 | tf_op jit(solution)/shard_map/ppermute | solution.py:22
  14.2 4.3 %collective-permute-start.9 = (f32[32,512]{1,0:T(8,128)S(1)}, f32[32,512]{1,0:T(8,128)S(1)}, u32[]{:S(2)}, u32[]{:S(2)}) collective-permute-start(f32[32,512]{1,0:T(8,128)S(1)} %get-tuple-element.108), channel_id=1, source_target_pairs={{0,2},{1,3},{2,0},{3,1},{4,6},{5,7},{6,4},{7,5},{8,10},{9,11},{10,... | collective-permute-start | bytes 196616 | tf_op jit(solution)/shard_map/ppermute | solution.py:22
  14.5 8.6 %collective-permute-start.6 = (f32[200,256]{1,0:T(8,128)S(1)}, f32[200,256]{1,0:T(8,128)S(1)}, u32[]{:S(2)}, u32[]{:S(2)}) collective-permute-start(f32[200,256]{1,0:T(8,128)S(1)} %get-tuple-element.104.carry_ref), channel_id=1, source_target_pairs={{8,0},{9,1},{10,2},{11,3},{12,4},{13,5},{14,6},{15,7},{24,16},{25,... | collective-permute-start | bytes 614408 | tf_op jit(solution)/shard_map/ppermute | solution.py:34
  15.9 2.8 %collective-permute-start.7 = (f32[200,256]{1,0:T(8,128)S(1)}, f32[200,256]{1,0:T(8,128)S(1)}, u32[]{:S(2)}, u32[]{:S(2)}) collective-permute-start(f32[200,256]{1,0:T(8,128)S(1)} %get-tuple-element.105.half_ref), channel_id=1, source_target_pairs={{0,1},{1,0},{2,3},{3,2},{4,5},{5,4},{6,7},{7,6},{8,9},{9,8},{10,11... | collective-permute-start | bytes 614408 | tf_op jit(solution)/shard_map/ppermute | solution.py:22
  18.9 5.3 %collective-permute-start.12 = (f32[32,512]{1,0:T(8,128)S(1)}, f32[32,512]{1,0:T(8,128)S(1)}, u32[]{:S(2)}, u32[]{:S(2)}) collective-permute-start(f32[32,512]{1,0:T(8,128)S(1)} %shard_map.104.up_ref), channel_id=1, source_target_pairs={{0,8},{1,9},{2,10},{3,11},{4,12},{5,13},{6,14},{7,15},{8,0},{9,1},... | collective-permute-start | bytes 196616 | tf_op jit(solution)/shard_map/ppermute | solution.py:22
  20.6 13.7 %collective-permute-start.19 = (f32[160,640]{1,0:T(8,128)S(1)}, f32[160,640]{1,0:T(8,128)S(1)}, u32[]{:S(2)}, u32[]{:S(2)}) collective-permute-start(f32[160,640]{1,0:T(8,128)S(1)} %get-tuple-element.157), channel_id=1, source_target_pairs={{2,0},{3,1},{6,4},{7,5},{10,8},{11,9},{14,12},{15,13},{18,16},{19,... | collective-permute-start | bytes 1228808 | tf_op jit(solution)/shard_map/ppermute | solution.py:22
  23.1 1.5 %collective-permute-start.13 = (f32[200,256]{1,0:T(8,128)S(1)}, f32[200,256]{1,0:T(8,128)S(1)}, u32[]{:S(2)}, u32[]{:S(2)}) collective-permute-start(f32[200,256]{1,0:T(8,128)S(1)} %get-tuple-element.129.half_ref), channel_id=1, source_target_pairs={{0,1},{1,0},{2,3},{3,2},{4,5},{5,4},{6,7},{7,6},{8,9},{9,8},{10,11... | collective-permute-start | bytes 614408 | tf_op jit(solution)/shard_map/ppermute | solution.py:22
  23.2 4.7 %collective-permute-start.11 = (f32[72,256]{1,0:T(8,128)S(1)}, f32[72,256]{1,0:T(8,128)S(1)}, u32[]{:S(2)}, u32[]{:S(2)}) collective-permute-start(f32[72,256]{1,0:T(8,128)S(1)} %get-tuple-element.126.root_ref), channel_id=1, source_target_pairs={{0,8},{1,9},{2,10},{3,11},{4,12},{5,13},{6,14},{7,15},{8,0},{9,1},... | collective-permute-start | bytes 221192 | tf_op jit(solution)/shard_map/ppermute | solution.py:22
  24.8 5.1 %collective-permute-start.15 = (f32[32,256]{1,0:T(8,128)S(1)}, f32[32,256]{1,0:T(8,128)S(1)}, u32[]{:S(2)}, u32[]{:S(2)}) collective-permute-start(f32[32,256]{1,0:T(8,128)S(1)} %shard_map.107.up_ref), channel_id=1, source_target_pairs={{0,16},{1,17},{2,18},{3,19},{4,20},{5,21},{6,22},{7,23},{8,24},{9,... | collective-permute-start | bytes 98312 | tf_op jit(solution)/shard_map/ppermute | solution.py:22
  27.9 2.1 %collective-permute-start.14 = (f32[72,256]{1,0:T(8,128)S(1)}, f32[72,256]{1,0:T(8,128)S(1)}, u32[]{:S(2)}, u32[]{:S(2)}) collective-permute-start(f32[72,256]{1,0:T(8,128)S(1)} %shard_map.109.root_ref), channel_id=1, source_target_pairs={{0,1},{1,0},{2,3},{3,2},{4,5},{5,4},{6,7},{7,6},{8,9},{9,8},{10,11... | collective-permute-start | bytes 221192 | tf_op jit(solution)/shard_map/ppermute | solution.py:22
  30.7 6.4 %collective-permute-start.16 = (f32[32,512]{1,0:T(8,128)S(1)}, f32[32,512]{1,0:T(8,128)S(1)}, u32[]{:S(2)}, u32[]{:S(2)}) collective-permute-start(f32[32,512]{1,0:T(8,128)S(1)} %get-tuple-element.153), channel_id=1, source_target_pairs={{0,6},{1,7},{2,4},{3,5},{4,2},{5,3},{6,0},{7,1},{8,14},{9,15},{10,... | collective-permute-start | bytes 196616 | tf_op jit(solution)/shard_map/ppermute | solution.py:22
  33.3 4.3 %collective-permute-start.17 = (f32[32,512]{1,0:T(8,128)S(1)}, f32[32,512]{1,0:T(8,128)S(1)}, u32[]{:S(2)}, u32[]{:S(2)}) collective-permute-start(f32[32,512]{1,0:T(8,128)S(1)} %get-tuple-element.154), channel_id=1, source_target_pairs={{0,2},{1,3},{2,0},{3,1},{4,6},{5,7},{6,4},{7,5},{8,10},{9,11},{10,... | collective-permute-start | bytes 196616 | tf_op jit(solution)/shard_map/ppermute | solution.py:22
  33.7 4.3 %collective-permute-start.18 = (f32[32,512]{1,0:T(8,128)S(1)}, f32[32,512]{1,0:T(8,128)S(1)}, u32[]{:S(2)}, u32[]{:S(2)}) collective-permute-start(f32[32,512]{1,0:T(8,128)S(1)} %get-tuple-element.155), channel_id=1, source_target_pairs={{0,4},{1,5},{2,6},{3,7},{4,0},{5,1},{6,2},{7,3},{8,12},{9,13},{10,... | collective-permute-start | bytes 196616 | tf_op jit(solution)/shard_map/ppermute | solution.py:22
  38.0 1.6 %collective-permute-start.20 = (f32[128,512]{1,0:T(8,128)S(1)}, f32[128,512]{1,0:T(8,128)S(1)}, u32[]{:S(2)}, u32[]{:S(2)}) collective-permute-start(f32[128,512]{1,0:T(8,128)S(1)} %shard_map.115.group_ref), channel_id=1, source_target_pairs={{0,1},{1,0},{2,3},{3,2},{4,5},{5,4},{6,7},{7,6},{8,9},{9,8},{10,11... | collective-permute-start | bytes 786440 | tf_op jit(solution)/shard_map/ppermute | solution.py:22
  38.1 1.6 %collective-permute-start.21 = (f32[160,128]{1,0:T(8,128)S(1)}, f32[160,128]{1,0:T(8,128)S(1)}, u32[]{:S(2)}, u32[]{:S(2)}) collective-permute-start(f32[160,128]{1,0:T(8,128)S(1)} %get-tuple-element.169), channel_id=1, source_target_pairs={{0,1},{1,0},{2,3},{3,2},{4,5},{5,4},{6,7},{7,6},{8,9},{9,8},{10,11... | collective-permute-start | bytes 245768 | tf_op jit(solution)/shard_map/ppermute | solution.py:22

commit v8 on v7

--- a/solution.py
+++ b/solution.py
@@ -152,8 +152,8 @@
 
     def operators(coupling_ref, inverse, lists, out_ref, packed, square):
         near_bit = place()[4]
-        out_ref[:middle] = dot(coupling_ref[at(near_bit, middle)], inverse[...])
-        square[...] = dot(inverse[...], inverse[...], 0, 0)
+        out_ref[:middle] = dot3(coupling_ref[at(near_bit, middle)], inverse[...])
+        square[...] = dot3(inverse[...], inverse[...], 0, 0)
         row = lax.broadcasted_iota(jnp.int32, (middle, middle), 0)
         lane = lax.broadcasted_iota(jnp.int32, (middle, middle), 1)
         last = square[middle:, middle:]
@@ -192,8 +192,8 @@
         first, second = whole[:, : 2 * rows], whole[:, 2 * rows :]
         far_ref[...] = by_bit(far_bit, second, first)
         y_ref[...] = dot3(by_bit(far_bit, first, second), chip_ref[...])
-        mine_ref[:, :rows] = by_bit(near_bit, first[:, :rows], first[:, rows:])
-        mine_ref[:, rows:] = by_bit(near_bit, second[:, :rows], second[:, rows:])
+        chip_block = by_bit(far_bit, first, second)
+        mine_ref[...] = by_bit(near_bit, chip_block[:, :rows], chip_block[:, rows:])
         turned, turned_near = jnp.transpose(rows_ref[...]), jnp.transpose(rows_near_ref[...])
         turned = by_bit(near_bit, turned[:half], turned[half:])
         turned_near = by_bit(near_bit, turned_near[:half], turned_near[half:])
@@ -207,7 +207,7 @@
     inverse_near, rows_near, payload = after(inverse_near, rows_near, payload)
     own_y, inverse_all, inverse_far, inverse_mine, update_all, turned = stage(
         own_part,
-        [(2 * rows, half), (2 * rows, size), (2 * rows, 2 * rows), (2 * rows, 2 * rows), (2 * rows, updates), (half, 2 * quarter)],
+        [(2 * rows, half), (2 * rows, size), (2 * rows, 2 * rows), (2 * rows, rows), (2 * rows, updates), (half, 2 * quarter)],
         inverse,
         inverse_near,
         update,
@@ -216,26 +216,38 @@
         rows_near,
         chip,
     )
-    far, own_y = after(far, own_y)
-
-    def leaf_part(own_ref, inverse_ref, far_ref, update_ref, turned_ref, y_ref, *refs):
+
+    def turned_update(far_ref, mine_ref, update_ref, y_ref, turned_far_ref, turned_mine_ref, terms_ref):
+        update = update_ref[...]
+        turned_far_ref[...] = dot3(far_ref[...], update, 0, 0)
+        turned_mine_ref[...] = dot3(mine_ref[...], update, 0, 0)
+        terms_ref[...] = dot3(y_ref[...], update, 0, 0)
+
+    turned_far, own_sum, own_terms = stage(
+        turned_update,
+        [(2 * rows, updates), (rows, updates), (half, updates)],
+        inverse_far,
+        inverse_mine,
+        update_all,
+        own_y,
+    )
+    far, own_terms = after(far, own_terms)
+
+    def leaf_part(own_ref, turned_far_ref, far_ref, turned_ref, *refs):
         _, _, odd, far_bit, _ = place()
         out_refs, terms = refs[:-1], refs[-1]
-        leaf_y = own_ref[...] + dot3(inverse_ref[...], far_ref[...])
-        y_ref[...] = leaf_y
-        terms[...] = dot3(leaf_y, update_ref[...], 0, 0)
+        terms[...] = own_ref[...] + dot3(far_ref[...], turned_far_ref[...], 0, 0)
         for flip, out_ref in enumerate(out_refs):
             part = at((2 * odd + far_bit) ^ flip, block)
             out_ref[:, :updates] = terms[part]
             out_ref[:, updates:] = turned_ref[part]
 
-    leaf_y, mine, to_far, to_odd, to_both = stage(
+    mine, to_far, to_odd, to_both = stage(
         leaf_part,
-        [(2 * rows, half)] + [(block, width)] * 4,
-        own_y,
-        inverse_far,
+        [(block, width)] * 4,
+        own_terms,
+        turned_far,
         far,
-        update_all,
         turned,
         scratch=[(half, updates)],
     )
@@ -286,28 +298,29 @@
         one_hots, [jax.ShapeDtypeStruct((depth, order, 2 * capacity), bf16)], payload, received
     )
 
-    def transposed(all_ref, mine_ref, update_ref, y_ref, own_ref, far_ref, work):
-        far_bit = place()[3]
-        work[:, :half] = dot3(all_ref[...], y_ref[...], 0, 0)
-        both = dot3(mine_ref[...], update_ref[...], 0, 0)
-        own_ref[:, :updates] = by_bit(far_bit, both[:rows], both[rows:])
-        far_ref[:, :updates] = by_bit(far_bit, both[rows:], both[:rows])
+    def transposed(all_ref, inverse_far_ref, own_y_ref, far_ref, turned_far_ref, own_ref, out_ref, work):
+        _, _, _, far_bit, near_bit = place()
+        leaf_y = own_y_ref[...] + dot3(inverse_far_ref[...], far_ref[...])
+        work[...] = dot3(all_ref[...], leaf_y, 0, 0)
+        out_ref[:, :updates] = turned_far_ref[at(near_bit, rows)]
         for index in range(2):
-            part = slice(updates + index * half, updates + (index + 1) * half)
+            part = slice(index * half, (index + 1) * half)
+            shifted = slice(updates + index * half, updates + (index + 1) * half)
             own_ref[:, part] = work[at(2 * far_bit + index, rows)]
-            far_ref[:, part] = work[at(2 - 2 * far_bit + index, rows)]
-
-    leaf_y, hots = after(leaf_y, hots)
-    own_sum, far_sum = stage(
+            out_ref[:, shifted] = work[at(2 - 2 * far_bit + index, rows)]
+
+    own_y, hots = after(own_y, hots)
+    own_ys, far_sum = stage(
         transposed,
-        [(rows, updates + columns)] * 2,
+        [(rows, columns), (rows, updates + columns)],
         inverse_all,
-        inverse_mine,
-        update_all,
-        leaf_y,
+        inverse_far,
+        own_y,
+        far,
+        turned_far,
         scratch=[(size, half)],
     )
-    by_both, by_far, by_odd, own_sum = after(by_both, by_far, by_odd, own_sum)
+    by_both, by_far, by_odd, own_ys = after(by_both, by_far, by_odd, own_ys)
 
     def gathered_part(mine_ref, far_ref, odd_ref, both_ref, hot_ref, residual_ref, up_ref):
         leaf, _, odd, far_bit, _ = place()
@@ -421,7 +434,7 @@
             [(block, order), (block, (depth - level) * order)],
             going_up,
             partner,
-            cost=3 * medium,
+            cost=2 * medium,
         )
         residuals.append(residual)
         halves_near[level - 1], residual, slots = after(halves_near[level - 1], residual, slots)
@@ -505,21 +518,21 @@
     beyond = swap(to_far, 0, 2)
     side = swap(to_odd, 1, 0)
 
-    def last_left(own_ref, far_ref, left_ref, keep_ref, pass_ref):
-        near_bit = place()[4]
-        total = own_ref[...] + far_ref[...]
-        left_ref[:rows, :updates] = -total[:, :updates]
+    def last_left(own_ref, own_y_ref, far_ref, left_ref, keep_ref, pass_ref):
+        near_bit = place()[4]
+        left_ref[:rows, :updates] = -(own_ref[...] + far_ref[:, :updates])
         left_ref[:rows, updates:] = jnp.zeros((rows, 2 * quarter), f32)
         row = lax.broadcasted_iota(jnp.int32, (quarter, width), 0)
         lane = lax.broadcasted_iota(jnp.int32, (quarter, width), 1)
         left_ref[rows:] = jnp.where(lane == updates + near_bit * quarter + row, 1.0, 0.0)
-        first, second = total[:, updates : updates + half], total[:, updates + half :]
+        total = own_y_ref[...] + far_ref[:, updates:]
+        first, second = total[:, :half], total[:, half:]
         keep_ref[...] = by_bit(near_bit, first, second)
         pass_ref[...] = by_bit(near_bit, second, first)
 
     from_far, stay = after(from_far, stay)
     left, base_keep, base_pass = stage(
-        last_left, [(rows + quarter, width), (rows, half), (rows, half)], own_sum, from_far
+        last_left, [(rows + quarter, width), (rows, half), (rows, half)], own_sum, own_ys, from_far
     )
     both, beyond, side, left = after(both, beyond, side, left)
 

time: 40.9 us -> 40.7 us (level)
  waiting for transfers between devices: 10.6 us -> 9.78 us
    ppermute x21, waiting for transfers between devices: 9.44 us -> 8.03 us  [swap(): return lax.ppermute(payload, axes, pairs)]
    ppermute x1, waiting for transfers between devices: 1.18 us -> 1.75 us  [quarter_swap(): return lax.ppermute(payload, axes, pairs)]
    pallas_call x23 -> x24, Pallas kernels: 7.52 us -> 7.8 us  [stage(): pl.pallas_call(body, out_shape=[jax.ShapeDtypeStruct(shape, f32) if isins...]
  transfers between devices with their start and end apart: 22 -> 22, of which waited for: 13 -> 11; matrix products, arithmetic and copies ran while one was open for 0% -> 0% of each run, Pallas kernels for 16% -> 17%
where the time goes in v8:
time: 40.7 us; the launch traced here: 40.5 us
  starting transfers between devices  21 us (52%)
  waiting for transfers between devices  9.78 us (24%)
  Pallas kernels  7.8 us (19%)
  local copies, waits for them, and re-layouts  0.95 us (2%)
  between operations  0.93 us (2%)
    ppermute x21, starting transfers between devices, swap(): return lax.ppermute(payload, axes, pairs)  19.7 us
    ppermute x21, waiting for transfers between devices, swap(): return lax.ppermute(payload, axes, pairs)  8.03 us
    pallas_call x24, Pallas kernels, stage(): pl.pallas_call(body, out_shape=[jax.ShapeDtypeStruct(shape, f32) if isins...  7.8 us
    ppermute x1, waiting for transfers between devices, quarter_swap(): return lax.ppermute(payload, axes, pairs)  1.75 us
    ppermute x1, starting transfers between devices, quarter_swap(): return lax.ppermute(payload, axes, pairs)  1.29 us
    unnamed x16, local copies, waits for them, and re-layouts  0.95 us
  transfers between devices with their start and end apart: 22, of which 11 were waited for; matrix products, arithmetic and copies ran while one was open for 0% of the time, Pallas kernels for 17%

profile of v8, /device:TPU:0, one launch (start us, length us, event | category | flops | bytes accessed | tf_op | source)
XLA Modules:
  0.0 40.5 jit_solution(8397550888929861389)
XLA Ops:
  0.6 0.5 %collective-permute-start.2 = (f32[160,256]{1,0:T(8,128)}, f32[160,256]{1,0:T(8,128)S(1)}, u32[]{:S(2)}, u32[]{:S(2)}) collective-permute-start(f32[160,256]{1,0:T(8,128)} %bitcast.14), channel_id=1, source_target_pairs={{0,1},{1,0},{2,3},{3,2},{4,5},{5,4},{6,7},{7,6},{8,9},{9,8},{10,11... | collective-permute-start | bytes 491528 | tf_op jit(solution)/shard_map/ppermute | solution.py:22
  1.2 0.1 collective-permute-start.5
  1.2 0.4 %collective-permute-start = (f32[160,640]{1,0:T(8,128)}, f32[160,640]{1,0:T(8,128)S(1)}, u32[]{:S(2)}, u32[]{:S(2)}) collective-permute-start(f32[160,640]{1,0:T(8,128)} %bitcast.10), channel_id=1, source_target_pairs={{0,1},{1,0},{2,3},{3,2},{4,5},{5,4},{6,7},{7,6},{8,9},{9,8},{10,11... | collective-permute-start | bytes 1228808 | tf_op jit(solution)/shard_map/ppermute | solution.py:22
  1.7 0.9 %copy-done.2 = f32[1,160,256]{2,1,0:T(8,128)S(1)} copy-done((f32[1,160,256]{2,1,0:T(8,128)S(1)}, f32[1,160,256]{2,1,0:T(8,128)}, u32[]{:S(2)}) %copy-start.2) | copy-done | bytes 163864
  2.7 2.6 %collective-permute-start.4 = (f32[320,128]{1,0:T(8,128)S(1)}, f32[320,128]{1,0:T(8,128)S(1)}, u32[]{:S(2)}, u32[]{:S(2)}) collective-permute-start(f32[320,128]{1,0:T(8,128)S(1)} %shard_map.96.chip_ref), channel_id=1, source_target_pairs={{0,2},{1,3},{2,0},{3,1},{4,6},{5,7},{6,4},{7,5},{8,10},{9,11},{10,... | collective-permute-start | bytes 491528 | tf_op jit(solution)/shard_map/ppermute | solution.py:22
  5.4 0.4 shard_map.97.carry_ref.own_ref
  5.7 1.6 %collective-permute-start.3 = (f32[208,256]{1,0:T(8,128)S(1)}, f32[208,256]{1,0:T(8,128)S(1)}, u32[]{:S(2)}, u32[]{:S(2)}) collective-permute-start(f32[208,256]{1,0:T(8,128)S(1)} %shard_map.97.carry_ref.own_ref), channel_id=1, source_target_pairs={{0,4},{1,5},{2,6},{3,7},{4,0},{5,1},{6,2},{7,3},{8,12},{9,13},{10,... | collective-permute-start | bytes 638984 | tf_op jit(solution)/shard_map/ppermute | solution.py:22
  7.3 1.3 %collective-permute-done.1.rows_near_ref = f32[64,256]{1,0:T(8,128)S(1)} collective-permute-done((f32[64,256]{1,0:T(8,128)S(1)}, f32[64,256]{1,0:T(8,128)S(1)}, u32[]{:S(2)}, u32[]{:S(2)}) %collective-permute-start.1) | collective-permute-done | bytes 65568 | tf_op jit(solution)/shard_map/ppermute | solution.py:22
  8.6 0.8 %shard_map.98 = (f32[320,128]{1,0:T(8,128)S(1)}, f32[320,640]{1,0:T(8,128)S(1)}, f32[320,320]{1,0:T(8,128)S(1)}, f32[320,160]{1,0:T(8,128)S(1)}, f32[320,384]{1,0:T(8,128)S(1)}, /*index=5*/f32[128,128]{1,0:T(8,128)S(1)}) custom-call(f32[160,640]{1,0:T(8,128)S(1)} %bitcast.11, f32[160,640]{1,0:T(8,128)S(1)} %collective-permute-done.inverse_near_ref, ...), custom_call_target="tpu_custom_call" | custom-call | tf_op jit(solution)/shard_map/pallas_call | solution.py:75
  9.4 1.1 %shard_map.99 = (f32[320,384]{1,0:T(8,128)S(1)}, f32[160,384]{1,0:T(8,128)S(1)}, f32[128,384]{1,0:T(8,128)S(1)}) custom-call(f32[320,320]{1,0:T(8,128)S(1)} %get-tuple-element.97.far_ref.inverse_far_ref, f32[320,160]{1,0:T(8,128)S(1)} %get-tuple-element.98.mine_ref, f32[320,384]{1,0:T(8,128)S(1)} %get-tuple-element.99.update_ref, ...), custom_call_target="tpu_custom_call" | custom-call | tf_op jit(solution)/shard_map/pallas_call | solution.py:75
  10.5 0.4 shard_map.100
  10.9 2.4 %collective-permute-start.8 = (f32[32,512]{1,0:T(8,128)S(1)}, f32[32,512]{1,0:T(8,128)S(1)}, u32[]{:S(2)}, u32[]{:S(2)}) collective-permute-start(f32[32,512]{1,0:T(8,128)S(1)} %get-tuple-element.112), channel_id=1, source_target_pairs={{0,6},{1,7},{2,4},{3,5},{4,2},{5,3},{6,0},{7,1},{8,14},{9,15},{10,... | collective-permute-start | bytes 196616 | tf_op jit(solution)/shard_map/ppermute | solution.py:22
  13.3 0.5 %collective-permute-start.9 = (f32[32,512]{1,0:T(8,128)S(1)}, f32[32,512]{1,0:T(8,128)S(1)}, u32[]{:S(2)}, u32[]{:S(2)}) collective-permute-start(f32[32,512]{1,0:T(8,128)S(1)} %get-tuple-element.113), channel_id=1, source_target_pairs={{0,2},{1,3},{2,0},{3,1},{4,6},{5,7},{6,4},{7,5},{8,10},{9,11},{10,... | collective-permute-start | bytes 196616 | tf_op jit(solution)/shard_map/ppermute | solution.py:22
  13.8 0.6 %collective-permute-start.10 = (f32[32,512]{1,0:T(8,128)S(1)}, f32[32,512]{1,0:T(8,128)S(1)}, u32[]{:S(2)}, u32[]{:S(2)}) collective-permute-start(f32[32,512]{1,0:T(8,128)S(1)} %get-tuple-element.114), channel_id=1, source_target_pairs={{0,4},{1,5},{2,6},{3,7},{4,0},{5,1},{6,2},{7,3},{8,12},{9,13},{10,... | collective-permute-start | bytes 196616 | tf_op jit(solution)/shard_map/ppermute | solution.py:22
  14.5 1.3 %collective-permute-start.6 = (f32[200,256]{1,0:T(8,128)S(1)}, f32[200,256]{1,0:T(8,128)S(1)}, u32[]{:S(2)}, u32[]{:S(2)}) collective-permute-start(f32[200,256]{1,0:T(8,128)S(1)} %get-tuple-element.109.carry_ref), channel_id=1, source_target_pairs={{8,0},{9,1},{10,2},{11,3},{12,4},{13,5},{14,6},{15,7},{24,16},{25,... | collective-permute-start | bytes 614408 | tf_op jit(solution)/shard_map/ppermute | solution.py:34
  15.8 0.1 shard_map.102.hot_ref
  15.9 0.1 collective-permute-start.7
  15.9 0.9 %shard_map.103 = (f32[160,256]{1,0:T(8,128)S(1)}, f32[160,640]{1,0:T(8,128)S(1)}) custom-call(f32[320,640]{1,0:T(8,128)S(1)} %get-tuple-element.115.all_ref, f32[320,320]{1,0:T(8,128)S(1)} %get-tuple-element.97.far_ref.inverse_far_ref, f32[320,128]{1,0:T(8,128)S(1)} %get-tuple-element.117.y_ref.own_y_ref, f32[320,128]{1,0:T(8,128)S(1)} %collective-permute-done.4.far_ref, ...), custom_call_target="tpu_custom_call" | custom-call | tf_op jit(solution)/shard_map/pallas_call | solution.py:75
  16.9 0.7 %collective-permute-done.9.far_ref = f32[32,512]{1,0:T(8,128)S(1)} collective-permute-done((f32[32,512]{1,0:T(8,128)S(1)}, f32[32,512]{1,0:T(8,128)S(1)}, u32[]{:S(2)}, u32[]{:S(2)}) %collective-permute-start.9) | collective-permute-done | bytes 65568 | tf_op jit(solution)/shard_map/ppermute | solution.py:22
  17.6 0.5 %collective-permute-done.10.odd_ref = f32[32,512]{1,0:T(8,128)S(1)} collective-permute-done((f32[32,512]{1,0:T(8,128)S(1)}, f32[32,512]{1,0:T(8,128)S(1)}, u32[]{:S(2)}, u32[]{:S(2)}) %collective-permute-start.10) | collective-permute-done | bytes 65568 | tf_op jit(solution)/shard_map/ppermute | solution.py:22
  18.1 0.3 shard_map.104
  18.4 0.2 shard_map.105.up_ref
  18.6 1.7 %collective-permute-start.12 = (f32[32,512]{1,0:T(8,128)S(1)}, f32[32,512]{1,0:T(8,128)S(1)}, u32[]{:S(2)}, u32[]{:S(2)}) collective-permute-start(f32[32,512]{1,0:T(8,128)S(1)} %shard_map.105.up_ref), channel_id=1, source_target_pairs={{0,8},{1,9},{2,10},{3,11},{4,12},{5,13},{6,14},{7,15},{8,0},{9,1},... | collective-permute-start | bytes 196616 | tf_op jit(solution)/shard_map/ppermute | solution.py:22
  20.3 1.3 %collective-permute-start.19 = (f32[160,640]{1,0:T(8,128)S(1)}, f32[160,640]{1,0:T(8,128)S(1)}, u32[]{:S(2)}, u32[]{:S(2)}) collective-permute-start(f32[160,640]{1,0:T(8,128)S(1)} %get-tuple-element.161), channel_id=1, source_target_pairs={{2,0},{3,1},{6,4},{7,5},{10,8},{11,9},{14,12},{15,13},{18,16},{19,... | collective-permute-start | bytes 1228808 | tf_op jit(solution)/shard_map/ppermute | solution.py:22
  21.6 1.8 %collective-permute-done.6.received_ref = f32[200,256]{1,0:T(8,128)S(1)} collective-permute-done((f32[200,256]{1,0:T(8,128)S(1)}, f32[200,256]{1,0:T(8,128)S(1)}, u32[]{:S(2)}, u32[]{:S(2)}) %collective-permute-start.6) | collective-permute-done | bytes 204832 | tf_op jit(solution)/shard_map/ppermute | solution.py:34
  23.4 0.1 collective-permute-start.13
  23.5 0.9 %collective-permute-start.11 = (f32[72,256]{1,0:T(8,128)S(1)}, f32[72,256]{1,0:T(8,128)S(1)}, u32[]{:S(2)}, u32[]{:S(2)}) collective-permute-start(f32[72,256]{1,0:T(8,128)S(1)} %get-tuple-element.129.root_ref), channel_id=1, source_target_pairs={{0,8},{1,9},{2,10},{3,11},{4,12},{5,13},{6,14},{7,15},{8,0},{9,1},... | collective-permute-start | bytes 221192 | tf_op jit(solution)/shard_map/ppermute | solution.py:22
  24.4 0.5 %collective-permute-done.13.near_ref = f32[200,256]{1,0:T(8,128)S(1)} collective-permute-done((f32[200,256]{1,0:T(8,128)S(1)}, f32[200,256]{1,0:T(8,128)S(1)}, u32[]{:S(2)}, u32[]{:S(2)}) %collective-permute-start.13) | collective-permute-done | bytes 204832 | tf_op jit(solution)/shard_map/ppermute | solution.py:22
  24.9 0.2 shard_map.108.up_ref
  25.1 2.7 %collective-permute-start.15 = (f32[32,256]{1,0:T(8,128)S(1)}, f32[32,256]{1,0:T(8,128)S(1)}, u32[]{:S(2)}, u32[]{:S(2)}) collective-permute-start(f32[32,256]{1,0:T(8,128)S(1)} %shard_map.108.up_ref), channel_id=1, source_target_pairs={{0,16},{1,17},{2,18},{3,19},{4,20},{5,21},{6,22},{7,23},{8,24},{9,... | collective-permute-start | bytes 98312 | tf_op jit(solution)/shard_map/ppermute | solution.py:22
  27.8 0.4 shard_map.109
  28.2 0.1 collective-permute-start.14
  28.3 0.4 shard_map.111
  28.7 0.4 shard_map.112
  29.0 1.3 %collective-permute-done.15.partner_ref = f32[32,256]{1,0:T(8,128)S(1)} collective-permute-done((f32[32,256]{1,0:T(8,128)S(1)}, f32[32,256]{1,0:T(8,128)S(1)}, u32[]{:S(2)}, u32[]{:S(2)}) %collective-permute-start.15) | collective-permute-done | bytes 32800 | tf_op jit(solution)/shard_map/ppermute | solution.py:22
  30.3 0.8 %shard_map.114 = (f32[32,512]{1,0:T(8,128)S(1)}, f32[32,512]{1,0:T(8,128)S(1)}, f32[32,512]{1,0:T(8,128)S(1)}, f32[32,512]{1,0:T(8,128)S(1)}) custom-call(f32[32,256]{1,0:T(8,128)S(1)} %shard_map.113.residual_ref, f32[72,256]{1,0:T(8,128)S(1)} %shard_map.110.root_ref, f32[72,256]{1,0:T(8,128)S(1)} %collective-permute-done.14.root_near_ref, ...), custom_call_target="tpu_custom_call" | custom-call | tf_op jit(solution)/shard_map/pallas_call | solution.py:75
  31.1 1.9 %collective-permute-start.16 = (f32[32,512]{1,0:T(8,128)S(1)}, f32[32,512]{1,0:T(8,128)S(1)}, u32[]{:S(2)}, u32[]{:S(2)}) collective-permute-start(f32[32,512]{1,0:T(8,128)S(1)} %get-tuple-element.156), channel_id=1, source_target_pairs={{0,6},{1,7},{2,4},{3,5},{4,2},{5,3},{6,0},{7,1},{8,14},{9,15},{10,... | collective-permute-start | bytes 196616 | tf_op jit(solution)/shard_map/ppermute | solution.py:22
  32.9 0.5 %collective-permute-start.17 = (f32[32,512]{1,0:T(8,128)S(1)}, f32[32,512]{1,0:T(8,128)S(1)}, u32[]{:S(2)}, u32[]{:S(2)}) collective-permute-start(f32[32,512]{1,0:T(8,128)S(1)} %get-tuple-element.157), channel_id=1, source_target_pairs={{0,2},{1,3},{2,0},{3,1},{4,6},{5,7},{6,4},{7,5},{8,10},{9,11},{10,... | collective-permute-start | bytes 196616 | tf_op jit(solution)/shard_map/ppermute | solution.py:22
  33.4 1.2 %collective-permute-start.18 = (f32[32,512]{1,0:T(8,128)S(1)}, f32[32,512]{1,0:T(8,128)S(1)}, u32[]{:S(2)}, u32[]{:S(2)}) collective-permute-start(f32[32,512]{1,0:T(8,128)S(1)} %get-tuple-element.158), channel_id=1, source_target_pairs={{0,4},{1,5},{2,6},{3,7},{4,0},{5,1},{6,2},{7,3},{8,12},{9,13},{10,... | collective-permute-start | bytes 196616 | tf_op jit(solution)/shard_map/ppermute | solution.py:22
  34.6 0.1 shard_map.115
  34.7 1.9 %collective-permute-done.16.refs_3_ = f32[32,512]{1,0:T(8,128)S(1)} collective-permute-done((f32[32,512]{1,0:T(8,128)S(1)}, f32[32,512]{1,0:T(8,128)S(1)}, u32[]{:S(2)}, u32[]{:S(2)}) %collective-permute-start.16) | collective-permute-done | bytes 65568 | tf_op jit(solution)/shard_map/ppermute | solution.py:22
  36.6 0.6 %collective-permute-done.17.refs_1_ = f32[32,512]{1,0:T(8,128)S(1)} collective-permute-done((f32[32,512]{1,0:T(8,128)S(1)}, f32[32,512]{1,0:T(8,128)S(1)}, u32[]{:S(2)}, u32[]{:S(2)}) %collective-permute-start.17) | collective-permute-done | bytes 65568 | tf_op jit(solution)/shard_map/ppermute | solution.py:22
  37.2 0.5 %collective-permute-done.18.refs_2_ = f32[32,512]{1,0:T(8,128)S(1)} collective-permute-done((f32[32,512]{1,0:T(8,128)S(1)}, f32[32,512]{1,0:T(8,128)S(1)}, u32[]{:S(2)}, u32[]{:S(2)}) %collective-permute-start.18) | collective-permute-done | bytes 65568 | tf_op jit(solution)/shard_map/ppermute | solution.py:22
  37.8 0.5 %collective-permute-start.21 = (f32[160,128]{1,0:T(8,128)S(1)}, f32[160,128]{1,0:T(8,128)S(1)}, u32[]{:S(2)}, u32[]{:S(2)}) collective-permute-start(f32[160,128]{1,0:T(8,128)S(1)} %get-tuple-element.173), channel_id=1, source_target_pairs={{0,1},{1,0},{2,3},{3,2},{4,5},{5,4},{6,7},{7,6},{8,9},{9,8},{10,11... | collective-permute-start | bytes 245768 | tf_op jit(solution)/shard_map/ppermute | solution.py:22
  38.3 0.3 shard_map.117.ours_ref
  38.7 0.7 %collective-permute-done.20.group_ref = f32[128,512]{1,0:T(8,128)S(1)} collective-permute-done((f32[128,512]{1,0:T(8,128)S(1)}, f32[128,512]{1,0:T(8,128)S(1)}, u32[]{:S(2)}, u32[]{:S(2)}) %collective-permute-start.20) | collective-permute-done | bytes 262176 | tf_op jit(solution)/shard_map/ppermute | solution.py:22
  39.3 0.1 collective-permute-done.21.base_near_ref
  39.5 1.0 %shard_map.118 = (f32[160,256]{1,0:T(8,128)}, f32[64,256]{1,0:T(8,128)}) custom-call(f32[224,512]{1,0:T(8,128)S(1)} %get-tuple-element.165.left_ref, f32[128,512]{1,0:T(8,128)S(1)} %collective-permute-done.20.group_ref, f32[224,128]{1,0:T(8,128)S(1)} %shard_map.117.ours_ref, f32[160,128]{1,0:T(8,128)S(1)} %get-tuple-element.172.base_ref, ...), custom_call_target="tpu_custom_call" | custom-call | tf_op jit(solution)/shard_map/pallas_call | solution.py:75
  (37 shorter events, 0.4 us)
Async XLA Ops:
  0.6 2.0 %copy-start.7 = (s32[1,3]{1,0:T(1,128)S(1)}, s32[1,3]{1,0:T(1,128)}, u32[]{:S(2)}) copy-start(s32[1,3]{1,0:T(1,128)} %param.12) | copy-start | bytes 40
  0.6 2.0 %collective-permute-start.2 = (f32[160,256]{1,0:T(8,128)}, f32[160,256]{1,0:T(8,128)S(1)}, u32[]{:S(2)}, u32[]{:S(2)}) collective-permute-start(f32[160,256]{1,0:T(8,128)} %bitcast.14), channel_id=1, source_target_pairs={{0,1},{1,0},{2,3},{3,2},{4,5},{5,4},{6,7},{7,6},{8,9},{9,8},{10,11... | collective-permute-start | bytes 491528 | tf_op jit(solution)/shard_map/ppermute | solution.py:22
  1.2 7.4 %collective-permute-start.5 = (f32[160,384]{1,0:T(8,128)}, f32[160,384]{1,0:T(8,128)S(1)}, u32[]{:S(2)}, u32[]{:S(2)}) collective-permute-start(f32[160,384]{1,0:T(8,128)} %bitcast.12), channel_id=1, source_target_pairs={{0,1},{1,0},{2,3},{3,2},{4,5},{5,4},{6,7},{7,6},{8,9},{9,8},{10,11... | collective-permute-start | bytes 737288 | tf_op jit(solution)/shard_map/ppermute | solution.py:22
  1.2 1.4 %copy-start.6 = (s32[1,384]{1,0:T(1,128)S(1)}, s32[1,384]{1,0:T(1,128)}, u32[]{:S(2)}) copy-start(s32[1,384]{1,0:T(1,128)} %param.11) | copy-start | bytes 4612
  1.2 7.3 %collective-permute-start = (f32[160,640]{1,0:T(8,128)}, f32[160,640]{1,0:T(8,128)S(1)}, u32[]{:S(2)}, u32[]{:S(2)}) collective-permute-start(f32[160,640]{1,0:T(8,128)} %bitcast.10), channel_id=1, source_target_pairs={{0,1},{1,0},{2,3},{3,2},{4,5},{5,4},{6,7},{7,6},{8,9},{9,8},{10,11... | collective-permute-start | bytes 1228808 | tf_op jit(solution)/shard_map/ppermute | solution.py:22
  1.7 0.9 %copy-start.2 = (f32[1,160,256]{2,1,0:T(8,128)S(1)}, f32[1,160,256]{2,1,0:T(8,128)}, u32[]{:S(2)}) copy-start(f32[1,160,256]{2,1,0:T(8,128)} %param.8) | copy-start | bytes 491524
  2.6 2.8 %copy-start.5 = (f32[1,256,256]{2,1,0:T(8,128)S(1)}, f32[1,256,256]{2,1,0:T(8,128)}, u32[]{:S(2)}) copy-start(f32[1,256,256]{2,1,0:T(8,128)} %param.14) | copy-start | bytes 786436
  2.6 2.7 %copy-start.4 = (f32[1,256,256]{2,1,0:T(8,128)S(1)}, f32[1,256,256]{2,1,0:T(8,128)}, u32[]{:S(2)}) copy-start(f32[1,256,256]{2,1,0:T(8,128)} %param.15) | copy-start | bytes 786436
  2.7 7.8 %collective-permute-start.4 = (f32[320,128]{1,0:T(8,128)S(1)}, f32[320,128]{1,0:T(8,128)S(1)}, u32[]{:S(2)}, u32[]{:S(2)}) collective-permute-start(f32[320,128]{1,0:T(8,128)S(1)} %shard_map.96.chip_ref), channel_id=1, source_target_pairs={{0,2},{1,3},{2,0},{3,1},{4,6},{5,7},{6,4},{7,5},{8,10},{9,11},{10,... | collective-permute-start | bytes 491528 | tf_op jit(solution)/shard_map/ppermute | solution.py:22
  5.3 2.0 %copy-start.3 = (f32[1,64,256]{2,1,0:T(8,128)S(1)}, f32[1,64,256]{2,1,0:T(8,128)}, u32[]{:S(2)}) copy-start(f32[1,64,256]{2,1,0:T(8,128)} %param.13) | copy-start | bytes 196612
  5.3 3.2 %copy-start = (f32[1,160,640]{2,1,0:T(8,128)S(1)}, f32[1,160,640]{2,1,0:T(8,128)}, u32[]{:S(2)}) copy-start(f32[1,160,640]{2,1,0:T(8,128)} %param.9) | copy-start | bytes 1228804
  5.4 3.2 %copy-start.1 = (f32[1,384,160]{1,2,0:T(8,128)S(1)}, f32[1,384,160]{1,2,0:T(8,128)}, u32[]{:S(2)}) copy-start(f32[1,384,160]{1,2,0:T(8,128)} %param.10) | copy-start | bytes 737284
  5.7 8.7 %collective-permute-start.3 = (f32[208,256]{1,0:T(8,128)S(1)}, f32[208,256]{1,0:T(8,128)S(1)}, u32[]{:S(2)}, u32[]{:S(2)}) collective-permute-start(f32[208,256]{1,0:T(8,128)S(1)} %shard_map.97.carry_ref.own_ref), channel_id=1, source_target_pairs={{0,4},{1,5},{2,6},{3,7},{4,0},{5,1},{6,2},{7,3},{8,12},{9,13},{10,... | collective-permute-start | bytes 638984 | tf_op jit(solution)/shard_map/ppermute | solution.py:22
  7.3 1.3 %collective-permute-start.1 = (f32[64,256]{1,0:T(8,128)S(1)}, f32[64,256]{1,0:T(8,128)S(1)}, u32[]{:S(2)}, u32[]{:S(2)}) collective-permute-start(f32[64,256]{1,0:T(8,128)S(1)} %bitcast.16), channel_id=1, source_target_pairs={{0,1},{1,0},{2,3},{3,2},{4,5},{5,4},{6,7},{7,6},{8,9},{9,8},{10,11... | collective-permute-start | bytes 196616 | tf_op jit(solution)/shard_map/ppermute | solution.py:22
  10.9 6.0 %collective-permute-start.8 = (f32[32,512]{1,0:T(8,128)S(1)}, f32[32,512]{1,0:T(8,128)S(1)}, u32[]{:S(2)}, u32[]{:S(2)}) collective-permute-start(f32[32,512]{1,0:T(8,128)S(1)} %get-tuple-element.112), channel_id=1, source_target_pairs={{0,6},{1,7},{2,4},{3,5},{4,2},{5,3},{6,0},{7,1},{8,14},{9,15},{10,... | collective-permute-start | bytes 196616 | tf_op jit(solution)/shard_map/ppermute | solution.py:22
  13.3 4.3 %collective-permute-start.9 = (f32[32,512]{1,0:T(8,128)S(1)}, f32[32,512]{1,0:T(8,128)S(1)}, u32[]{:S(2)}, u32[]{:S(2)}) collective-permute-start(f32[32,512]{1,0:T(8,128)S(1)} %get-tuple-element.113), channel_id=1, source_target_pairs={{0,2},{1,3},{2,0},{3,1},{4,6},{5,7},{6,4},{7,5},{8,10},{9,11},{10,... | collective-permute-start | bytes 196616 | tf_op jit(solution)/shard_map/ppermute | solution.py:22
  13.8 4.3 %collective-permute-start.10 = (f32[32,512]{1,0:T(8,128)S(1)}, f32[32,512]{1,0:T(8,128)S(1)}, u32[]{:S(2)}, u32[]{:S(2)}) collective-permute-start(f32[32,512]{1,0:T(8,128)S(1)} %get-tuple-element.114), channel_id=1, source_target_pairs={{0,4},{1,5},{2,6},{3,7},{4,0},{5,1},{6,2},{7,3},{8,12},{9,13},{10,... | collective-permute-start | bytes 196616 | tf_op jit(solution)/shard_map/ppermute | solution.py:22
  14.5 8.9 %collective-permute-start.6 = (f32[200,256]{1,0:T(8,128)S(1)}, f32[200,256]{1,0:T(8,128)S(1)}, u32[]{:S(2)}, u32[]{:S(2)}) collective-permute-start(f32[200,256]{1,0:T(8,128)S(1)} %get-tuple-element.109.carry_ref), channel_id=1, source_target_pairs={{8,0},{9,1},{10,2},{11,3},{12,4},{13,5},{14,6},{15,7},{24,16},{25,... | collective-permute-start | bytes 614408 | tf_op jit(solution)/shard_map/ppermute | solution.py:34
  15.9 2.5 %collective-permute-start.7 = (f32[200,256]{1,0:T(8,128)S(1)}, f32[200,256]{1,0:T(8,128)S(1)}, u32[]{:S(2)}, u32[]{:S(2)}) collective-permute-start(f32[200,256]{1,0:T(8,128)S(1)} %get-tuple-element.110.half_ref), channel_id=1, source_target_pairs={{0,1},{1,0},{2,3},{3,2},{4,5},{5,4},{6,7},{7,6},{8,9},{9,8},{10,11... | collective-permute-start | bytes 614408 | tf_op jit(solution)/shard_map/ppermute | solution.py:22
  18.6 5.8 %collective-permute-start.12 = (f32[32,512]{1,0:T(8,128)S(1)}, f32[32,512]{1,0:T(8,128)S(1)}, u32[]{:S(2)}, u32[]{:S(2)}) collective-permute-start(f32[32,512]{1,0:T(8,128)S(1)} %shard_map.105.up_ref), channel_id=1, source_target_pairs={{0,8},{1,9},{2,10},{3,11},{4,12},{5,13},{6,14},{7,15},{8,0},{9,1},... | collective-permute-start | bytes 196616 | tf_op jit(solution)/shard_map/ppermute | solution.py:22
  20.3 14.3 %collective-permute-start.19 = (f32[160,640]{1,0:T(8,128)S(1)}, f32[160,640]{1,0:T(8,128)S(1)}, u32[]{:S(2)}, u32[]{:S(2)}) collective-permute-start(f32[160,640]{1,0:T(8,128)S(1)} %get-tuple-element.161), channel_id=1, source_target_pairs={{2,0},{3,1},{6,4},{7,5},{10,8},{11,9},{14,12},{15,13},{18,16},{19,... | collective-permute-start | bytes 1228808 | tf_op jit(solution)/shard_map/ppermute | solution.py:22
  23.4 1.5 %collective-permute-start.13 = (f32[200,256]{1,0:T(8,128)S(1)}, f32[200,256]{1,0:T(8,128)S(1)}, u32[]{:S(2)}, u32[]{:S(2)}) collective-permute-start(f32[200,256]{1,0:T(8,128)S(1)} %get-tuple-element.132.half_ref), channel_id=1, source_target_pairs={{0,1},{1,0},{2,3},{3,2},{4,5},{5,4},{6,7},{7,6},{8,9},{9,8},{10,11... | collective-permute-start | bytes 614408 | tf_op jit(solution)/shard_map/ppermute | solution.py:22
  23.5 4.7 %collective-permute-start.11 = (f32[72,256]{1,0:T(8,128)S(1)}, f32[72,256]{1,0:T(8,128)S(1)}, u32[]{:S(2)}, u32[]{:S(2)}) collective-permute-start(f32[72,256]{1,0:T(8,128)S(1)} %get-tuple-element.129.root_ref), channel_id=1, source_target_pairs={{0,8},{1,9},{2,10},{3,11},{4,12},{5,13},{6,14},{7,15},{8,0},{9,1},... | collective-permute-start | bytes 221192 | tf_op jit(solution)/shard_map/ppermute | solution.py:22
  25.1 5.2 %collective-permute-start.15 = (f32[32,256]{1,0:T(8,128)S(1)}, f32[32,256]{1,0:T(8,128)S(1)}, u32[]{:S(2)}, u32[]{:S(2)}) collective-permute-start(f32[32,256]{1,0:T(8,128)S(1)} %shard_map.108.up_ref), channel_id=1, source_target_pairs={{0,16},{1,17},{2,18},{3,19},{4,20},{5,21},{6,22},{7,23},{8,24},{9,... | collective-permute-start | bytes 98312 | tf_op jit(solution)/shard_map/ppermute | solution.py:22
  28.2 2.1 %collective-permute-start.14 = (f32[72,256]{1,0:T(8,128)S(1)}, f32[72,256]{1,0:T(8,128)S(1)}, u32[]{:S(2)}, u32[]{:S(2)}) collective-permute-start(f32[72,256]{1,0:T(8,128)S(1)} %shard_map.110.root_ref), channel_id=1, source_target_pairs={{0,1},{1,0},{2,3},{3,2},{4,5},{5,4},{6,7},{7,6},{8,9},{9,8},{10,11... | collective-permute-start | bytes 221192 | tf_op jit(solution)/shard_map/ppermute | solution.py:22
  31.1 5.5 %collective-permute-start.16 = (f32[32,512]{1,0:T(8,128)S(1)}, f32[32,512]{1,0:T(8,128)S(1)}, u32[]{:S(2)}, u32[]{:S(2)}) collective-permute-start(f32[32,512]{1,0:T(8,128)S(1)} %get-tuple-element.156), channel_id=1, source_target_pairs={{0,6},{1,7},{2,4},{3,5},{4,2},{5,3},{6,0},{7,1},{8,14},{9,15},{10,... | collective-permute-start | bytes 196616 | tf_op jit(solution)/shard_map/ppermute | solution.py:22
  32.9 4.3 %collective-permute-start.17 = (f32[32,512]{1,0:T(8,128)S(1)}, f32[32,512]{1,0:T(8,128)S(1)}, u32[]{:S(2)}, u32[]{:S(2)}) collective-permute-start(f32[32,512]{1,0:T(8,128)S(1)} %get-tuple-element.157), channel_id=1, source_target_pairs={{0,2},{1,3},{2,0},{3,1},{4,6},{5,7},{6,4},{7,5},{8,10},{9,11},{10,... | collective-permute-start | bytes 196616 | tf_op jit(solution)/shard_map/ppermute | solution.py:22
  33.4 4.3 %collective-permute-start.18 = (f32[32,512]{1,0:T(8,128)S(1)}, f32[32,512]{1,0:T(8,128)S(1)}, u32[]{:S(2)}, u32[]{:S(2)}) collective-permute-start(f32[32,512]{1,0:T(8,128)S(1)} %get-tuple-element.158), channel_id=1, source_target_pairs={{0,4},{1,5},{2,6},{3,7},{4,0},{5,1},{6,2},{7,3},{8,12},{9,13},{10,... | collective-permute-start | bytes 196616 | tf_op jit(solution)/shard_map/ppermute | solution.py:22
  37.7 1.6 %collective-permute-start.20 = (f32[128,512]{1,0:T(8,128)S(1)}, f32[128,512]{1,0:T(8,128)S(1)}, u32[]{:S(2)}, u32[]{:S(2)}) collective-permute-start(f32[128,512]{1,0:T(8,128)S(1)} %shard_map.116.group_ref), channel_id=1, source_target_pairs={{0,1},{1,0},{2,3},{3,2},{4,5},{5,4},{6,7},{7,6},{8,9},{9,8},{10,11... | collective-permute-start | bytes 786440 | tf_op jit(solution)/shard_map/ppermute | solution.py:22
  37.8 1.6 %collective-permute-start.21 = (f32[160,128]{1,0:T(8,128)S(1)}, f32[160,128]{1,0:T(8,128)S(1)}, u32[]{:S(2)}, u32[]{:S(2)}) collective-permute-start(f32[160,128]{1,0:T(8,128)S(1)} %get-tuple-element.173), channel_id=1, source_target_pairs={{0,1},{1,0},{2,3},{3,2},{4,5},{5,4},{6,7},{7,6},{8,9},{9,8},{10,11... | collective-permute-start | bytes 245768 | tf_op jit(solution)/shard_map/ppermute | solution.py:22

commit v9 on v8

--- a/solution.py
+++ b/solution.py
@@ -181,7 +181,7 @@
         cost=3 * medium,
     )
 
-    def own_part(inverse_ref, inverse_near_ref, update_ref, update_near_ref, rows_ref, rows_near_ref, chip_ref, y_ref, all_ref, far_ref, mine_ref, update_out_ref, turned_ref):
+    def own_part(inverse_ref, inverse_near_ref, update_ref, update_near_ref, chip_ref, y_ref, all_ref, far_ref, mine_ref, update_out_ref):
         _, _, _, far_bit, near_bit = place()
         own, other = at(near_bit, rows), at(1 - near_bit, rows)
         all_ref[own] = inverse_ref[...]
@@ -194,26 +194,16 @@
         y_ref[...] = dot3(by_bit(far_bit, first, second), chip_ref[...])
         chip_block = by_bit(far_bit, first, second)
         mine_ref[...] = by_bit(near_bit, chip_block[:, :rows], chip_block[:, rows:])
-        turned, turned_near = jnp.transpose(rows_ref[...]), jnp.transpose(rows_near_ref[...])
-        turned = by_bit(near_bit, turned[:half], turned[half:])
-        turned_near = by_bit(near_bit, turned_near[:half], turned_near[half:])
-        turned_ref[...] = by_bit(
-            near_bit,
-            jnp.concatenate([turned, turned_near], 1),
-            jnp.concatenate([turned_near, turned], 1),
-        )
 
     received = swap(payload, 1, 0)
-    inverse_near, rows_near, payload = after(inverse_near, rows_near, payload)
-    own_y, inverse_all, inverse_far, inverse_mine, update_all, turned = stage(
+    inverse_near, payload = after(inverse_near, payload)
+    own_y, inverse_all, inverse_far, inverse_mine, update_all = stage(
         own_part,
-        [(2 * rows, half), (2 * rows, size), (2 * rows, 2 * rows), (2 * rows, rows), (2 * rows, updates), (half, 2 * quarter)],
+        [(2 * rows, half), (2 * rows, size), (2 * rows, 2 * rows), (2 * rows, rows), (2 * rows, updates)],
         inverse,
         inverse_near,
         update,
         update_near,
-        rows_source,
-        rows_near,
         chip,
     )
 
@@ -231,7 +221,21 @@
         update_all,
         own_y,
     )
-    far, own_terms = after(far, own_terms)
+
+    def turned_rows(rows_ref, rows_near_ref, out_ref):
+        near_bit = place()[4]
+        turned, turned_near = jnp.transpose(rows_ref[...]), jnp.transpose(rows_near_ref[...])
+        turned = by_bit(near_bit, turned[:half], turned[half:])
+        turned_near = by_bit(near_bit, turned_near[:half], turned_near[half:])
+        out_ref[...] = by_bit(
+            near_bit,
+            jnp.concatenate([turned, turned_near], 1),
+            jnp.concatenate([turned_near, turned], 1),
+        )
+
+    rows_near, own_terms = after(rows_near, own_terms)
+    (turned,) = stage(turned_rows, [(half, 2 * quarter)], rows_source, rows_near)
+    far, turned = after(far, turned)
 
     def leaf_part(own_ref, turned_far_ref, far_ref, turned_ref, *refs):
         _, _, odd, far_bit, _ = place()

time: 40.7 us -> 40.7 us (level)
    ppermute x21, waiting for transfers between devices: 8.03 us -> 8.76 us  [swap(): return lax.ppermute(payload, axes, pairs)]
    ppermute x1, waiting for transfers between devices: 1.75 us -> 1.17 us  [quarter_swap(): return lax.ppermute(payload, axes, pairs)]
    pallas_call x24 -> x25, Pallas kernels: 7.8 us -> 7.85 us  [stage(): pl.pallas_call(body, out_shape=[jax.ShapeDtypeStruct(shape, f32) if isins...]
  transfers between devices with their start and end apart: 22 -> 22, of which waited for: 11 -> 12; matrix products, arithmetic and copies ran while one was open for 0% -> 0% of each run, Pallas kernels for 17% -> 17%
where the time goes in v9:
time: 40.7 us; the launch traced here: 40.5 us
  starting transfers between devices  20.8 us (51%)
  waiting for transfers between devices  9.93 us (24%)
  Pallas kernels  7.85 us (19%)
  local copies, waits for them, and re-layouts  0.95 us (2%)
  between operations  0.94 us (2%)
    ppermute x21, starting transfers between devices, swap(): return lax.ppermute(payload, axes, pairs)  19.5 us
    ppermute x21, waiting for transfers between devices, swap(): return lax.ppermute(payload, axes, pairs)  8.76 us
    pallas_call x25, Pallas kernels, stage(): pl.pallas_call(body, out_shape=[jax.ShapeDtypeStruct(shape, f32) if isins...  7.85 us
    ppermute x1, starting transfers between devices, quarter_swap(): return lax.ppermute(payload, axes, pairs)  1.29 us
    ppermute x1, waiting for transfers between devices, quarter_swap(): return lax.ppermute(payload, axes, pairs)  1.17 us
    unnamed x16, local copies, waits for them, and re-layouts  0.95 us
  transfers between devices with their start and end apart: 22, of which 12 were waited for; matrix products, arithmetic and copies ran while one was open for 0% of the time, Pallas kernels for 17%

profile of v9, /device:TPU:0, one launch (start us, length us, event | category | flops | bytes accessed | tf_op | source)
XLA Modules:
  0.0 40.5 jit_solution(6935325573949701612)
XLA Ops:
  0.6 0.5 %collective-permute-start.1 = (f32[160,256]{1,0:T(8,128)}, f32[160,256]{1,0:T(8,128)S(1)}, u32[]{:S(2)}, u32[]{:S(2)}) collective-permute-start(f32[160,256]{1,0:T(8,128)} %bitcast.14), channel_id=1, source_target_pairs={{0,1},{1,0},{2,3},{3,2},{4,5},{5,4},{6,7},{7,6},{8,9},{9,8},{10,11... | collective-permute-start | bytes 491528 | tf_op jit(solution)/shard_map/ppermute | solution.py:22
  1.2 0.1 collective-permute-start.4
  1.2 0.4 %collective-permute-start = (f32[160,640]{1,0:T(8,128)}, f32[160,640]{1,0:T(8,128)S(1)}, u32[]{:S(2)}, u32[]{:S(2)}) collective-permute-start(f32[160,640]{1,0:T(8,128)} %bitcast.10), channel_id=1, source_target_pairs={{0,1},{1,0},{2,3},{3,2},{4,5},{5,4},{6,7},{7,6},{8,9},{9,8},{10,11... | collective-permute-start | bytes 1228808 | tf_op jit(solution)/shard_map/ppermute | solution.py:22
  1.7 0.9 %copy-done.2 = f32[1,160,256]{2,1,0:T(8,128)S(1)} copy-done((f32[1,160,256]{2,1,0:T(8,128)S(1)}, f32[1,160,256]{2,1,0:T(8,128)}, u32[]{:S(2)}) %copy-start.2) | copy-done | bytes 163864
  2.7 2.6 %collective-permute-start.5 = (f32[320,128]{1,0:T(8,128)S(1)}, f32[320,128]{1,0:T(8,128)S(1)}, u32[]{:S(2)}, u32[]{:S(2)}) collective-permute-start(f32[320,128]{1,0:T(8,128)S(1)} %shard_map.96.chip_ref), channel_id=1, source_target_pairs={{0,2},{1,3},{2,0},{3,1},{4,6},{5,7},{6,4},{7,5},{8,10},{9,11},{10,... | collective-permute-start | bytes 491528 | tf_op jit(solution)/shard_map/ppermute | solution.py:22
  5.4 0.4 shard_map.97.carry_ref.own_ref
  5.7 1.6 %collective-permute-start.2 = (f32[208,256]{1,0:T(8,128)S(1)}, f32[208,256]{1,0:T(8,128)S(1)}, u32[]{:S(2)}, u32[]{:S(2)}) collective-permute-start(f32[208,256]{1,0:T(8,128)S(1)} %shard_map.97.carry_ref.own_ref), channel_id=1, source_target_pairs={{0,4},{1,5},{2,6},{3,7},{4,0},{5,1},{6,2},{7,3},{8,12},{9,13},{10,... | collective-permute-start | bytes 638984 | tf_op jit(solution)/shard_map/ppermute | solution.py:22
  7.4 0.6 %shard_map.98 = (f32[320,128]{1,0:T(8,128)S(1)}, f32[320,640]{1,0:T(8,128)S(1)}, f32[320,320]{1,0:T(8,128)S(1)}, f32[320,160]{1,0:T(8,128)S(1)}, f32[320,384]{1,0:T(8,128)S(1)}) custom-call(f32[160,640]{1,0:T(8,128)S(1)} %bitcast.11, f32[160,640]{1,0:T(8,128)S(1)} %collective-permute-done.inverse_near_ref, f32[160,384]{1,0:T(8,128)S(1)} %bitcast.13, ...), custom_call_target="tpu_custom_call" | custom-call | tf_op jit(solution)/shard_map/pallas_call | solution.py:75
  8.0 1.1 %shard_map.99 = (f32[320,384]{1,0:T(8,128)S(1)}, f32[160,384]{1,0:T(8,128)S(1)}, f32[128,384]{1,0:T(8,128)S(1)}) custom-call(f32[320,320]{1,0:T(8,128)S(1)} %get-tuple-element.96.far_ref.inverse_far_ref, f32[320,160]{1,0:T(8,128)S(1)} %get-tuple-element.97.mine_ref, f32[320,384]{1,0:T(8,128)S(1)} %get-tuple-element.98.update_ref, ...), custom_call_target="tpu_custom_call" | custom-call | tf_op jit(solution)/shard_map/pallas_call | solution.py:75
  9.1 0.2 shard_map.100.turned_ref
  9.3 0.8 %collective-permute-done.5.far_ref = f32[320,128]{1,0:T(8,128)S(1)} collective-permute-done((f32[320,128]{1,0:T(8,128)S(1)}, f32[320,128]{1,0:T(8,128)S(1)}, u32[]{:S(2)}, u32[]{:S(2)}) %collective-permute-start.5) | collective-permute-done | bytes 163872 | tf_op jit(solution)/shard_map/ppermute | solution.py:22
  10.1 0.4 shard_map.101
  10.5 2.8 %collective-permute-start.8 = (f32[32,512]{1,0:T(8,128)S(1)}, f32[32,512]{1,0:T(8,128)S(1)}, u32[]{:S(2)}, u32[]{:S(2)}) collective-permute-start(f32[32,512]{1,0:T(8,128)S(1)} %get-tuple-element.112), channel_id=1, source_target_pairs={{0,6},{1,7},{2,4},{3,5},{4,2},{5,3},{6,0},{7,1},{8,14},{9,15},{10,... | collective-permute-start | bytes 196616 | tf_op jit(solution)/shard_map/ppermute | solution.py:22
  13.3 0.5 %collective-permute-start.9 = (f32[32,512]{1,0:T(8,128)S(1)}, f32[32,512]{1,0:T(8,128)S(1)}, u32[]{:S(2)}, u32[]{:S(2)}) collective-permute-start(f32[32,512]{1,0:T(8,128)S(1)} %get-tuple-element.113), channel_id=1, source_target_pairs={{0,2},{1,3},{2,0},{3,1},{4,6},{5,7},{6,4},{7,5},{8,10},{9,11},{10,... | collective-permute-start | bytes 196616 | tf_op jit(solution)/shard_map/ppermute | solution.py:22
  13.8 0.2 collective-permute-start.10
  14.1 1.3 %collective-permute-start.6 = (f32[200,256]{1,0:T(8,128)S(1)}, f32[200,256]{1,0:T(8,128)S(1)}, u32[]{:S(2)}, u32[]{:S(2)}) collective-permute-start(f32[200,256]{1,0:T(8,128)S(1)} %get-tuple-element.109.carry_ref), channel_id=1, source_target_pairs={{8,0},{9,1},{10,2},{11,3},{12,4},{13,5},{14,6},{15,7},{24,16},{25,... | collective-permute-start | bytes 614408 | tf_op jit(solution)/shard_map/ppermute | solution.py:34
  15.4 0.1 shard_map.103.hot_ref
  15.6 0.9 %shard_map.104 = (f32[160,256]{1,0:T(8,128)S(1)}, f32[160,640]{1,0:T(8,128)S(1)}) custom-call(f32[320,640]{1,0:T(8,128)S(1)} %get-tuple-element.115.all_ref, f32[320,320]{1,0:T(8,128)S(1)} %get-tuple-element.96.far_ref.inverse_far_ref, f32[320,128]{1,0:T(8,128)S(1)} %get-tuple-element.117.y_ref.own_y_ref, f32[320,128]{1,0:T(8,128)S(1)} %collective-permute-done.5.far_ref, ...), custom_call_target="tpu_custom_call" | custom-call | tf_op jit(solution)/shard_map/pallas_call | solution.py:75
  16.6 1.0 %collective-permute-done.9.far_ref = f32[32,512]{1,0:T(8,128)S(1)} collective-permute-done((f32[32,512]{1,0:T(8,128)S(1)}, f32[32,512]{1,0:T(8,128)S(1)}, u32[]{:S(2)}, u32[]{:S(2)}) %collective-permute-start.9) | collective-permute-done | bytes 65568 | tf_op jit(solution)/shard_map/ppermute | solution.py:22
  17.6 0.5 %collective-permute-done.10.odd_ref = f32[32,512]{1,0:T(8,128)S(1)} collective-permute-done((f32[32,512]{1,0:T(8,128)S(1)}, f32[32,512]{1,0:T(8,128)S(1)}, u32[]{:S(2)}, u32[]{:S(2)}) %collective-permute-start.10) | collective-permute-done | bytes 65568 | tf_op jit(solution)/shard_map/ppermute | solution.py:22
  18.1 0.3 shard_map.105
  18.4 0.2 shard_map.106.up_ref
  18.6 1.6 %collective-permute-start.12 = (f32[32,512]{1,0:T(8,128)S(1)}, f32[32,512]{1,0:T(8,128)S(1)}, u32[]{:S(2)}, u32[]{:S(2)}) collective-permute-start(f32[32,512]{1,0:T(8,128)S(1)} %shard_map.106.up_ref), channel_id=1, source_target_pairs={{0,8},{1,9},{2,10},{3,11},{4,12},{5,13},{6,14},{7,15},{8,0},{9,1},... | collective-permute-start | bytes 196616 | tf_op jit(solution)/shard_map/ppermute | solution.py:22
  20.3 1.3 %collective-permute-start.19 = (f32[160,640]{1,0:T(8,128)S(1)}, f32[160,640]{1,0:T(8,128)S(1)}, u32[]{:S(2)}, u32[]{:S(2)}) collective-permute-start(f32[160,640]{1,0:T(8,128)S(1)} %get-tuple-element.161), channel_id=1, source_target_pairs={{2,0},{3,1},{6,4},{7,5},{10,8},{11,9},{14,12},{15,13},{18,16},{19,... | collective-permute-start | bytes 1228808 | tf_op jit(solution)/shard_map/ppermute | solution.py:22
  21.5 1.2 %collective-permute-done.6.received_ref = f32[200,256]{1,0:T(8,128)S(1)} collective-permute-done((f32[200,256]{1,0:T(8,128)S(1)}, f32[200,256]{1,0:T(8,128)S(1)}, u32[]{:S(2)}, u32[]{:S(2)}) %collective-permute-start.6) | collective-permute-done | bytes 204832 | tf_op jit(solution)/shard_map/ppermute | solution.py:34
  22.8 1.0 %collective-permute-start.11 = (f32[72,256]{1,0:T(8,128)S(1)}, f32[72,256]{1,0:T(8,128)S(1)}, u32[]{:S(2)}, u32[]{:S(2)}) collective-permute-start(f32[72,256]{1,0:T(8,128)S(1)} %get-tuple-element.129.root_ref), channel_id=1, source_target_pairs={{0,8},{1,9},{2,10},{3,11},{4,12},{5,13},{6,14},{7,15},{8,0},{9,1},... | collective-permute-start | bytes 221192 | tf_op jit(solution)/shard_map/ppermute | solution.py:22
  23.8 0.4 %collective-permute-done.13.near_ref = f32[200,256]{1,0:T(8,128)S(1)} collective-permute-done((f32[200,256]{1,0:T(8,128)S(1)}, f32[200,256]{1,0:T(8,128)S(1)}, u32[]{:S(2)}, u32[]{:S(2)}) %collective-permute-start.13) | collective-permute-done | bytes 204832 | tf_op jit(solution)/shard_map/ppermute | solution.py:22
  24.3 0.2 shard_map.109.up_ref
  24.5 2.4 %collective-permute-start.15 = (f32[32,256]{1,0:T(8,128)S(1)}, f32[32,256]{1,0:T(8,128)S(1)}, u32[]{:S(2)}, u32[]{:S(2)}) collective-permute-start(f32[32,256]{1,0:T(8,128)S(1)} %shard_map.109.up_ref), channel_id=1, source_target_pairs={{0,16},{1,17},{2,18},{3,19},{4,20},{5,21},{6,22},{7,23},{8,24},{9,... | collective-permute-start | bytes 98312 | tf_op jit(solution)/shard_map/ppermute | solution.py:22
  26.9 0.4 shard_map.110
  27.3 0.2 collective-permute-done.11.received_ref
  27.5 0.1 collective-permute-start.14
  27.6 0.4 shard_map.112
  28.0 0.4 shard_map.113
  28.3 1.3 %collective-permute-done.15.partner_ref = f32[32,256]{1,0:T(8,128)S(1)} collective-permute-done((f32[32,256]{1,0:T(8,128)S(1)}, f32[32,256]{1,0:T(8,128)S(1)}, u32[]{:S(2)}, u32[]{:S(2)}) %collective-permute-start.15) | collective-permute-done | bytes 32800 | tf_op jit(solution)/shard_map/ppermute | solution.py:22
  29.7 0.7 %shard_map.115 = (f32[32,512]{1,0:T(8,128)S(1)}, f32[32,512]{1,0:T(8,128)S(1)}, f32[32,512]{1,0:T(8,128)S(1)}, f32[32,512]{1,0:T(8,128)S(1)}) custom-call(f32[32,256]{1,0:T(8,128)S(1)} %shard_map.114.residual_ref, f32[72,256]{1,0:T(8,128)S(1)} %shard_map.111.root_ref, f32[72,256]{1,0:T(8,128)S(1)} %collective-permute-done.14.root_near_ref, ...), custom_call_target="tpu_custom_call" | custom-call | tf_op jit(solution)/shard_map/pallas_call | solution.py:75
  30.4 2.5 %collective-permute-start.16 = (f32[32,512]{1,0:T(8,128)S(1)}, f32[32,512]{1,0:T(8,128)S(1)}, u32[]{:S(2)}, u32[]{:S(2)}) collective-permute-start(f32[32,512]{1,0:T(8,128)S(1)} %get-tuple-element.156), channel_id=1, source_target_pairs={{0,6},{1,7},{2,4},{3,5},{4,2},{5,3},{6,0},{7,1},{8,14},{9,15},{10,... | collective-permute-start | bytes 196616 | tf_op jit(solution)/shard_map/ppermute | solution.py:22
  32.9 0.5 %collective-permute-start.17 = (f32[32,512]{1,0:T(8,128)S(1)}, f32[32,512]{1,0:T(8,128)S(1)}, u32[]{:S(2)}, u32[]{:S(2)}) collective-permute-start(f32[32,512]{1,0:T(8,128)S(1)} %get-tuple-element.157), channel_id=1, source_target_pairs={{0,2},{1,3},{2,0},{3,1},{4,6},{5,7},{6,4},{7,5},{8,10},{9,11},{10,... | collective-permute-start | bytes 196616 | tf_op jit(solution)/shard_map/ppermute | solution.py:22
  33.4 0.5 %collective-permute-start.18 = (f32[32,512]{1,0:T(8,128)S(1)}, f32[32,512]{1,0:T(8,128)S(1)}, u32[]{:S(2)}, u32[]{:S(2)}) collective-permute-start(f32[32,512]{1,0:T(8,128)S(1)} %get-tuple-element.158), channel_id=1, source_target_pairs={{0,4},{1,5},{2,6},{3,7},{4,0},{5,1},{6,2},{7,3},{8,12},{9,13},{10,... | collective-permute-start | bytes 196616 | tf_op jit(solution)/shard_map/ppermute | solution.py:22
  34.0 0.1 shard_map.116
  34.0 2.6 %collective-permute-done.16.refs_3_ = f32[32,512]{1,0:T(8,128)S(1)} collective-permute-done((f32[32,512]{1,0:T(8,128)S(1)}, f32[32,512]{1,0:T(8,128)S(1)}, u32[]{:S(2)}, u32[]{:S(2)}) %collective-permute-start.16) | collective-permute-done | bytes 65568 | tf_op jit(solution)/shard_map/ppermute | solution.py:22
  36.6 0.6 %collective-permute-done.17.refs_1_ = f32[32,512]{1,0:T(8,128)S(1)} collective-permute-done((f32[32,512]{1,0:T(8,128)S(1)}, f32[32,512]{1,0:T(8,128)S(1)}, u32[]{:S(2)}, u32[]{:S(2)}) %collective-permute-start.17) | collective-permute-done | bytes 65568 | tf_op jit(solution)/shard_map/ppermute | solution.py:22
  37.2 0.5 %collective-permute-done.18.refs_2_ = f32[32,512]{1,0:T(8,128)S(1)} collective-permute-done((f32[32,512]{1,0:T(8,128)S(1)}, f32[32,512]{1,0:T(8,128)S(1)}, u32[]{:S(2)}, u32[]{:S(2)}) %collective-permute-start.18) | collective-permute-done | bytes 65568 | tf_op jit(solution)/shard_map/ppermute | solution.py:22
  37.8 0.5 %collective-permute-start.21 = (f32[160,128]{1,0:T(8,128)S(1)}, f32[160,128]{1,0:T(8,128)S(1)}, u32[]{:S(2)}, u32[]{:S(2)}) collective-permute-start(f32[160,128]{1,0:T(8,128)S(1)} %get-tuple-element.173), channel_id=1, source_target_pairs={{0,1},{1,0},{2,3},{3,2},{4,5},{5,4},{6,7},{7,6},{8,9},{9,8},{10,11... | collective-permute-start | bytes 245768 | tf_op jit(solution)/shard_map/ppermute | solution.py:22
  38.3 0.3 shard_map.118.ours_ref
  38.7 0.7 %collective-permute-done.20.group_ref = f32[128,512]{1,0:T(8,128)S(1)} collective-permute-done((f32[128,512]{1,0:T(8,128)S(1)}, f32[128,512]{1,0:T(8,128)S(1)}, u32[]{:S(2)}, u32[]{:S(2)}) %collective-permute-start.20) | collective-permute-done | bytes 262176 | tf_op jit(solution)/shard_map/ppermute | solution.py:22
  39.3 0.1 collective-permute-done.21.base_near_ref
  39.5 1.0 %shard_map.119 = (f32[160,256]{1,0:T(8,128)}, f32[64,256]{1,0:T(8,128)}) custom-call(f32[224,512]{1,0:T(8,128)S(1)} %get-tuple-element.165.left_ref, f32[128,512]{1,0:T(8,128)S(1)} %collective-permute-done.20.group_ref, f32[224,128]{1,0:T(8,128)S(1)} %shard_map.118.ours_ref, f32[160,128]{1,0:T(8,128)S(1)} %get-tuple-element.172.base_ref, ...), custom_call_target="tpu_custom_call" | custom-call | tf_op jit(solution)/shard_map/pallas_call | solution.py:75
  (38 shorter events, 0.5 us)
Async XLA Ops:
  0.6 2.0 %copy-start.7 = (s32[1,3]{1,0:T(1,128)S(1)}, s32[1,3]{1,0:T(1,128)}, u32[]{:S(2)}) copy-start(s32[1,3]{1,0:T(1,128)} %param.12) | copy-start | bytes 40
  0.6 2.0 %collective-permute-start.1 = (f32[160,256]{1,0:T(8,128)}, f32[160,256]{1,0:T(8,128)S(1)}, u32[]{:S(2)}, u32[]{:S(2)}) collective-permute-start(f32[160,256]{1,0:T(8,128)} %bitcast.14), channel_id=1, source_target_pairs={{0,1},{1,0},{2,3},{3,2},{4,5},{5,4},{6,7},{7,6},{8,9},{9,8},{10,11... | collective-permute-start | bytes 491528 | tf_op jit(solution)/shard_map/ppermute | solution.py:22
  1.2 6.2 %collective-permute-start.4 = (f32[160,384]{1,0:T(8,128)}, f32[160,384]{1,0:T(8,128)S(1)}, u32[]{:S(2)}, u32[]{:S(2)}) collective-permute-start(f32[160,384]{1,0:T(8,128)} %bitcast.12), channel_id=1, source_target_pairs={{0,1},{1,0},{2,3},{3,2},{4,5},{5,4},{6,7},{7,6},{8,9},{9,8},{10,11... | collective-permute-start | bytes 737288 | tf_op jit(solution)/shard_map/ppermute | solution.py:22
  1.2 1.4 %copy-start.6 = (s32[1,384]{1,0:T(1,128)S(1)}, s32[1,384]{1,0:T(1,128)}, u32[]{:S(2)}) copy-start(s32[1,384]{1,0:T(1,128)} %param.11) | copy-start | bytes 4612
  1.2 6.1 %collective-permute-start = (f32[160,640]{1,0:T(8,128)}, f32[160,640]{1,0:T(8,128)S(1)}, u32[]{:S(2)}, u32[]{:S(2)}) collective-permute-start(f32[160,640]{1,0:T(8,128)} %bitcast.10), channel_id=1, source_target_pairs={{0,1},{1,0},{2,3},{3,2},{4,5},{5,4},{6,7},{7,6},{8,9},{9,8},{10,11... | collective-permute-start | bytes 1228808 | tf_op jit(solution)/shard_map/ppermute | solution.py:22
  1.7 0.9 %copy-start.2 = (f32[1,160,256]{2,1,0:T(8,128)S(1)}, f32[1,160,256]{2,1,0:T(8,128)}, u32[]{:S(2)}) copy-start(f32[1,160,256]{2,1,0:T(8,128)} %param.8) | copy-start | bytes 491524
  2.6 2.8 %copy-start.5 = (f32[1,256,256]{2,1,0:T(8,128)S(1)}, f32[1,256,256]{2,1,0:T(8,128)}, u32[]{:S(2)}) copy-start(f32[1,256,256]{2,1,0:T(8,128)} %param.14) | copy-start | bytes 786436
  2.6 2.7 %copy-start.4 = (f32[1,256,256]{2,1,0:T(8,128)S(1)}, f32[1,256,256]{2,1,0:T(8,128)}, u32[]{:S(2)}) copy-start(f32[1,256,256]{2,1,0:T(8,128)} %param.15) | copy-start | bytes 786436
  2.7 7.4 %collective-permute-start.5 = (f32[320,128]{1,0:T(8,128)S(1)}, f32[320,128]{1,0:T(8,128)S(1)}, u32[]{:S(2)}, u32[]{:S(2)}) collective-permute-start(f32[320,128]{1,0:T(8,128)S(1)} %shard_map.96.chip_ref), channel_id=1, source_target_pairs={{0,2},{1,3},{2,0},{3,1},{4,6},{5,7},{6,4},{7,5},{8,10},{9,11},{10,... | collective-permute-start | bytes 491528 | tf_op jit(solution)/shard_map/ppermute | solution.py:22
  5.3 2.0 %copy-start.3 = (f32[1,64,256]{2,1,0:T(8,128)S(1)}, f32[1,64,256]{2,1,0:T(8,128)}, u32[]{:S(2)}) copy-start(f32[1,64,256]{2,1,0:T(8,128)} %param.13) | copy-start | bytes 196612
  5.3 2.0 %copy-start = (f32[1,160,640]{2,1,0:T(8,128)S(1)}, f32[1,160,640]{2,1,0:T(8,128)}, u32[]{:S(2)}) copy-start(f32[1,160,640]{2,1,0:T(8,128)} %param.9) | copy-start | bytes 1228804
  5.4 2.0 %copy-start.1 = (f32[1,384,160]{1,2,0:T(8,128)S(1)}, f32[1,384,160]{1,2,0:T(8,128)}, u32[]{:S(2)}) copy-start(f32[1,384,160]{1,2,0:T(8,128)} %param.10) | copy-start | bytes 737284
  5.7 8.3 %collective-permute-start.2 = (f32[208,256]{1,0:T(8,128)S(1)}, f32[208,256]{1,0:T(8,128)S(1)}, u32[]{:S(2)}, u32[]{:S(2)}) collective-permute-start(f32[208,256]{1,0:T(8,128)S(1)} %shard_map.97.carry_ref.own_ref), channel_id=1, source_target_pairs={{0,4},{1,5},{2,6},{3,7},{4,0},{5,1},{6,2},{7,3},{8,12},{9,13},{10,... | collective-permute-start | bytes 638984 | tf_op jit(solution)/shard_map/ppermute | solution.py:22
  7.3 1.8 %collective-permute-start.3 = (f32[64,256]{1,0:T(8,128)S(1)}, f32[64,256]{1,0:T(8,128)S(1)}, u32[]{:S(2)}, u32[]{:S(2)}) collective-permute-start(f32[64,256]{1,0:T(8,128)S(1)} %bitcast.16), channel_id=1, source_target_pairs={{0,1},{1,0},{2,3},{3,2},{4,5},{5,4},{6,7},{7,6},{8,9},{9,8},{10,11... | collective-permute-start | bytes 196616 | tf_op jit(solution)/shard_map/ppermute | solution.py:22
  10.5 6.0 %collective-permute-start.8 = (f32[32,512]{1,0:T(8,128)S(1)}, f32[32,512]{1,0:T(8,128)S(1)}, u32[]{:S(2)}, u32[]{:S(2)}) collective-permute-start(f32[32,512]{1,0:T(8,128)S(1)} %get-tuple-element.112), channel_id=1, source_target_pairs={{0,6},{1,7},{2,4},{3,5},{4,2},{5,3},{6,0},{7,1},{8,14},{9,15},{10,... | collective-permute-start | bytes 196616 | tf_op jit(solution)/shard_map/ppermute | solution.py:22
  13.3 4.3 %collective-permute-start.9 = (f32[32,512]{1,0:T(8,128)S(1)}, f32[32,512]{1,0:T(8,128)S(1)}, u32[]{:S(2)}, u32[]{:S(2)}) collective-permute-start(f32[32,512]{1,0:T(8,128)S(1)} %get-tuple-element.113), channel_id=1, source_target_pairs={{0,2},{1,3},{2,0},{3,1},{4,6},{5,7},{6,4},{7,5},{8,10},{9,11},{10,... | collective-permute-start | bytes 196616 | tf_op jit(solution)/shard_map/ppermute | solution.py:22
  13.8 4.3 %collective-permute-start.10 = (f32[32,512]{1,0:T(8,128)S(1)}, f32[32,512]{1,0:T(8,128)S(1)}, u32[]{:S(2)}, u32[]{:S(2)}) collective-permute-start(f32[32,512]{1,0:T(8,128)S(1)} %get-tuple-element.114), channel_id=1, source_target_pairs={{0,4},{1,5},{2,6},{3,7},{4,0},{5,1},{6,2},{7,3},{8,12},{9,13},{10,... | collective-permute-start | bytes 196616 | tf_op jit(solution)/shard_map/ppermute | solution.py:22
  14.1 8.6 %collective-permute-start.6 = (f32[200,256]{1,0:T(8,128)S(1)}, f32[200,256]{1,0:T(8,128)S(1)}, u32[]{:S(2)}, u32[]{:S(2)}) collective-permute-start(f32[200,256]{1,0:T(8,128)S(1)} %get-tuple-element.109.carry_ref), channel_id=1, source_target_pairs={{8,0},{9,1},{10,2},{11,3},{12,4},{13,5},{14,6},{15,7},{24,16},{25,... | collective-permute-start | bytes 614408 | tf_op jit(solution)/shard_map/ppermute | solution.py:34
  15.5 2.8 %collective-permute-start.7 = (f32[200,256]{1,0:T(8,128)S(1)}, f32[200,256]{1,0:T(8,128)S(1)}, u32[]{:S(2)}, u32[]{:S(2)}) collective-permute-start(f32[200,256]{1,0:T(8,128)S(1)} %get-tuple-element.110.half_ref), channel_id=1, source_target_pairs={{0,1},{1,0},{2,3},{3,2},{4,5},{5,4},{6,7},{7,6},{8,9},{9,8},{10,11... | collective-permute-start | bytes 614408 | tf_op jit(solution)/shard_map/ppermute | solution.py:22
  18.6 5.2 %collective-permute-start.12 = (f32[32,512]{1,0:T(8,128)S(1)}, f32[32,512]{1,0:T(8,128)S(1)}, u32[]{:S(2)}, u32[]{:S(2)}) collective-permute-start(f32[32,512]{1,0:T(8,128)S(1)} %shard_map.106.up_ref), channel_id=1, source_target_pairs={{0,8},{1,9},{2,10},{3,11},{4,12},{5,13},{6,14},{7,15},{8,0},{9,1},... | collective-permute-start | bytes 196616 | tf_op jit(solution)/shard_map/ppermute | solution.py:22
  20.3 13.7 %collective-permute-start.19 = (f32[160,640]{1,0:T(8,128)S(1)}, f32[160,640]{1,0:T(8,128)S(1)}, u32[]{:S(2)}, u32[]{:S(2)}) collective-permute-start(f32[160,640]{1,0:T(8,128)S(1)} %get-tuple-element.161), channel_id=1, source_target_pairs={{2,0},{3,1},{6,4},{7,5},{10,8},{11,9},{14,12},{15,13},{18,16},{19,... | collective-permute-start | bytes 1228808 | tf_op jit(solution)/shard_map/ppermute | solution.py:22
  22.7 1.5 %collective-permute-start.13 = (f32[200,256]{1,0:T(8,128)S(1)}, f32[200,256]{1,0:T(8,128)S(1)}, u32[]{:S(2)}, u32[]{:S(2)}) collective-permute-start(f32[200,256]{1,0:T(8,128)S(1)} %get-tuple-element.132.half_ref), channel_id=1, source_target_pairs={{0,1},{1,0},{2,3},{3,2},{4,5},{5,4},{6,7},{7,6},{8,9},{9,8},{10,11... | collective-permute-start | bytes 614408 | tf_op jit(solution)/shard_map/ppermute | solution.py:22
  22.8 4.7 %collective-permute-start.11 = (f32[72,256]{1,0:T(8,128)S(1)}, f32[72,256]{1,0:T(8,128)S(1)}, u32[]{:S(2)}, u32[]{:S(2)}) collective-permute-start(f32[72,256]{1,0:T(8,128)S(1)} %get-tuple-element.129.root_ref), channel_id=1, source_target_pairs={{0,8},{1,9},{2,10},{3,11},{4,12},{5,13},{6,14},{7,15},{8,0},{9,1},... | collective-permute-start | bytes 221192 | tf_op jit(solution)/shard_map/ppermute | solution.py:22
  24.5 5.2 %collective-permute-start.15 = (f32[32,256]{1,0:T(8,128)S(1)}, f32[32,256]{1,0:T(8,128)S(1)}, u32[]{:S(2)}, u32[]{:S(2)}) collective-permute-start(f32[32,256]{1,0:T(8,128)S(1)} %shard_map.109.up_ref), channel_id=1, source_target_pairs={{0,16},{1,17},{2,18},{3,19},{4,20},{5,21},{6,22},{7,23},{8,24},{9,... | collective-permute-start | bytes 98312 | tf_op jit(solution)/shard_map/ppermute | solution.py:22
  27.5 2.1 %collective-permute-start.14 = (f32[72,256]{1,0:T(8,128)S(1)}, f32[72,256]{1,0:T(8,128)S(1)}, u32[]{:S(2)}, u32[]{:S(2)}) collective-permute-start(f32[72,256]{1,0:T(8,128)S(1)} %shard_map.111.root_ref), channel_id=1, source_target_pairs={{0,1},{1,0},{2,3},{3,2},{4,5},{5,4},{6,7},{7,6},{8,9},{9,8},{10,11... | collective-permute-start | bytes 221192 | tf_op jit(solution)/shard_map/ppermute | solution.py:22
  30.4 6.2 %collective-permute-start.16 = (f32[32,512]{1,0:T(8,128)S(1)}, f32[32,512]{1,0:T(8,128)S(1)}, u32[]{:S(2)}, u32[]{:S(2)}) collective-permute-start(f32[32,512]{1,0:T(8,128)S(1)} %get-tuple-element.156), channel_id=1, source_target_pairs={{0,6},{1,7},{2,4},{3,5},{4,2},{5,3},{6,0},{7,1},{8,14},{9,15},{10,... | collective-permute-start | bytes 196616 | tf_op jit(solution)/shard_map/ppermute | solution.py:22
  32.9 4.3 %collective-permute-start.17 = (f32[32,512]{1,0:T(8,128)S(1)}, f32[32,512]{1,0:T(8,128)S(1)}, u32[]{:S(2)}, u32[]{:S(2)}) collective-permute-start(f32[32,512]{1,0:T(8,128)S(1)} %get-tuple-element.157), channel_id=1, source_target_pairs={{0,2},{1,3},{2,0},{3,1},{4,6},{5,7},{6,4},{7,5},{8,10},{9,11},{10,... | collective-permute-start | bytes 196616 | tf_op jit(solution)/shard_map/ppermute | solution.py:22
  33.4 4.3 %collective-permute-start.18 = (f32[32,512]{1,0:T(8,128)S(1)}, f32[32,512]{1,0:T(8,128)S(1)}, u32[]{:S(2)}, u32[]{:S(2)}) collective-permute-start(f32[32,512]{1,0:T(8,128)S(1)} %get-tuple-element.158), channel_id=1, source_target_pairs={{0,4},{1,5},{2,6},{3,7},{4,0},{5,1},{6,2},{7,3},{8,12},{9,13},{10,... | collective-permute-start | bytes 196616 | tf_op jit(solution)/shard_map/ppermute | solution.py:22
  37.7 1.6 %collective-permute-start.20 = (f32[128,512]{1,0:T(8,128)S(1)}, f32[128,512]{1,0:T(8,128)S(1)}, u32[]{:S(2)}, u32[]{:S(2)}) collective-permute-start(f32[128,512]{1,0:T(8,128)S(1)} %shard_map.117.group_ref), channel_id=1, source_target_pairs={{0,1},{1,0},{2,3},{3,2},{4,5},{5,4},{6,7},{7,6},{8,9},{9,8},{10,11... | collective-permute-start | bytes 786440 | tf_op jit(solution)/shard_map/ppermute | solution.py:22
  37.8 1.6 %collective-permute-start.21 = (f32[160,128]{1,0:T(8,128)S(1)}, f32[160,128]{1,0:T(8,128)S(1)}, u32[]{:S(2)}, u32[]{:S(2)}) collective-permute-start(f32[160,128]{1,0:T(8,128)S(1)} %get-tuple-element.173), channel_id=1, source_target_pairs={{0,1},{1,0},{2,3},{3,2},{4,5},{5,4},{6,7},{7,6},{8,9},{9,8},{10,11... | collective-permute-start | bytes 245768 | tf_op jit(solution)/shard_map/ppermute | solution.py:22

commit v10 on v9

--- a/solution.py
+++ b/solution.py
@@ -181,7 +181,7 @@
         cost=3 * medium,
     )
 
-    def own_part(inverse_ref, inverse_near_ref, update_ref, update_near_ref, chip_ref, y_ref, all_ref, far_ref, mine_ref, update_out_ref):
+    def own_part(inverse_ref, inverse_near_ref, update_ref, update_near_ref, chip_ref, y_ref, block_ref, far_ref, mine_ref, update_out_ref, all_ref):
         _, _, _, far_bit, near_bit = place()
         own, other = at(near_bit, rows), at(1 - near_bit, rows)
         all_ref[own] = inverse_ref[...]
@@ -193,18 +193,20 @@
         far_ref[...] = by_bit(far_bit, second, first)
         y_ref[...] = dot3(by_bit(far_bit, first, second), chip_ref[...])
         chip_block = by_bit(far_bit, first, second)
+        block_ref[...] = chip_block
         mine_ref[...] = by_bit(near_bit, chip_block[:, :rows], chip_block[:, rows:])
 
     received = swap(payload, 1, 0)
     inverse_near, payload = after(inverse_near, payload)
-    own_y, inverse_all, inverse_far, inverse_mine, update_all = stage(
+    own_y, inverse_chip, inverse_far, inverse_mine, update_all = stage(
         own_part,
-        [(2 * rows, half), (2 * rows, size), (2 * rows, 2 * rows), (2 * rows, rows), (2 * rows, updates)],
+        [(2 * rows, half), (2 * rows, 2 * rows), (2 * rows, 2 * rows), (2 * rows, rows), (2 * rows, updates)],
         inverse,
         inverse_near,
         update,
         update_near,
         chip,
+        scratch=[(2 * rows, size)],
     )
 
     def turned_update(far_ref, mine_ref, update_ref, y_ref, turned_far_ref, turned_mine_ref, terms_ref):
@@ -302,29 +304,26 @@
         one_hots, [jax.ShapeDtypeStruct((depth, order, 2 * capacity), bf16)], payload, received
     )
 
-    def transposed(all_ref, inverse_far_ref, own_y_ref, far_ref, turned_far_ref, own_ref, out_ref, work):
-        _, _, _, far_bit, near_bit = place()
-        leaf_y = own_y_ref[...] + dot3(inverse_far_ref[...], far_ref[...])
-        work[...] = dot3(all_ref[...], leaf_y, 0, 0)
+    def transposed(inverse_far_ref, own_y_ref, far_ref, turned_far_ref, y_ref, out_ref):
+        near_bit = place()[4]
+        inverse_far = inverse_far_ref[...]
+        leaf_y = own_y_ref[...] + dot3(inverse_far, far_ref[...])
+        y_ref[...] = leaf_y
+        turned_y = dot3(inverse_far, leaf_y, 0, 0)
         out_ref[:, :updates] = turned_far_ref[at(near_bit, rows)]
-        for index in range(2):
-            part = slice(index * half, (index + 1) * half)
-            shifted = slice(updates + index * half, updates + (index + 1) * half)
-            own_ref[:, part] = work[at(2 * far_bit + index, rows)]
-            out_ref[:, shifted] = work[at(2 - 2 * far_bit + index, rows)]
+        out_ref[:, updates : updates + half] = turned_y[:rows]
+        out_ref[:, updates + half :] = turned_y[rows:]
 
     own_y, hots = after(own_y, hots)
-    own_ys, far_sum = stage(
+    leaf_y, far_sum = stage(
         transposed,
-        [(rows, columns), (rows, updates + columns)],
-        inverse_all,
+        [(2 * rows, half), (rows, updates + columns)],
         inverse_far,
         own_y,
         far,
         turned_far,
-        scratch=[(size, half)],
-    )
-    by_both, by_far, by_odd, own_ys = after(by_both, by_far, by_odd, own_ys)
+    )
+    by_both, by_far, by_odd, leaf_y = after(by_both, by_far, by_odd, leaf_y)
 
     def gathered_part(mine_ref, far_ref, odd_ref, both_ref, hot_ref, residual_ref, up_ref):
         leaf, _, odd, far_bit, _ = place()
@@ -522,21 +521,22 @@
     beyond = swap(to_far, 0, 2)
     side = swap(to_odd, 1, 0)
 
-    def last_left(own_ref, own_y_ref, far_ref, left_ref, keep_ref, pass_ref):
+    def last_left(own_ref, chip_ref, y_ref, far_ref, left_ref, keep_ref, pass_ref):
         near_bit = place()[4]
         left_ref[:rows, :updates] = -(own_ref[...] + far_ref[:, :updates])
         left_ref[:rows, updates:] = jnp.zeros((rows, 2 * quarter), f32)
         row = lax.broadcasted_iota(jnp.int32, (quarter, width), 0)
         lane = lax.broadcasted_iota(jnp.int32, (quarter, width), 1)
         left_ref[rows:] = jnp.where(lane == updates + near_bit * quarter + row, 1.0, 0.0)
-        total = own_y_ref[...] + far_ref[:, updates:]
-        first, second = total[:, :half], total[:, half:]
+        turned_y = dot3(chip_ref[...], y_ref[...], 0, 0)
+        first = turned_y[:rows] + far_ref[:, updates : updates + half]
+        second = turned_y[rows:] + far_ref[:, updates + half :]
         keep_ref[...] = by_bit(near_bit, first, second)
         pass_ref[...] = by_bit(near_bit, second, first)
 
     from_far, stay = after(from_far, stay)
     left, base_keep, base_pass = stage(
-        last_left, [(rows + quarter, width), (rows, half), (rows, half)], own_sum, own_ys, from_far
+        last_left, [(rows + quarter, width), (rows, half), (rows, half)], own_sum, inverse_chip, leaf_y, from_far
     )
     both, beyond, side, left = after(both, beyond, side, left)
 

time: 40.7 us -> 40.9 us (level)
  starting transfers between devices: 20.8 us -> 22.4 us
  waiting for transfers between devices: 9.93 us -> 8.45 us
    ppermute x21, starting transfers between devices: 19.5 us -> 21.1 us  [swap(): return lax.ppermute(payload, axes, pairs)]
    ppermute x1, waiting for transfers between devices: 1.17 us -> 0.34 us  [quarter_swap(): return lax.ppermute(payload, axes, pairs)]
    ppermute x21, waiting for transfers between devices: 8.76 us -> 8.1 us  [swap(): return lax.ppermute(payload, axes, pairs)]
  transfers between devices with their start and end apart: 22 -> 22, of which waited for: 12 -> 11; matrix products, arithmetic and copies ran while one was open for 0% -> 0% of each run, Pallas kernels for 17% -> 17%
where the time goes in v10:
time: 40.9 us; the launch traced here: 40.7 us
  starting transfers between devices  22.4 us (55%)
  waiting for transfers between devices  8.45 us (21%)
  Pallas kernels  7.93 us (19%)
  local copies, waits for them, and re-layouts  0.95 us (2%)
  between operations  0.94 us (2%)
    ppermute x21, starting transfers between devices, swap(): return lax.ppermute(payload, axes, pairs)  21.1 us
    ppermute x21, waiting for transfers between devices, swap(): return lax.ppermute(payload, axes, pairs)  8.1 us
    pallas_call x25, Pallas kernels, stage(): pl.pallas_call(body, out_shape=[jax.ShapeDtypeStruct(shape, f32) if isins...  7.93 us
    ppermute x1, starting transfers between devices, quarter_swap(): return lax.ppermute(payload, axes, pairs)  1.29 us
    unnamed x16, local copies, waits for them, and re-layouts  0.95 us
  transfers between devices with their start and end apart: 22, of which 11 were waited for; matrix products, arithmetic and copies ran while one was open for 0% of the time, Pallas kernels for 17%

profile of v10, /device:TPU:0, one launch (start us, length us, event | category | flops | bytes accessed | tf_op | source)
XLA Modules:
  0.0 40.7 jit_solution(13104118426418610115)
XLA Ops:
  0.6 0.5 %collective-permute-start.1 = (f32[160,256]{1,0:T(8,128)}, f32[160,256]{1,0:T(8,128)S(1)}, u32[]{:S(2)}, u32[]{:S(2)}) collective-permute-start(f32[160,256]{1,0:T(8,128)} %bitcast.14), channel_id=1, source_target_pairs={{0,1},{1,0},{2,3},{3,2},{4,5},{5,4},{6,7},{7,6},{8,9},{9,8},{10,11... | collective-permute-start | bytes 491528 | tf_op jit(solution)/shard_map/ppermute | solution.py:22
  1.2 0.1 collective-permute-start.4
  1.2 0.4 %collective-permute-start = (f32[160,640]{1,0:T(8,128)}, f32[160,640]{1,0:T(8,128)S(1)}, u32[]{:S(2)}, u32[]{:S(2)}) collective-permute-start(f32[160,640]{1,0:T(8,128)} %bitcast.10), channel_id=1, source_target_pairs={{0,1},{1,0},{2,3},{3,2},{4,5},{5,4},{6,7},{7,6},{8,9},{9,8},{10,11... | collective-permute-start | bytes 1228808 | tf_op jit(solution)/shard_map/ppermute | solution.py:22
  1.7 0.9 %copy-done.2 = f32[1,160,256]{2,1,0:T(8,128)S(1)} copy-done((f32[1,160,256]{2,1,0:T(8,128)S(1)}, f32[1,160,256]{2,1,0:T(8,128)}, u32[]{:S(2)}) %copy-start.2) | copy-done | bytes 163864
  2.7 2.6 %collective-permute-start.5 = (f32[320,128]{1,0:T(8,128)S(1)}, f32[320,128]{1,0:T(8,128)S(1)}, u32[]{:S(2)}, u32[]{:S(2)}) collective-permute-start(f32[320,128]{1,0:T(8,128)S(1)} %shard_map.96.chip_ref), channel_id=1, source_target_pairs={{0,2},{1,3},{2,0},{3,1},{4,6},{5,7},{6,4},{7,5},{8,10},{9,11},{10,... | collective-permute-start | bytes 491528 | tf_op jit(solution)/shard_map/ppermute | solution.py:22
  5.4 0.4 shard_map.97.carry_ref.own_ref
  5.7 1.6 %collective-permute-start.2 = (f32[208,256]{1,0:T(8,128)S(1)}, f32[208,256]{1,0:T(8,128)S(1)}, u32[]{:S(2)}, u32[]{:S(2)}) collective-permute-start(f32[208,256]{1,0:T(8,128)S(1)} %shard_map.97.carry_ref.own_ref), channel_id=1, source_target_pairs={{0,4},{1,5},{2,6},{3,7},{4,0},{5,1},{6,2},{7,3},{8,12},{9,13},{10,... | collective-permute-start | bytes 638984 | tf_op jit(solution)/shard_map/ppermute | solution.py:22
  7.4 0.6 %shard_map.98 = (f32[320,128]{1,0:T(8,128)S(1)}, f32[320,320]{1,0:T(8,128)S(1)}, f32[320,320]{1,0:T(8,128)S(1)}, f32[320,160]{1,0:T(8,128)S(1)}, f32[320,384]{1,0:T(8,128)S(1)}) custom-call(f32[160,640]{1,0:T(8,128)S(1)} %bitcast.11, f32[160,640]{1,0:T(8,128)S(1)} %collective-permute-done.inverse_near_ref, f32[160,384]{1,0:T(8,128)S(1)} %bitcast.13, ...), custom_call_target="tpu_custom_call" | custom-call | tf_op jit(solution)/shard_map/pallas_call | solution.py:75
  8.0 1.1 %shard_map.99 = (f32[320,384]{1,0:T(8,128)S(1)}, f32[160,384]{1,0:T(8,128)S(1)}, f32[128,384]{1,0:T(8,128)S(1)}) custom-call(f32[320,320]{1,0:T(8,128)S(1)} %get-tuple-element.96.far_ref.inverse_far_ref, f32[320,160]{1,0:T(8,128)S(1)} %get-tuple-element.97.mine_ref, f32[320,384]{1,0:T(8,128)S(1)} %get-tuple-element.98.update_ref, ...), custom_call_target="tpu_custom_call" | custom-call | tf_op jit(solution)/shard_map/pallas_call | solution.py:75
  9.1 0.2 shard_map.100.turned_ref
  9.3 0.8 %collective-permute-done.5.far_ref = f32[320,128]{1,0:T(8,128)S(1)} collective-permute-done((f32[320,128]{1,0:T(8,128)S(1)}, f32[320,128]{1,0:T(8,128)S(1)}, u32[]{:S(2)}, u32[]{:S(2)}) %collective-permute-start.5) | collective-permute-done | bytes 163872 | tf_op jit(solution)/shard_map/ppermute | solution.py:22
  10.1 0.4 shard_map.101
  10.5 2.8 %collective-permute-start.8 = (f32[32,512]{1,0:T(8,128)S(1)}, f32[32,512]{1,0:T(8,128)S(1)}, u32[]{:S(2)}, u32[]{:S(2)}) collective-permute-start(f32[32,512]{1,0:T(8,128)S(1)} %get-tuple-element.112), channel_id=1, source_target_pairs={{0,6},{1,7},{2,4},{3,5},{4,2},{5,3},{6,0},{7,1},{8,14},{9,15},{10,... | collective-permute-start | bytes 196616 | tf_op jit(solution)/shard_map/ppermute | solution.py:22
  13.3 0.5 %collective-permute-start.9 = (f32[32,512]{1,0:T(8,128)S(1)}, f32[32,512]{1,0:T(8,128)S(1)}, u32[]{:S(2)}, u32[]{:S(2)}) collective-permute-start(f32[32,512]{1,0:T(8,128)S(1)} %get-tuple-element.113), channel_id=1, source_target_pairs={{0,2},{1,3},{2,0},{3,1},{4,6},{5,7},{6,4},{7,5},{8,10},{9,11},{10,... | collective-permute-start | bytes 196616 | tf_op jit(solution)/shard_map/ppermute | solution.py:22
  13.8 0.2 collective-permute-start.10
  14.1 1.3 %collective-permute-start.6 = (f32[200,256]{1,0:T(8,128)S(1)}, f32[200,256]{1,0:T(8,128)S(1)}, u32[]{:S(2)}, u32[]{:S(2)}) collective-permute-start(f32[200,256]{1,0:T(8,128)S(1)} %get-tuple-element.109.carry_ref), channel_id=1, source_target_pairs={{8,0},{9,1},{10,2},{11,3},{12,4},{13,5},{14,6},{15,7},{24,16},{25,... | collective-permute-start | bytes 614408 | tf_op jit(solution)/shard_map/ppermute | solution.py:34
  15.4 0.1 shard_map.103.hot_ref
  15.5 0.7 %shard_map.104 = (f32[320,128]{1,0:T(8,128)S(1)}, f32[160,640]{1,0:T(8,128)S(1)}) custom-call(f32[320,320]{1,0:T(8,128)S(1)} %get-tuple-element.96.far_ref.inverse_far_ref, f32[320,128]{1,0:T(8,128)S(1)} %get-tuple-element.116.y_ref.own_y_ref, f32[320,128]{1,0:T(8,128)S(1)} %collective-permute-done.5.far_ref, f32[320,384]{1,0:T(8,128)S(1)} %get-tuple-element.102.turned_far_ref), custom_call_target="tpu_custom_call" | custom-call | tf_op jit(solution)/shard_map/pallas_call | solution.py:75
  16.2 0.1 collective-permute-start.7
  16.3 1.3 %collective-permute-done.9.far_ref = f32[32,512]{1,0:T(8,128)S(1)} collective-permute-done((f32[32,512]{1,0:T(8,128)S(1)}, f32[32,512]{1,0:T(8,128)S(1)}, u32[]{:S(2)}, u32[]{:S(2)}) %collective-permute-start.9) | collective-permute-done | bytes 65568 | tf_op jit(solution)/shard_map/ppermute | solution.py:22
  17.6 0.5 %collective-permute-done.10.odd_ref = f32[32,512]{1,0:T(8,128)S(1)} collective-permute-done((f32[32,512]{1,0:T(8,128)S(1)}, f32[32,512]{1,0:T(8,128)S(1)}, u32[]{:S(2)}, u32[]{:S(2)}) %collective-permute-start.10) | collective-permute-done | bytes 65568 | tf_op jit(solution)/shard_map/ppermute | solution.py:22
  18.1 0.3 shard_map.105
  18.4 0.2 shard_map.106.up_ref
  18.6 2.1 %collective-permute-start.12 = (f32[32,512]{1,0:T(8,128)S(1)}, f32[32,512]{1,0:T(8,128)S(1)}, u32[]{:S(2)}, u32[]{:S(2)}) collective-permute-start(f32[32,512]{1,0:T(8,128)S(1)} %shard_map.106.up_ref), channel_id=1, source_target_pairs={{0,8},{1,9},{2,10},{3,11},{4,12},{5,13},{6,14},{7,15},{8,0},{9,1},... | collective-permute-start | bytes 196616 | tf_op jit(solution)/shard_map/ppermute | solution.py:22
  20.7 1.3 %collective-permute-start.19 = (f32[160,640]{1,0:T(8,128)S(1)}, f32[160,640]{1,0:T(8,128)S(1)}, u32[]{:S(2)}, u32[]{:S(2)}) collective-permute-start(f32[160,640]{1,0:T(8,128)S(1)} %get-tuple-element.161), channel_id=1, source_target_pairs={{2,0},{3,1},{6,4},{7,5},{10,8},{11,9},{14,12},{15,13},{18,16},{19,... | collective-permute-start | bytes 1228808 | tf_op jit(solution)/shard_map/ppermute | solution.py:22
  21.9 0.3 collective-permute-done.6.received_ref
  22.3 0.1 collective-permute-start.13
  22.4 1.4 %collective-permute-start.11 = (f32[72,256]{1,0:T(8,128)S(1)}, f32[72,256]{1,0:T(8,128)S(1)}, u32[]{:S(2)}, u32[]{:S(2)}) collective-permute-start(f32[72,256]{1,0:T(8,128)S(1)} %get-tuple-element.128.root_ref), channel_id=1, source_target_pairs={{0,8},{1,9},{2,10},{3,11},{4,12},{5,13},{6,14},{7,15},{8,0},{9,1},... | collective-permute-start | bytes 221192 | tf_op jit(solution)/shard_map/ppermute | solution.py:22
  23.9 0.2 shard_map.109.up_ref
  24.1 2.6 %collective-permute-start.15 = (f32[32,256]{1,0:T(8,128)S(1)}, f32[32,256]{1,0:T(8,128)S(1)}, u32[]{:S(2)}, u32[]{:S(2)}) collective-permute-start(f32[32,256]{1,0:T(8,128)S(1)} %shard_map.109.up_ref), channel_id=1, source_target_pairs={{0,16},{1,17},{2,18},{3,19},{4,20},{5,21},{6,22},{7,23},{8,24},{9,... | collective-permute-start | bytes 98312 | tf_op jit(solution)/shard_map/ppermute | solution.py:22
  26.7 0.4 shard_map.110
  27.1 0.1 collective-permute-start.14
  27.2 0.4 shard_map.112
  27.6 0.4 shard_map.113
  27.9 1.4 %collective-permute-done.15.partner_ref = f32[32,256]{1,0:T(8,128)S(1)} collective-permute-done((f32[32,256]{1,0:T(8,128)S(1)}, f32[32,256]{1,0:T(8,128)S(1)}, u32[]{:S(2)}, u32[]{:S(2)}) %collective-permute-start.15) | collective-permute-done | bytes 32800 | tf_op jit(solution)/shard_map/ppermute | solution.py:22
  29.3 0.7 %shard_map.115 = (f32[32,512]{1,0:T(8,128)S(1)}, f32[32,512]{1,0:T(8,128)S(1)}, f32[32,512]{1,0:T(8,128)S(1)}, f32[32,512]{1,0:T(8,128)S(1)}) custom-call(f32[32,256]{1,0:T(8,128)S(1)} %shard_map.114.residual_ref, f32[72,256]{1,0:T(8,128)S(1)} %shard_map.111.root_ref, f32[72,256]{1,0:T(8,128)S(1)} %collective-permute-done.14.root_near_ref, ...), custom_call_target="tpu_custom_call" | custom-call | tf_op jit(solution)/shard_map/pallas_call | solution.py:75
  30.1 3.5 %collective-permute-start.16 = (f32[32,512]{1,0:T(8,128)S(1)}, f32[32,512]{1,0:T(8,128)S(1)}, u32[]{:S(2)}, u32[]{:S(2)}) collective-permute-start(f32[32,512]{1,0:T(8,128)S(1)} %get-tuple-element.155), channel_id=1, source_target_pairs={{0,6},{1,7},{2,4},{3,5},{4,2},{5,3},{6,0},{7,1},{8,14},{9,15},{10,... | collective-permute-start | bytes 196616 | tf_op jit(solution)/shard_map/ppermute | solution.py:22
  33.6 0.6 %collective-permute-start.18 = (f32[32,512]{1,0:T(8,128)S(1)}, f32[32,512]{1,0:T(8,128)S(1)}, u32[]{:S(2)}, u32[]{:S(2)}) collective-permute-start(f32[32,512]{1,0:T(8,128)S(1)} %get-tuple-element.157), channel_id=1, source_target_pairs={{0,4},{1,5},{2,6},{3,7},{4,0},{5,1},{6,2},{7,3},{8,12},{9,13},{10,... | collective-permute-start | bytes 196616 | tf_op jit(solution)/shard_map/ppermute | solution.py:22
  34.3 0.2 collective-permute-done.19.far_ref
  34.5 0.4 shard_map.116
  34.9 2.2 %collective-permute-done.16.refs_3_ = f32[32,512]{1,0:T(8,128)S(1)} collective-permute-done((f32[32,512]{1,0:T(8,128)S(1)}, f32[32,512]{1,0:T(8,128)S(1)}, u32[]{:S(2)}, u32[]{:S(2)}) %collective-permute-start.16) | collective-permute-done | bytes 65568 | tf_op jit(solution)/shard_map/ppermute | solution.py:22
  37.1 0.8 %collective-permute-done.17.refs_1_ = f32[32,512]{1,0:T(8,128)S(1)} collective-permute-done((f32[32,512]{1,0:T(8,128)S(1)}, f32[32,512]{1,0:T(8,128)S(1)}, u32[]{:S(2)}, u32[]{:S(2)}) %collective-permute-start.17) | collective-permute-done | bytes 65568 | tf_op jit(solution)/shard_map/ppermute | solution.py:22
  37.9 0.1 collective-permute-start.20
  38.0 0.5 %collective-permute-start.21 = (f32[160,128]{1,0:T(8,128)S(1)}, f32[160,128]{1,0:T(8,128)S(1)}, u32[]{:S(2)}, u32[]{:S(2)}) collective-permute-start(f32[160,128]{1,0:T(8,128)S(1)} %get-tuple-element.173), channel_id=1, source_target_pairs={{0,1},{1,0},{2,3},{3,2},{4,5},{5,4},{6,7},{7,6},{8,9},{9,8},{10,11... | collective-permute-start | bytes 245768 | tf_op jit(solution)/shard_map/ppermute | solution.py:22
  38.5 0.4 shard_map.118.ours_ref
  38.9 0.7 %collective-permute-done.20.group_ref = f32[128,512]{1,0:T(8,128)S(1)} collective-permute-done((f32[128,512]{1,0:T(8,128)S(1)}, f32[128,512]{1,0:T(8,128)S(1)}, u32[]{:S(2)}, u32[]{:S(2)}) %collective-permute-start.20) | collective-permute-done | bytes 262176 | tf_op jit(solution)/shard_map/ppermute | solution.py:22
  39.5 0.1 collective-permute-done.21.base_near_ref
  39.6 1.0 %shard_map.119 = (f32[160,256]{1,0:T(8,128)}, f32[64,256]{1,0:T(8,128)}) custom-call(f32[224,512]{1,0:T(8,128)S(1)} %get-tuple-element.165.left_ref, f32[128,512]{1,0:T(8,128)S(1)} %collective-permute-done.20.group_ref, f32[224,128]{1,0:T(8,128)S(1)} %shard_map.118.ours_ref, f32[160,128]{1,0:T(8,128)S(1)} %get-tuple-element.172.base_ref, ...), custom_call_target="tpu_custom_call" | custom-call | tf_op jit(solution)/shard_map/pallas_call | solution.py:75
  (38 shorter events, 0.3 us)
Async XLA Ops:
  0.6 2.0 %copy-start.7 = (s32[1,3]{1,0:T(1,128)S(1)}, s32[1,3]{1,0:T(1,128)}, u32[]{:S(2)}) copy-start(s32[1,3]{1,0:T(1,128)} %param.12) | copy-start | bytes 40
  0.6 2.0 %collective-permute-start.1 = (f32[160,256]{1,0:T(8,128)}, f32[160,256]{1,0:T(8,128)S(1)}, u32[]{:S(2)}, u32[]{:S(2)}) collective-permute-start(f32[160,256]{1,0:T(8,128)} %bitcast.14), channel_id=1, source_target_pairs={{0,1},{1,0},{2,3},{3,2},{4,5},{5,4},{6,7},{7,6},{8,9},{9,8},{10,11... | collective-permute-start | bytes 491528 | tf_op jit(solution)/shard_map/ppermute | solution.py:22
  1.2 6.2 %collective-permute-start.4 = (f32[160,384]{1,0:T(8,128)}, f32[160,384]{1,0:T(8,128)S(1)}, u32[]{:S(2)}, u32[]{:S(2)}) collective-permute-start(f32[160,384]{1,0:T(8,128)} %bitcast.12), channel_id=1, source_target_pairs={{0,1},{1,0},{2,3},{3,2},{4,5},{5,4},{6,7},{7,6},{8,9},{9,8},{10,11... | collective-permute-start | bytes 737288 | tf_op jit(solution)/shard_map/ppermute | solution.py:22
  1.2 1.4 %copy-start.6 = (s32[1,384]{1,0:T(1,128)S(1)}, s32[1,384]{1,0:T(1,128)}, u32[]{:S(2)}) copy-start(s32[1,384]{1,0:T(1,128)} %param.11) | copy-start | bytes 4612
  1.2 6.1 %collective-permute-start = (f32[160,640]{1,0:T(8,128)}, f32[160,640]{1,0:T(8,128)S(1)}, u32[]{:S(2)}, u32[]{:S(2)}) collective-permute-start(f32[160,640]{1,0:T(8,128)} %bitcast.10), channel_id=1, source_target_pairs={{0,1},{1,0},{2,3},{3,2},{4,5},{5,4},{6,7},{7,6},{8,9},{9,8},{10,11... | collective-permute-start | bytes 1228808 | tf_op jit(solution)/shard_map/ppermute | solution.py:22
  1.7 0.9 %copy-start.2 = (f32[1,160,256]{2,1,0:T(8,128)S(1)}, f32[1,160,256]{2,1,0:T(8,128)}, u32[]{:S(2)}) copy-start(f32[1,160,256]{2,1,0:T(8,128)} %param.8) | copy-start | bytes 491524
  2.6 2.8 %copy-start.5 = (f32[1,256,256]{2,1,0:T(8,128)S(1)}, f32[1,256,256]{2,1,0:T(8,128)}, u32[]{:S(2)}) copy-start(f32[1,256,256]{2,1,0:T(8,128)} %param.14) | copy-start | bytes 786436
  2.6 2.7 %copy-start.4 = (f32[1,256,256]{2,1,0:T(8,128)S(1)}, f32[1,256,256]{2,1,0:T(8,128)}, u32[]{:S(2)}) copy-start(f32[1,256,256]{2,1,0:T(8,128)} %param.15) | copy-start | bytes 786436
  2.7 7.4 %collective-permute-start.5 = (f32[320,128]{1,0:T(8,128)S(1)}, f32[320,128]{1,0:T(8,128)S(1)}, u32[]{:S(2)}, u32[]{:S(2)}) collective-permute-start(f32[320,128]{1,0:T(8,128)S(1)} %shard_map.96.chip_ref), channel_id=1, source_target_pairs={{0,2},{1,3},{2,0},{3,1},{4,6},{5,7},{6,4},{7,5},{8,10},{9,11},{10,... | collective-permute-start | bytes 491528 | tf_op jit(solution)/shard_map/ppermute | solution.py:22
  5.3 2.0 %copy-start.3 = (f32[1,64,256]{2,1,0:T(8,128)S(1)}, f32[1,64,256]{2,1,0:T(8,128)}, u32[]{:S(2)}) copy-start(f32[1,64,256]{2,1,0:T(8,128)} %param.13) | copy-start | bytes 196612
  5.3 2.0 %copy-start = (f32[1,160,640]{2,1,0:T(8,128)S(1)}, f32[1,160,640]{2,1,0:T(8,128)}, u32[]{:S(2)}) copy-start(f32[1,160,640]{2,1,0:T(8,128)} %param.9) | copy-start | bytes 1228804
  5.4 2.0 %copy-start.1 = (f32[1,384,160]{1,2,0:T(8,128)S(1)}, f32[1,384,160]{1,2,0:T(8,128)}, u32[]{:S(2)}) copy-start(f32[1,384,160]{1,2,0:T(8,128)} %param.10) | copy-start | bytes 737284
  5.7 8.3 %collective-permute-start.2 = (f32[208,256]{1,0:T(8,128)S(1)}, f32[208,256]{1,0:T(8,128)S(1)}, u32[]{:S(2)}, u32[]{:S(2)}) collective-permute-start(f32[208,256]{1,0:T(8,128)S(1)} %shard_map.97.carry_ref.own_ref), channel_id=1, source_target_pairs={{0,4},{1,5},{2,6},{3,7},{4,0},{5,1},{6,2},{7,3},{8,12},{9,13},{10,... | collective-permute-start | bytes 638984 | tf_op jit(solution)/shard_map/ppermute | solution.py:22
  7.3 1.8 %collective-permute-start.3 = (f32[64,256]{1,0:T(8,128)S(1)}, f32[64,256]{1,0:T(8,128)S(1)}, u32[]{:S(2)}, u32[]{:S(2)}) collective-permute-start(f32[64,256]{1,0:T(8,128)S(1)} %bitcast.16), channel_id=1, source_target_pairs={{0,1},{1,0},{2,3},{3,2},{4,5},{5,4},{6,7},{7,6},{8,9},{9,8},{10,11... | collective-permute-start | bytes 196616 | tf_op jit(solution)/shard_map/ppermute | solution.py:22
  10.5 5.8 %collective-permute-start.8 = (f32[32,512]{1,0:T(8,128)S(1)}, f32[32,512]{1,0:T(8,128)S(1)}, u32[]{:S(2)}, u32[]{:S(2)}) collective-permute-start(f32[32,512]{1,0:T(8,128)S(1)} %get-tuple-element.112), channel_id=1, source_target_pairs={{0,6},{1,7},{2,4},{3,5},{4,2},{5,3},{6,0},{7,1},{8,14},{9,15},{10,... | collective-permute-start | bytes 196616 | tf_op jit(solution)/shard_map/ppermute | solution.py:22
  13.3 4.3 %collective-permute-start.9 = (f32[32,512]{1,0:T(8,128)S(1)}, f32[32,512]{1,0:T(8,128)S(1)}, u32[]{:S(2)}, u32[]{:S(2)}) collective-permute-start(f32[32,512]{1,0:T(8,128)S(1)} %get-tuple-element.113), channel_id=1, source_target_pairs={{0,2},{1,3},{2,0},{3,1},{4,6},{5,7},{6,4},{7,5},{8,10},{9,11},{10,... | collective-permute-start | bytes 196616 | tf_op jit(solution)/shard_map/ppermute | solution.py:22
  13.8 4.3 %collective-permute-start.10 = (f32[32,512]{1,0:T(8,128)S(1)}, f32[32,512]{1,0:T(8,128)S(1)}, u32[]{:S(2)}, u32[]{:S(2)}) collective-permute-start(f32[32,512]{1,0:T(8,128)S(1)} %get-tuple-element.114), channel_id=1, source_target_pairs={{0,4},{1,5},{2,6},{3,7},{4,0},{5,1},{6,2},{7,3},{8,12},{9,13},{10,... | collective-permute-start | bytes 196616 | tf_op jit(solution)/shard_map/ppermute | solution.py:22
  14.1 8.2 %collective-permute-start.6 = (f32[200,256]{1,0:T(8,128)S(1)}, f32[200,256]{1,0:T(8,128)S(1)}, u32[]{:S(2)}, u32[]{:S(2)}) collective-permute-start(f32[200,256]{1,0:T(8,128)S(1)} %get-tuple-element.109.carry_ref), channel_id=1, source_target_pairs={{8,0},{9,1},{10,2},{11,3},{12,4},{13,5},{14,6},{15,7},{24,16},{25,... | collective-permute-start | bytes 614408 | tf_op jit(solution)/shard_map/ppermute | solution.py:34
  16.2 2.2 %collective-permute-start.7 = (f32[200,256]{1,0:T(8,128)S(1)}, f32[200,256]{1,0:T(8,128)S(1)}, u32[]{:S(2)}, u32[]{:S(2)}) collective-permute-start(f32[200,256]{1,0:T(8,128)S(1)} %get-tuple-element.110.half_ref), channel_id=1, source_target_pairs={{0,1},{1,0},{2,3},{3,2},{4,5},{5,4},{6,7},{7,6},{8,9},{9,8},{10,11... | collective-permute-start | bytes 614408 | tf_op jit(solution)/shard_map/ppermute | solution.py:22
  18.6 5.2 %collective-permute-start.12 = (f32[32,512]{1,0:T(8,128)S(1)}, f32[32,512]{1,0:T(8,128)S(1)}, u32[]{:S(2)}, u32[]{:S(2)}) collective-permute-start(f32[32,512]{1,0:T(8,128)S(1)} %shard_map.106.up_ref), channel_id=1, source_target_pairs={{0,8},{1,9},{2,10},{3,11},{4,12},{5,13},{6,14},{7,15},{8,0},{9,1},... | collective-permute-start | bytes 196616 | tf_op jit(solution)/shard_map/ppermute | solution.py:22
  20.7 13.8 %collective-permute-start.19 = (f32[160,640]{1,0:T(8,128)S(1)}, f32[160,640]{1,0:T(8,128)S(1)}, u32[]{:S(2)}, u32[]{:S(2)}) collective-permute-start(f32[160,640]{1,0:T(8,128)S(1)} %get-tuple-element.161), channel_id=1, source_target_pairs={{2,0},{3,1},{6,4},{7,5},{10,8},{11,9},{14,12},{15,13},{18,16},{19,... | collective-permute-start | bytes 1228808 | tf_op jit(solution)/shard_map/ppermute | solution.py:22
  22.3 1.5 %collective-permute-start.13 = (f32[200,256]{1,0:T(8,128)S(1)}, f32[200,256]{1,0:T(8,128)S(1)}, u32[]{:S(2)}, u32[]{:S(2)}) collective-permute-start(f32[200,256]{1,0:T(8,128)S(1)} %get-tuple-element.131.half_ref), channel_id=1, source_target_pairs={{0,1},{1,0},{2,3},{3,2},{4,5},{5,4},{6,7},{7,6},{8,9},{9,8},{10,11... | collective-permute-start | bytes 614408 | tf_op jit(solution)/shard_map/ppermute | solution.py:22
  22.4 4.7 %collective-permute-start.11 = (f32[72,256]{1,0:T(8,128)S(1)}, f32[72,256]{1,0:T(8,128)S(1)}, u32[]{:S(2)}, u32[]{:S(2)}) collective-permute-start(f32[72,256]{1,0:T(8,128)S(1)} %get-tuple-element.128.root_ref), channel_id=1, source_target_pairs={{0,8},{1,9},{2,10},{3,11},{4,12},{5,13},{6,14},{7,15},{8,0},{9,1},... | collective-permute-start | bytes 221192 | tf_op jit(solution)/shard_map/ppermute | solution.py:22
  24.1 5.2 %collective-permute-start.15 = (f32[32,256]{1,0:T(8,128)S(1)}, f32[32,256]{1,0:T(8,128)S(1)}, u32[]{:S(2)}, u32[]{:S(2)}) collective-permute-start(f32[32,256]{1,0:T(8,128)S(1)} %shard_map.109.up_ref), channel_id=1, source_target_pairs={{0,16},{1,17},{2,18},{3,19},{4,20},{5,21},{6,22},{7,23},{8,24},{9,... | collective-permute-start | bytes 98312 | tf_op jit(solution)/shard_map/ppermute | solution.py:22
  27.1 2.2 %collective-permute-start.14 = (f32[72,256]{1,0:T(8,128)S(1)}, f32[72,256]{1,0:T(8,128)S(1)}, u32[]{:S(2)}, u32[]{:S(2)}) collective-permute-start(f32[72,256]{1,0:T(8,128)S(1)} %shard_map.111.root_ref), channel_id=1, source_target_pairs={{0,1},{1,0},{2,3},{3,2},{4,5},{5,4},{6,7},{7,6},{8,9},{9,8},{10,11... | collective-permute-start | bytes 221192 | tf_op jit(solution)/shard_map/ppermute | solution.py:22
  30.1 7.0 %collective-permute-start.16 = (f32[32,512]{1,0:T(8,128)S(1)}, f32[32,512]{1,0:T(8,128)S(1)}, u32[]{:S(2)}, u32[]{:S(2)}) collective-permute-start(f32[32,512]{1,0:T(8,128)S(1)} %get-tuple-element.155), channel_id=1, source_target_pairs={{0,6},{1,7},{2,4},{3,5},{4,2},{5,3},{6,0},{7,1},{8,14},{9,15},{10,... | collective-permute-start | bytes 196616 | tf_op jit(solution)/shard_map/ppermute | solution.py:22
  33.6 4.3 %collective-permute-start.17 = (f32[32,512]{1,0:T(8,128)S(1)}, f32[32,512]{1,0:T(8,128)S(1)}, u32[]{:S(2)}, u32[]{:S(2)}) collective-permute-start(f32[32,512]{1,0:T(8,128)S(1)} %get-tuple-element.156), channel_id=1, source_target_pairs={{0,2},{1,3},{2,0},{3,1},{4,6},{5,7},{6,4},{7,5},{8,10},{9,11},{10,... | collective-permute-start | bytes 196616 | tf_op jit(solution)/shard_map/ppermute | solution.py:22
  33.6 4.3 %collective-permute-start.18 = (f32[32,512]{1,0:T(8,128)S(1)}, f32[32,512]{1,0:T(8,128)S(1)}, u32[]{:S(2)}, u32[]{:S(2)}) collective-permute-start(f32[32,512]{1,0:T(8,128)S(1)} %get-tuple-element.157), channel_id=1, source_target_pairs={{0,4},{1,5},{2,6},{3,7},{4,0},{5,1},{6,2},{7,3},{8,12},{9,13},{10,... | collective-permute-start | bytes 196616 | tf_op jit(solution)/shard_map/ppermute | solution.py:22
  37.9 1.6 %collective-permute-start.20 = (f32[128,512]{1,0:T(8,128)S(1)}, f32[128,512]{1,0:T(8,128)S(1)}, u32[]{:S(2)}, u32[]{:S(2)}) collective-permute-start(f32[128,512]{1,0:T(8,128)S(1)} %shard_map.117.group_ref), channel_id=1, source_target_pairs={{0,1},{1,0},{2,3},{3,2},{4,5},{5,4},{6,7},{7,6},{8,9},{9,8},{10,11... | collective-permute-start | bytes 786440 | tf_op jit(solution)/shard_map/ppermute | solution.py:22
  38.0 1.6 %collective-permute-start.21 = (f32[160,128]{1,0:T(8,128)S(1)}, f32[160,128]{1,0:T(8,128)S(1)}, u32[]{:S(2)}, u32[]{:S(2)}) collective-permute-start(f32[160,128]{1,0:T(8,128)S(1)} %get-tuple-element.173), channel_id=1, source_target_pairs={{0,1},{1,0},{2,3},{3,2},{4,5},{5,4},{6,7},{7,6},{8,9},{9,8},{10,11... | collective-permute-start | bytes 245768 | tf_op jit(solution)/shard_map/ppermute | solution.py:22

commit v11 on v10

--- a/solution.py
+++ b/solution.py
@@ -429,7 +429,7 @@
                 last_forward, [(carried, order), (packed_rows, order)], carry, reached
             )
             halves.append(new_half)
-            from_far = swap(far_sum, 0, 2, lambda leaf, sep: sep // 2 == 1)
+            from_far = swap(far_sum, 0, 2)
             halves_near.append(swap(new_half, 0, 1))
             by_root = swap(root, leaves // 4, 0)
         residual, slots = stage(

time: 40.9 us -> 40.4 us (0.988)
  transfers between devices with their start and end apart: 22 -> 22, of which waited for: 11 -> 10; matrix products, arithmetic and copies ran while one was open for 0% -> 0% of each run, Pallas kernels for 17% -> 17%
where the time goes in v11:
time: 40.4 us; the launch traced here: 40.2 us
  starting transfers between devices  22.2 us (55%)
  waiting for transfers between devices  8.18 us (20%)
  Pallas kernels  7.96 us (20%)
  local copies, waits for them, and re-layouts  0.95 us (2%)
  between operations  0.93 us (2%)
    ppermute x21, starting transfers between devices, swap(): return lax.ppermute(payload, axes, pairs)  20.9 us
    ppermute x21, waiting for transfers between devices, swap(): return lax.ppermute(payload, axes, pairs)  8.18 us
    pallas_call x25, Pallas kernels, stage(): pl.pallas_call(body, out_shape=[jax.ShapeDtypeStruct(shape, f32) if isins...  7.96 us
    ppermute x1, starting transfers between devices, quarter_swap(): return lax.ppermute(payload, axes, pairs)  1.29 us
    unnamed x16, local copies, waits for them, and re-layouts  0.95 us
  transfers between devices with their start and end apart: 22, of which 10 were waited for; matrix products, arithmetic and copies ran while one was open for 0% of the time, Pallas kernels for 17%

profile of v11, /device:TPU:0, one launch (start us, length us, event | category | flops | bytes accessed | tf_op | source)
XLA Modules:
  0.0 40.2 jit_solution(9953056920296218417)
XLA Ops:
  0.6 0.5 %collective-permute-start.1 = (f32[160,256]{1,0:T(8,128)}, f32[160,256]{1,0:T(8,128)S(1)}, u32[]{:S(2)}, u32[]{:S(2)}) collective-permute-start(f32[160,256]{1,0:T(8,128)} %bitcast.14), channel_id=1, source_target_pairs={{0,1},{1,0},{2,3},{3,2},{4,5},{5,4},{6,7},{7,6},{8,9},{9,8},{10,11... | collective-permute-start | bytes 491528 | tf_op jit(solution)/shard_map/ppermute | solution.py:22
  1.2 0.1 collective-permute-start.4
  1.2 0.4 %collective-permute-start = (f32[160,640]{1,0:T(8,128)}, f32[160,640]{1,0:T(8,128)S(1)}, u32[]{:S(2)}, u32[]{:S(2)}) collective-permute-start(f32[160,640]{1,0:T(8,128)} %bitcast.10), channel_id=1, source_target_pairs={{0,1},{1,0},{2,3},{3,2},{4,5},{5,4},{6,7},{7,6},{8,9},{9,8},{10,11... | collective-permute-start | bytes 1228808 | tf_op jit(solution)/shard_map/ppermute | solution.py:22
  1.7 0.9 %copy-done.2 = f32[1,160,256]{2,1,0:T(8,128)S(1)} copy-done((f32[1,160,256]{2,1,0:T(8,128)S(1)}, f32[1,160,256]{2,1,0:T(8,128)}, u32[]{:S(2)}) %copy-start.2) | copy-done | bytes 163864
  2.7 2.6 %collective-permute-start.5 = (f32[320,128]{1,0:T(8,128)S(1)}, f32[320,128]{1,0:T(8,128)S(1)}, u32[]{:S(2)}, u32[]{:S(2)}) collective-permute-start(f32[320,128]{1,0:T(8,128)S(1)} %shard_map.96.chip_ref), channel_id=1, source_target_pairs={{0,2},{1,3},{2,0},{3,1},{4,6},{5,7},{6,4},{7,5},{8,10},{9,11},{10,... | collective-permute-start | bytes 491528 | tf_op jit(solution)/shard_map/ppermute | solution.py:22
  5.4 0.4 shard_map.97.carry_ref.own_ref
  5.7 1.6 %collective-permute-start.2 = (f32[208,256]{1,0:T(8,128)S(1)}, f32[208,256]{1,0:T(8,128)S(1)}, u32[]{:S(2)}, u32[]{:S(2)}) collective-permute-start(f32[208,256]{1,0:T(8,128)S(1)} %shard_map.97.carry_ref.own_ref), channel_id=1, source_target_pairs={{0,4},{1,5},{2,6},{3,7},{4,0},{5,1},{6,2},{7,3},{8,12},{9,13},{10,... | collective-permute-start | bytes 638984 | tf_op jit(solution)/shard_map/ppermute | solution.py:22
  7.4 0.6 %shard_map.98 = (f32[320,128]{1,0:T(8,128)S(1)}, f32[320,320]{1,0:T(8,128)S(1)}, f32[320,320]{1,0:T(8,128)S(1)}, f32[320,160]{1,0:T(8,128)S(1)}, f32[320,384]{1,0:T(8,128)S(1)}) custom-call(f32[160,640]{1,0:T(8,128)S(1)} %bitcast.11, f32[160,640]{1,0:T(8,128)S(1)} %collective-permute-done.inverse_near_ref, f32[160,384]{1,0:T(8,128)S(1)} %bitcast.13, ...), custom_call_target="tpu_custom_call" | custom-call | tf_op jit(solution)/shard_map/pallas_call | solution.py:75
  8.0 1.1 %shard_map.99 = (f32[320,384]{1,0:T(8,128)S(1)}, f32[160,384]{1,0:T(8,128)S(1)}, f32[128,384]{1,0:T(8,128)S(1)}) custom-call(f32[320,320]{1,0:T(8,128)S(1)} %get-tuple-element.96.far_ref.inverse_far_ref, f32[320,160]{1,0:T(8,128)S(1)} %get-tuple-element.97.mine_ref, f32[320,384]{1,0:T(8,128)S(1)} %get-tuple-element.98.update_ref, ...), custom_call_target="tpu_custom_call" | custom-call | tf_op jit(solution)/shard_map/pallas_call | solution.py:75
  9.1 0.2 shard_map.100.turned_ref
  9.3 0.8 %collective-permute-done.5.far_ref = f32[320,128]{1,0:T(8,128)S(1)} collective-permute-done((f32[320,128]{1,0:T(8,128)S(1)}, f32[320,128]{1,0:T(8,128)S(1)}, u32[]{:S(2)}, u32[]{:S(2)}) %collective-permute-start.5) | collective-permute-done | bytes 163872 | tf_op jit(solution)/shard_map/ppermute | solution.py:22
  10.1 0.4 shard_map.101
  10.5 2.8 %collective-permute-start.8 = (f32[32,512]{1,0:T(8,128)S(1)}, f32[32,512]{1,0:T(8,128)S(1)}, u32[]{:S(2)}, u32[]{:S(2)}) collective-permute-start(f32[32,512]{1,0:T(8,128)S(1)} %get-tuple-element.112), channel_id=1, source_target_pairs={{0,6},{1,7},{2,4},{3,5},{4,2},{5,3},{6,0},{7,1},{8,14},{9,15},{10,... | collective-permute-start | bytes 196616 | tf_op jit(solution)/shard_map/ppermute | solution.py:22
  13.3 0.5 %collective-permute-start.9 = (f32[32,512]{1,0:T(8,128)S(1)}, f32[32,512]{1,0:T(8,128)S(1)}, u32[]{:S(2)}, u32[]{:S(2)}) collective-permute-start(f32[32,512]{1,0:T(8,128)S(1)} %get-tuple-element.113), channel_id=1, source_target_pairs={{0,2},{1,3},{2,0},{3,1},{4,6},{5,7},{6,4},{7,5},{8,10},{9,11},{10,... | collective-permute-start | bytes 196616 | tf_op jit(solution)/shard_map/ppermute | solution.py:22
  13.8 0.2 collective-permute-start.10
  14.1 1.3 %collective-permute-start.6 = (f32[200,256]{1,0:T(8,128)S(1)}, f32[200,256]{1,0:T(8,128)S(1)}, u32[]{:S(2)}, u32[]{:S(2)}) collective-permute-start(f32[200,256]{1,0:T(8,128)S(1)} %get-tuple-element.109.carry_ref), channel_id=1, source_target_pairs={{8,0},{9,1},{10,2},{11,3},{12,4},{13,5},{14,6},{15,7},{24,16},{25,... | collective-permute-start | bytes 614408 | tf_op jit(solution)/shard_map/ppermute | solution.py:34
  15.4 0.1 shard_map.103.hot_ref
  15.5 0.7 %shard_map.104 = (f32[320,128]{1,0:T(8,128)S(1)}, f32[160,640]{1,0:T(8,128)S(1)}) custom-call(f32[320,320]{1,0:T(8,128)S(1)} %get-tuple-element.96.far_ref.inverse_far_ref, f32[320,128]{1,0:T(8,128)S(1)} %get-tuple-element.116.y_ref.own_y_ref, f32[320,128]{1,0:T(8,128)S(1)} %collective-permute-done.5.far_ref, f32[320,384]{1,0:T(8,128)S(1)} %get-tuple-element.102.turned_far_ref), custom_call_target="tpu_custom_call" | custom-call | tf_op jit(solution)/shard_map/pallas_call | solution.py:75
  16.2 0.1 collective-permute-start.7
  16.3 1.3 %collective-permute-done.9.far_ref = f32[32,512]{1,0:T(8,128)S(1)} collective-permute-done((f32[32,512]{1,0:T(8,128)S(1)}, f32[32,512]{1,0:T(8,128)S(1)}, u32[]{:S(2)}, u32[]{:S(2)}) %collective-permute-start.9) | collective-permute-done | bytes 65568 | tf_op jit(solution)/shard_map/ppermute | solution.py:22
  17.6 0.5 %collective-permute-done.10.odd_ref = f32[32,512]{1,0:T(8,128)S(1)} collective-permute-done((f32[32,512]{1,0:T(8,128)S(1)}, f32[32,512]{1,0:T(8,128)S(1)}, u32[]{:S(2)}, u32[]{:S(2)}) %collective-permute-start.10) | collective-permute-done | bytes 65568 | tf_op jit(solution)/shard_map/ppermute | solution.py:22
  18.1 0.3 shard_map.105
  18.4 0.2 shard_map.106.up_ref
  18.6 2.1 %collective-permute-start.12 = (f32[32,512]{1,0:T(8,128)S(1)}, f32[32,512]{1,0:T(8,128)S(1)}, u32[]{:S(2)}, u32[]{:S(2)}) collective-permute-start(f32[32,512]{1,0:T(8,128)S(1)} %shard_map.106.up_ref), channel_id=1, source_target_pairs={{0,8},{1,9},{2,10},{3,11},{4,12},{5,13},{6,14},{7,15},{8,0},{9,1},... | collective-permute-start | bytes 196616 | tf_op jit(solution)/shard_map/ppermute | solution.py:22
  20.7 1.8 %collective-permute-start.19 = (f32[160,640]{1,0:T(8,128)S(1)}, f32[160,640]{1,0:T(8,128)S(1)}, u32[]{:S(2)}, u32[]{:S(2)}) collective-permute-start(f32[160,640]{1,0:T(8,128)S(1)} %get-tuple-element.161), channel_id=1, source_target_pairs={{0,2},{1,3},{2,0},{3,1},{4,6},{5,7},{6,4},{7,5},{8,10},{9,11},{10,... | collective-permute-start | bytes 1228808 | tf_op jit(solution)/shard_map/ppermute | solution.py:22
  22.5 0.1 collective-permute-start.13
  22.5 1.3 %collective-permute-start.11 = (f32[72,256]{1,0:T(8,128)S(1)}, f32[72,256]{1,0:T(8,128)S(1)}, u32[]{:S(2)}, u32[]{:S(2)}) collective-permute-start(f32[72,256]{1,0:T(8,128)S(1)} %get-tuple-element.128.root_ref), channel_id=1, source_target_pairs={{0,8},{1,9},{2,10},{3,11},{4,12},{5,13},{6,14},{7,15},{8,0},{9,1},... | collective-permute-start | bytes 221192 | tf_op jit(solution)/shard_map/ppermute | solution.py:22
  23.8 0.1 collective-permute-done.13.near_ref
  24.0 0.2 shard_map.109.up_ref
  24.2 2.7 %collective-permute-start.15 = (f32[32,256]{1,0:T(8,128)S(1)}, f32[32,256]{1,0:T(8,128)S(1)}, u32[]{:S(2)}, u32[]{:S(2)}) collective-permute-start(f32[32,256]{1,0:T(8,128)S(1)} %shard_map.109.up_ref), channel_id=1, source_target_pairs={{0,16},{1,17},{2,18},{3,19},{4,20},{5,21},{6,22},{7,23},{8,24},{9,... | collective-permute-start | bytes 98312 | tf_op jit(solution)/shard_map/ppermute | solution.py:22
  26.9 0.4 shard_map.110
  27.3 0.1 collective-permute-start.14
  27.4 0.4 shard_map.112
  27.7 0.4 shard_map.113
  28.1 1.2 %collective-permute-done.15.partner_ref = f32[32,256]{1,0:T(8,128)S(1)} collective-permute-done((f32[32,256]{1,0:T(8,128)S(1)}, f32[32,256]{1,0:T(8,128)S(1)}, u32[]{:S(2)}, u32[]{:S(2)}) %collective-permute-start.15) | collective-permute-done | bytes 32800 | tf_op jit(solution)/shard_map/ppermute | solution.py:22
  29.4 0.7 %shard_map.115 = (f32[32,512]{1,0:T(8,128)S(1)}, f32[32,512]{1,0:T(8,128)S(1)}, f32[32,512]{1,0:T(8,128)S(1)}, f32[32,512]{1,0:T(8,128)S(1)}) custom-call(f32[32,256]{1,0:T(8,128)S(1)} %shard_map.114.residual_ref, f32[72,256]{1,0:T(8,128)S(1)} %shard_map.111.root_ref, f32[72,256]{1,0:T(8,128)S(1)} %collective-permute-done.14.root_near_ref, ...), custom_call_target="tpu_custom_call" | custom-call | tf_op jit(solution)/shard_map/pallas_call | solution.py:75
  30.1 2.4 %collective-permute-start.16 = (f32[32,512]{1,0:T(8,128)S(1)}, f32[32,512]{1,0:T(8,128)S(1)}, u32[]{:S(2)}, u32[]{:S(2)}) collective-permute-start(f32[32,512]{1,0:T(8,128)S(1)} %get-tuple-element.155), channel_id=1, source_target_pairs={{0,6},{1,7},{2,4},{3,5},{4,2},{5,3},{6,0},{7,1},{8,14},{9,15},{10,... | collective-permute-start | bytes 196616 | tf_op jit(solution)/shard_map/ppermute | solution.py:22
  32.5 0.6 %collective-permute-start.17 = (f32[32,512]{1,0:T(8,128)S(1)}, f32[32,512]{1,0:T(8,128)S(1)}, u32[]{:S(2)}, u32[]{:S(2)}) collective-permute-start(f32[32,512]{1,0:T(8,128)S(1)} %get-tuple-element.156), channel_id=1, source_target_pairs={{0,2},{1,3},{2,0},{3,1},{4,6},{5,7},{6,4},{7,5},{8,10},{9,11},{10,... | collective-permute-start | bytes 196616 | tf_op jit(solution)/shard_map/ppermute | solution.py:22
  33.2 0.5 %collective-permute-start.18 = (f32[32,512]{1,0:T(8,128)S(1)}, f32[32,512]{1,0:T(8,128)S(1)}, u32[]{:S(2)}, u32[]{:S(2)}) collective-permute-start(f32[32,512]{1,0:T(8,128)S(1)} %get-tuple-element.157), channel_id=1, source_target_pairs={{0,4},{1,5},{2,6},{3,7},{4,0},{5,1},{6,2},{7,3},{8,12},{9,13},{10,... | collective-permute-start | bytes 196616 | tf_op jit(solution)/shard_map/ppermute | solution.py:22
  33.7 0.4 %shard_map.116 = (f32[224,512]{1,0:T(8,128)S(1)}, f32[160,128]{1,0:T(8,128)S(1)}, f32[160,128]{1,0:T(8,128)S(1)}) custom-call(f32[160,384]{1,0:T(8,128)S(1)} %get-tuple-element.158.own_ref, f32[320,320]{1,0:T(8,128)S(1)} %get-tuple-element.159.chip_ref, f32[320,128]{1,0:T(8,128)S(1)} %get-tuple-element.160.y_ref, f32[160,640]{1,0:T(8,128)S(1)} %collective-permute-done.19.far_ref), custom_call_target="tpu_custom_call" | custom-call | tf_op jit(solution)/shard_map/pallas_call | solution.py:75
  34.1 1.4 %collective-permute-done.16.refs_3_ = f32[32,512]{1,0:T(8,128)S(1)} collective-permute-done((f32[32,512]{1,0:T(8,128)S(1)}, f32[32,512]{1,0:T(8,128)S(1)}, u32[]{:S(2)}, u32[]{:S(2)}) %collective-permute-start.16) | collective-permute-done | bytes 65568 | tf_op jit(solution)/shard_map/ppermute | solution.py:22
  35.5 1.4 %collective-permute-done.17.refs_1_ = f32[32,512]{1,0:T(8,128)S(1)} collective-permute-done((f32[32,512]{1,0:T(8,128)S(1)}, f32[32,512]{1,0:T(8,128)S(1)}, u32[]{:S(2)}, u32[]{:S(2)}) %collective-permute-start.17) | collective-permute-done | bytes 65568 | tf_op jit(solution)/shard_map/ppermute | solution.py:22
  36.8 0.6 %collective-permute-done.18.refs_2_ = f32[32,512]{1,0:T(8,128)S(1)} collective-permute-done((f32[32,512]{1,0:T(8,128)S(1)}, f32[32,512]{1,0:T(8,128)S(1)}, u32[]{:S(2)}, u32[]{:S(2)}) %collective-permute-start.18) | collective-permute-done | bytes 65568 | tf_op jit(solution)/shard_map/ppermute | solution.py:22
  37.6 0.5 %collective-permute-start.21 = (f32[160,128]{1,0:T(8,128)S(1)}, f32[160,128]{1,0:T(8,128)S(1)}, u32[]{:S(2)}, u32[]{:S(2)}) collective-permute-start(f32[160,128]{1,0:T(8,128)S(1)} %get-tuple-element.173), channel_id=1, source_target_pairs={{0,1},{1,0},{2,3},{3,2},{4,5},{5,4},{6,7},{7,6},{8,9},{9,8},{10,11... | collective-permute-start | bytes 245768 | tf_op jit(solution)/shard_map/ppermute | solution.py:22
  38.1 0.3 shard_map.118.ours_ref
  38.4 0.7 %collective-permute-done.20.group_ref = f32[128,512]{1,0:T(8,128)S(1)} collective-permute-done((f32[128,512]{1,0:T(8,128)S(1)}, f32[128,512]{1,0:T(8,128)S(1)}, u32[]{:S(2)}, u32[]{:S(2)}) %collective-permute-start.20) | collective-permute-done | bytes 262176 | tf_op jit(solution)/shard_map/ppermute | solution.py:22
  39.1 0.1 collective-permute-done.21.base_near_ref
  39.2 1.0 %shard_map.119 = (f32[160,256]{1,0:T(8,128)}, f32[64,256]{1,0:T(8,128)}) custom-call(f32[224,512]{1,0:T(8,128)S(1)} %get-tuple-element.165.left_ref, f32[128,512]{1,0:T(8,128)S(1)} %collective-permute-done.20.group_ref, f32[224,128]{1,0:T(8,128)S(1)} %shard_map.118.ours_ref, f32[160,128]{1,0:T(8,128)S(1)} %get-tuple-element.172.base_ref, ...), custom_call_target="tpu_custom_call" | custom-call | tf_op jit(solution)/shard_map/pallas_call | solution.py:75
  (38 shorter events, 0.4 us)
Async XLA Ops:
  0.6 2.0 %copy-start.7 = (s32[1,3]{1,0:T(1,128)S(1)}, s32[1,3]{1,0:T(1,128)}, u32[]{:S(2)}) copy-start(s32[1,3]{1,0:T(1,128)} %param.12) | copy-start | bytes 40
  0.6 2.0 %collective-permute-start.1 = (f32[160,256]{1,0:T(8,128)}, f32[160,256]{1,0:T(8,128)S(1)}, u32[]{:S(2)}, u32[]{:S(2)}) collective-permute-start(f32[160,256]{1,0:T(8,128)} %bitcast.14), channel_id=1, source_target_pairs={{0,1},{1,0},{2,3},{3,2},{4,5},{5,4},{6,7},{7,6},{8,9},{9,8},{10,11... | collective-permute-start | bytes 491528 | tf_op jit(solution)/shard_map/ppermute | solution.py:22
  1.2 6.2 %collective-permute-start.4 = (f32[160,384]{1,0:T(8,128)}, f32[160,384]{1,0:T(8,128)S(1)}, u32[]{:S(2)}, u32[]{:S(2)}) collective-permute-start(f32[160,384]{1,0:T(8,128)} %bitcast.12), channel_id=1, source_target_pairs={{0,1},{1,0},{2,3},{3,2},{4,5},{5,4},{6,7},{7,6},{8,9},{9,8},{10,11... | collective-permute-start | bytes 737288 | tf_op jit(solution)/shard_map/ppermute | solution.py:22
  1.2 1.4 %copy-start.6 = (s32[1,384]{1,0:T(1,128)S(1)}, s32[1,384]{1,0:T(1,128)}, u32[]{:S(2)}) copy-start(s32[1,384]{1,0:T(1,128)} %param.11) | copy-start | bytes 4612
  1.2 6.1 %collective-permute-start = (f32[160,640]{1,0:T(8,128)}, f32[160,640]{1,0:T(8,128)S(1)}, u32[]{:S(2)}, u32[]{:S(2)}) collective-permute-start(f32[160,640]{1,0:T(8,128)} %bitcast.10), channel_id=1, source_target_pairs={{0,1},{1,0},{2,3},{3,2},{4,5},{5,4},{6,7},{7,6},{8,9},{9,8},{10,11... | collective-permute-start | bytes 1228808 | tf_op jit(solution)/shard_map/ppermute | solution.py:22
  1.7 0.9 %copy-start.2 = (f32[1,160,256]{2,1,0:T(8,128)S(1)}, f32[1,160,256]{2,1,0:T(8,128)}, u32[]{:S(2)}) copy-start(f32[1,160,256]{2,1,0:T(8,128)} %param.8) | copy-start | bytes 491524
  2.6 2.8 %copy-start.5 = (f32[1,256,256]{2,1,0:T(8,128)S(1)}, f32[1,256,256]{2,1,0:T(8,128)}, u32[]{:S(2)}) copy-start(f32[1,256,256]{2,1,0:T(8,128)} %param.14) | copy-start | bytes 786436
  2.6 2.7 %copy-start.4 = (f32[1,256,256]{2,1,0:T(8,128)S(1)}, f32[1,256,256]{2,1,0:T(8,128)}, u32[]{:S(2)}) copy-start(f32[1,256,256]{2,1,0:T(8,128)} %param.15) | copy-start | bytes 786436
  2.7 7.4 %collective-permute-start.5 = (f32[320,128]{1,0:T(8,128)S(1)}, f32[320,128]{1,0:T(8,128)S(1)}, u32[]{:S(2)}, u32[]{:S(2)}) collective-permute-start(f32[320,128]{1,0:T(8,128)S(1)} %shard_map.96.chip_ref), channel_id=1, source_target_pairs={{0,2},{1,3},{2,0},{3,1},{4,6},{5,7},{6,4},{7,5},{8,10},{9,11},{10,... | collective-permute-start | bytes 491528 | tf_op jit(solution)/shard_map/ppermute | solution.py:22
  5.3 2.0 %copy-start.3 = (f32[1,64,256]{2,1,0:T(8,128)S(1)}, f32[1,64,256]{2,1,0:T(8,128)}, u32[]{:S(2)}) copy-start(f32[1,64,256]{2,1,0:T(8,128)} %param.13) | copy-start | bytes 196612
  5.3 2.0 %copy-start = (f32[1,160,640]{2,1,0:T(8,128)S(1)}, f32[1,160,640]{2,1,0:T(8,128)}, u32[]{:S(2)}) copy-start(f32[1,160,640]{2,1,0:T(8,128)} %param.9) | copy-start | bytes 1228804
  5.4 2.0 %copy-start.1 = (f32[1,384,160]{1,2,0:T(8,128)S(1)}, f32[1,384,160]{1,2,0:T(8,128)}, u32[]{:S(2)}) copy-start(f32[1,384,160]{1,2,0:T(8,128)} %param.10) | copy-start | bytes 737284
  5.7 8.3 %collective-permute-start.2 = (f32[208,256]{1,0:T(8,128)S(1)}, f32[208,256]{1,0:T(8,128)S(1)}, u32[]{:S(2)}, u32[]{:S(2)}) collective-permute-start(f32[208,256]{1,0:T(8,128)S(1)} %shard_map.97.carry_ref.own_ref), channel_id=1, source_target_pairs={{0,4},{1,5},{2,6},{3,7},{4,0},{5,1},{6,2},{7,3},{8,12},{9,13},{10,... | collective-permute-start | bytes 638984 | tf_op jit(solution)/shard_map/ppermute | solution.py:22
  7.3 1.8 %collective-permute-start.3 = (f32[64,256]{1,0:T(8,128)S(1)}, f32[64,256]{1,0:T(8,128)S(1)}, u32[]{:S(2)}, u32[]{:S(2)}) collective-permute-start(f32[64,256]{1,0:T(8,128)S(1)} %bitcast.16), channel_id=1, source_target_pairs={{0,1},{1,0},{2,3},{3,2},{4,5},{5,4},{6,7},{7,6},{8,9},{9,8},{10,11... | collective-permute-start | bytes 196616 | tf_op jit(solution)/shard_map/ppermute | solution.py:22
  10.5 5.8 %collective-permute-start.8 = (f32[32,512]{1,0:T(8,128)S(1)}, f32[32,512]{1,0:T(8,128)S(1)}, u32[]{:S(2)}, u32[]{:S(2)}) collective-permute-start(f32[32,512]{1,0:T(8,128)S(1)} %get-tuple-element.112), channel_id=1, source_target_pairs={{0,6},{1,7},{2,4},{3,5},{4,2},{5,3},{6,0},{7,1},{8,14},{9,15},{10,... | collective-permute-start | bytes 196616 | tf_op jit(solution)/shard_map/ppermute | solution.py:22
  13.3 4.3 %collective-permute-start.9 = (f32[32,512]{1,0:T(8,128)S(1)}, f32[32,512]{1,0:T(8,128)S(1)}, u32[]{:S(2)}, u32[]{:S(2)}) collective-permute-start(f32[32,512]{1,0:T(8,128)S(1)} %get-tuple-element.113), channel_id=1, source_target_pairs={{0,2},{1,3},{2,0},{3,1},{4,6},{5,7},{6,4},{7,5},{8,10},{9,11},{10,... | collective-permute-start | bytes 196616 | tf_op jit(solution)/shard_map/ppermute | solution.py:22
  13.8 4.3 %collective-permute-start.10 = (f32[32,512]{1,0:T(8,128)S(1)}, f32[32,512]{1,0:T(8,128)S(1)}, u32[]{:S(2)}, u32[]{:S(2)}) collective-permute-start(f32[32,512]{1,0:T(8,128)S(1)} %get-tuple-element.114), channel_id=1, source_target_pairs={{0,4},{1,5},{2,6},{3,7},{4,0},{5,1},{6,2},{7,3},{8,12},{9,13},{10,... | collective-permute-start | bytes 196616 | tf_op jit(solution)/shard_map/ppermute | solution.py:22
  14.1 8.3 %collective-permute-start.6 = (f32[200,256]{1,0:T(8,128)S(1)}, f32[200,256]{1,0:T(8,128)S(1)}, u32[]{:S(2)}, u32[]{:S(2)}) collective-permute-start(f32[200,256]{1,0:T(8,128)S(1)} %get-tuple-element.109.carry_ref), channel_id=1, source_target_pairs={{8,0},{9,1},{10,2},{11,3},{12,4},{13,5},{14,6},{15,7},{24,16},{25,... | collective-permute-start | bytes 614408 | tf_op jit(solution)/shard_map/ppermute | solution.py:34
  16.2 2.2 %collective-permute-start.7 = (f32[200,256]{1,0:T(8,128)S(1)}, f32[200,256]{1,0:T(8,128)S(1)}, u32[]{:S(2)}, u32[]{:S(2)}) collective-permute-start(f32[200,256]{1,0:T(8,128)S(1)} %get-tuple-element.110.half_ref), channel_id=1, source_target_pairs={{0,1},{1,0},{2,3},{3,2},{4,5},{5,4},{6,7},{7,6},{8,9},{9,8},{10,11... | collective-permute-start | bytes 614408 | tf_op jit(solution)/shard_map/ppermute | solution.py:22
  18.6 5.2 %collective-permute-start.12 = (f32[32,512]{1,0:T(8,128)S(1)}, f32[32,512]{1,0:T(8,128)S(1)}, u32[]{:S(2)}, u32[]{:S(2)}) collective-permute-start(f32[32,512]{1,0:T(8,128)S(1)} %shard_map.106.up_ref), channel_id=1, source_target_pairs={{0,8},{1,9},{2,10},{3,11},{4,12},{5,13},{6,14},{7,15},{8,0},{9,1},... | collective-permute-start | bytes 196616 | tf_op jit(solution)/shard_map/ppermute | solution.py:22
  20.7 13.0 %collective-permute-start.19 = (f32[160,640]{1,0:T(8,128)S(1)}, f32[160,640]{1,0:T(8,128)S(1)}, u32[]{:S(2)}, u32[]{:S(2)}) collective-permute-start(f32[160,640]{1,0:T(8,128)S(1)} %get-tuple-element.161), channel_id=1, source_target_pairs={{0,2},{1,3},{2,0},{3,1},{4,6},{5,7},{6,4},{7,5},{8,10},{9,11},{10,... | collective-permute-start | bytes 1228808 | tf_op jit(solution)/shard_map/ppermute | solution.py:22
  22.5 1.5 %collective-permute-start.13 = (f32[200,256]{1,0:T(8,128)S(1)}, f32[200,256]{1,0:T(8,128)S(1)}, u32[]{:S(2)}, u32[]{:S(2)}) collective-permute-start(f32[200,256]{1,0:T(8,128)S(1)} %get-tuple-element.131.half_ref), channel_id=1, source_target_pairs={{0,1},{1,0},{2,3},{3,2},{4,5},{5,4},{6,7},{7,6},{8,9},{9,8},{10,11... | collective-permute-start | bytes 614408 | tf_op jit(solution)/shard_map/ppermute | solution.py:22
  22.5 4.7 %collective-permute-start.11 = (f32[72,256]{1,0:T(8,128)S(1)}, f32[72,256]{1,0:T(8,128)S(1)}, u32[]{:S(2)}, u32[]{:S(2)}) collective-permute-start(f32[72,256]{1,0:T(8,128)S(1)} %get-tuple-element.128.root_ref), channel_id=1, source_target_pairs={{0,8},{1,9},{2,10},{3,11},{4,12},{5,13},{6,14},{7,15},{8,0},{9,1},... | collective-permute-start | bytes 221192 | tf_op jit(solution)/shard_map/ppermute | solution.py:22
  24.2 5.2 %collective-permute-start.15 = (f32[32,256]{1,0:T(8,128)S(1)}, f32[32,256]{1,0:T(8,128)S(1)}, u32[]{:S(2)}, u32[]{:S(2)}) collective-permute-start(f32[32,256]{1,0:T(8,128)S(1)} %shard_map.109.up_ref), channel_id=1, source_target_pairs={{0,16},{1,17},{2,18},{3,19},{4,20},{5,21},{6,22},{7,23},{8,24},{9,... | collective-permute-start | bytes 98312 | tf_op jit(solution)/shard_map/ppermute | solution.py:22
  27.3 2.1 %collective-permute-start.14 = (f32[72,256]{1,0:T(8,128)S(1)}, f32[72,256]{1,0:T(8,128)S(1)}, u32[]{:S(2)}, u32[]{:S(2)}) collective-permute-start(f32[72,256]{1,0:T(8,128)S(1)} %shard_map.111.root_ref), channel_id=1, source_target_pairs={{0,1},{1,0},{2,3},{3,2},{4,5},{5,4},{6,7},{7,6},{8,9},{9,8},{10,11... | collective-permute-start | bytes 221192 | tf_op jit(solution)/shard_map/ppermute | solution.py:22
  30.1 5.3 %collective-permute-start.16 = (f32[32,512]{1,0:T(8,128)S(1)}, f32[32,512]{1,0:T(8,128)S(1)}, u32[]{:S(2)}, u32[]{:S(2)}) collective-permute-start(f32[32,512]{1,0:T(8,128)S(1)} %get-tuple-element.155), channel_id=1, source_target_pairs={{0,6},{1,7},{2,4},{3,5},{4,2},{5,3},{6,0},{7,1},{8,14},{9,15},{10,... | collective-permute-start | bytes 196616 | tf_op jit(solution)/shard_map/ppermute | solution.py:22
  32.5 4.3 %collective-permute-start.17 = (f32[32,512]{1,0:T(8,128)S(1)}, f32[32,512]{1,0:T(8,128)S(1)}, u32[]{:S(2)}, u32[]{:S(2)}) collective-permute-start(f32[32,512]{1,0:T(8,128)S(1)} %get-tuple-element.156), channel_id=1, source_target_pairs={{0,2},{1,3},{2,0},{3,1},{4,6},{5,7},{6,4},{7,5},{8,10},{9,11},{10,... | collective-permute-start | bytes 196616 | tf_op jit(solution)/shard_map/ppermute | solution.py:22
  33.2 4.3 %collective-permute-start.18 = (f32[32,512]{1,0:T(8,128)S(1)}, f32[32,512]{1,0:T(8,128)S(1)}, u32[]{:S(2)}, u32[]{:S(2)}) collective-permute-start(f32[32,512]{1,0:T(8,128)S(1)} %get-tuple-element.157), channel_id=1, source_target_pairs={{0,4},{1,5},{2,6},{3,7},{4,0},{5,1},{6,2},{7,3},{8,12},{9,13},{10,... | collective-permute-start | bytes 196616 | tf_op jit(solution)/shard_map/ppermute | solution.py:22
  37.5 1.6 %collective-permute-start.20 = (f32[128,512]{1,0:T(8,128)S(1)}, f32[128,512]{1,0:T(8,128)S(1)}, u32[]{:S(2)}, u32[]{:S(2)}) collective-permute-start(f32[128,512]{1,0:T(8,128)S(1)} %shard_map.117.group_ref), channel_id=1, source_target_pairs={{0,1},{1,0},{2,3},{3,2},{4,5},{5,4},{6,7},{7,6},{8,9},{9,8},{10,11... | collective-permute-start | bytes 786440 | tf_op jit(solution)/shard_map/ppermute | solution.py:22
  37.6 1.6 %collective-permute-start.21 = (f32[160,128]{1,0:T(8,128)S(1)}, f32[160,128]{1,0:T(8,128)S(1)}, u32[]{:S(2)}, u32[]{:S(2)}) collective-permute-start(f32[160,128]{1,0:T(8,128)S(1)} %get-tuple-element.173), channel_id=1, source_target_pairs={{0,1},{1,0},{2,3},{3,2},{4,5},{5,4},{6,7},{7,6},{8,9},{9,8},{10,11... | collective-permute-start | bytes 245768 | tf_op jit(solution)/shard_map/ppermute | solution.py:22

commit v12 on v11

--- a/solution.py
+++ b/solution.py
@@ -521,13 +521,14 @@
     beyond = swap(to_far, 0, 2)
     side = swap(to_odd, 1, 0)
 
-    def last_left(own_ref, chip_ref, y_ref, far_ref, left_ref, keep_ref, pass_ref):
+    def last_left(own_ref, chip_ref, y_ref, far_ref, high_ref, low_ref, keep_ref, pass_ref, left_ref):
         near_bit = place()[4]
         left_ref[:rows, :updates] = -(own_ref[...] + far_ref[:, :updates])
         left_ref[:rows, updates:] = jnp.zeros((rows, 2 * quarter), f32)
         row = lax.broadcasted_iota(jnp.int32, (quarter, width), 0)
         lane = lax.broadcasted_iota(jnp.int32, (quarter, width), 1)
         left_ref[rows:] = jnp.where(lane == updates + near_bit * quarter + row, 1.0, 0.0)
+        high_ref[...], low_ref[...] = pieces_of(left_ref[...])
         turned_y = dot3(chip_ref[...], y_ref[...], 0, 0)
         first = turned_y[:rows] + far_ref[:, updates : updates + half]
         second = turned_y[rows:] + far_ref[:, updates + half :]
@@ -535,8 +536,9 @@
         pass_ref[...] = by_bit(near_bit, second, first)
 
     from_far, stay = after(from_far, stay)
-    left, base_keep, base_pass = stage(
-        last_left, [(rows + quarter, width), (rows, half), (rows, half)], own_sum, inverse_chip, leaf_y, from_far
+    left_pieces = jax.ShapeDtypeStruct((rows + quarter, width), bf16)
+    left, left_low, base_keep, base_pass = stage(
+        last_left, [left_pieces, left_pieces, (rows, half), (rows, half)], own_sum, inverse_chip, leaf_y, from_far, scratch=[(rows + quarter, width)]
     )
     both, beyond, side, left = after(both, beyond, side, left)
 
@@ -550,16 +552,21 @@
     base_near = swap(base_pass, 0, 1)
     group_near = swap(group, 0, 1)
 
-    def own_columns(left_ref, group_ref, out_ref):
-        out_ref[...] = dot3(left_ref[...], group_ref[...], 1, 1)
-
-    (ours,) = stage(own_columns, [(rows + quarter, half)], left, group)
+    def last_product(high_ref, low_ref, group_ref):
+        high, low = pieces_of(group_ref[...])
+        small = product(high_ref[...], low, 1, 1) + product(low_ref[...], high, 1, 1)
+        return product(high_ref[...], high, 1, 1) + small
+
+    def own_columns(high_ref, low_ref, group_ref, out_ref):
+        out_ref[...] = last_product(high_ref, low_ref, group_ref)
+
+    (ours,) = stage(own_columns, [(rows + quarter, half)], left, left_low, group)
     group_near, ours = after(group_near, ours)
 
-    def finish(left_ref, group_ref, ours_ref, base_ref, base_near_ref, leaf_ref, rows_ref):
+    def finish(high_ref, low_ref, group_ref, ours_ref, base_ref, base_near_ref, leaf_ref, rows_ref):
         near_bit = place()[4]
         ours = ours_ref[...]
-        theirs = dot3(left_ref[...], group_ref[...], 1, 1)
+        theirs = last_product(high_ref, low_ref, group_ref)
         ours_x, theirs_x = base_ref[...] + ours[:rows], base_near_ref[...] + theirs[:rows]
         leaf_ref[:, :half] = by_bit(near_bit, ours_x, theirs_x)
         leaf_ref[:, half:] = by_bit(near_bit, theirs_x, ours_x)
@@ -570,6 +577,7 @@
         finish,
         [(rows, columns), (quarter, columns)],
         left,
+        left_low,
         group_near,
         ours,
         base_keep,

time: 40.4 us -> 40.4 us (level)
  no operation moved by 1% of the time
where the time goes in v12:
time: 40.4 us; the launch traced here: 40.2 us
  starting transfers between devices  22.2 us (55%)
  waiting for transfers between devices  8.15 us (20%)
  Pallas kernels  7.98 us (20%)
  local copies, waits for them, and re-layouts  0.95 us (2%)
  between operations  0.93 us (2%)
    ppermute x21, starting transfers between devices, swap(): return lax.ppermute(payload, axes, pairs)  20.9 us
    ppermute x21, waiting for transfers between devices, swap(): return lax.ppermute(payload, axes, pairs)  8.15 us
    pallas_call x25, Pallas kernels, stage(): pl.pallas_call(body, out_shape=[jax.ShapeDtypeStruct(shape, f32) if isins...  7.98 us
    ppermute x1, starting transfers between devices, quarter_swap(): return lax.ppermute(payload, axes, pairs)  1.29 us
    unnamed x16, local copies, waits for them, and re-layouts  0.95 us
  transfers between devices with their start and end apart: 22, of which 10 were waited for; matrix products, arithmetic and copies ran while one was open for 0% of the time, Pallas kernels for 17%

profile of v12, /device:TPU:0, one launch (start us, length us, event | category | flops | bytes accessed | tf_op | source)
XLA Modules:
  0.0 40.2 jit_solution(5346578634223265740)
XLA Ops:
  0.6 0.5 %collective-permute-start.1 = (f32[160,256]{1,0:T(8,128)}, f32[160,256]{1,0:T(8,128)S(1)}, u32[]{:S(2)}, u32[]{:S(2)}) collective-permute-start(f32[160,256]{1,0:T(8,128)} %bitcast.14), channel_id=1, source_target_pairs={{0,1},{1,0},{2,3},{3,2},{4,5},{5,4},{6,7},{7,6},{8,9},{9,8},{10,11... | collective-permute-start | bytes 491528 | tf_op jit(solution)/shard_map/ppermute | solution.py:22
  1.2 0.1 collective-permute-start.4
  1.2 0.4 %collective-permute-start = (f32[160,640]{1,0:T(8,128)}, f32[160,640]{1,0:T(8,128)S(1)}, u32[]{:S(2)}, u32[]{:S(2)}) collective-permute-start(f32[160,640]{1,0:T(8,128)} %bitcast.10), channel_id=1, source_target_pairs={{0,1},{1,0},{2,3},{3,2},{4,5},{5,4},{6,7},{7,6},{8,9},{9,8},{10,11... | collective-permute-start | bytes 1228808 | tf_op jit(solution)/shard_map/ppermute | solution.py:22
  1.7 0.9 %copy-done.2 = f32[1,160,256]{2,1,0:T(8,128)S(1)} copy-done((f32[1,160,256]{2,1,0:T(8,128)S(1)}, f32[1,160,256]{2,1,0:T(8,128)}, u32[]{:S(2)}) %copy-start.2) | copy-done | bytes 163864
  2.7 2.6 %collective-permute-start.5 = (f32[320,128]{1,0:T(8,128)S(1)}, f32[320,128]{1,0:T(8,128)S(1)}, u32[]{:S(2)}, u32[]{:S(2)}) collective-permute-start(f32[320,128]{1,0:T(8,128)S(1)} %shard_map.96.chip_ref), channel_id=1, source_target_pairs={{0,2},{1,3},{2,0},{3,1},{4,6},{5,7},{6,4},{7,5},{8,10},{9,11},{10,... | collective-permute-start | bytes 491528 | tf_op jit(solution)/shard_map/ppermute | solution.py:22
  5.4 0.4 shard_map.97.carry_ref.own_ref
  5.7 1.6 %collective-permute-start.2 = (f32[208,256]{1,0:T(8,128)S(1)}, f32[208,256]{1,0:T(8,128)S(1)}, u32[]{:S(2)}, u32[]{:S(2)}) collective-permute-start(f32[208,256]{1,0:T(8,128)S(1)} %shard_map.97.carry_ref.own_ref), channel_id=1, source_target_pairs={{0,4},{1,5},{2,6},{3,7},{4,0},{5,1},{6,2},{7,3},{8,12},{9,13},{10,... | collective-permute-start | bytes 638984 | tf_op jit(solution)/shard_map/ppermute | solution.py:22
  7.4 0.6 %shard_map.98 = (f32[320,128]{1,0:T(8,128)S(1)}, f32[320,320]{1,0:T(8,128)S(1)}, f32[320,320]{1,0:T(8,128)S(1)}, f32[320,160]{1,0:T(8,128)S(1)}, f32[320,384]{1,0:T(8,128)S(1)}) custom-call(f32[160,640]{1,0:T(8,128)S(1)} %bitcast.11, f32[160,640]{1,0:T(8,128)S(1)} %collective-permute-done.inverse_near_ref, f32[160,384]{1,0:T(8,128)S(1)} %bitcast.13, ...), custom_call_target="tpu_custom_call" | custom-call | tf_op jit(solution)/shard_map/pallas_call | solution.py:75
  8.0 1.1 %shard_map.99 = (f32[320,384]{1,0:T(8,128)S(1)}, f32[160,384]{1,0:T(8,128)S(1)}, f32[128,384]{1,0:T(8,128)S(1)}) custom-call(f32[320,320]{1,0:T(8,128)S(1)} %get-tuple-element.97.far_ref.inverse_far_ref, f32[320,160]{1,0:T(8,128)S(1)} %get-tuple-element.98.mine_ref, f32[320,384]{1,0:T(8,128)S(1)} %get-tuple-element.99.update_ref, ...), custom_call_target="tpu_custom_call" | custom-call | tf_op jit(solution)/shard_map/pallas_call | solution.py:75
  9.1 0.2 shard_map.100.turned_ref
  9.3 0.8 %collective-permute-done.5.far_ref = f32[320,128]{1,0:T(8,128)S(1)} collective-permute-done((f32[320,128]{1,0:T(8,128)S(1)}, f32[320,128]{1,0:T(8,128)S(1)}, u32[]{:S(2)}, u32[]{:S(2)}) %collective-permute-start.5) | collective-permute-done | bytes 163872 | tf_op jit(solution)/shard_map/ppermute | solution.py:22
  10.1 0.4 shard_map.101
  10.5 2.8 %collective-permute-start.8 = (f32[32,512]{1,0:T(8,128)S(1)}, f32[32,512]{1,0:T(8,128)S(1)}, u32[]{:S(2)}, u32[]{:S(2)}) collective-permute-start(f32[32,512]{1,0:T(8,128)S(1)} %get-tuple-element.113), channel_id=1, source_target_pairs={{0,6},{1,7},{2,4},{3,5},{4,2},{5,3},{6,0},{7,1},{8,14},{9,15},{10,... | collective-permute-start | bytes 196616 | tf_op jit(solution)/shard_map/ppermute | solution.py:22
  13.3 0.5 %collective-permute-start.9 = (f32[32,512]{1,0:T(8,128)S(1)}, f32[32,512]{1,0:T(8,128)S(1)}, u32[]{:S(2)}, u32[]{:S(2)}) collective-permute-start(f32[32,512]{1,0:T(8,128)S(1)} %get-tuple-element.114), channel_id=1, source_target_pairs={{0,2},{1,3},{2,0},{3,1},{4,6},{5,7},{6,4},{7,5},{8,10},{9,11},{10,... | collective-permute-start | bytes 196616 | tf_op jit(solution)/shard_map/ppermute | solution.py:22
  13.8 0.2 collective-permute-start.10
  14.1 1.3 %collective-permute-start.6 = (f32[200,256]{1,0:T(8,128)S(1)}, f32[200,256]{1,0:T(8,128)S(1)}, u32[]{:S(2)}, u32[]{:S(2)}) collective-permute-start(f32[200,256]{1,0:T(8,128)S(1)} %get-tuple-element.110.carry_ref), channel_id=1, source_target_pairs={{8,0},{9,1},{10,2},{11,3},{12,4},{13,5},{14,6},{15,7},{24,16},{25,... | collective-permute-start | bytes 614408 | tf_op jit(solution)/shard_map/ppermute | solution.py:34
  15.4 0.1 shard_map.103.hot_ref
  15.5 0.7 %shard_map.104 = (f32[320,128]{1,0:T(8,128)S(1)}, f32[160,640]{1,0:T(8,128)S(1)}) custom-call(f32[320,320]{1,0:T(8,128)S(1)} %get-tuple-element.97.far_ref.inverse_far_ref, f32[320,128]{1,0:T(8,128)S(1)} %get-tuple-element.117.y_ref.own_y_ref, f32[320,128]{1,0:T(8,128)S(1)} %collective-permute-done.5.far_ref, f32[320,384]{1,0:T(8,128)S(1)} %get-tuple-element.103.turned_far_ref), custom_call_target="tpu_custom_call" | custom-call | tf_op jit(solution)/shard_map/pallas_call | solution.py:75
  16.2 0.1 collective-permute-start.7
  16.3 1.3 %collective-permute-done.9.far_ref = f32[32,512]{1,0:T(8,128)S(1)} collective-permute-done((f32[32,512]{1,0:T(8,128)S(1)}, f32[32,512]{1,0:T(8,128)S(1)}, u32[]{:S(2)}, u32[]{:S(2)}) %collective-permute-start.9) | collective-permute-done | bytes 65568 | tf_op jit(solution)/shard_map/ppermute | solution.py:22
  17.6 0.5 %collective-permute-done.10.odd_ref = f32[32,512]{1,0:T(8,128)S(1)} collective-permute-done((f32[32,512]{1,0:T(8,128)S(1)}, f32[32,512]{1,0:T(8,128)S(1)}, u32[]{:S(2)}, u32[]{:S(2)}) %collective-permute-start.10) | collective-permute-done | bytes 65568 | tf_op jit(solution)/shard_map/ppermute | solution.py:22
  18.1 0.3 shard_map.105
  18.4 0.2 shard_map.106.up_ref
  18.6 2.1 %collective-permute-start.12 = (f32[32,512]{1,0:T(8,128)S(1)}, f32[32,512]{1,0:T(8,128)S(1)}, u32[]{:S(2)}, u32[]{:S(2)}) collective-permute-start(f32[32,512]{1,0:T(8,128)S(1)} %shard_map.106.up_ref), channel_id=1, source_target_pairs={{0,8},{1,9},{2,10},{3,11},{4,12},{5,13},{6,14},{7,15},{8,0},{9,1},... | collective-permute-start | bytes 196616 | tf_op jit(solution)/shard_map/ppermute | solution.py:22
  20.7 1.8 %collective-permute-start.19 = (f32[160,640]{1,0:T(8,128)S(1)}, f32[160,640]{1,0:T(8,128)S(1)}, u32[]{:S(2)}, u32[]{:S(2)}) collective-permute-start(f32[160,640]{1,0:T(8,128)S(1)} %get-tuple-element.162), channel_id=1, source_target_pairs={{0,2},{1,3},{2,0},{3,1},{4,6},{5,7},{6,4},{7,5},{8,10},{9,11},{10,... | collective-permute-start | bytes 1228808 | tf_op jit(solution)/shard_map/ppermute | solution.py:22
  22.5 0.1 collective-permute-start.13
  22.5 1.3 %collective-permute-start.11 = (f32[72,256]{1,0:T(8,128)S(1)}, f32[72,256]{1,0:T(8,128)S(1)}, u32[]{:S(2)}, u32[]{:S(2)}) collective-permute-start(f32[72,256]{1,0:T(8,128)S(1)} %get-tuple-element.129.root_ref), channel_id=1, source_target_pairs={{0,8},{1,9},{2,10},{3,11},{4,12},{5,13},{6,14},{7,15},{8,0},{9,1},... | collective-permute-start | bytes 221192 | tf_op jit(solution)/shard_map/ppermute | solution.py:22
  23.8 0.1 collective-permute-done.13.near_ref
  24.0 0.2 shard_map.109.up_ref
  24.2 2.7 %collective-permute-start.15 = (f32[32,256]{1,0:T(8,128)S(1)}, f32[32,256]{1,0:T(8,128)S(1)}, u32[]{:S(2)}, u32[]{:S(2)}) collective-permute-start(f32[32,256]{1,0:T(8,128)S(1)} %shard_map.109.up_ref), channel_id=1, source_target_pairs={{0,16},{1,17},{2,18},{3,19},{4,20},{5,21},{6,22},{7,23},{8,24},{9,... | collective-permute-start | bytes 98312 | tf_op jit(solution)/shard_map/ppermute | solution.py:22
  26.9 0.4 shard_map.110
  27.3 0.1 collective-permute-start.14
  27.4 0.4 shard_map.112
  27.7 0.4 shard_map.113
  28.1 1.2 %collective-permute-done.15.partner_ref = f32[32,256]{1,0:T(8,128)S(1)} collective-permute-done((f32[32,256]{1,0:T(8,128)S(1)}, f32[32,256]{1,0:T(8,128)S(1)}, u32[]{:S(2)}, u32[]{:S(2)}) %collective-permute-start.15) | collective-permute-done | bytes 32800 | tf_op jit(solution)/shard_map/ppermute | solution.py:22
  29.4 0.7 %shard_map.115 = (f32[32,512]{1,0:T(8,128)S(1)}, f32[32,512]{1,0:T(8,128)S(1)}, f32[32,512]{1,0:T(8,128)S(1)}, f32[32,512]{1,0:T(8,128)S(1)}) custom-call(f32[32,256]{1,0:T(8,128)S(1)} %shard_map.114.residual_ref, f32[72,256]{1,0:T(8,128)S(1)} %shard_map.111.root_ref, f32[72,256]{1,0:T(8,128)S(1)} %collective-permute-done.14.root_near_ref, ...), custom_call_target="tpu_custom_call" | custom-call | tf_op jit(solution)/shard_map/pallas_call | solution.py:75
  30.1 2.4 %collective-permute-start.16 = (f32[32,512]{1,0:T(8,128)S(1)}, f32[32,512]{1,0:T(8,128)S(1)}, u32[]{:S(2)}, u32[]{:S(2)}) collective-permute-start(f32[32,512]{1,0:T(8,128)S(1)} %get-tuple-element.156), channel_id=1, source_target_pairs={{0,6},{1,7},{2,4},{3,5},{4,2},{5,3},{6,0},{7,1},{8,14},{9,15},{10,... | collective-permute-start | bytes 196616 | tf_op jit(solution)/shard_map/ppermute | solution.py:22
  32.5 0.6 %collective-permute-start.17 = (f32[32,512]{1,0:T(8,128)S(1)}, f32[32,512]{1,0:T(8,128)S(1)}, u32[]{:S(2)}, u32[]{:S(2)}) collective-permute-start(f32[32,512]{1,0:T(8,128)S(1)} %get-tuple-element.157), channel_id=1, source_target_pairs={{0,2},{1,3},{2,0},{3,1},{4,6},{5,7},{6,4},{7,5},{8,10},{9,11},{10,... | collective-permute-start | bytes 196616 | tf_op jit(solution)/shard_map/ppermute | solution.py:22
  33.2 0.5 %collective-permute-start.18 = (f32[32,512]{1,0:T(8,128)S(1)}, f32[32,512]{1,0:T(8,128)S(1)}, u32[]{:S(2)}, u32[]{:S(2)}) collective-permute-start(f32[32,512]{1,0:T(8,128)S(1)} %get-tuple-element.158), channel_id=1, source_target_pairs={{0,4},{1,5},{2,6},{3,7},{4,0},{5,1},{6,2},{7,3},{8,12},{9,13},{10,... | collective-permute-start | bytes 196616 | tf_op jit(solution)/shard_map/ppermute | solution.py:22
  33.7 0.4 %shard_map.116 = (bf16[224,512]{1,0:T(8,128)(2,1)S(1)}, bf16[224,512]{1,0:T(8,128)(2,1)S(1)}, f32[160,128]{1,0:T(8,128)S(1)}, f32[160,128]{1,0:T(8,128)S(1)}) custom-call(f32[160,384]{1,0:T(8,128)S(1)} %get-tuple-element.159.own_ref, f32[320,320]{1,0:T(8,128)S(1)} %get-tuple-element.160.chip_ref, f32[320,128]{1,0:T(8,128)S(1)} %get-tuple-element.161.y_ref, ...), custom_call_target="tpu_custom_call" | custom-call | tf_op jit(solution)/shard_map/pallas_call | solution.py:75
  34.1 1.3 %collective-permute-done.16.refs_3_ = f32[32,512]{1,0:T(8,128)S(1)} collective-permute-done((f32[32,512]{1,0:T(8,128)S(1)}, f32[32,512]{1,0:T(8,128)S(1)}, u32[]{:S(2)}, u32[]{:S(2)}) %collective-permute-start.16) | collective-permute-done | bytes 65568 | tf_op jit(solution)/shard_map/ppermute | solution.py:22
  35.5 1.4 %collective-permute-done.17.refs_1_ = f32[32,512]{1,0:T(8,128)S(1)} collective-permute-done((f32[32,512]{1,0:T(8,128)S(1)}, f32[32,512]{1,0:T(8,128)S(1)}, u32[]{:S(2)}, u32[]{:S(2)}) %collective-permute-start.17) | collective-permute-done | bytes 65568 | tf_op jit(solution)/shard_map/ppermute | solution.py:22
  36.8 0.6 %collective-permute-done.18.refs_2_ = f32[32,512]{1,0:T(8,128)S(1)} collective-permute-done((f32[32,512]{1,0:T(8,128)S(1)}, f32[32,512]{1,0:T(8,128)S(1)}, u32[]{:S(2)}, u32[]{:S(2)}) %collective-permute-start.18) | collective-permute-done | bytes 65568 | tf_op jit(solution)/shard_map/ppermute | solution.py:22
  37.6 0.5 %collective-permute-start.21 = (f32[160,128]{1,0:T(8,128)S(1)}, f32[160,128]{1,0:T(8,128)S(1)}, u32[]{:S(2)}, u32[]{:S(2)}) collective-permute-start(f32[160,128]{1,0:T(8,128)S(1)} %get-tuple-element.175), channel_id=1, source_target_pairs={{0,1},{1,0},{2,3},{3,2},{4,5},{5,4},{6,7},{7,6},{8,9},{9,8},{10,11... | collective-permute-start | bytes 245768 | tf_op jit(solution)/shard_map/ppermute | solution.py:22
  38.1 0.3 shard_map.118.ours_ref
  38.4 0.7 %collective-permute-done.20.group_ref = f32[128,512]{1,0:T(8,128)S(1)} collective-permute-done((f32[128,512]{1,0:T(8,128)S(1)}, f32[128,512]{1,0:T(8,128)S(1)}, u32[]{:S(2)}, u32[]{:S(2)}) %collective-permute-start.20) | collective-permute-done | bytes 262176 | tf_op jit(solution)/shard_map/ppermute | solution.py:22
  39.1 0.1 collective-permute-done.21.base_near_ref
  39.2 1.0 %shard_map.119 = (f32[160,256]{1,0:T(8,128)}, f32[64,256]{1,0:T(8,128)}) custom-call(bf16[224,512]{1,0:T(8,128)(2,1)S(1)} %get-tuple-element.166.high_ref, bf16[224,512]{1,0:T(8,128)(2,1)S(1)} %get-tuple-element.167.low_ref, f32[128,512]{1,0:T(8,128)S(1)} %collective-permute-done.20.group_ref, f32[224,128]{1,0:T(8,128)S(1)} %shard_map.118.ours_ref, ...), custom_call_target="tpu_custom_call" | custom-call | tf_op jit(solution)/shard_map/pallas_call | solution.py:75
  (38 shorter events, 0.4 us)
Async XLA Ops:
  0.6 2.0 %copy-start.7 = (s32[1,3]{1,0:T(1,128)S(1)}, s32[1,3]{1,0:T(1,128)}, u32[]{:S(2)}) copy-start(s32[1,3]{1,0:T(1,128)} %param.12) | copy-start | bytes 40
  0.6 2.0 %collective-permute-start.1 = (f32[160,256]{1,0:T(8,128)}, f32[160,256]{1,0:T(8,128)S(1)}, u32[]{:S(2)}, u32[]{:S(2)}) collective-permute-start(f32[160,256]{1,0:T(8,128)} %bitcast.14), channel_id=1, source_target_pairs={{0,1},{1,0},{2,3},{3,2},{4,5},{5,4},{6,7},{7,6},{8,9},{9,8},{10,11... | collective-permute-start | bytes 491528 | tf_op jit(solution)/shard_map/ppermute | solution.py:22
  1.2 6.2 %collective-permute-start.4 = (f32[160,384]{1,0:T(8,128)}, f32[160,384]{1,0:T(8,128)S(1)}, u32[]{:S(2)}, u32[]{:S(2)}) collective-permute-start(f32[160,384]{1,0:T(8,128)} %bitcast.12), channel_id=1, source_target_pairs={{0,1},{1,0},{2,3},{3,2},{4,5},{5,4},{6,7},{7,6},{8,9},{9,8},{10,11... | collective-permute-start | bytes 737288 | tf_op jit(solution)/shard_map/ppermute | solution.py:22
  1.2 1.4 %copy-start.6 = (s32[1,384]{1,0:T(1,128)S(1)}, s32[1,384]{1,0:T(1,128)}, u32[]{:S(2)}) copy-start(s32[1,384]{1,0:T(1,128)} %param.11) | copy-start | bytes 4612
  1.2 6.1 %collective-permute-start = (f32[160,640]{1,0:T(8,128)}, f32[160,640]{1,0:T(8,128)S(1)}, u32[]{:S(2)}, u32[]{:S(2)}) collective-permute-start(f32[160,640]{1,0:T(8,128)} %bitcast.10), channel_id=1, source_target_pairs={{0,1},{1,0},{2,3},{3,2},{4,5},{5,4},{6,7},{7,6},{8,9},{9,8},{10,11... | collective-permute-start | bytes 1228808 | tf_op jit(solution)/shard_map/ppermute | solution.py:22
  1.7 0.9 %copy-start.2 = (f32[1,160,256]{2,1,0:T(8,128)S(1)}, f32[1,160,256]{2,1,0:T(8,128)}, u32[]{:S(2)}) copy-start(f32[1,160,256]{2,1,0:T(8,128)} %param.8) | copy-start | bytes 491524
  2.6 2.8 %copy-start.5 = (f32[1,256,256]{2,1,0:T(8,128)S(1)}, f32[1,256,256]{2,1,0:T(8,128)}, u32[]{:S(2)}) copy-start(f32[1,256,256]{2,1,0:T(8,128)} %param.14) | copy-start | bytes 786436
  2.6 2.7 %copy-start.4 = (f32[1,256,256]{2,1,0:T(8,128)S(1)}, f32[1,256,256]{2,1,0:T(8,128)}, u32[]{:S(2)}) copy-start(f32[1,256,256]{2,1,0:T(8,128)} %param.15) | copy-start | bytes 786436
  2.7 7.4 %collective-permute-start.5 = (f32[320,128]{1,0:T(8,128)S(1)}, f32[320,128]{1,0:T(8,128)S(1)}, u32[]{:S(2)}, u32[]{:S(2)}) collective-permute-start(f32[320,128]{1,0:T(8,128)S(1)} %shard_map.96.chip_ref), channel_id=1, source_target_pairs={{0,2},{1,3},{2,0},{3,1},{4,6},{5,7},{6,4},{7,5},{8,10},{9,11},{10,... | collective-permute-start | bytes 491528 | tf_op jit(solution)/shard_map/ppermute | solution.py:22
  5.3 2.0 %copy-start.3 = (f32[1,64,256]{2,1,0:T(8,128)S(1)}, f32[1,64,256]{2,1,0:T(8,128)}, u32[]{:S(2)}) copy-start(f32[1,64,256]{2,1,0:T(8,128)} %param.13) | copy-start | bytes 196612
  5.3 2.0 %copy-start = (f32[1,160,640]{2,1,0:T(8,128)S(1)}, f32[1,160,640]{2,1,0:T(8,128)}, u32[]{:S(2)}) copy-start(f32[1,160,640]{2,1,0:T(8,128)} %param.9) | copy-start | bytes 1228804
  5.4 2.0 %copy-start.1 = (f32[1,384,160]{1,2,0:T(8,128)S(1)}, f32[1,384,160]{1,2,0:T(8,128)}, u32[]{:S(2)}) copy-start(f32[1,384,160]{1,2,0:T(8,128)} %param.10) | copy-start | bytes 737284
  5.7 8.3 %collective-permute-start.2 = (f32[208,256]{1,0:T(8,128)S(1)}, f32[208,256]{1,0:T(8,128)S(1)}, u32[]{:S(2)}, u32[]{:S(2)}) collective-permute-start(f32[208,256]{1,0:T(8,128)S(1)} %shard_map.97.carry_ref.own_ref), channel_id=1, source_target_pairs={{0,4},{1,5},{2,6},{3,7},{4,0},{5,1},{6,2},{7,3},{8,12},{9,13},{10,... | collective-permute-start | bytes 638984 | tf_op jit(solution)/shard_map/ppermute | solution.py:22
  7.3 1.8 %collective-permute-start.3 = (f32[64,256]{1,0:T(8,128)S(1)}, f32[64,256]{1,0:T(8,128)S(1)}, u32[]{:S(2)}, u32[]{:S(2)}) collective-permute-start(f32[64,256]{1,0:T(8,128)S(1)} %bitcast.16), channel_id=1, source_target_pairs={{0,1},{1,0},{2,3},{3,2},{4,5},{5,4},{6,7},{7,6},{8,9},{9,8},{10,11... | collective-permute-start | bytes 196616 | tf_op jit(solution)/shard_map/ppermute | solution.py:22
  10.5 5.8 %collective-permute-start.8 = (f32[32,512]{1,0:T(8,128)S(1)}, f32[32,512]{1,0:T(8,128)S(1)}, u32[]{:S(2)}, u32[]{:S(2)}) collective-permute-start(f32[32,512]{1,0:T(8,128)S(1)} %get-tuple-element.113), channel_id=1, source_target_pairs={{0,6},{1,7},{2,4},{3,5},{4,2},{5,3},{6,0},{7,1},{8,14},{9,15},{10,... | collective-permute-start | bytes 196616 | tf_op jit(solution)/shard_map/ppermute | solution.py:22
  13.3 4.3 %collective-permute-start.9 = (f32[32,512]{1,0:T(8,128)S(1)}, f32[32,512]{1,0:T(8,128)S(1)}, u32[]{:S(2)}, u32[]{:S(2)}) collective-permute-start(f32[32,512]{1,0:T(8,128)S(1)} %get-tuple-element.114), channel_id=1, source_target_pairs={{0,2},{1,3},{2,0},{3,1},{4,6},{5,7},{6,4},{7,5},{8,10},{9,11},{10,... | collective-permute-start | bytes 196616 | tf_op jit(solution)/shard_map/ppermute | solution.py:22
  13.8 4.3 %collective-permute-start.10 = (f32[32,512]{1,0:T(8,128)S(1)}, f32[32,512]{1,0:T(8,128)S(1)}, u32[]{:S(2)}, u32[]{:S(2)}) collective-permute-start(f32[32,512]{1,0:T(8,128)S(1)} %get-tuple-element.115), channel_id=1, source_target_pairs={{0,4},{1,5},{2,6},{3,7},{4,0},{5,1},{6,2},{7,3},{8,12},{9,13},{10,... | collective-permute-start | bytes 196616 | tf_op jit(solution)/shard_map/ppermute | solution.py:22
  14.1 8.3 %collective-permute-start.6 = (f32[200,256]{1,0:T(8,128)S(1)}, f32[200,256]{1,0:T(8,128)S(1)}, u32[]{:S(2)}, u32[]{:S(2)}) collective-permute-start(f32[200,256]{1,0:T(8,128)S(1)} %get-tuple-element.110.carry_ref), channel_id=1, source_target_pairs={{8,0},{9,1},{10,2},{11,3},{12,4},{13,5},{14,6},{15,7},{24,16},{25,... | collective-permute-start | bytes 614408 | tf_op jit(solution)/shard_map/ppermute | solution.py:34
  16.2 2.2 %collective-permute-start.7 = (f32[200,256]{1,0:T(8,128)S(1)}, f32[200,256]{1,0:T(8,128)S(1)}, u32[]{:S(2)}, u32[]{:S(2)}) collective-permute-start(f32[200,256]{1,0:T(8,128)S(1)} %get-tuple-element.111.half_ref), channel_id=1, source_target_pairs={{0,1},{1,0},{2,3},{3,2},{4,5},{5,4},{6,7},{7,6},{8,9},{9,8},{10,11... | collective-permute-start | bytes 614408 | tf_op jit(solution)/shard_map/ppermute | solution.py:22
  18.6 5.2 %collective-permute-start.12 = (f32[32,512]{1,0:T(8,128)S(1)}, f32[32,512]{1,0:T(8,128)S(1)}, u32[]{:S(2)}, u32[]{:S(2)}) collective-permute-start(f32[32,512]{1,0:T(8,128)S(1)} %shard_map.106.up_ref), channel_id=1, source_target_pairs={{0,8},{1,9},{2,10},{3,11},{4,12},{5,13},{6,14},{7,15},{8,0},{9,1},... | collective-permute-start | bytes 196616 | tf_op jit(solution)/shard_map/ppermute | solution.py:22
  20.7 13.0 %collective-permute-start.19 = (f32[160,640]{1,0:T(8,128)S(1)}, f32[160,640]{1,0:T(8,128)S(1)}, u32[]{:S(2)}, u32[]{:S(2)}) collective-permute-start(f32[160,640]{1,0:T(8,128)S(1)} %get-tuple-element.162), channel_id=1, source_target_pairs={{0,2},{1,3},{2,0},{3,1},{4,6},{5,7},{6,4},{7,5},{8,10},{9,11},{10,... | collective-permute-start | bytes 1228808 | tf_op jit(solution)/shard_map/ppermute | solution.py:22
  22.5 1.5 %collective-permute-start.13 = (f32[200,256]{1,0:T(8,128)S(1)}, f32[200,256]{1,0:T(8,128)S(1)}, u32[]{:S(2)}, u32[]{:S(2)}) collective-permute-start(f32[200,256]{1,0:T(8,128)S(1)} %get-tuple-element.132.half_ref), channel_id=1, source_target_pairs={{0,1},{1,0},{2,3},{3,2},{4,5},{5,4},{6,7},{7,6},{8,9},{9,8},{10,11... | collective-permute-start | bytes 614408 | tf_op jit(solution)/shard_map/ppermute | solution.py:22
  22.5 4.7 %collective-permute-start.11 = (f32[72,256]{1,0:T(8,128)S(1)}, f32[72,256]{1,0:T(8,128)S(1)}, u32[]{:S(2)}, u32[]{:S(2)}) collective-permute-start(f32[72,256]{1,0:T(8,128)S(1)} %get-tuple-element.129.root_ref), channel_id=1, source_target_pairs={{0,8},{1,9},{2,10},{3,11},{4,12},{5,13},{6,14},{7,15},{8,0},{9,1},... | collective-permute-start | bytes 221192 | tf_op jit(solution)/shard_map/ppermute | solution.py:22
  24.2 5.2 %collective-permute-start.15 = (f32[32,256]{1,0:T(8,128)S(1)}, f32[32,256]{1,0:T(8,128)S(1)}, u32[]{:S(2)}, u32[]{:S(2)}) collective-permute-start(f32[32,256]{1,0:T(8,128)S(1)} %shard_map.109.up_ref), channel_id=1, source_target_pairs={{0,16},{1,17},{2,18},{3,19},{4,20},{5,21},{6,22},{7,23},{8,24},{9,... | collective-permute-start | bytes 98312 | tf_op jit(solution)/shard_map/ppermute | solution.py:22
  27.3 2.1 %collective-permute-start.14 = (f32[72,256]{1,0:T(8,128)S(1)}, f32[72,256]{1,0:T(8,128)S(1)}, u32[]{:S(2)}, u32[]{:S(2)}) collective-permute-start(f32[72,256]{1,0:T(8,128)S(1)} %shard_map.111.root_ref), channel_id=1, source_target_pairs={{0,1},{1,0},{2,3},{3,2},{4,5},{5,4},{6,7},{7,6},{8,9},{9,8},{10,11... | collective-permute-start | bytes 221192 | tf_op jit(solution)/shard_map/ppermute | solution.py:22
  30.1 5.3 %collective-permute-start.16 = (f32[32,512]{1,0:T(8,128)S(1)}, f32[32,512]{1,0:T(8,128)S(1)}, u32[]{:S(2)}, u32[]{:S(2)}) collective-permute-start(f32[32,512]{1,0:T(8,128)S(1)} %get-tuple-element.156), channel_id=1, source_target_pairs={{0,6},{1,7},{2,4},{3,5},{4,2},{5,3},{6,0},{7,1},{8,14},{9,15},{10,... | collective-permute-start | bytes 196616 | tf_op jit(solution)/shard_map/ppermute | solution.py:22
  32.5 4.3 %collective-permute-start.17 = (f32[32,512]{1,0:T(8,128)S(1)}, f32[32,512]{1,0:T(8,128)S(1)}, u32[]{:S(2)}, u32[]{:S(2)}) collective-permute-start(f32[32,512]{1,0:T(8,128)S(1)} %get-tuple-element.157), channel_id=1, source_target_pairs={{0,2},{1,3},{2,0},{3,1},{4,6},{5,7},{6,4},{7,5},{8,10},{9,11},{10,... | collective-permute-start | bytes 196616 | tf_op jit(solution)/shard_map/ppermute | solution.py:22
  33.2 4.3 %collective-permute-start.18 = (f32[32,512]{1,0:T(8,128)S(1)}, f32[32,512]{1,0:T(8,128)S(1)}, u32[]{:S(2)}, u32[]{:S(2)}) collective-permute-start(f32[32,512]{1,0:T(8,128)S(1)} %get-tuple-element.158), channel_id=1, source_target_pairs={{0,4},{1,5},{2,6},{3,7},{4,0},{5,1},{6,2},{7,3},{8,12},{9,13},{10,... | collective-permute-start | bytes 196616 | tf_op jit(solution)/shard_map/ppermute | solution.py:22
  37.5 1.6 %collective-permute-start.20 = (f32[128,512]{1,0:T(8,128)S(1)}, f32[128,512]{1,0:T(8,128)S(1)}, u32[]{:S(2)}, u32[]{:S(2)}) collective-permute-start(f32[128,512]{1,0:T(8,128)S(1)} %shard_map.117.group_ref), channel_id=1, source_target_pairs={{0,1},{1,0},{2,3},{3,2},{4,5},{5,4},{6,7},{7,6},{8,9},{9,8},{10,11... | collective-permute-start | bytes 786440 | tf_op jit(solution)/shard_map/ppermute | solution.py:22
  37.6 1.6 %collective-permute-start.21 = (f32[160,128]{1,0:T(8,128)S(1)}, f32[160,128]{1,0:T(8,128)S(1)}, u32[]{:S(2)}, u32[]{:S(2)}) collective-permute-start(f32[160,128]{1,0:T(8,128)S(1)} %get-tuple-element.175), channel_id=1, source_target_pairs={{0,1},{1,0},{2,3},{3,2},{4,5},{5,4},{6,7},{7,6},{8,9},{9,8},{10,11... | collective-permute-start | bytes 245768 | tf_op jit(solution)/shard_map/ppermute | solution.py:22
